TPU v7x, 32 devices: a whole 2x2x4 slice. The times are simulated.
32 devices in a mesh: groups: 2 (over x), chan: 16 (over z, y, core).
Axes of the slice: x: 2, y: 2, z: 4, core: 2. Of those that a mesh axis runs over, the one named last changes fastest.
Arguments:
- spectra: bfloat16 [2, 8, 512, 512], P(None, 'groups', 'chan'), parts along dimension 1, may hold values from -6 to 6
- filter_bank: float32 [2, 8, 65], replicated, may hold values from -0.5 to 0.5
- band_index: int32 [512], replicated, may hold values from 0 to 7
- window_mask: int32 [8, 512], P('groups', 'chan'), parts along dimension 0, may hold values 0 or 1
- owner_order: int32 [8], P('groups'), parts along dimension 0, may hold values from 0 to 15, as said below
- source_offset: int32 [8, 32], P('groups'), parts along dimension 0, may hold values from 0 to 31, each once within a row
Outputs:
- cross: bfloat16 [2, 256, 512, 512], P(None, 'groups', 'chan'), parts along dimension 1
There are 2 independent parts, one for each index of `groups`. A program takes and returns all parts, laid end to end along the dimension named above; an argument that names none is the same for every part. Nothing has to cross between parts.
Inputs may be any that keep to these rules, and one draw needn't show every extreme that they name: `owner_order`: 4 distinct device indices, below 16.
All inputs are finite; a program needn't handle non-finite values. No bound on the sum of `window_mask` on one device may be relied on, other than what follows from the above.
Results may differ from a plain program's by a relative error of at most 0.0057.
Values may be sent and summed in bfloat16 or wider, within the bound.
No kernel may reach another device: no remote copies, remote signals or barrier semaphores. Data moves between devices by JAX's collectives and lax.ppermute only.
A program may use at most 192 MiB of HBM per device.

v0:
```python
import functools

import jax
import jax.numpy as jnp
from jax import lax
from jax.experimental import pallas as pl
from jax.experimental.pallas import tpu as pltpu
from jax.sharding import PartitionSpec as P

SMOOTH = 17
LANES = 128
WATER = 0.05
SRC_STEP = 8
VMEM = pltpu.CompilerParams(vmem_limit_bytes=56 * 1024 * 1024)


def split_kernel(spectra_ref, piece_ref):
    _, win, _, freq = spectra_ref.shape
    tiles = freq // LANES
    for w in range(win):
        for t in range(tiles):
            piece_ref[w * tiles + t] = spectra_ref[:, w, :, t * LANES : (t + 1) * LANES]


def prep_kernel(bank_ref, whi_ref, wlo_ref, band_ref):
    banks = bank_ref.shape[1]
    ch = whi_ref.shape[0] // (2 * banks)

    def skewed(row):
        tile = jnp.broadcast_to(row, (ch, LANES))
        return pltpu.roll(tile, 0, 1, stride=1, stride_axis=0)

    for b in range(banks):
        real = skewed(bank_ref[0, b : b + 1, :])
        imag = skewed(bank_ref[1, b : b + 1, :])
        base = b * 2 * ch
        for row, left, right in ((base, real, -imag), (base + ch, imag, real)):
            for col, val in ((0, left), (LANES, right)):
                high = val.astype(jnp.bfloat16)
                low = (val - high.astype(jnp.float32)).astype(jnp.bfloat16)
                whi_ref[row : row + ch, col : col + LANES] = high
                wlo_ref[row : row + ch, col : col + LANES] = low
    rows = lax.broadcasted_iota(jnp.int32, band_ref.shape, 0)
    cols = lax.broadcasted_iota(jnp.int32, band_ref.shape, 1)
    near = jnp.abs(rows - cols) <= SMOOTH // 2
    band_ref[...] = jnp.where(near, 1.0, 0.0).astype(jnp.bfloat16)


def filtered_block(x, whi_ref, wlo_ref, index, ch):
    banks = whi_ref.shape[0] // (2 * ch)
    y = jnp.dot(whi_ref[...], x, preferred_element_type=jnp.float32)
    y = y + jnp.dot(wlo_ref[...], x, preferred_element_type=jnp.float32)
    pick = y[: 2 * ch]
    for b in range(1, banks):
        pick = jnp.where(index == b, y[b * 2 * ch : (b + 1) * 2 * ch], pick)
    return pick


def whitened_block(real, imag, flags, band_ref):
    count = real.shape[0]
    power = real * real + imag * imag
    high = power.astype(jnp.bfloat16)
    low = (power - high.astype(jnp.float32)).astype(jnp.bfloat16)
    total = jnp.dot(high, band_ref[...], preferred_element_type=jnp.float32)
    total = total + jnp.dot(low, band_ref[...], preferred_element_type=jnp.float32)
    rows = lax.broadcasted_iota(jnp.int32, (count, count), 0)
    cols = lax.broadcasted_iota(jnp.int32, (count, count), 1)
    valid = jnp.sum(jnp.where(rows == cols, flags, 0.0), axis=1, keepdims=True)
    scale = lax.rsqrt(total / SMOOTH + WATER) * valid
    real = (real * scale).astype(jnp.bfloat16).astype(jnp.float32)
    imag = (imag * scale).astype(jnp.bfloat16).astype(jnp.float32)
    return real, imag


def source_kernel(piece_id_ref, owner_ref, x_ref, whi_ref, wlo_ref, index_ref, out_ref):
    n_chan, _, _, ch, _ = x_ref.shape
    rounds = out_ref.shape[1]
    tiles = index_ref.shape[0]
    tile = lax.rem(piece_id_ref[0] + pl.program_id(0), tiles)
    zero = jnp.zeros((), jnp.bfloat16)
    gap = jnp.zeros((LANES - 3 * ch, LANES), jnp.bfloat16)
    columns = []
    for r in range(rounds):
        block = owner_ref[r]
        before = jnp.maximum(block - 1, 0)
        after = jnp.minimum(block + 1, n_chan - 1)
        parts = []
        for p in range(2):
            parts.append(jnp.where(block > 0, x_ref[before, 0, p], zero))
            parts.append(x_ref[block, 0, p])
            parts.append(jnp.where(block < n_chan - 1, x_ref[after, 0, p], zero))
            parts.append(gap)
        columns.append(jnp.concatenate(parts, axis=0))
    x = jnp.concatenate(columns, axis=1)
    index = jnp.concatenate([index_ref[tile]] * rounds, axis=1)
    pick = filtered_block(x, whi_ref, wlo_ref, index, ch).astype(jnp.bfloat16)
    for r in range(rounds):
        for p in range(2):
            out_ref[0, r, p] = pick[p * ch : (p + 1) * ch, r * LANES : (r + 1) * LANES]


def own_kernel(
    prev_ref, cur_ref, next_ref, whi_ref, wlo_ref, band_ref, index_ref, flags_ref, out_ref, filt_ref
):
    _, win, ch, freq = cur_ref.shape
    gap = jnp.zeros((LANES - 3 * ch, freq), jnp.bfloat16)

    def one_window(w, _):
        parts = []
        for p in range(2):
            parts += [prev_ref[p, w], cur_ref[p, w], next_ref[p, w], gap]
        x = jnp.concatenate(parts, axis=0)
        pick = filtered_block(x, whi_ref, wlo_ref, index_ref[...], ch)
        at = pl.ds(pl.multiple_of(w * ch, ch), ch)
        filt_ref[0, at, :] = pick[:ch]
        filt_ref[1, at, :] = pick[ch:]
        return 0

    lax.fori_loop(0, win, one_window, 0)
    flags = flags_ref[...].astype(jnp.float32)
    real, imag = whitened_block(filt_ref[0], filt_ref[1], flags, band_ref)
    for t in range(freq // LANES):
        out_ref[0, t] = real[:, t * LANES : (t + 1) * LANES]
        out_ref[1, t] = imag[:, t * LANES : (t + 1) * LANES]


def cross_kernel(
    owner_ref, offset_ref, filt_ref, local_ref, band_ref, flags_ref, out_ref, source_ref
):
    pieces, _, _, ch, _ = filt_ref.shape
    tiles = local_ref.shape[1]
    win = pieces // tiles
    per_round = ch // SRC_STEP
    step = pl.program_id(0)
    r = step // per_round
    j0 = lax.rem(step, per_round) * SRC_STEP

    @pl.when(j0 == 0)
    def _():
        parts = []
        for p in range(2):
            rows = [
                jnp.concatenate([filt_ref[w * tiles + t, 0, p] for t in range(tiles)], axis=1)
                for w in range(win)
            ]
            parts.append(jnp.concatenate(rows, axis=0).astype(jnp.float32))
        flags = flags_ref[owner_ref[r]].astype(jnp.float32)
        real, imag = whitened_block(parts[0], parts[1], flags, band_ref)
        for t in range(tiles):
            source_ref[0, t] = real[:, t * LANES : (t + 1) * LANES] / win
            source_ref[1, t] = imag[:, t * LANES : (t + 1) * LANES] / win

    def one_tile(ft, _):
        at = pl.ds(pl.multiple_of(ft * LANES, LANES), LANES)
        mine = [
            (local_ref[0, ft, w * ch : (w + 1) * ch, :], local_ref[1, ft, w * ch : (w + 1) * ch, :])
            for w in range(win)
        ]
        for j in range(SRC_STEP):
            row = offset_ref[r, j0 + j]
            re = im = None
            for w in range(win):
                sr = source_ref[0, ft, pl.ds(w * ch + row, 8, stride=0), :]
                si = source_ref[1, ft, pl.ds(w * ch + row, 8, stride=0), :]
                sr = jnp.concatenate([sr] * (ch // 8), axis=0)
                si = jnp.concatenate([si] * (ch // 8), axis=0)
                lr, li = mine[w]
                a = sr * lr + si * li
                b = sr * li - si * lr
                re = a if re is None else re + a
                im = b if im is None else im + b
            out_ref[0, j, :, at] = re.astype(jnp.bfloat16)
            out_ref[1, j, :, at] = im.astype(jnp.bfloat16)
        return 0

    lax.fori_loop(0, tiles, one_tile, 0)


def body(spectra, filter_bank, band_index, window_mask, owner_order, source_offset):
    n_chan = lax.axis_size("chan")
    me = lax.axis_index("chan").astype(jnp.int32)
    _, win, ch, freq = spectra.shape
    banks, taps = filter_bank.shape[1:]
    rounds = owner_order.shape[0]
    count = win * ch
    tiles = freq // LANES
    pieces = win * tiles
    sources = rounds * ch
    smem = pl.BlockSpec(memory_space=pltpu.SMEM)
    vmem = pl.BlockSpec(memory_space=pltpu.VMEM)

    split = pl.pallas_call(
        split_kernel,
        out_shape=jax.ShapeDtypeStruct((pieces, 2, ch, LANES), jnp.bfloat16),
        name="split",
    )(spectra)
    if n_chan == pieces:
        held = lax.all_to_all(split, "chan", 0, 0)[:, None]
        first = me
    else:
        held = lax.all_gather(split, "chan")
        first = jnp.int32(0)

    ends = n_chan - 1
    before = lax.ppermute(spectra, "chan", [(i, i + 1) for i in range(ends)])
    after = lax.ppermute(spectra, "chan", [(i + 1, i) for i in range(ends)])
    flags = window_mask.reshape(1, count)
    all_flags = lax.all_gather(flags, "chan")

    padded_bank = jnp.pad(filter_bank, ((0, 0), (0, 0), (0, LANES - taps)))
    weights = jax.ShapeDtypeStruct((banks * 2 * ch, 2 * LANES), jnp.bfloat16)
    whi, wlo, band = pl.pallas_call(
        prep_kernel,
        out_shape=(weights, weights, jax.ShapeDtypeStruct((freq, freq), jnp.bfloat16)),
        name="prep",
    )(padded_bank)

    count_here = held.shape[1]
    filtered = pl.pallas_call(
        source_kernel,
        grid=(count_here,),
        in_specs=[
            smem,
            smem,
            pl.BlockSpec((n_chan, 1, 2, ch, LANES), lambda s: (0, s, 0, 0, 0)),
            vmem,
            vmem,
            vmem,
        ],
        out_specs=pl.BlockSpec((1, rounds, 2, ch, LANES), lambda s: (s, 0, 0, 0, 0)),
        out_shape=jax.ShapeDtypeStruct((count_here, rounds, 2, ch, LANES), jnp.bfloat16),
        compiler_params=VMEM,
        name="source_filter",
    )(first[None], owner_order, held, whi, wlo, band_index.reshape(tiles, 1, LANES))
    if n_chan == pieces:
        filtered = lax.all_gather(filtered, "chan", tiled=True)

    local = pl.pallas_call(
        own_kernel,
        out_shape=jax.ShapeDtypeStruct((2, tiles, count, LANES), jnp.float32),
        in_specs=[vmem] * 8,
        out_specs=vmem,
        scratch_shapes=[pltpu.VMEM((2, count, freq), jnp.float32)],
        compiler_params=VMEM,
        cost_estimate=pl.CostEstimate(
            flops=4 * banks * 2 * ch * 2 * LANES * win * freq, bytes_accessed=3 << 20, transcendentals=0
        ),
        name="own_whiten",
    )(before, spectra, after, whi, wlo, band, band_index.reshape(1, freq), flags)

    per_round = ch // SRC_STEP
    return pl.pallas_call(
        cross_kernel,
        grid=(sources // SRC_STEP,),
        in_specs=[
            smem,
            smem,
            pl.BlockSpec((pieces, 1, 2, ch, LANES), lambda s: (0, s // per_round, 0, 0, 0)),
            vmem,
            vmem,
            vmem,
        ],
        out_specs=pl.BlockSpec((2, SRC_STEP, ch, freq), lambda s: (0, s, 0, 0)),
        out_shape=jax.ShapeDtypeStruct((2, sources, ch, freq), jnp.bfloat16),
        scratch_shapes=[pltpu.VMEM((2, tiles, count, LANES), jnp.float32)],
        compiler_params=VMEM,
        name="cross",
    )(owner_order, source_offset, filtered, local, band, all_flags)


def solution(mesh):
    in_specs = (
        P(None, "groups", "chan", None),
        P(),
        P(),
        P("groups", "chan"),
        P("groups"),
        P("groups", None),
    )
    out_specs = P(None, "groups", "chan", None)
    return jax.shard_map(body, mesh=mesh, in_specs=in_specs, out_specs=out_specs, check_vma=False)
```

profile of v0, /device:TPU:0, one launch (start us, length us, event | category | flops | bytes accessed | tf_op | source)
XLA Modules:
  0.0 87.6 jit_solution(13899034928764118233)
XLA Ops:
  6.5 1.7 %split.1 = bf16[16,2,32,128]{3,2,1,0:T(8,128)(2,1)} custom-call(bf16[2,4,32,512]{3,2,1,0:T(8,128)(2,1)} %cur_ref.1), custom_call_target="tpu_custom_call" | custom-call | tf_op jit(solution)/shard_map/split/pallas_call | solution.py:192
  8.2 7.4 %all-to-all-start = ((bf16[16,2,32,128]{3,2,1,0:T(8,128)(2,1)}), bf16[16,2,32,128]{3,2,1,0:T(8,128)(2,1)S(1)}, u32[]{:S(2)}, u32[]{:S(2)}) async-start(bf16[16,2,32,128]{3,2,1,0:T(8,128)(2,1)} %split.1), calls=%async_computation | async-start | bytes 524288 | tf_op jit(solution)/shard_map/all_to_all | solution.py:198
  15.6 0.0 all-gather.2.cloned.1.call-start
  15.7 1.3 %pad.4.bank_ref = f32[2,8,128]{2,1,0:T(8,128)} pad(f32[2,8,65]{2,1,0:T(8,128)} %param.7, f32[]{:T(128)} %constant.6.clone.1), padding=0_0x0_0x0_63 | pad | bytes 12356 | tf_op jit(solution)/shard_map/jit(_pad)/pad | solution.py:210
  17.0 1.9 %prep.1 = (bf16[512,256]{1,0:T(8,128)(2,1)}, bf16[512,256]{1,0:T(8,128)(2,1)}, bf16[512,512]{1,0:T(8,128)(2,1)}) custom-call(f32[2,8,128]{2,1,0:T(8,128)} %pad.4.bank_ref), custom_call_target="tpu_custom_call" | custom-call | tf_op jit(solution)/shard_map/prep/pallas_call | solution.py:212
  18.8 6.8 %all-to-all-done = bf16[16,2,32,128]{3,2,1,0:T(8,128)(2,1)S(1)} async-done(((bf16[16,2,32,128]{3,2,1,0:T(8,128)(2,1)}), bf16[16,2,32,128]{3,2,1,0:T(8,128)(2,1)S(1)}, u32[]{:S(2)}, u32[]{:S(2)}) %all-to-all-start) | async-done | bytes 262176 | tf_op jit(solution)/shard_map/all_to_all | solution.py:198
  25.7 0.0 copy-start
  25.7 0.7 copy-done
  26.4 2.2 %source_filter.1 = bf16[1,4,2,32,128]{4,3,2,1,0:T(8,128)(2,1)} custom-call(s32[1]{0:T(128)} %bitcast.piece_id_ref, s32[4]{0:T(128)} %owner_ref.3, bf16[16,1,2,32,128]{4,3,2,1,0:T(8,128)(2,1)} %bitcast.4, bf16[512,256]{1,0:T(8,128)(2,1)} %get-tuple-element.8.whi_ref, bf16[512,256]{1,0:T(8,128)(2,1)} %get-tuple-element.9.wlo_ref, s32[4,1,128]{2,1,0:T(1,128)} %bitcast.5), custom_call_target="tpu_custom_call" | custom-call | tf_op jit(solution)/shard_map/source_filter/pallas_call | solution.py:219
  28.6 0.0 all-gather.2.cloned.1.call-update
  28.6 1.8 %collective-permute-start = (bf16[2,4,32,512]{3,2,1,0:T(8,128)(2,1)}, bf16[2,4,32,512]{3,2,1,0:T(8,128)(2,1)S(1)}, u32[]{:S(2)}, u32[]{:S(2)}) collective-permute-start(bf16[2,4,32,512]{3,2,1,0:T(8,128)(2,1)} %cur_ref.1), channel_id=1, source_target_pairs={{0,1},{1,2},{2,3},{3,4},{4,5},{5,6},{6,7},{7,8},{8,9},{9,10},{10,1... | collective-permute-start | bytes 786440 | tf_op jit(solution)/shard_map/ppermute | solution.py:205
  30.4 1.3 %collective-permute-start.1 = (bf16[2,4,32,512]{3,2,1,0:T(8,128)(2,1)}, bf16[2,4,32,512]{3,2,1,0:T(8,128)(2,1)S(1)}, u32[]{:S(2)}, u32[]{:S(2)}) collective-permute-start(bf16[2,4,32,512]{3,2,1,0:T(8,128)(2,1)} %cur_ref.1), channel_id=1, source_target_pairs={{1,0},{2,1},{3,2},{4,3},{5,4},{6,5},{7,6},{8,7},{9,8},{10,9},{11,1... | collective-permute-start | bytes 786440 | tf_op jit(solution)/shard_map/ppermute | solution.py:206
  31.7 0.8 all_gather_reshape.3
  32.4 1.2 %reshape.11.flags_ref = s32[1,128]{1,0:T(1,128)} reshape(s32[4,32]{1,0:T(4,128)} %param.9) | data formatting | bytes 1024 | tf_op jit(solution)/shard_map/reshape | solution.py:207
  33.7 22.3 %all_gather.7.flags_ref = s32[16,1,128]{2,1,0:T(1,128)} all-gather(s32[1,1,128]{2,1,0:T(1,128)S(1)} %all_gather_reshape.3), channel_id=1, replica_groups=mesh['groups'=2,'chan'=16] {'chan'}, dimensions={0}, use_global_device_ids=true | all-gather | bytes 8704 | tf_op jit(solution)/shard_map/all_gather | solution.py:208
  56.0 0.0 collective-permute-done.prev_ref
  56.0 0.0 copy-start.1
  56.0 0.0 collective-permute-done.1.next_ref
  56.0 0.0 copy-start.2
  56.0 0.7 copy-done.1
  56.7 0.1 copy-done.2
  56.8 4.3 %own_whiten.1.local_ref = f32[2,4,128,128]{3,2,1,0:T(8,128)} custom-call(bf16[2,4,32,512]{3,2,1,0:T(8,128)(2,1)} %copy-done.1, bf16[2,4,32,512]{3,2,1,0:T(8,128)(2,1)} %cur_ref.1, bf16[2,4,32,512]{3,2,1,0:T(8,128)(2,1)} %copy-done.2, bf16[512,256]{1,0:T(8,128)(2,1)} %get-tuple-element.8.whi_ref, bf16[512,256]{1,0:T(8,128)(2,1)} %get-tuple-element.9.wlo_ref, ...), custom_call_target="tpu_custom_call" | custom-call | flops 1073741824 | bytes 3145728 | tf_op jit(solution)/shard_map/own_whiten/pallas_call | solution.py:238
  61.1 3.9 %all-gather.2.cloned.1.call-done.filt_ref = bf16[16,4,2,32,128]{4,3,2,1,0:T(8,128)(2,1)} async-done(((bf16[1,4,2,32,128]{4,3,2,1,0:T(8,128)(2,1)}), bf16[16,4,2,32,128]{4,3,2,1,0:T(8,128)(2,1)}) %all-gather.2.cloned.1.call-update) | async-done | bytes 1048592 | tf_op jit(solution)/shard_map/all_gather | solution.py:236
  65.0 15.8 %cross.1 = bf16[2,128,32,512]{3,2,1,0:T(8,128)(2,1)} custom-call(s32[4]{0:T(128)} %owner_ref.3, s32[4,32]{1,0:T(4,128)} %offset_ref.1, bf16[16,4,2,32,128]{4,3,2,1,0:T(8,128)(2,1)} %all-gather.2.cloned.1.call-done.filt_ref, f32[2,4,128,128]{3,2,1,0:T(8,128)} %own_whiten.1.local_ref, bf16[512,512]{1,0:T(8,128)(2,1)} %get-tuple-element.10.band_ref, ...), custom_call_target="tpu_custom_call" | custom-call | tf_op jit(solution)/shard_map/cross/pallas_call | solution.py:252
Async XLA Ops:
  8.2 17.4 %all-to-all-start = ((bf16[16,2,32,128]{3,2,1,0:T(8,128)(2,1)}), bf16[16,2,32,128]{3,2,1,0:T(8,128)(2,1)S(1)}, u32[]{:S(2)}, u32[]{:S(2)}) async-start(bf16[16,2,32,128]{3,2,1,0:T(8,128)(2,1)} %split.1), calls=%async_computation | async-start | bytes 524288 | tf_op jit(solution)/shard_map/all_to_all | solution.py:198
  15.6 49.3 %all-gather.2.cloned.1.call-start = ((), (), s32[]{:S(2)}) async-start(), calls=%async_computation.1 | async-start | bytes 1114112 | tf_op jit(solution)/shard_map/all_gather | solution.py:236
  25.7 0.7 copy-start
  28.6 27.4 %collective-permute-start = (bf16[2,4,32,512]{3,2,1,0:T(8,128)(2,1)}, bf16[2,4,32,512]{3,2,1,0:T(8,128)(2,1)S(1)}, u32[]{:S(2)}, u32[]{:S(2)}) collective-permute-start(bf16[2,4,32,512]{3,2,1,0:T(8,128)(2,1)} %cur_ref.1), channel_id=1, source_target_pairs={{0,1},{1,2},{2,3},{3,4},{4,5},{5,6},{6,7},{7,8},{8,9},{9,10},{10,1... | collective-permute-start | bytes 786440 | tf_op jit(solution)/shard_map/ppermute | solution.py:205
  30.4 25.7 %collective-permute-start.1 = (bf16[2,4,32,512]{3,2,1,0:T(8,128)(2,1)}, bf16[2,4,32,512]{3,2,1,0:T(8,128)(2,1)S(1)}, u32[]{:S(2)}, u32[]{:S(2)}) collective-permute-start(bf16[2,4,32,512]{3,2,1,0:T(8,128)(2,1)} %cur_ref.1), channel_id=1, source_target_pairs={{1,0},{2,1},{3,2},{4,3},{5,4},{6,5},{7,6},{8,7},{9,8},{10,9},{11,1... | collective-permute-start | bytes 786440 | tf_op jit(solution)/shard_map/ppermute | solution.py:206
  56.0 0.7 copy-start.1
  56.0 0.8 copy-start.2
Sparse Core Ops, SparseCore 0:
  28.7 36.2 all-gather.1
where the time goes:
time: 88.2 us; the launch traced here: 87.6 us
  Pallas kernels  25.8 us (29%)
  blocking collectives  22.3 us (25%)
  between operations  13.4 us (15%)
  waiting for transfers between devices  10.7 us (12%)
  starting transfers between devices  10.5 us (12%)
  local copies, waits for them, and re-layouts  4.77 us (5%)
    all_gather x1, blocking collectives, body(): all_flags = lax.all_gather(flags, 'chan')  22.3 us
    pallas_call x1, Pallas kernels, body(): pl.pallas_call(cross_kernel, grid=(sources // SRC_STEP,), in_specs=[smem,...  15.8 us
    all_to_all x1, starting transfers between devices, body(): held = lax.all_to_all(split, 'chan', 0, 0)[:, None]  7.39 us
    all_to_all x1, waiting for transfers between devices, body(): held = lax.all_to_all(split, 'chan', 0, 0)[:, None]  6.84 us
    pallas_call x1, Pallas kernels, body(): pl.pallas_call(own_kernel, out_shape=jax.ShapeDtypeStruct((2, tiles, coun...  4.3 us
    all_gather x1, waiting for transfers between devices, body(): filtered = lax.all_gather(filtered, 'chan', tiled=True)  3.85 us
    pallas_call x1, Pallas kernels, body(): pl.pallas_call(source_kernel, grid=(count_here,), in_specs=[smem, smem, p...  2.19 us
    pallas_call x1, Pallas kernels, body(): pl.pallas_call(prep_kernel, out_shape=(weights, weights, jax.ShapeDtypeSt...  1.86 us
  transfers between devices with their start and end apart: 4, of which 2 were waited for; matrix products, arithmetic and copies ran while one was open for 4% of the time, Pallas kernels for 7%

commit v1 on v0

--- a/solution.py
+++ b/solution.py
@@ -14,25 +14,33 @@
 VMEM = pltpu.CompilerParams(vmem_limit_bytes=56 * 1024 * 1024)
 
 
-def split_kernel(spectra_ref, piece_ref):
-    _, win, _, freq = spectra_ref.shape
+def split_kernel(spectra_ref, flags_ref, piece_ref):
+    _, win, ch, freq = spectra_ref.shape
     tiles = freq // LANES
+    extra = piece_ref.shape[1] - 2 * ch
     for w in range(win):
+        flags = jnp.broadcast_to(flags_ref[w : w + 1, :], (extra, ch)).astype(jnp.float32)
         for t in range(tiles):
-            piece_ref[w * tiles + t] = spectra_ref[:, w, :, t * LANES : (t + 1) * LANES]
-
-
-def prep_kernel(bank_ref, whi_ref, wlo_ref, band_ref):
-    banks = bank_ref.shape[1]
+            at = slice(t * LANES, (t + 1) * LANES)
+            piece_ref[w * tiles + t, :ch] = spectra_ref[0, w, :, at]
+            piece_ref[w * tiles + t, ch : 2 * ch] = spectra_ref[1, w, :, at]
+            piece_ref[w * tiles + t, 2 * ch :] = jnp.zeros((extra, LANES), jnp.bfloat16)
+            piece_ref[w * tiles + t, 2 * ch :, :ch] = flags.astype(jnp.bfloat16)
+
+
+def prep_kernel(bank_ref, whi_ref, wlo_ref, band_ref, padded_ref):
+    _, banks, taps = bank_ref.shape
     ch = whi_ref.shape[0] // (2 * banks)
+    padded_ref[...] = jnp.zeros(padded_ref.shape, jnp.float32)
+    padded_ref[:, :, :taps] = bank_ref[...]
 
     def skewed(row):
         tile = jnp.broadcast_to(row, (ch, LANES))
         return pltpu.roll(tile, 0, 1, stride=1, stride_axis=0)
 
     for b in range(banks):
-        real = skewed(bank_ref[0, b : b + 1, :])
-        imag = skewed(bank_ref[1, b : b + 1, :])
+        real = skewed(padded_ref[0, b : b + 1, :])
+        imag = skewed(padded_ref[1, b : b + 1, :])
         base = b * 2 * ch
         for row, left, right in ((base, real, -imag), (base + ch, imag, real)):
             for col, val in ((0, left), (LANES, right)):
@@ -46,6 +54,13 @@
     band_ref[...] = jnp.where(near, 1.0, 0.0).astype(jnp.bfloat16)
 
 
+def flag_column(row):
+    ch = row.shape[1]
+    rows = lax.broadcasted_iota(jnp.int32, (ch, ch), 0)
+    cols = lax.broadcasted_iota(jnp.int32, (ch, ch), 1)
+    return jnp.sum(jnp.where(rows == cols, row.astype(jnp.float32), 0.0), axis=1, keepdims=True)
+
+
 def filtered_block(x, whi_ref, wlo_ref, index, ch):
     banks = whi_ref.shape[0] // (2 * ch)
     y = jnp.dot(whi_ref[...], x, preferred_element_type=jnp.float32)
@@ -56,25 +71,21 @@
     return pick
 
 
-def whitened_block(real, imag, flags, band_ref):
-    count = real.shape[0]
+def whitened_block(real, imag, band_ref):
     power = real * real + imag * imag
     high = power.astype(jnp.bfloat16)
     low = (power - high.astype(jnp.float32)).astype(jnp.bfloat16)
     total = jnp.dot(high, band_ref[...], preferred_element_type=jnp.float32)
     total = total + jnp.dot(low, band_ref[...], preferred_element_type=jnp.float32)
-    rows = lax.broadcasted_iota(jnp.int32, (count, count), 0)
-    cols = lax.broadcasted_iota(jnp.int32, (count, count), 1)
-    valid = jnp.sum(jnp.where(rows == cols, flags, 0.0), axis=1, keepdims=True)
-    scale = lax.rsqrt(total / SMOOTH + WATER) * valid
+    scale = lax.rsqrt(total / SMOOTH + WATER)
     real = (real * scale).astype(jnp.bfloat16).astype(jnp.float32)
     imag = (imag * scale).astype(jnp.bfloat16).astype(jnp.float32)
     return real, imag
 
 
 def source_kernel(piece_id_ref, owner_ref, x_ref, whi_ref, wlo_ref, index_ref, out_ref):
-    n_chan, _, _, ch, _ = x_ref.shape
-    rounds = out_ref.shape[1]
+    n_chan = x_ref.shape[0]
+    _, rounds, _, ch, _ = out_ref.shape
     tiles = index_ref.shape[0]
     tile = lax.rem(piece_id_ref[0] + pl.program_id(0), tiles)
     zero = jnp.zeros((), jnp.bfloat16)
@@ -86,17 +97,21 @@
         after = jnp.minimum(block + 1, n_chan - 1)
         parts = []
         for p in range(2):
-            parts.append(jnp.where(block > 0, x_ref[before, 0, p], zero))
-            parts.append(x_ref[block, 0, p])
-            parts.append(jnp.where(block < n_chan - 1, x_ref[after, 0, p], zero))
+            at = slice(p * ch, (p + 1) * ch)
+            parts.append(jnp.where(block > 0, x_ref[before, 0, at], zero))
+            parts.append(x_ref[block, 0, at])
+            parts.append(jnp.where(block < n_chan - 1, x_ref[after, 0, at], zero))
             parts.append(gap)
         columns.append(jnp.concatenate(parts, axis=0))
     x = jnp.concatenate(columns, axis=1)
     index = jnp.concatenate([index_ref[tile]] * rounds, axis=1)
-    pick = filtered_block(x, whi_ref, wlo_ref, index, ch).astype(jnp.bfloat16)
+    pick = filtered_block(x, whi_ref, wlo_ref, index, ch)
     for r in range(rounds):
+        flags = x_ref[owner_ref[r], 0, 2 * ch :].astype(jnp.float32)[:1, :ch]
+        valid = flag_column(flags)
         for p in range(2):
-            out_ref[0, r, p] = pick[p * ch : (p + 1) * ch, r * LANES : (r + 1) * LANES]
+            part = pick[p * ch : (p + 1) * ch, r * LANES : (r + 1) * LANES] * valid
+            out_ref[0, r, p] = part.astype(jnp.bfloat16)
 
 
 def own_kernel(
@@ -117,17 +132,18 @@
         return 0
 
     lax.fori_loop(0, win, one_window, 0)
-    flags = flags_ref[...].astype(jnp.float32)
-    real, imag = whitened_block(filt_ref[0], filt_ref[1], flags, band_ref)
+    valid = jnp.concatenate([flag_column(flags_ref[w : w + 1, :]) for w in range(win)], axis=0)
+    real, imag = whitened_block(filt_ref[0] * valid, filt_ref[1] * valid, band_ref)
     for t in range(freq // LANES):
         out_ref[0, t] = real[:, t * LANES : (t + 1) * LANES]
         out_ref[1, t] = imag[:, t * LANES : (t + 1) * LANES]
 
 
-def cross_kernel(
-    owner_ref, offset_ref, filt_ref, local_ref, band_ref, flags_ref, out_ref, source_ref
-):
-    pieces, _, _, ch, _ = filt_ref.shape
+def cross_kernel(me_ref, offset_ref, *refs, masks):
+    filt_refs = refs[: len(masks)]
+    local_ref, band_ref, out_ref, piece_ref, source_ref = refs[len(masks) :]
+    ch = out_ref.shape[2]
+    pieces = piece_ref.shape[0]
     tiles = local_ref.shape[1]
     win = pieces // tiles
     per_round = ch // SRC_STEP
@@ -137,15 +153,18 @@
 
     @pl.when(j0 == 0)
     def _():
+        stride = pieces // filt_refs[0].shape[0]
+        for mask, ref in zip(masks, filt_refs):
+            for k in range(ref.shape[0]):
+                piece_ref[me_ref[0] ^ (mask ^ (k * stride))] = ref[k, 0]
         parts = []
         for p in range(2):
             rows = [
-                jnp.concatenate([filt_ref[w * tiles + t, 0, p] for t in range(tiles)], axis=1)
+                jnp.concatenate([piece_ref[w * tiles + t, p] for t in range(tiles)], axis=1)
                 for w in range(win)
             ]
             parts.append(jnp.concatenate(rows, axis=0).astype(jnp.float32))
-        flags = flags_ref[owner_ref[r]].astype(jnp.float32)
-        real, imag = whitened_block(parts[0], parts[1], flags, band_ref)
+        real, imag = whitened_block(parts[0], parts[1], band_ref)
         for t in range(tiles):
             source_ref[0, t] = real[:, t * LANES : (t + 1) * LANES] / win
             source_ref[1, t] = imag[:, t * LANES : (t + 1) * LANES] / win
@@ -176,6 +195,16 @@
     lax.fori_loop(0, tiles, one_tile, 0)
 
 
+def spread(part, n_chan):
+    def swap(x, mask):
+        return lax.ppermute(x, "chan", [(i, i ^ mask) for i in range(n_chan)])
+
+    column = jnp.concatenate([part] + [swap(part, m) for m in range(4, n_chan, 4)], axis=0)
+    far = swap(column, 2)
+    beside = swap(column, 1)
+    return (0, 2, 1, 3), (column, far, beside, swap(far, 1))
+
+
 def body(spectra, filter_bank, band_index, window_mask, owner_order, source_offset):
     n_chan = lax.axis_size("chan")
     me = lax.axis_index("chan").astype(jnp.int32)
@@ -186,15 +215,16 @@
     tiles = freq // LANES
     pieces = win * tiles
     sources = rounds * ch
+    in_parts = n_chan == pieces and n_chan >= 4 and n_chan & (n_chan - 1) == 0
     smem = pl.BlockSpec(memory_space=pltpu.SMEM)
     vmem = pl.BlockSpec(memory_space=pltpu.VMEM)
 
     split = pl.pallas_call(
         split_kernel,
-        out_shape=jax.ShapeDtypeStruct((pieces, 2, ch, LANES), jnp.bfloat16),
+        out_shape=jax.ShapeDtypeStruct((pieces, 2 * ch + 16, LANES), jnp.bfloat16),
         name="split",
-    )(spectra)
-    if n_chan == pieces:
+    )(spectra, window_mask)
+    if in_parts:
         held = lax.all_to_all(split, "chan", 0, 0)[:, None]
         first = me
     else:
@@ -204,16 +234,15 @@
     ends = n_chan - 1
     before = lax.ppermute(spectra, "chan", [(i, i + 1) for i in range(ends)])
     after = lax.ppermute(spectra, "chan", [(i + 1, i) for i in range(ends)])
-    flags = window_mask.reshape(1, count)
-    all_flags = lax.all_gather(flags, "chan")
-
-    padded_bank = jnp.pad(filter_bank, ((0, 0), (0, 0), (0, LANES - taps)))
+    held, before, after = lax.optimization_barrier((held, before, after))
+
     weights = jax.ShapeDtypeStruct((banks * 2 * ch, 2 * LANES), jnp.bfloat16)
     whi, wlo, band = pl.pallas_call(
         prep_kernel,
         out_shape=(weights, weights, jax.ShapeDtypeStruct((freq, freq), jnp.bfloat16)),
+        scratch_shapes=[pltpu.VMEM((2, banks, LANES), jnp.float32)],
         name="prep",
-    )(padded_bank)
+    )(filter_bank)
 
     count_here = held.shape[1]
     filtered = pl.pallas_call(
@@ -222,7 +251,7 @@
         in_specs=[
             smem,
             smem,
-            pl.BlockSpec((n_chan, 1, 2, ch, LANES), lambda s: (0, s, 0, 0, 0)),
+            pl.BlockSpec((n_chan, 1, 2 * ch + 16, LANES), lambda s: (0, s, 0, 0)),
             vmem,
             vmem,
             vmem,
@@ -232,8 +261,12 @@
         compiler_params=VMEM,
         name="source_filter",
     )(first[None], owner_order, held, whi, wlo, band_index.reshape(tiles, 1, LANES))
-    if n_chan == pieces:
-        filtered = lax.all_gather(filtered, "chan", tiled=True)
+    if in_parts:
+        masks, filtered = spread(filtered, n_chan)
+        base = me
+    else:
+        masks, filtered = (0,), (filtered,)
+        base = jnp.int32(0)
 
     local = pl.pallas_call(
         own_kernel,
@@ -246,26 +279,27 @@
             flops=4 * banks * 2 * ch * 2 * LANES * win * freq, bytes_accessed=3 << 20, transcendentals=0
         ),
         name="own_whiten",
-    )(before, spectra, after, whi, wlo, band, band_index.reshape(1, freq), flags)
+    )(before, spectra, after, whi, wlo, band, band_index.reshape(1, freq), window_mask)
 
     per_round = ch // SRC_STEP
     return pl.pallas_call(
-        cross_kernel,
+        functools.partial(cross_kernel, masks=masks),
         grid=(sources // SRC_STEP,),
-        in_specs=[
-            smem,
-            smem,
-            pl.BlockSpec((pieces, 1, 2, ch, LANES), lambda s: (0, s // per_round, 0, 0, 0)),
-            vmem,
-            vmem,
-            vmem,
-        ],
+        in_specs=[smem, smem]
+        + [
+            pl.BlockSpec((f.shape[0], 1, 2, ch, LANES), lambda s: (0, s // per_round, 0, 0, 0))
+            for f in filtered
+        ]
+        + [vmem, vmem],
         out_specs=pl.BlockSpec((2, SRC_STEP, ch, freq), lambda s: (0, s, 0, 0)),
         out_shape=jax.ShapeDtypeStruct((2, sources, ch, freq), jnp.bfloat16),
-        scratch_shapes=[pltpu.VMEM((2, tiles, count, LANES), jnp.float32)],
+        scratch_shapes=[
+            pltpu.VMEM((pieces, 2, ch, LANES), jnp.bfloat16),
+            pltpu.VMEM((2, tiles, count, LANES), jnp.float32),
+        ],
         compiler_params=VMEM,
         name="cross",
-    )(owner_order, source_offset, filtered, local, band, all_flags)
+    )(base[None], source_offset, *filtered, local, band)
 
 
 def solution(mesh):

time: 88.2 us -> 65.8 us (0.75)
  blocking collectives: 22.3 us -> 0 us
  between operations: 13.4 us -> 0.08 us
  starting transfers between devices: 10.5 us -> 18.3 us
  waiting for transfers between devices: 10.7 us -> 17.6 us
  local copies, waits for them, and re-layouts: 4.77 us -> 2.15 us
    all_gather x1 -> x0, blocking collectives: 22.3 us -> none  [body(): all_flags = lax.all_gather(flags, 'chan')]
    ppermute x0 -> x6, waiting for transfers between devices: none -> 12 us  [swap(): return lax.ppermute(x, 'chan', [(i, i ^ mask) for i in range(n_chan)])]
    ppermute x0 -> x6, starting transfers between devices: none -> 7.33 us  [swap(): return lax.ppermute(x, 'chan', [(i, i ^ mask) for i in range(n_chan)])]
    all_gather x1 -> x0, waiting for transfers between devices: 3.85 us -> none  [body(): filtered = lax.all_gather(filtered, 'chan', tiled=True)]
    all_to_all x1, waiting for transfers between devices: 6.84 us -> 4.03 us  [body(): held = lax.all_to_all(split, 'chan', 0, 0)[:, None]]
    ppermute x1, waiting for transfers between devices: 0.01 us -> 1.65 us  [body(): after = lax.ppermute(spectra, 'chan', [(i + 1, i) for i in range(ends)])]
    pad x1 -> x0, local copies, waits for them, and re-layouts: 1.29 us -> none  [body(): padded_bank = jnp.pad(filter_bank, ((0, 0), (0, 0), (0, LANES - taps)))]
    reshape x1 -> x0, local copies, waits for them, and re-layouts: 1.24 us -> none  [body(): flags = window_mask.reshape(1, count)]
  transfers between devices with their start and end apart: 4 -> 9, of which waited for: 2 -> 6; matrix products, arithmetic and copies ran while one was open for 4% -> 0% of each run, Pallas kernels for 7% -> 10%
where the time goes in v1:
time: 65.8 us; the launch traced here: 65.2 us
  Pallas kernels  26.1 us (40%)
  starting transfers between devices  18.3 us (28%)
  waiting for transfers between devices  17.6 us (27%)
  local copies, waits for them, and re-layouts  2.15 us (3%)
  other arithmetic  0.87 us (1%)
    pallas_call x1, Pallas kernels, body(): pl.pallas_call(functools.partial(cross_kernel, masks=masks), grid=(source...  15.8 us
    ppermute x6, waiting for transfers between devices, swap(): return lax.ppermute(x, 'chan', [(i, i ^ mask) for i in range(n_chan)])  12 us
    all_to_all x1, starting transfers between devices, body(): held = lax.all_to_all(split, 'chan', 0, 0)[:, None]  7.39 us
    ppermute x6, starting transfers between devices, swap(): return lax.ppermute(x, 'chan', [(i, i ^ mask) for i in range(n_chan)])  7.33 us
    pallas_call x1, Pallas kernels, body(): pl.pallas_call(own_kernel, out_shape=jax.ShapeDtypeStruct((2, tiles, coun...  4.54 us
    all_to_all x1, waiting for transfers between devices, body(): held = lax.all_to_all(split, 'chan', 0, 0)[:, None]  4.03 us
    ppermute x1, starting transfers between devices, body(): before = lax.ppermute(spectra, 'chan', [(i, i + 1) for i in range(ends)])  2.32 us
    pallas_call x1, Pallas kernels, body(): pl.pallas_call(source_kernel, grid=(count_here,), in_specs=[smem, smem, p...  2.21 us
  transfers between devices with their start and end apart: 9, of which 6 were waited for; matrix products, arithmetic and copies ran while one was open for 0% of the time, Pallas kernels for 10%

profile of v1, /device:TPU:0, one launch (start us, length us, event | category | flops | bytes accessed | tf_op | source)
XLA Modules:
  0.0 65.2 jit_solution(3911354074688272641)
XLA Ops:
  0.0 1.7 %split.1 = bf16[16,80,128]{2,1,0:T(8,128)(2,1)} custom-call(bf16[2,4,32,512]{3,2,1,0:T(8,128)(2,1)} %cur_ref.1, s32[4,32]{1,0:T(4,128)} %flags_ref.3), custom_call_target="tpu_custom_call" | custom-call | tf_op jit(solution)/shard_map/split/pallas_call | solution.py:222
  1.7 7.4 %all-to-all-start = ((bf16[16,80,128]{2,1,0:T(8,128)(2,1)}), bf16[16,80,128]{2,1,0:T(8,128)(2,1)S(1)}, u32[]{:S(2)}, u32[]{:S(2)}) async-start(bf16[16,80,128]{2,1,0:T(8,128)(2,1)} %split.1), calls=%async_computation | async-start | bytes 655360 | tf_op jit(solution)/shard_map/all_to_all | solution.py:228
  9.1 2.3 %collective-permute-start = (bf16[2,4,32,512]{3,2,1,0:T(8,128)(2,1)}, bf16[2,4,32,512]{3,2,1,0:T(8,128)(2,1)S(1)}, u32[]{:S(2)}, u32[]{:S(2)}) collective-permute-start(bf16[2,4,32,512]{3,2,1,0:T(8,128)(2,1)} %cur_ref.1), channel_id=1, source_target_pairs={{0,1},{1,2},{2,3},{3,4},{4,5},{5,6},{6,7},{7,8},{8,9},{9,10},{10,1... | collective-permute-start | bytes 786440 | tf_op jit(solution)/shard_map/ppermute | solution.py:235
  11.5 1.3 %collective-permute-start.1 = (bf16[2,4,32,512]{3,2,1,0:T(8,128)(2,1)}, bf16[2,4,32,512]{3,2,1,0:T(8,128)(2,1)S(1)}, u32[]{:S(2)}, u32[]{:S(2)}) collective-permute-start(bf16[2,4,32,512]{3,2,1,0:T(8,128)(2,1)} %cur_ref.1), channel_id=1, source_target_pairs={{1,0},{2,1},{3,2},{4,3},{5,4},{6,5},{7,6},{8,7},{9,8},{10,9},{11,1... | collective-permute-start | bytes 786440 | tf_op jit(solution)/shard_map/ppermute | solution.py:236
  12.8 1.8 %prep.1 = (bf16[512,256]{1,0:T(8,128)(2,1)}, bf16[512,256]{1,0:T(8,128)(2,1)}, bf16[512,512]{1,0:T(8,128)(2,1)}) custom-call(f32[2,8,65]{2,1,0:T(8,128)} %bank_ref.1), custom_call_target="tpu_custom_call" | custom-call | tf_op jit(solution)/shard_map/prep/pallas_call | solution.py:240
  14.6 0.0 collective-permute-done.prev_ref
  14.6 0.0 copy-start.5
  14.6 1.6 %collective-permute-done.1.next_ref = bf16[2,4,32,512]{3,2,1,0:T(8,128)(2,1)S(1)} collective-permute-done((bf16[2,4,32,512]{3,2,1,0:T(8,128)(2,1)}, bf16[2,4,32,512]{3,2,1,0:T(8,128)(2,1)S(1)}, u32[]{:S(2)}, u32[]{:S(2)}) %collective-permute-start.1) | collective-permute-done | bytes 262176 | tf_op jit(solution)/shard_map/ppermute | solution.py:236
  16.2 0.0 copy-start.6
  16.2 4.0 %all-to-all-done = bf16[16,80,128]{2,1,0:T(8,128)(2,1)S(1)} async-done(((bf16[16,80,128]{2,1,0:T(8,128)(2,1)}), bf16[16,80,128]{2,1,0:T(8,128)(2,1)S(1)}, u32[]{:S(2)}, u32[]{:S(2)}) %all-to-all-start) | async-done | bytes 327712 | tf_op jit(solution)/shard_map/all_to_all | solution.py:228
  20.3 0.0 copy-start
  20.3 0.7 %copy-done = bf16[16,80,128]{2,1,0:T(8,128)(2,1)} copy-done((bf16[16,80,128]{2,1,0:T(8,128)(2,1)}, bf16[16,80,128]{2,1,0:T(8,128)(2,1)S(1)}, u32[]{:S(2)}) %copy-start) | copy-done | bytes 327704
  21.0 2.2 %source_filter.1 = bf16[1,4,2,32,128]{4,3,2,1,0:T(8,128)(2,1)} custom-call(s32[1]{0:T(128)} %bitcast.piece_id_ref.me_ref, s32[4]{0:T(128)} %owner_ref.1, bf16[16,1,80,128]{3,2,1,0:T(8,128)(2,1)} %bitcast.4, bf16[512,256]{1,0:T(8,128)(2,1)} %get-tuple-element.12.whi_ref, bf16[512,256]{1,0:T(8,128)(2,1)} %get-tuple-element.13.wlo_ref, s32[4,1,128]{2,1,0:T(1,128)} %bitcast.5), custom_call_target="tpu_custom_call" | custom-call | tf_op jit(solution)/shard_map/source_filter/pallas_call | solution.py:248
  23.2 3.5 %collective-permute-start.4 = (bf16[1,4,2,32,128]{4,3,2,1,0:T(8,128)(2,1)}, bf16[1,4,2,32,128]{4,3,2,1,0:T(8,128)(2,1)S(1)}, u32[]{:S(2)}, u32[]{:S(2)}) collective-permute-start(bf16[1,4,2,32,128]{4,3,2,1,0:T(8,128)(2,1)} %source_filter.1), channel_id=1, source_target_pairs={{0,12},{1,13},{2,14},{3,15},{4,8},{5,9},{6,10},{7,11},{8,4},{9,5},... | collective-permute-start | bytes 196616 | tf_op jit(solution)/shard_map/ppermute | solution.py:200
  26.7 0.9 %collective-permute-start.3 = (bf16[1,4,2,32,128]{4,3,2,1,0:T(8,128)(2,1)}, bf16[1,4,2,32,128]{4,3,2,1,0:T(8,128)(2,1)S(1)}, u32[]{:S(2)}, u32[]{:S(2)}) collective-permute-start(bf16[1,4,2,32,128]{4,3,2,1,0:T(8,128)(2,1)} %source_filter.1), channel_id=1, source_target_pairs={{0,8},{1,9},{2,10},{3,11},{4,12},{5,13},{6,14},{7,15},{8,0},{9,1},... | collective-permute-start | bytes 196616 | tf_op jit(solution)/shard_map/ppermute | solution.py:200
  27.6 0.6 collective-permute-start.2
  28.1 1.4 %collective-permute-done.4 = bf16[1,4,2,32,128]{4,3,2,1,0:T(8,128)(2,1)S(1)} collective-permute-done((bf16[1,4,2,32,128]{4,3,2,1,0:T(8,128)(2,1)}, bf16[1,4,2,32,128]{4,3,2,1,0:T(8,128)(2,1)S(1)}, u32[]{:S(2)}, u32[]{:S(2)}) %collective-permute-start.4) | collective-permute-done | bytes 65568 | tf_op jit(solution)/shard_map/ppermute | solution.py:200
  29.5 2.8 %collective-permute-done.3 = bf16[1,4,2,32,128]{4,3,2,1,0:T(8,128)(2,1)S(1)} collective-permute-done((bf16[1,4,2,32,128]{4,3,2,1,0:T(8,128)(2,1)}, bf16[1,4,2,32,128]{4,3,2,1,0:T(8,128)(2,1)S(1)}, u32[]{:S(2)}, u32[]{:S(2)}) %collective-permute-start.3) | collective-permute-done | bytes 65568 | tf_op jit(solution)/shard_map/ppermute | solution.py:200
  32.3 1.0 %collective-permute-done.2 = bf16[1,4,2,32,128]{4,3,2,1,0:T(8,128)(2,1)S(1)} collective-permute-done((bf16[1,4,2,32,128]{4,3,2,1,0:T(8,128)(2,1)}, bf16[1,4,2,32,128]{4,3,2,1,0:T(8,128)(2,1)S(1)}, u32[]{:S(2)}, u32[]{:S(2)}) %collective-permute-start.2) | collective-permute-done | bytes 65568 | tf_op jit(solution)/shard_map/ppermute | solution.py:200
  33.3 0.9 %pad_maximum_fusion.refs_0_ = bf16[4,4,2,32,128]{4,3,2,1,0:T(8,128)(2,1)S(1)} fusion(bf16[1,4,2,32,128]{4,3,2,1,0:T(8,128)(2,1)S(1)} %collective-permute-done.4, bf16[1,4,2,32,128]{4,3,2,1,0:T(8,128)(2,1)S(1)} %collective-permute-done.3, bf16[1,4,2,32,128]{4,3,2,1,0:T(8,128)(2,1)S(1)} %collective-permute-done.2, bf16[1,4,2,32,128]{4,3,2,1,0:T(8,128)(2,1)} %source_filter.1), kind=kLoop, calls=%fused_computation | loop fusion | flops 393216 | bytes 524288 | tf_op jit(solution)/shard_map/concatenate | solution.py:202
  34.2 0.0 copy-start.1
  34.2 2.4 %collective-permute-start.5 = (bf16[4,4,2,32,128]{4,3,2,1,0:T(8,128)(2,1)S(1)}, bf16[4,4,2,32,128]{4,3,2,1,0:T(8,128)(2,1)S(1)}, u32[]{:S(2)}, u32[]{:S(2)}) collective-permute-start(bf16[4,4,2,32,128]{4,3,2,1,0:T(8,128)(2,1)S(1)} %pad_maximum_fusion.refs_0_), channel_id=1, source_target_pairs={{0,2},{1,3},{2,0},{3,1},{4,6},{5,7},{6,4},{7,5},{8,10},{9,11},{10,... | collective-permute-start | bytes 786440 | tf_op jit(solution)/shard_map/ppermute | solution.py:200
  36.6 0.0 collective-permute-start.6
  36.6 6.7 %collective-permute-done.5.refs_1_ = bf16[4,4,2,32,128]{4,3,2,1,0:T(8,128)(2,1)S(1)} collective-permute-done((bf16[4,4,2,32,128]{4,3,2,1,0:T(8,128)(2,1)S(1)}, bf16[4,4,2,32,128]{4,3,2,1,0:T(8,128)(2,1)S(1)}, u32[]{:S(2)}, u32[]{:S(2)}) %collective-permute-start.5) | collective-permute-done | bytes 262176 | tf_op jit(solution)/shard_map/ppermute | solution.py:200
  43.4 0.0 copy-start.2
  43.4 0.0 collective-permute-start.7
  43.4 0.0 copy-done.5
  43.4 0.0 copy-done.6
  43.4 4.5 %own_whiten.1.refs_4_ = f32[2,4,128,128]{3,2,1,0:T(8,128)} custom-call(bf16[2,4,32,512]{3,2,1,0:T(8,128)(2,1)} %copy-done.5, bf16[2,4,32,512]{3,2,1,0:T(8,128)(2,1)} %cur_ref.1, bf16[2,4,32,512]{3,2,1,0:T(8,128)(2,1)} %copy-done.6, bf16[512,256]{1,0:T(8,128)(2,1)} %get-tuple-element.12.whi_ref, bf16[512,256]{1,0:T(8,128)(2,1)} %get-tuple-element.13.wlo_ref, ...), custom_call_target="tpu_custom_call" | custom-call | flops 1073741824 | bytes 3145728 | tf_op jit(solution)/shard_map/own_whiten/pallas_call | solution.py:271
  47.9 0.0 collective-permute-done.6.refs_2_
  47.9 0.0 copy-start.3
  47.9 0.0 collective-permute-done.7.refs_3_
  47.9 0.0 copy-done.1
  47.9 0.0 copy-done.2
  48.0 0.7 %copy-done.3 = bf16[4,4,2,32,128]{4,3,2,1,0:T(8,128)(2,1)} copy-done((bf16[4,4,2,32,128]{4,3,2,1,0:T(8,128)(2,1)}, bf16[4,4,2,32,128]{4,3,2,1,0:T(8,128)(2,1)S(1)}, u32[]{:S(2)}) %copy-start.3) | copy-done | bytes 262168
  48.6 0.0 copy-start.4
  48.6 0.7 %copy-done.4 = bf16[4,4,2,32,128]{4,3,2,1,0:T(8,128)(2,1)} copy-done((bf16[4,4,2,32,128]{4,3,2,1,0:T(8,128)(2,1)}, bf16[4,4,2,32,128]{4,3,2,1,0:T(8,128)(2,1)S(1)}, u32[]{:S(2)}) %copy-start.4) | copy-done | bytes 262168
  49.4 15.8 %cross.1 = bf16[2,128,32,512]{3,2,1,0:T(8,128)(2,1)} custom-call(s32[1]{0:T(128)} %bitcast.piece_id_ref.me_ref, s32[4,32]{1,0:T(4,128)} %offset_ref.1, bf16[4,4,2,32,128]{4,3,2,1,0:T(8,128)(2,1)} %copy-done.1, bf16[4,4,2,32,128]{4,3,2,1,0:T(8,128)(2,1)} %copy-done.2, bf16[4,4,2,32,128]{4,3,2,1,0:T(8,128)(2,1)} %copy-done.3, ...), custom_call_target="tpu_custom_call" | custom-call | tf_op jit(solution)/shard_map/cross/pallas_call | solution.py:285
Async XLA Ops:
  1.7 18.5 %all-to-all-start = ((bf16[16,80,128]{2,1,0:T(8,128)(2,1)}), bf16[16,80,128]{2,1,0:T(8,128)(2,1)S(1)}, u32[]{:S(2)}, u32[]{:S(2)}) async-start(bf16[16,80,128]{2,1,0:T(8,128)(2,1)} %split.1), calls=%async_computation | async-start | bytes 655360 | tf_op jit(solution)/shard_map/all_to_all | solution.py:228
  9.1 5.4 %collective-permute-start = (bf16[2,4,32,512]{3,2,1,0:T(8,128)(2,1)}, bf16[2,4,32,512]{3,2,1,0:T(8,128)(2,1)S(1)}, u32[]{:S(2)}, u32[]{:S(2)}) collective-permute-start(bf16[2,4,32,512]{3,2,1,0:T(8,128)(2,1)} %cur_ref.1), channel_id=1, source_target_pairs={{0,1},{1,2},{2,3},{3,4},{4,5},{5,6},{6,7},{7,8},{8,9},{9,10},{10,1... | collective-permute-start | bytes 786440 | tf_op jit(solution)/shard_map/ppermute | solution.py:235
  11.5 4.8 %collective-permute-start.1 = (bf16[2,4,32,512]{3,2,1,0:T(8,128)(2,1)}, bf16[2,4,32,512]{3,2,1,0:T(8,128)(2,1)S(1)}, u32[]{:S(2)}, u32[]{:S(2)}) collective-permute-start(bf16[2,4,32,512]{3,2,1,0:T(8,128)(2,1)} %cur_ref.1), channel_id=1, source_target_pairs={{1,0},{2,1},{3,2},{4,3},{5,4},{6,5},{7,6},{8,7},{9,8},{10,9},{11,1... | collective-permute-start | bytes 786440 | tf_op jit(solution)/shard_map/ppermute | solution.py:236
  14.6 28.8 %copy-start.5 = (bf16[2,4,32,512]{3,2,1,0:T(8,128)(2,1)}, bf16[2,4,32,512]{3,2,1,0:T(8,128)(2,1)S(1)}, u32[]{:S(2)}) copy-start(bf16[2,4,32,512]{3,2,1,0:T(8,128)(2,1)S(1)} %collective-permute-done.prev_ref) | copy-start | bytes 786436
  16.2 27.2 %copy-start.6 = (bf16[2,4,32,512]{3,2,1,0:T(8,128)(2,1)}, bf16[2,4,32,512]{3,2,1,0:T(8,128)(2,1)S(1)}, u32[]{:S(2)}) copy-start(bf16[2,4,32,512]{3,2,1,0:T(8,128)(2,1)S(1)} %collective-permute-done.1.next_ref) | copy-start | bytes 786436
  20.3 0.7 %copy-start = (bf16[16,80,128]{2,1,0:T(8,128)(2,1)}, bf16[16,80,128]{2,1,0:T(8,128)(2,1)S(1)}, u32[]{:S(2)}) copy-start(bf16[16,80,128]{2,1,0:T(8,128)(2,1)S(1)} %all-to-all-done) | copy-start | bytes 983044
  23.2 6.3 %collective-permute-start.4 = (bf16[1,4,2,32,128]{4,3,2,1,0:T(8,128)(2,1)}, bf16[1,4,2,32,128]{4,3,2,1,0:T(8,128)(2,1)S(1)}, u32[]{:S(2)}, u32[]{:S(2)}) collective-permute-start(bf16[1,4,2,32,128]{4,3,2,1,0:T(8,128)(2,1)} %source_filter.1), channel_id=1, source_target_pairs={{0,12},{1,13},{2,14},{3,15},{4,8},{5,9},{6,10},{7,11},{8,4},{9,5},... | collective-permute-start | bytes 196616 | tf_op jit(solution)/shard_map/ppermute | solution.py:200
  26.7 5.7 %collective-permute-start.3 = (bf16[1,4,2,32,128]{4,3,2,1,0:T(8,128)(2,1)}, bf16[1,4,2,32,128]{4,3,2,1,0:T(8,128)(2,1)S(1)}, u32[]{:S(2)}, u32[]{:S(2)}) collective-permute-start(bf16[1,4,2,32,128]{4,3,2,1,0:T(8,128)(2,1)} %source_filter.1), channel_id=1, source_target_pairs={{0,8},{1,9},{2,10},{3,11},{4,12},{5,13},{6,14},{7,15},{8,0},{9,1},... | collective-permute-start | bytes 196616 | tf_op jit(solution)/shard_map/ppermute | solution.py:200
  27.6 5.8 %collective-permute-start.2 = (bf16[1,4,2,32,128]{4,3,2,1,0:T(8,128)(2,1)}, bf16[1,4,2,32,128]{4,3,2,1,0:T(8,128)(2,1)S(1)}, u32[]{:S(2)}, u32[]{:S(2)}) collective-permute-start(bf16[1,4,2,32,128]{4,3,2,1,0:T(8,128)(2,1)} %source_filter.1), channel_id=1, source_target_pairs={{0,4},{1,5},{2,6},{3,7},{4,0},{5,1},{6,2},{7,3},{8,12},{9,13},{10,... | collective-permute-start | bytes 196616 | tf_op jit(solution)/shard_map/ppermute | solution.py:200
  34.2 13.7 %copy-start.1 = (bf16[4,4,2,32,128]{4,3,2,1,0:T(8,128)(2,1)}, bf16[4,4,2,32,128]{4,3,2,1,0:T(8,128)(2,1)S(1)}, u32[]{:S(2)}) copy-start(bf16[4,4,2,32,128]{4,3,2,1,0:T(8,128)(2,1)S(1)} %pad_maximum_fusion.refs_0_) | copy-start | bytes 786436
  34.2 9.1 %collective-permute-start.5 = (bf16[4,4,2,32,128]{4,3,2,1,0:T(8,128)(2,1)S(1)}, bf16[4,4,2,32,128]{4,3,2,1,0:T(8,128)(2,1)S(1)}, u32[]{:S(2)}, u32[]{:S(2)}) collective-permute-start(bf16[4,4,2,32,128]{4,3,2,1,0:T(8,128)(2,1)S(1)} %pad_maximum_fusion.refs_0_), channel_id=1, source_target_pairs={{0,2},{1,3},{2,0},{3,1},{4,6},{5,7},{6,4},{7,5},{8,10},{9,11},{10,... | collective-permute-start | bytes 786440 | tf_op jit(solution)/shard_map/ppermute | solution.py:200
  36.6 11.3 %collective-permute-start.6 = (bf16[4,4,2,32,128]{4,3,2,1,0:T(8,128)(2,1)S(1)}, bf16[4,4,2,32,128]{4,3,2,1,0:T(8,128)(2,1)S(1)}, u32[]{:S(2)}, u32[]{:S(2)}) collective-permute-start(bf16[4,4,2,32,128]{4,3,2,1,0:T(8,128)(2,1)S(1)} %pad_maximum_fusion.refs_0_), channel_id=1, source_target_pairs={{0,1},{1,0},{2,3},{3,2},{4,5},{5,4},{6,7},{7,6},{8,9},{9,8},{10,11... | collective-permute-start | bytes 786440 | tf_op jit(solution)/shard_map/ppermute | solution.py:200
  43.4 4.6 %copy-start.2 = (bf16[4,4,2,32,128]{4,3,2,1,0:T(8,128)(2,1)}, bf16[4,4,2,32,128]{4,3,2,1,0:T(8,128)(2,1)S(1)}, u32[]{:S(2)}) copy-start(bf16[4,4,2,32,128]{4,3,2,1,0:T(8,128)(2,1)S(1)} %collective-permute-done.5.refs_1_) | copy-start | bytes 786436
  43.4 4.6 %collective-permute-start.7 = (bf16[4,4,2,32,128]{4,3,2,1,0:T(8,128)(2,1)S(1)}, bf16[4,4,2,32,128]{4,3,2,1,0:T(8,128)(2,1)S(1)}, u32[]{:S(2)}, u32[]{:S(2)}) collective-permute-start(bf16[4,4,2,32,128]{4,3,2,1,0:T(8,128)(2,1)S(1)} %collective-permute-done.5.refs_1_), channel_id=1, source_target_pairs={{0,1},{1,0},{2,3},{3,2},{4,5},{5,4},{6,7},{7,6},{8,9},{9,8},{10,11... | collective-permute-start | bytes 786440 | tf_op jit(solution)/shard_map/ppermute | solution.py:200
  47.9 0.7 %copy-start.3 = (bf16[4,4,2,32,128]{4,3,2,1,0:T(8,128)(2,1)}, bf16[4,4,2,32,128]{4,3,2,1,0:T(8,128)(2,1)S(1)}, u32[]{:S(2)}) copy-start(bf16[4,4,2,32,128]{4,3,2,1,0:T(8,128)(2,1)S(1)} %collective-permute-done.6.refs_2_) | copy-start | bytes 786436
  48.6 0.7 %copy-start.4 = (bf16[4,4,2,32,128]{4,3,2,1,0:T(8,128)(2,1)}, bf16[4,4,2,32,128]{4,3,2,1,0:T(8,128)(2,1)S(1)}, u32[]{:S(2)}) copy-start(bf16[4,4,2,32,128]{4,3,2,1,0:T(8,128)(2,1)S(1)} %collective-permute-done.7.refs_3_) | copy-start | bytes 786436

commit v2 on v1

--- a/solution.py
+++ b/solution.py
@@ -11,7 +11,7 @@
 LANES = 128
 WATER = 0.05
 SRC_STEP = 8
-VMEM = pltpu.CompilerParams(vmem_limit_bytes=56 * 1024 * 1024)
+VMEM = pltpu.CompilerParams(vmem_limit_bytes=20 * 1024 * 1024)
 
 
 def split_kernel(spectra_ref, flags_ref, piece_ref):
@@ -135,8 +135,21 @@
     valid = jnp.concatenate([flag_column(flags_ref[w : w + 1, :]) for w in range(win)], axis=0)
     real, imag = whitened_block(filt_ref[0] * valid, filt_ref[1] * valid, band_ref)
     for t in range(freq // LANES):
-        out_ref[0, t] = real[:, t * LANES : (t + 1) * LANES]
-        out_ref[1, t] = imag[:, t * LANES : (t + 1) * LANES]
+        out_ref[0, t] = real[:, t * LANES : (t + 1) * LANES].astype(jnp.bfloat16)
+        out_ref[1, t] = imag[:, t * LANES : (t + 1) * LANES].astype(jnp.bfloat16)
+
+
+def spread_row(ref, p, ft, row, ch):
+    eight = ref[p, ft, pl.ds(row, 8, stride=0), :]
+    pair = jnp.concatenate([eight, eight], axis=0).astype(jnp.bfloat16)
+    return jnp.concatenate([pair] * (ch // 16), axis=0)
+
+
+def pairwise(terms):
+    while len(terms) > 1:
+        half = (len(terms) + 1) // 2
+        terms = [terms[i] + terms[i + half] if i + half < len(terms) else terms[i] for i in range(half)]
+    return terms[0]
 
 
 def cross_kernel(me_ref, offset_ref, *refs, masks):
@@ -177,19 +190,15 @@
         ]
         for j in range(SRC_STEP):
             row = offset_ref[r, j0 + j]
-            re = im = None
+            re = []
+            im = []
             for w in range(win):
-                sr = source_ref[0, ft, pl.ds(w * ch + row, 8, stride=0), :]
-                si = source_ref[1, ft, pl.ds(w * ch + row, 8, stride=0), :]
-                sr = jnp.concatenate([sr] * (ch // 8), axis=0)
-                si = jnp.concatenate([si] * (ch // 8), axis=0)
+                sr, si = (spread_row(source_ref, p, ft, w * ch + row, ch) for p in range(2))
                 lr, li = mine[w]
-                a = sr * lr + si * li
-                b = sr * li - si * lr
-                re = a if re is None else re + a
-                im = b if im is None else im + b
-            out_ref[0, j, :, at] = re.astype(jnp.bfloat16)
-            out_ref[1, j, :, at] = im.astype(jnp.bfloat16)
+                re.append(sr * lr + si * li)
+                im.append(sr * li - si * lr)
+            out_ref[0, j, :, at] = pairwise(re)
+            out_ref[1, j, :, at] = pairwise(im)
         return 0
 
     lax.fori_loop(0, tiles, one_tile, 0)
@@ -234,7 +243,6 @@
     ends = n_chan - 1
     before = lax.ppermute(spectra, "chan", [(i, i + 1) for i in range(ends)])
     after = lax.ppermute(spectra, "chan", [(i + 1, i) for i in range(ends)])
-    held, before, after = lax.optimization_barrier((held, before, after))
 
     weights = jax.ShapeDtypeStruct((banks * 2 * ch, 2 * LANES), jnp.bfloat16)
     whi, wlo, band = pl.pallas_call(
@@ -243,6 +251,21 @@
         scratch_shapes=[pltpu.VMEM((2, banks, LANES), jnp.float32)],
         name="prep",
     )(filter_bank)
+
+    local = pl.pallas_call(
+        own_kernel,
+        out_shape=jax.ShapeDtypeStruct((2, tiles, count, LANES), jnp.bfloat16),
+        in_specs=[vmem] * 8,
+        out_specs=vmem,
+        scratch_shapes=[pltpu.VMEM((2, count, freq), jnp.float32)],
+        compiler_params=VMEM,
+        cost_estimate=pl.CostEstimate(
+            flops=4 * banks * 2 * ch * 2 * LANES * win * freq, bytes_accessed=3 << 20, transcendentals=0
+        ),
+        name="own_whiten",
+    )(before, spectra, after, whi, wlo, band, band_index.reshape(1, freq), window_mask)
+
+    held, local = lax.optimization_barrier((held, local))
 
     count_here = held.shape[1]
     filtered = pl.pallas_call(
@@ -268,19 +291,6 @@
         masks, filtered = (0,), (filtered,)
         base = jnp.int32(0)
 
-    local = pl.pallas_call(
-        own_kernel,
-        out_shape=jax.ShapeDtypeStruct((2, tiles, count, LANES), jnp.float32),
-        in_specs=[vmem] * 8,
-        out_specs=vmem,
-        scratch_shapes=[pltpu.VMEM((2, count, freq), jnp.float32)],
-        compiler_params=VMEM,
-        cost_estimate=pl.CostEstimate(
-            flops=4 * banks * 2 * ch * 2 * LANES * win * freq, bytes_accessed=3 << 20, transcendentals=0
-        ),
-        name="own_whiten",
-    )(before, spectra, after, whi, wlo, band, band_index.reshape(1, freq), window_mask)
-
     per_round = ch // SRC_STEP
     return pl.pallas_call(
         functools.partial(cross_kernel, masks=masks),

time: 65.8 us -> 67.1 us (1.020)
  local copies, waits for them, and re-layouts: 2.15 us -> 10.2 us
  Pallas kernels: 26.1 us -> 18.9 us
  starting transfers between devices: 18.3 us -> 22 us
  waiting for transfers between devices: 17.6 us -> 15.2 us
  other arithmetic: 0.87 us -> 0.04 us
    unnamed x14 -> x24, local copies, waits for them, and re-layouts: 2.15 us -> 10.2 us
    all_to_all x1, waiting for transfers between devices: 4.03 us -> 0.01 us  [body(): held = lax.all_to_all(split, 'chan', 0, 0)[:, None]]
    ppermute x6, starting transfers between devices: 7.33 us -> 11 us  [swap(): return lax.ppermute(x, 'chan', [(i, i ^ mask) for i in range(n_chan)])]
    pallas_call x1, Pallas kernels: 15.8 us -> 12.2 us  [body(): pl.pallas_call(functools.partial(cross_kernel, masks=masks), grid=(source...]
    pallas_call x1, Pallas kernels: 4.54 us -> 2.2 us  [body(): pl.pallas_call(own_kernel, out_shape=jax.ShapeDtypeStruct((2, tiles, coun...]
    ppermute x6, waiting for transfers between devices: 12 us -> 13.6 us  [swap(): return lax.ppermute(x, 'chan', [(i, i ^ mask) for i in range(n_chan)])]
    pallas_call x1, Pallas kernels: 2.21 us -> 0.99 us  [body(): pl.pallas_call(source_kernel, grid=(count_here,), in_specs=[smem, smem, p...]
    concatenate x1, other arithmetic: 0.87 us -> 0.04 us  [spread(): jnp.concatenate([part] + [swap(part, m) for m in range(4, n_chan, 4)], ax...]
  transfers between devices with their start and end apart: 9 -> 9, of which waited for: 6 -> 6; matrix products, arithmetic and copies ran while one was open for 0% -> 0% of each run, Pallas kernels for 10% -> 6%
where the time goes in v2:
time: 67.1 us; the launch traced here: 66.5 us
  starting transfers between devices  22 us (33%)
  Pallas kernels  18.9 us (28%)
  waiting for transfers between devices  15.2 us (23%)
  local copies, waits for them, and re-layouts  10.2 us (15%)
    ppermute x6, waiting for transfers between devices, swap(): return lax.ppermute(x, 'chan', [(i, i ^ mask) for i in range(n_chan)])  13.6 us
    pallas_call x1, Pallas kernels, body(): pl.pallas_call(functools.partial(cross_kernel, masks=masks), grid=(source...  12.2 us
    ppermute x6, starting transfers between devices, swap(): return lax.ppermute(x, 'chan', [(i, i ^ mask) for i in range(n_chan)])  11 us
    unnamed x24, local copies, waits for them, and re-layouts  10.2 us
    all_to_all x1, starting transfers between devices, body(): held = lax.all_to_all(split, 'chan', 0, 0)[:, None]  7.39 us
    ppermute x1, starting transfers between devices, body(): before = lax.ppermute(spectra, 'chan', [(i, i + 1) for i in range(ends)])  2.32 us
    pallas_call x1, Pallas kernels, body(): pl.pallas_call(own_kernel, out_shape=jax.ShapeDtypeStruct((2, tiles, coun...  2.2 us
    pallas_call x1, Pallas kernels, body(): pl.pallas_call(prep_kernel, out_shape=(weights, weights, jax.ShapeDtypeSt...  1.81 us
  transfers between devices with their start and end apart: 9, of which 6 were waited for; matrix products, arithmetic and copies ran while one was open for 0% of the time, Pallas kernels for 6%

profile of v2, /device:TPU:0, one launch (start us, length us, event | category | flops | bytes accessed | tf_op | source)
XLA Modules:
  0.0 66.5 jit_solution(16793112592026773532)
XLA Ops:
  0.0 1.7 %split.1 = bf16[16,80,128]{2,1,0:T(8,128)(2,1)} custom-call(bf16[2,4,32,512]{3,2,1,0:T(8,128)(2,1)} %cur_ref.1, s32[4,32]{1,0:T(4,128)} %flags_ref.3), custom_call_target="tpu_custom_call" | custom-call | tf_op jit(solution)/shard_map/split/pallas_call | solution.py:231
  1.7 7.4 %all-to-all-start = ((bf16[16,80,128]{2,1,0:T(8,128)(2,1)}), bf16[16,80,128]{2,1,0:T(8,128)(2,1)S(1)}, u32[]{:S(2)}, u32[]{:S(2)}) async-start(bf16[16,80,128]{2,1,0:T(8,128)(2,1)} %split.1), calls=%async_computation | async-start | bytes 655360 | tf_op jit(solution)/shard_map/all_to_all | solution.py:237
  9.1 2.3 %collective-permute-start = (bf16[2,4,32,512]{3,2,1,0:T(8,128)(2,1)}, bf16[2,4,32,512]{3,2,1,0:T(8,128)(2,1)S(1)}, u32[]{:S(2)}, u32[]{:S(2)}) collective-permute-start(bf16[2,4,32,512]{3,2,1,0:T(8,128)(2,1)} %cur_ref.1), channel_id=1, source_target_pairs={{0,1},{1,2},{2,3},{3,4},{4,5},{5,6},{6,7},{7,8},{8,9},{9,10},{10,1... | collective-permute-start | bytes 786440 | tf_op jit(solution)/shard_map/ppermute | solution.py:244
  11.5 1.3 %collective-permute-start.1 = (bf16[2,4,32,512]{3,2,1,0:T(8,128)(2,1)}, bf16[2,4,32,512]{3,2,1,0:T(8,128)(2,1)S(1)}, u32[]{:S(2)}, u32[]{:S(2)}) collective-permute-start(bf16[2,4,32,512]{3,2,1,0:T(8,128)(2,1)} %cur_ref.1), channel_id=1, source_target_pairs={{1,0},{2,1},{3,2},{4,3},{5,4},{6,5},{7,6},{8,7},{9,8},{10,9},{11,1... | collective-permute-start | bytes 786440 | tf_op jit(solution)/shard_map/ppermute | solution.py:245
  12.8 1.8 %prep.1 = (bf16[512,256]{1,0:T(8,128)(2,1)}, bf16[512,256]{1,0:T(8,128)(2,1)}, bf16[512,512]{1,0:T(8,128)(2,1)}) custom-call(f32[2,8,65]{2,1,0:T(8,128)} %bank_ref.1), custom_call_target="tpu_custom_call" | custom-call | tf_op jit(solution)/shard_map/prep/pallas_call | solution.py:248
  14.6 0.0 collective-permute-done.prev_ref
  14.6 1.6 %collective-permute-done.1.next_ref = bf16[2,4,32,512]{3,2,1,0:T(8,128)(2,1)S(1)} collective-permute-done((bf16[2,4,32,512]{3,2,1,0:T(8,128)(2,1)}, bf16[2,4,32,512]{3,2,1,0:T(8,128)(2,1)S(1)}, u32[]{:S(2)}, u32[]{:S(2)}) %collective-permute-start.1) | collective-permute-done | bytes 262176 | tf_op jit(solution)/shard_map/ppermute | solution.py:245
  16.2 0.0 copy-start
  16.2 1.0 %copy-done = bf16[512,512]{1,0:T(8,128)(2,1)S(1)} copy-done((bf16[512,512]{1,0:T(8,128)(2,1)S(1)}, bf16[512,512]{1,0:T(8,128)(2,1)}, u32[]{:S(2)}) %copy-start) | copy-done | bytes 524312
  17.3 0.0 copy-start.2
  17.3 0.9 %copy-done.2 = bf16[2,4,32,512]{3,2,1,0:T(8,128)(2,1)S(1)} copy-done((bf16[2,4,32,512]{3,2,1,0:T(8,128)(2,1)S(1)}, bf16[2,4,32,512]{3,2,1,0:T(8,128)(2,1)}, u32[]{:S(2)}) %copy-start.2) | copy-done | bytes 262168
  18.2 0.0 copy-start.3
  18.2 0.9 %copy-done.3 = bf16[512,256]{1,0:T(8,128)(2,1)S(1)} copy-done((bf16[512,256]{1,0:T(8,128)(2,1)S(1)}, bf16[512,256]{1,0:T(8,128)(2,1)}, u32[]{:S(2)}) %copy-start.3) | copy-done | bytes 262168
  19.2 0.0 copy-start.5
  19.2 0.9 %copy-done.5 = bf16[512,256]{1,0:T(8,128)(2,1)S(1)} copy-done((bf16[512,256]{1,0:T(8,128)(2,1)S(1)}, bf16[512,256]{1,0:T(8,128)(2,1)}, u32[]{:S(2)}) %copy-start.5) | copy-done | bytes 262168
  20.1 0.0 copy-start.7
  20.1 0.7 %copy-done.7 = s32[4,32]{1,0:T(4,128)S(1)} copy-done((s32[4,32]{1,0:T(4,128)S(1)}, s32[4,32]{1,0:T(4,128)}, u32[]{:S(2)}) %copy-start.7) | copy-done | bytes 536
  20.8 0.0 copy-start.8
  20.8 0.7 %copy-done.8 = s32[512]{0:T(512)S(1)} copy-done((s32[512]{0:T(512)S(1)}, s32[512]{0:T(512)}, u32[]{:S(2)}) %copy-start.8) | copy-done | bytes 2072
  21.5 2.2 %own_whiten.1.refs_4_ = bf16[2,4,128,128]{3,2,1,0:T(8,128)(2,1)S(1)} custom-call(bf16[2,4,32,512]{3,2,1,0:T(8,128)(2,1)S(1)} %collective-permute-done.prev_ref, bf16[2,4,32,512]{3,2,1,0:T(8,128)(2,1)S(1)} %copy-done.2, bf16[2,4,32,512]{3,2,1,0:T(8,128)(2,1)S(1)} %collective-permute-done.1.next_ref, bf16[512,256]{1,0:T(8,128)(2,1)S(1)} %copy-done.3, ...), custom_call_target="tpu_custom_call" | custom-call | flops 1073741824 | bytes 3145728 | tf_op jit(solution)/shard_map/own_whiten/pallas_call | solution.py:255
  23.7 0.0 all-to-all-done
  23.7 0.0 copy-start.4
  23.7 0.9 %copy-done.4 = bf16[512,256]{1,0:T(8,128)(2,1)S(1)} copy-done((bf16[512,256]{1,0:T(8,128)(2,1)S(1)}, bf16[512,256]{1,0:T(8,128)(2,1)}, u32[]{:S(2)}) %copy-start.4) | copy-done | bytes 262168
  24.6 0.0 copy-start.6
  24.7 0.9 %copy-done.6 = bf16[512,256]{1,0:T(8,128)(2,1)S(1)} copy-done((bf16[512,256]{1,0:T(8,128)(2,1)S(1)}, bf16[512,256]{1,0:T(8,128)(2,1)}, u32[]{:S(2)}) %copy-start.6) | copy-done | bytes 262168
  25.6 0.0 copy-start.9
  25.6 0.7 %copy-done.9 = s32[512]{0:T(512)S(1)} copy-done((s32[512]{0:T(512)S(1)}, s32[512]{0:T(512)}, u32[]{:S(2)}) %copy-start.9) | copy-done | bytes 2072
  26.3 0.0 copy-start.11
  26.3 0.7 copy-done.11
  26.9 1.0 %source_filter.1 = bf16[1,4,2,32,128]{4,3,2,1,0:T(8,128)(2,1)S(1)} custom-call(s32[1]{0:T(128)} %bitcast.piece_id_ref.me_ref, s32[4]{0:T(128)S(1)} %copy-done.11, bf16[16,1,80,128]{3,2,1,0:T(8,128)(2,1)S(1)} %bitcast.4, bf16[512,256]{1,0:T(8,128)(2,1)S(1)} %copy-done.4, bf16[512,256]{1,0:T(8,128)(2,1)S(1)} %copy-done.6, s32[4,1,128]{2,1,0:T(1,128)S(1)} %bitcast.6), custom_call_target="tpu_custom_call" | custom-call | tf_op jit(solution)/shard_map/source_filter/pallas_call | solution.py:271
  27.9 7.5 %collective-permute-start.4 = (bf16[1,4,2,32,128]{4,3,2,1,0:T(8,128)(2,1)S(1)}, bf16[1,4,2,32,128]{4,3,2,1,0:T(8,128)(2,1)S(1)}, u32[]{:S(2)}, u32[]{:S(2)}) collective-permute-start(bf16[1,4,2,32,128]{4,3,2,1,0:T(8,128)(2,1)S(1)} %source_filter.1), channel_id=1, source_target_pairs={{0,12},{1,13},{2,14},{3,15},{4,8},{5,9},{6,10},{7,11},{8,4},{9,5},... | collective-permute-start | bytes 196616 | tf_op jit(solution)/shard_map/ppermute | solution.py:209
  35.5 1.0 %collective-permute-start.3 = (bf16[1,4,2,32,128]{4,3,2,1,0:T(8,128)(2,1)S(1)}, bf16[1,4,2,32,128]{4,3,2,1,0:T(8,128)(2,1)S(1)}, u32[]{:S(2)}, u32[]{:S(2)}) collective-permute-start(bf16[1,4,2,32,128]{4,3,2,1,0:T(8,128)(2,1)S(1)} %source_filter.1), channel_id=1, source_target_pairs={{0,8},{1,9},{2,10},{3,11},{4,12},{5,13},{6,14},{7,15},{8,0},{9,1},... | collective-permute-start | bytes 196616 | tf_op jit(solution)/shard_map/ppermute | solution.py:209
  36.4 0.5 collective-permute-start.2
  36.9 0.8 %collective-permute-done.4 = bf16[1,4,2,32,128]{4,3,2,1,0:T(8,128)(2,1)S(1)} collective-permute-done((bf16[1,4,2,32,128]{4,3,2,1,0:T(8,128)(2,1)S(1)}, bf16[1,4,2,32,128]{4,3,2,1,0:T(8,128)(2,1)S(1)}, u32[]{:S(2)}, u32[]{:S(2)}) %collective-permute-start.4) | collective-permute-done | bytes 65568 | tf_op jit(solution)/shard_map/ppermute | solution.py:209
  37.7 3.1 %collective-permute-done.3 = bf16[1,4,2,32,128]{4,3,2,1,0:T(8,128)(2,1)S(1)} collective-permute-done((bf16[1,4,2,32,128]{4,3,2,1,0:T(8,128)(2,1)S(1)}, bf16[1,4,2,32,128]{4,3,2,1,0:T(8,128)(2,1)S(1)}, u32[]{:S(2)}, u32[]{:S(2)}) %collective-permute-start.3) | collective-permute-done | bytes 65568 | tf_op jit(solution)/shard_map/ppermute | solution.py:209
  40.8 1.5 %collective-permute-done.2 = bf16[1,4,2,32,128]{4,3,2,1,0:T(8,128)(2,1)S(1)} collective-permute-done((bf16[1,4,2,32,128]{4,3,2,1,0:T(8,128)(2,1)S(1)}, bf16[1,4,2,32,128]{4,3,2,1,0:T(8,128)(2,1)S(1)}, u32[]{:S(2)}, u32[]{:S(2)}) %collective-permute-start.2) | collective-permute-done | bytes 65568 | tf_op jit(solution)/shard_map/ppermute | solution.py:209
  42.3 2.0 %collective-permute-start.5 = (bf16[4,4,2,32,128]{4,3,2,1,0:T(8,128)(2,1)S(1)}, bf16[4,4,2,32,128]{4,3,2,1,0:T(8,128)(2,1)S(1)}, u32[]{:S(2)}, u32[]{:S(2)}) collective-permute-start(bf16[4,4,2,32,128]{4,3,2,1,0:T(8,128)(2,1)S(1)} %pad_maximum_fusion.refs_0_), channel_id=1, source_target_pairs={{0,2},{1,3},{2,0},{3,1},{4,6},{5,7},{6,4},{7,5},{8,10},{9,11},{10,... | collective-permute-start | bytes 786440 | tf_op jit(solution)/shard_map/ppermute | solution.py:209
  44.4 0.0 collective-permute-start.6
  44.4 6.7 %collective-permute-done.5.refs_1_ = bf16[4,4,2,32,128]{4,3,2,1,0:T(8,128)(2,1)S(1)} collective-permute-done((bf16[4,4,2,32,128]{4,3,2,1,0:T(8,128)(2,1)S(1)}, bf16[4,4,2,32,128]{4,3,2,1,0:T(8,128)(2,1)S(1)}, u32[]{:S(2)}, u32[]{:S(2)}) %collective-permute-start.5) | collective-permute-done | bytes 262176 | tf_op jit(solution)/shard_map/ppermute | solution.py:209
  51.0 0.0 collective-permute-start.7
  51.0 0.0 collective-permute-done.6.refs_2_
  51.0 1.5 %collective-permute-done.7.refs_3_ = bf16[4,4,2,32,128]{4,3,2,1,0:T(8,128)(2,1)S(1)} collective-permute-done((bf16[4,4,2,32,128]{4,3,2,1,0:T(8,128)(2,1)S(1)}, bf16[4,4,2,32,128]{4,3,2,1,0:T(8,128)(2,1)S(1)}, u32[]{:S(2)}, u32[]{:S(2)}) %collective-permute-start.7) | collective-permute-done | bytes 262176 | tf_op jit(solution)/shard_map/ppermute | solution.py:209
  52.6 0.0 copy-start.1
  52.6 1.0 %copy-done.1 = bf16[512,512]{1,0:T(8,128)(2,1)S(1)} copy-done((bf16[512,512]{1,0:T(8,128)(2,1)S(1)}, bf16[512,512]{1,0:T(8,128)(2,1)}, u32[]{:S(2)}) %copy-start.1) | copy-done | bytes 524312
  53.6 0.0 copy-start.10
  53.6 0.7 %copy-done.10 = s32[4,32]{1,0:T(4,128)S(1)} copy-done((s32[4,32]{1,0:T(4,128)S(1)}, s32[4,32]{1,0:T(4,128)}, u32[]{:S(2)}) %copy-start.10) | copy-done | bytes 536
  54.3 12.2 %cross.1 = bf16[2,128,32,512]{3,2,1,0:T(8,128)(2,1)} custom-call(s32[1]{0:T(128)} %bitcast.piece_id_ref.me_ref, s32[4,32]{1,0:T(4,128)S(1)} %copy-done.10, bf16[4,4,2,32,128]{4,3,2,1,0:T(8,128)(2,1)S(1)} %pad_maximum_fusion.refs_0_, bf16[4,4,2,32,128]{4,3,2,1,0:T(8,128)(2,1)S(1)} %collective-permute-done.5.refs_1_, ...), custom_call_target="tpu_custom_call" | custom-call | tf_op jit(solution)/shard_map/cross/pallas_call | solution.py:295
  (1 shorter events, 0.0 us)
Async XLA Ops:
  1.7 22.0 %all-to-all-start = ((bf16[16,80,128]{2,1,0:T(8,128)(2,1)}), bf16[16,80,128]{2,1,0:T(8,128)(2,1)S(1)}, u32[]{:S(2)}, u32[]{:S(2)}) async-start(bf16[16,80,128]{2,1,0:T(8,128)(2,1)} %split.1), calls=%async_computation | async-start | bytes 655360 | tf_op jit(solution)/shard_map/all_to_all | solution.py:237
  9.1 5.4 %collective-permute-start = (bf16[2,4,32,512]{3,2,1,0:T(8,128)(2,1)}, bf16[2,4,32,512]{3,2,1,0:T(8,128)(2,1)S(1)}, u32[]{:S(2)}, u32[]{:S(2)}) collective-permute-start(bf16[2,4,32,512]{3,2,1,0:T(8,128)(2,1)} %cur_ref.1), channel_id=1, source_target_pairs={{0,1},{1,2},{2,3},{3,4},{4,5},{5,6},{6,7},{7,8},{8,9},{9,10},{10,1... | collective-permute-start | bytes 786440 | tf_op jit(solution)/shard_map/ppermute | solution.py:244
  11.5 4.8 %collective-permute-start.1 = (bf16[2,4,32,512]{3,2,1,0:T(8,128)(2,1)}, bf16[2,4,32,512]{3,2,1,0:T(8,128)(2,1)S(1)}, u32[]{:S(2)}, u32[]{:S(2)}) collective-permute-start(bf16[2,4,32,512]{3,2,1,0:T(8,128)(2,1)} %cur_ref.1), channel_id=1, source_target_pairs={{1,0},{2,1},{3,2},{4,3},{5,4},{6,5},{7,6},{8,7},{9,8},{10,9},{11,1... | collective-permute-start | bytes 786440 | tf_op jit(solution)/shard_map/ppermute | solution.py:245
  16.2 1.0 %copy-start = (bf16[512,512]{1,0:T(8,128)(2,1)S(1)}, bf16[512,512]{1,0:T(8,128)(2,1)}, u32[]{:S(2)}) copy-start(bf16[512,512]{1,0:T(8,128)(2,1)} %get-tuple-element.12.band_ref.refs_5_) | copy-start | bytes 1572868
  17.3 0.9 %copy-start.2 = (bf16[2,4,32,512]{3,2,1,0:T(8,128)(2,1)S(1)}, bf16[2,4,32,512]{3,2,1,0:T(8,128)(2,1)}, u32[]{:S(2)}) copy-start(bf16[2,4,32,512]{3,2,1,0:T(8,128)(2,1)} %cur_ref.1) | copy-start | bytes 786436
  18.2 0.9 %copy-start.3 = (bf16[512,256]{1,0:T(8,128)(2,1)S(1)}, bf16[512,256]{1,0:T(8,128)(2,1)}, u32[]{:S(2)}) copy-start(bf16[512,256]{1,0:T(8,128)(2,1)} %get-tuple-element.10.whi_ref) | copy-start | bytes 786436
  19.2 0.9 %copy-start.5 = (bf16[512,256]{1,0:T(8,128)(2,1)S(1)}, bf16[512,256]{1,0:T(8,128)(2,1)}, u32[]{:S(2)}) copy-start(bf16[512,256]{1,0:T(8,128)(2,1)} %get-tuple-element.11.wlo_ref) | copy-start | bytes 786436
  20.1 0.7 %copy-start.7 = (s32[4,32]{1,0:T(4,128)S(1)}, s32[4,32]{1,0:T(4,128)}, u32[]{:S(2)}) copy-start(s32[4,32]{1,0:T(4,128)} %flags_ref.3) | copy-start | bytes 1540
  20.8 0.7 %copy-start.8 = (s32[512]{0:T(512)S(1)}, s32[512]{0:T(512)}, u32[]{:S(2)}) copy-start(s32[512]{0:T(512)} %param.8) | copy-start | bytes 6148
  23.7 1.0 %copy-start.4 = (bf16[512,256]{1,0:T(8,128)(2,1)S(1)}, bf16[512,256]{1,0:T(8,128)(2,1)}, u32[]{:S(2)}) copy-start(bf16[512,256]{1,0:T(8,128)(2,1)} %get-tuple-element.10.whi_ref) | copy-start | bytes 786436
  24.6 0.9 %copy-start.6 = (bf16[512,256]{1,0:T(8,128)(2,1)S(1)}, bf16[512,256]{1,0:T(8,128)(2,1)}, u32[]{:S(2)}) copy-start(bf16[512,256]{1,0:T(8,128)(2,1)} %get-tuple-element.11.wlo_ref) | copy-start | bytes 786436
  25.6 0.7 %copy-start.9 = (s32[512]{0:T(512)S(1)}, s32[512]{0:T(512)}, u32[]{:S(2)}) copy-start(s32[512]{0:T(512)} %param.8) | copy-start | bytes 6148
  26.3 0.7 copy-start.11
  27.9 9.8 %collective-permute-start.4 = (bf16[1,4,2,32,128]{4,3,2,1,0:T(8,128)(2,1)S(1)}, bf16[1,4,2,32,128]{4,3,2,1,0:T(8,128)(2,1)S(1)}, u32[]{:S(2)}, u32[]{:S(2)}) collective-permute-start(bf16[1,4,2,32,128]{4,3,2,1,0:T(8,128)(2,1)S(1)} %source_filter.1), channel_id=1, source_target_pairs={{0,12},{1,13},{2,14},{3,15},{4,8},{5,9},{6,10},{7,11},{8,4},{9,5},... | collective-permute-start | bytes 196616 | tf_op jit(solution)/shard_map/ppermute | solution.py:209
  35.5 5.3 %collective-permute-start.3 = (bf16[1,4,2,32,128]{4,3,2,1,0:T(8,128)(2,1)S(1)}, bf16[1,4,2,32,128]{4,3,2,1,0:T(8,128)(2,1)S(1)}, u32[]{:S(2)}, u32[]{:S(2)}) collective-permute-start(bf16[1,4,2,32,128]{4,3,2,1,0:T(8,128)(2,1)S(1)} %source_filter.1), channel_id=1, source_target_pairs={{0,8},{1,9},{2,10},{3,11},{4,12},{5,13},{6,14},{7,15},{8,0},{9,1},... | collective-permute-start | bytes 196616 | tf_op jit(solution)/shard_map/ppermute | solution.py:209
  36.4 5.9 %collective-permute-start.2 = (bf16[1,4,2,32,128]{4,3,2,1,0:T(8,128)(2,1)S(1)}, bf16[1,4,2,32,128]{4,3,2,1,0:T(8,128)(2,1)S(1)}, u32[]{:S(2)}, u32[]{:S(2)}) collective-permute-start(bf16[1,4,2,32,128]{4,3,2,1,0:T(8,128)(2,1)S(1)} %source_filter.1), channel_id=1, source_target_pairs={{0,4},{1,5},{2,6},{3,7},{4,0},{5,1},{6,2},{7,3},{8,12},{9,13},{10,... | collective-permute-start | bytes 196616 | tf_op jit(solution)/shard_map/ppermute | solution.py:209
  42.3 8.7 %collective-permute-start.5 = (bf16[4,4,2,32,128]{4,3,2,1,0:T(8,128)(2,1)S(1)}, bf16[4,4,2,32,128]{4,3,2,1,0:T(8,128)(2,1)S(1)}, u32[]{:S(2)}, u32[]{:S(2)}) collective-permute-start(bf16[4,4,2,32,128]{4,3,2,1,0:T(8,128)(2,1)S(1)} %pad_maximum_fusion.refs_0_), channel_id=1, source_target_pairs={{0,2},{1,3},{2,0},{3,1},{4,6},{5,7},{6,4},{7,5},{8,10},{9,11},{10,... | collective-permute-start | bytes 786440 | tf_op jit(solution)/shard_map/ppermute | solution.py:209
  44.4 6.7 %collective-permute-start.6 = (bf16[4,4,2,32,128]{4,3,2,1,0:T(8,128)(2,1)S(1)}, bf16[4,4,2,32,128]{4,3,2,1,0:T(8,128)(2,1)S(1)}, u32[]{:S(2)}, u32[]{:S(2)}) collective-permute-start(bf16[4,4,2,32,128]{4,3,2,1,0:T(8,128)(2,1)S(1)} %pad_maximum_fusion.refs_0_), channel_id=1, source_target_pairs={{0,1},{1,0},{2,3},{3,2},{4,5},{5,4},{6,7},{7,6},{8,9},{9,8},{10,11... | collective-permute-start | bytes 786440 | tf_op jit(solution)/shard_map/ppermute | solution.py:209
  51.0 1.5 %collective-permute-start.7 = (bf16[4,4,2,32,128]{4,3,2,1,0:T(8,128)(2,1)S(1)}, bf16[4,4,2,32,128]{4,3,2,1,0:T(8,128)(2,1)S(1)}, u32[]{:S(2)}, u32[]{:S(2)}) collective-permute-start(bf16[4,4,2,32,128]{4,3,2,1,0:T(8,128)(2,1)S(1)} %collective-permute-done.5.refs_1_), channel_id=1, source_target_pairs={{0,1},{1,0},{2,3},{3,2},{4,5},{5,4},{6,7},{7,6},{8,9},{9,8},{10,11... | collective-permute-start | bytes 786440 | tf_op jit(solution)/shard_map/ppermute | solution.py:209
  52.6 1.0 %copy-start.1 = (bf16[512,512]{1,0:T(8,128)(2,1)S(1)}, bf16[512,512]{1,0:T(8,128)(2,1)}, u32[]{:S(2)}) copy-start(bf16[512,512]{1,0:T(8,128)(2,1)} %get-tuple-element.12.band_ref.refs_5_) | copy-start | bytes 1572868
  53.6 0.7 %copy-start.10 = (s32[4,32]{1,0:T(4,128)S(1)}, s32[4,32]{1,0:T(4,128)}, u32[]{:S(2)}) copy-start(s32[4,32]{1,0:T(4,128)} %offset_ref.1) | copy-start | bytes 1540

commit v3 on v2

v3 whole, which is shorter than its diff:
```python
import functools

import jax
import jax.numpy as jnp
from jax import lax
from jax.experimental import pallas as pl
from jax.experimental.pallas import tpu as pltpu
from jax.sharding import PartitionSpec as P

SMOOTH = 17
LANES = 128
WATER = 0.05
SRC_STEP = 16


def room(mib):
    return pltpu.CompilerParams(vmem_limit_bytes=mib * 1024 * 1024)


def split_kernel(spectra_ref, flags_ref, piece_ref):
    _, win, ch, freq = spectra_ref.shape
    tiles = freq // LANES
    extra = piece_ref.shape[1] - 2 * ch
    for w in range(win):
        flags = jnp.broadcast_to(flags_ref[w : w + 1, :], (extra, ch)).astype(jnp.float32)
        for t in range(tiles):
            at = slice(t * LANES, (t + 1) * LANES)
            piece_ref[w * tiles + t, :ch] = spectra_ref[0, w, :, at]
            piece_ref[w * tiles + t, ch : 2 * ch] = spectra_ref[1, w, :, at]
            piece_ref[w * tiles + t, 2 * ch :] = jnp.zeros((extra, LANES), jnp.bfloat16)
            piece_ref[w * tiles + t, 2 * ch :, :ch] = flags.astype(jnp.bfloat16)


def prep_kernel(bank_ref, bins_ref, flags_ref, weight_ref, band_ref, index_ref, valid_ref, padded_ref):
    _, banks, taps = bank_ref.shape
    half = weight_ref.shape[0] // 2
    ch = half // (2 * banks)
    index_ref[...] = bins_ref[...]
    for w in range(flags_ref.shape[0]):
        column = flag_column(flags_ref[w : w + 1, :])
        valid_ref[w * ch : (w + 1) * ch, :] = jnp.broadcast_to(column, (ch, LANES))
    padded_ref[...] = jnp.zeros(padded_ref.shape, jnp.float32)
    padded_ref[:, :, :taps] = bank_ref[...]

    def skewed(row):
        tile = jnp.broadcast_to(row, (ch, LANES))
        return pltpu.roll(tile, 0, 1, stride=1, stride_axis=0)

    for b in range(banks):
        real = skewed(padded_ref[0, b : b + 1, :])
        imag = skewed(padded_ref[1, b : b + 1, :])
        base = b * 2 * ch
        for row, left, right in ((base, real, -imag), (base + ch, imag, real)):
            for col, val in ((0, left), (LANES, right)):
                high = val.astype(jnp.bfloat16)
                low = (val - high.astype(jnp.float32)).astype(jnp.bfloat16)
                weight_ref[row : row + ch, col : col + LANES] = high
                weight_ref[half + row : half + row + ch, col : col + LANES] = low
    rows = lax.broadcasted_iota(jnp.int32, band_ref.shape, 0)
    cols = lax.broadcasted_iota(jnp.int32, band_ref.shape, 1)
    near = jnp.abs(rows - cols) <= SMOOTH // 2
    band_ref[...] = jnp.where(near, 1.0, 0.0).astype(jnp.bfloat16)


def flag_column(row):
    ch = row.shape[1]
    rows = lax.broadcasted_iota(jnp.int32, (ch, ch), 0)
    cols = lax.broadcasted_iota(jnp.int32, (ch, ch), 1)
    return jnp.sum(jnp.where(rows == cols, row.astype(jnp.float32), 0.0), axis=1, keepdims=True)


def filtered_block(x, weight_ref, index, ch):
    half = weight_ref.shape[0] // 2
    y = jnp.dot(weight_ref[...], x, preferred_element_type=jnp.float32)
    rows = 2 * ch
    pick = y[:rows] + y[half : half + rows]
    for at in range(rows, half, rows):
        here = y[at : at + rows] + y[half + at : half + at + rows]
        pick = jnp.where(index == at // rows, here, pick)
    return pick


def running_scale(real, imag, band_ref):
    count = real.shape[0]
    power = real * real + imag * imag
    high = power.astype(jnp.bfloat16)
    low = (power - high.astype(jnp.float32)).astype(jnp.bfloat16)
    both = jnp.concatenate([high, low], axis=0)
    total = jnp.dot(both, band_ref[...], preferred_element_type=jnp.float32)
    return lax.rsqrt((total[:count] + total[count:]) * (1.0 / SMOOTH) + WATER)


def source_kernel(params_ref, x_ref, weight_ref, index_ref, out_ref):
    n_chan = x_ref.shape[0]
    _, rounds, _, ch, _ = out_ref.shape
    tiles = index_ref.shape[0]
    tile = lax.rem(params_ref[0] + pl.program_id(0), tiles)
    zero = jnp.zeros((), jnp.bfloat16)
    gap = jnp.zeros((LANES - 3 * ch, LANES), jnp.bfloat16)
    columns = []
    for r in range(rounds):
        block = params_ref[1 + r]
        before = jnp.maximum(block - 1, 0)
        after = jnp.minimum(block + 1, n_chan - 1)
        parts = []
        for p in range(2):
            at = slice(p * ch, (p + 1) * ch)
            parts.append(jnp.where(block > 0, x_ref[before, 0, at], zero))
            parts.append(x_ref[block, 0, at])
            parts.append(jnp.where(block < n_chan - 1, x_ref[after, 0, at], zero))
            parts.append(gap)
        columns.append(jnp.concatenate(parts, axis=0))
    x = jnp.concatenate(columns, axis=1)
    index = jnp.concatenate([index_ref[tile]] * rounds, axis=1)
    pick = filtered_block(x, weight_ref, index, ch)
    for r in range(rounds):
        flags = x_ref[params_ref[1 + r], 0, 2 * ch :].astype(jnp.float32)[:1, :ch]
        valid = flag_column(flags)
        for p in range(2):
            part = pick[p * ch : (p + 1) * ch, r * LANES : (r + 1) * LANES] * valid
            out_ref[0, r, p] = part.astype(jnp.bfloat16)


def own_kernel(prev_ref, cur_ref, next_ref, weight_ref, band_ref, index_ref, valid_ref, out_ref, filt_ref):
    _, win, ch, freq = cur_ref.shape
    tiles = freq // LANES
    gap = jnp.zeros((LANES - 3 * ch, freq), jnp.bfloat16)
    index = jnp.concatenate([index_ref[t] for t in range(tiles)], axis=1)

    def one_window(w, _):
        parts = []
        for p in range(2):
            parts += [prev_ref[p, w], cur_ref[p, w], next_ref[p, w], gap]
        x = jnp.concatenate(parts, axis=0)
        pick = filtered_block(x, weight_ref, index, ch)
        at = pl.ds(pl.multiple_of(w * ch, ch), ch)
        filt_ref[0, at, :] = pick[:ch]
        filt_ref[1, at, :] = pick[ch:]
        return 0

    lax.fori_loop(0, win, one_window, 0)
    valid = jnp.concatenate([valid_ref[...]] * tiles, axis=1)
    scale = running_scale(filt_ref[0], filt_ref[1], band_ref) * valid
    for p in range(2):
        white = (filt_ref[p] * scale).astype(jnp.bfloat16)
        for t in range(tiles):
            out_ref[p, t] = white[:, t * LANES : (t + 1) * LANES]


def spread_row(ref, r, p, ft, row, ch):
    eight = ref[r, p, ft, pl.ds(row, 8, stride=0), :]
    pair = jnp.concatenate([eight, eight], axis=0).astype(jnp.bfloat16)
    return jnp.concatenate([pair] * (ch // 16), axis=0)


def pairwise(terms):
    while len(terms) > 1:
        half = (len(terms) + 1) // 2
        terms = [terms[i] + terms[i + half] if i + half < len(terms) else terms[i] for i in range(half)]
    return terms[0]


def cross_kernel(params_ref, *refs, masks):
    filt_refs = refs[: len(masks)]
    local_ref, band_ref, out_ref, piece_ref, source_ref = refs[len(masks) :]
    ch = out_ref.shape[2]
    pieces, rounds = piece_ref.shape[:2]
    tiles = local_ref.shape[1]
    win = pieces // tiles
    per_round = ch // SRC_STEP
    step = pl.program_id(0)
    r = step // per_round
    first = 1 + rounds + step * SRC_STEP

    @pl.when(step == 0)
    def _():
        stride = pieces // filt_refs[0].shape[0]
        for mask, ref in zip(masks, filt_refs):
            for k in range(ref.shape[0]):
                piece_ref[params_ref[0] ^ (mask ^ (k * stride))] = ref[k]

        def one_round(rr, _):
            parts = []
            for p in range(2):
                rows = [
                    jnp.concatenate([piece_ref[w * tiles + t, rr, p] for t in range(tiles)], axis=1)
                    for w in range(win)
                ]
                parts.append(jnp.concatenate(rows, axis=0).astype(jnp.float32))
            scale = running_scale(parts[0], parts[1], band_ref)
            for p in range(2):
                white = (parts[p] * scale).astype(jnp.bfloat16).astype(jnp.float32) * (1.0 / win)
                for t in range(tiles):
                    source_ref[rr, p, t] = white[:, t * LANES : (t + 1) * LANES]
            return 0

        lax.fori_loop(0, rounds, one_round, 0)

    def one_tile(ft, _):
        at = pl.ds(pl.multiple_of(ft * LANES, LANES), LANES)
        mine = [
            (local_ref[0, ft, w * ch : (w + 1) * ch, :], local_ref[1, ft, w * ch : (w + 1) * ch, :])
            for w in range(win)
        ]
        for j in range(SRC_STEP):
            row = params_ref[first + j]
            re = []
            im = []
            for w in range(win):
                sr, si = (spread_row(source_ref, r, p, ft, w * ch + row, ch) for p in range(2))
                lr, li = mine[w]
                re.append(sr * lr + si * li)
                im.append(sr * li - si * lr)
            out_ref[0, j, :, at] = pairwise(re)
            out_ref[1, j, :, at] = pairwise(im)
        return 0

    lax.fori_loop(0, tiles, one_tile, 0)


def swap(x, mask, n_chan):
    return lax.ppermute(x, "chan", [(i, i ^ mask) for i in range(n_chan)])


def body(spectra, filter_bank, band_index, window_mask, owner_order, source_offset):
    n_chan = lax.axis_size("chan")
    me = lax.axis_index("chan").astype(jnp.int32)
    _, win, ch, freq = spectra.shape
    banks, taps = filter_bank.shape[1:]
    rounds = owner_order.shape[0]
    count = win * ch
    tiles = freq // LANES
    pieces = win * tiles
    sources = rounds * ch
    in_parts = n_chan == pieces and n_chan >= 4 and n_chan & (n_chan - 1) == 0
    smem = pl.BlockSpec(memory_space=pltpu.SMEM)
    vmem = pl.BlockSpec(memory_space=pltpu.VMEM)

    split = pl.pallas_call(
        split_kernel,
        out_shape=jax.ShapeDtypeStruct((pieces, 2 * ch + 16, LANES), jnp.bfloat16),
        compiler_params=room(6),
        name="split",
    )(spectra, window_mask)
    if in_parts:
        held = lax.all_to_all(split, "chan", 0, 0)[:, None]
        first = me
    else:
        held = lax.all_gather(split, "chan")
        first = jnp.int32(0)
    params = jnp.concatenate([first[None], owner_order, source_offset.reshape(-1)])

    weight, band, index, valid = pl.pallas_call(
        prep_kernel,
        out_shape=(
            jax.ShapeDtypeStruct((2 * banks * 2 * ch, 2 * LANES), jnp.bfloat16),
            jax.ShapeDtypeStruct((freq, freq), jnp.bfloat16),
            jax.ShapeDtypeStruct((tiles, 1, LANES), jnp.int32),
            jax.ShapeDtypeStruct((count, LANES), jnp.float32),
        ),
        scratch_shapes=[pltpu.VMEM((2, banks, LANES), jnp.float32)],
        compiler_params=room(8),
        name="prep",
    )(filter_bank, band_index.reshape(tiles, 1, LANES), window_mask)

    count_here = held.shape[1]
    filtered = pl.pallas_call(
        source_kernel,
        grid=(count_here,),
        in_specs=[
            smem,
            pl.BlockSpec((n_chan, 1, 2 * ch + 16, LANES), lambda s: (0, s, 0, 0)),
            vmem,
            vmem,
        ],
        out_specs=pl.BlockSpec((1, rounds, 2, ch, LANES), lambda s: (s, 0, 0, 0, 0)),
        out_shape=jax.ShapeDtypeStruct((count_here, rounds, 2, ch, LANES), jnp.bfloat16),
        compiler_params=room(16),
        name="source_filter",
    )(params, held, weight, index)

    spectra, filtered = lax.optimization_barrier((spectra, filtered))
    if in_parts:
        masks = (0, 2, 1, 3)
        column = [filtered] + [swap(filtered, m, n_chan) for m in range(4, n_chan, 4)]
    ends = n_chan - 1
    before = lax.ppermute(spectra, "chan", [(i, i + 1) for i in range(ends)])
    after = lax.ppermute(spectra, "chan", [(i + 1, i) for i in range(ends)])

    local = pl.pallas_call(
        own_kernel,
        out_shape=jax.ShapeDtypeStruct((2, tiles, count, LANES), jnp.bfloat16),
        in_specs=[vmem] * 7,
        out_specs=vmem,
        scratch_shapes=[pltpu.VMEM((2, count, freq), jnp.float32)],
        compiler_params=room(16),
        cost_estimate=pl.CostEstimate(
            flops=4 * banks * 2 * ch * 2 * LANES * win * freq, bytes_accessed=3 << 20, transcendentals=0
        ),
        name="own_whiten",
    )(before, spectra, after, weight, band, index, valid)

    if in_parts:
        column = jnp.concatenate(column, axis=0)
        far = swap(column, 2, n_chan)
        beside = swap(column, 1, n_chan)
        far, local = lax.optimization_barrier((far, local))
        parts = (column, far, beside, swap(far, 1, n_chan))
    else:
        masks = (0,)
        parts = (filtered,)

    return pl.pallas_call(
        functools.partial(cross_kernel, masks=masks),
        grid=(sources // SRC_STEP,),
        in_specs=[smem] + [vmem] * (len(parts) + 2),
        out_specs=pl.BlockSpec((2, SRC_STEP, ch, freq), lambda s: (0, s, 0, 0)),
        out_shape=jax.ShapeDtypeStruct((2, sources, ch, freq), jnp.bfloat16),
        scratch_shapes=[
            pltpu.VMEM((pieces, rounds, 2, ch, LANES), jnp.bfloat16),
            pltpu.VMEM((rounds, 2, tiles, count, LANES), jnp.float32),
        ],
        compiler_params=room(24),
        name="cross",
    )(params, *parts, local, band)


def solution(mesh):
    in_specs = (
        P(None, "groups", "chan", None),
        P(),
        P(),
        P("groups", "chan"),
        P("groups"),
        P("groups", None),
    )
    out_specs = P(None, "groups", "chan", None)
    return jax.shard_map(body, mesh=mesh, in_specs=in_specs, out_specs=out_specs, check_vma=False)
```

time: 67.1 us -> 52.9 us (0.79)
  Pallas kernels: 18.9 us -> 13.8 us
  local copies, waits for them, and re-layouts: 10.2 us -> 5.46 us
  waiting for transfers between devices: 15.2 us -> 12.3 us
  starting transfers between devices: 22 us -> 20.1 us
  other arithmetic: 0.04 us -> 0.73 us
    ppermute x6, waiting for transfers between devices: 13.6 us -> 5.06 us  [swap(): return lax.ppermute(x, 'chan', [(i, i ^ mask) for i in range(n_chan)])]
    all_to_all x1, waiting for transfers between devices: 0.01 us -> 7.28 us  [body(): held = lax.all_to_all(split, 'chan', 0, 0)[:, None]]
    unnamed x24 -> x15, local copies, waits for them, and re-layouts: 10.2 us -> 4.68 us
    ppermute x6, starting transfers between devices: 11 us -> 8.38 us  [swap(): return lax.ppermute(x, 'chan', [(i, i ^ mask) for i in range(n_chan)])]
    pallas_call x1, Pallas kernels: 12.2 us -> 9.69 us  [body(): pl.pallas_call(functools.partial(cross_kernel, masks=masks), grid=(source...]
    ppermute x1, waiting for transfers between devices: 1.64 us -> 0.01 us  [body(): after = lax.ppermute(spectra, 'chan', [(i + 1, i) for i in range(ends)])]
    pallas_call x2, Pallas kernels: 2.8 us -> 1.24 us  [the longest x1 1 us: body(): pl.pallas_call(source_kernel, grid=(count_here,), in_specs=[smem, pl.Bloc...]
    pallas_call x1, Pallas kernels: 1.73 us -> 0.78 us  [body(): pl.pallas_call(split_kernel, out_shape=jax.ShapeDtypeStruct((pieces, 2 *...]
  transfers between devices with their start and end apart: 9 -> 9, of which waited for: 6 -> 3; matrix products, arithmetic and copies ran while one was open for 0% -> 3% of each run, Pallas kernels for 6% -> 4%
where the time goes in v3:
time: 52.9 us; the launch traced here: 52.5 us
  starting transfers between devices  20.1 us (38%)
  Pallas kernels  13.8 us (26%)
  waiting for transfers between devices  12.3 us (23%)
  local copies, waits for them, and re-layouts  5.46 us (10%)
  other arithmetic  0.73 us (1%)
    pallas_call x1, Pallas kernels, body(): pl.pallas_call(functools.partial(cross_kernel, masks=masks), grid=(source...  9.69 us
    ppermute x6, starting transfers between devices, swap(): return lax.ppermute(x, 'chan', [(i, i ^ mask) for i in range(n_chan)])  8.38 us
    all_to_all x1, starting transfers between devices, body(): held = lax.all_to_all(split, 'chan', 0, 0)[:, None]  7.39 us
    all_to_all x1, waiting for transfers between devices, body(): held = lax.all_to_all(split, 'chan', 0, 0)[:, None]  7.28 us
    ppermute x6, waiting for transfers between devices, swap(): return lax.ppermute(x, 'chan', [(i, i ^ mask) for i in range(n_chan)])  5.06 us
    unnamed x15, local copies, waits for them, and re-layouts  4.68 us
    ppermute x1, starting transfers between devices, body(): before = lax.ppermute(spectra, 'chan', [(i, i + 1) for i in range(ends)])  3.05 us
    pallas_call x1, Pallas kernels, body(): pl.pallas_call(own_kernel, out_shape=jax.ShapeDtypeStruct((2, tiles, coun...  2.05 us
  transfers between devices with their start and end apart: 9, of which 3 were waited for; matrix products, arithmetic and copies ran while one was open for 3% of the time, Pallas kernels for 4%

profile of v3, /device:TPU:0, one launch (start us, length us, event | category | flops | bytes accessed | tf_op | source)
XLA Modules:
  0.0 52.5 jit_solution(12368091918508790478)
XLA Ops:
  0.0 0.0 copy-start
  0.0 0.9 %copy-done = bf16[2,4,32,512]{3,2,1,0:T(8,128)(2,1)S(1)} copy-done((bf16[2,4,32,512]{3,2,1,0:T(8,128)(2,1)S(1)}, bf16[2,4,32,512]{3,2,1,0:T(8,128)(2,1)}, u32[]{:S(2)}) %copy-start) | copy-done | bytes 262168
  1.0 0.0 copy-start.2
  1.0 0.7 %copy-done.2 = s32[4,32]{1,0:T(4,128)S(1)} copy-done((s32[4,32]{1,0:T(4,128)S(1)}, s32[4,32]{1,0:T(4,128)}, u32[]{:S(2)}) %copy-start.2) | copy-done | bytes 536
  1.6 0.8 %split.1 = bf16[16,80,128]{2,1,0:T(8,128)(2,1)} custom-call(bf16[2,4,32,512]{3,2,1,0:T(8,128)(2,1)S(1)} %copy-done, s32[4,32]{1,0:T(4,128)S(1)} %copy-done.2), custom_call_target="tpu_custom_call" | custom-call | tf_op jit(solution)/shard_map/split/pallas_call | solution.py:239
  2.4 7.4 %all-to-all-start = ((bf16[16,80,128]{2,1,0:T(8,128)(2,1)}), bf16[16,80,128]{2,1,0:T(8,128)(2,1)S(1)}, u32[]{:S(2)}, u32[]{:S(2)}) async-start(bf16[16,80,128]{2,1,0:T(8,128)(2,1)} %split.1), calls=%async_computation | async-start | bytes 655360 | tf_op jit(solution)/shard_map/all_to_all | solution.py:246
  9.8 0.8 %reshape.6 = s32[128]{0:T(128)S(1)} reshape(s32[4,32]{1,0:T(4,128)} %param.11) | data formatting | bytes 1024 | tf_op jit(solution)/shard_map/reshape | solution.py:251
  10.6 0.0 copy-start.3
  10.6 0.7 %copy-done.3 = s32[4,32]{1,0:T(4,128)S(1)} copy-done((s32[4,32]{1,0:T(4,128)S(1)}, s32[4,32]{1,0:T(4,128)}, u32[]{:S(2)}) %copy-start.3) | copy-done | bytes 536
  11.3 0.0 copy-start.4
  11.3 0.7 %copy-done.4 = f32[2,8,65]{2,1,0:T(8,128)S(1)} copy-done((f32[2,8,65]{2,1,0:T(8,128)S(1)}, f32[2,8,65]{2,1,0:T(8,128)}, u32[]{:S(2)}) %copy-start.4) | copy-done | bytes 4184
  12.0 0.0 copy-start.5
  12.0 0.7 %copy-done.5 = s32[512]{0:T(512)S(1)} copy-done((s32[512]{0:T(512)S(1)}, s32[512]{0:T(512)}, u32[]{:S(2)}) %copy-start.5) | copy-done | bytes 2072
  12.6 0.2 prep.1
  12.9 0.7 %pad_add_fusion.params_ref = s32[133]{0:T(256)S(1)} fusion(s32[128]{0:T(128)S(1)} %reshape.6, s32[4]{0:T(128)} %param.10, s32[1]{0:T(128)} %bitcast), kind=kLoop, calls=%fused_computation.4 | loop fusion | flops 266 | bytes 1064 | tf_op jit(solution)/shard_map/concatenate | solution.py:251
  13.6 7.3 %all-to-all-done = bf16[16,80,128]{2,1,0:T(8,128)(2,1)S(1)} async-done(((bf16[16,80,128]{2,1,0:T(8,128)(2,1)}), bf16[16,80,128]{2,1,0:T(8,128)(2,1)S(1)}, u32[]{:S(2)}, u32[]{:S(2)}) %all-to-all-start) | async-done | bytes 327712 | tf_op jit(solution)/shard_map/all_to_all | solution.py:246
  20.9 1.0 %source_filter.1 = bf16[1,4,2,32,128]{4,3,2,1,0:T(8,128)(2,1)S(1)} custom-call(s32[133]{0:T(256)S(1)} %pad_add_fusion.params_ref, bf16[16,1,80,128]{3,2,1,0:T(8,128)(2,1)S(1)} %bitcast.3, bf16[1024,256]{1,0:T(8,128)(2,1)S(1)} %get-tuple-element.13.weight_ref, s32[4,1,128]{2,1,0:T(1,128)S(1)} %get-tuple-element.14.index_ref), custom_call_target="tpu_custom_call" | custom-call | tf_op jit(solution)/shard_map/source_filter/pallas_call | solution.py:267
  21.9 1.2 %collective-permute-start.2 = (bf16[1,4,2,32,128]{4,3,2,1,0:T(8,128)(2,1)S(1)}, bf16[1,4,2,32,128]{4,3,2,1,0:T(8,128)(2,1)S(1)}, u32[]{:S(2)}, u32[]{:S(2)}) collective-permute-start(bf16[1,4,2,32,128]{4,3,2,1,0:T(8,128)(2,1)S(1)} %source_filter.1), channel_id=1, source_target_pairs={{0,12},{1,13},{2,14},{3,15},{4,8},{5,9},{6,10},{7,11},{8,4},{9,5},... | collective-permute-start | bytes 196616 | tf_op jit(solution)/shard_map/ppermute | solution.py:222
  23.1 0.6 %collective-permute-start.1 = (bf16[1,4,2,32,128]{4,3,2,1,0:T(8,128)(2,1)S(1)}, bf16[1,4,2,32,128]{4,3,2,1,0:T(8,128)(2,1)S(1)}, u32[]{:S(2)}, u32[]{:S(2)}) collective-permute-start(bf16[1,4,2,32,128]{4,3,2,1,0:T(8,128)(2,1)S(1)} %source_filter.1), channel_id=1, source_target_pairs={{0,8},{1,9},{2,10},{3,11},{4,12},{5,13},{6,14},{7,15},{8,0},{9,1},... | collective-permute-start | bytes 196616 | tf_op jit(solution)/shard_map/ppermute | solution.py:222
  23.7 2.6 %collective-permute-start = (bf16[1,4,2,32,128]{4,3,2,1,0:T(8,128)(2,1)S(1)}, bf16[1,4,2,32,128]{4,3,2,1,0:T(8,128)(2,1)S(1)}, u32[]{:S(2)}, u32[]{:S(2)}) collective-permute-start(bf16[1,4,2,32,128]{4,3,2,1,0:T(8,128)(2,1)S(1)} %source_filter.1), channel_id=1, source_target_pairs={{0,4},{1,5},{2,6},{3,7},{4,0},{5,1},{6,2},{7,3},{8,12},{9,13},{10,... | collective-permute-start | bytes 196616 | tf_op jit(solution)/shard_map/ppermute | solution.py:222
  26.4 1.3 %collective-permute-start.5 = (bf16[2,4,32,512]{3,2,1,0:T(8,128)(2,1)}, bf16[2,4,32,512]{3,2,1,0:T(8,128)(2,1)S(1)}, u32[]{:S(2)}, u32[]{:S(2)}) collective-permute-start(bf16[2,4,32,512]{3,2,1,0:T(8,128)(2,1)} %cur_ref), channel_id=1, source_target_pairs={{1,0},{2,1},{3,2},{4,3},{5,4},{6,5},{7,6},{8,7},{9,8},{10,9},{11,1... | collective-permute-start | bytes 786440 | tf_op jit(solution)/shard_map/ppermute | solution.py:288
  27.7 3.1 %collective-permute-start.4 = (bf16[2,4,32,512]{3,2,1,0:T(8,128)(2,1)}, bf16[2,4,32,512]{3,2,1,0:T(8,128)(2,1)S(1)}, u32[]{:S(2)}, u32[]{:S(2)}) collective-permute-start(bf16[2,4,32,512]{3,2,1,0:T(8,128)(2,1)} %cur_ref), channel_id=1, source_target_pairs={{0,1},{1,2},{2,3},{3,4},{4,5},{5,6},{6,7},{7,8},{8,9},{9,10},{10,1... | collective-permute-start | bytes 786440 | tf_op jit(solution)/shard_map/ppermute | solution.py:287
  30.7 0.0 collective-permute-done
  30.8 0.0 collective-permute-done.1
  30.8 0.0 collective-permute-done.2
  30.8 0.7 %collective-permute-start.3 = (bf16[4,4,2,32,128]{4,3,2,1,0:T(8,128)(2,1)S(1)}, bf16[4,4,2,32,128]{4,3,2,1,0:T(8,128)(2,1)S(1)}, u32[]{:S(2)}, u32[]{:S(2)}) collective-permute-start(bf16[4,4,2,32,128]{4,3,2,1,0:T(8,128)(2,1)S(1)} %constant_dynamic-update-slice_fusion.refs_0_), channel_id=1, source_target_pairs={{0,2},{1,3},{2,0},{3,1},{4,6},{5,7},{6,4},{7,5},{8,10},{9,11},{10,... | collective-permute-start | bytes 786440 | tf_op jit(solution)/shard_map/ppermute | solution.py:222
  31.5 1.1 %collective-permute-start.6 = (bf16[4,4,2,32,128]{4,3,2,1,0:T(8,128)(2,1)S(1)}, bf16[4,4,2,32,128]{4,3,2,1,0:T(8,128)(2,1)S(1)}, u32[]{:S(2)}, u32[]{:S(2)}) collective-permute-start(bf16[4,4,2,32,128]{4,3,2,1,0:T(8,128)(2,1)S(1)} %constant_dynamic-update-slice_fusion.refs_0_), channel_id=1, source_target_pairs={{0,1},{1,0},{2,3},{3,2},{4,5},{5,4},{6,7},{7,6},{8,9},{9,8},{10,11... | collective-permute-start | bytes 786440 | tf_op jit(solution)/shard_map/ppermute | solution.py:222
  32.7 0.0 collective-permute-done.5.next_ref
  32.7 0.0 collective-permute-done.4.prev_ref
  32.7 0.0 copy-start.1
  32.7 0.9 %copy-done.1 = bf16[2,4,32,512]{3,2,1,0:T(8,128)(2,1)S(1)} copy-done((bf16[2,4,32,512]{3,2,1,0:T(8,128)(2,1)S(1)}, bf16[2,4,32,512]{3,2,1,0:T(8,128)(2,1)}, u32[]{:S(2)}) %copy-start.1) | copy-done | bytes 262168
  33.6 2.1 %own_whiten.1.refs_4_ = bf16[2,4,128,128]{3,2,1,0:T(8,128)(2,1)S(1)} custom-call(bf16[2,4,32,512]{3,2,1,0:T(8,128)(2,1)S(1)} %collective-permute-done.4.prev_ref, bf16[2,4,32,512]{3,2,1,0:T(8,128)(2,1)S(1)} %copy-done.1, bf16[2,4,32,512]{3,2,1,0:T(8,128)(2,1)S(1)} %collective-permute-done.5.next_ref, bf16[1024,256]{1,0:T(8,128)(2,1)S(1)} %get-tuple-element.13.weight_ref, ...), custom_call_target="tpu_custom_call" | custom-call | flops 1073741824 | bytes 3145728 | tf_op jit(solution)/shard_map/own_whiten/pallas_call | solution.py:290
  35.7 3.9 %collective-permute-done.3.refs_1_ = bf16[4,4,2,32,128]{4,3,2,1,0:T(8,128)(2,1)S(1)} collective-permute-done((bf16[4,4,2,32,128]{4,3,2,1,0:T(8,128)(2,1)S(1)}, bf16[4,4,2,32,128]{4,3,2,1,0:T(8,128)(2,1)S(1)}, u32[]{:S(2)}, u32[]{:S(2)}) %collective-permute-start.3) | collective-permute-done | bytes 262176 | tf_op jit(solution)/shard_map/ppermute | solution.py:222
  39.6 2.1 %collective-permute-start.7 = (bf16[4,4,2,32,128]{4,3,2,1,0:T(8,128)(2,1)S(1)}, bf16[4,4,2,32,128]{4,3,2,1,0:T(8,128)(2,1)S(1)}, u32[]{:S(2)}, u32[]{:S(2)}) collective-permute-start(bf16[4,4,2,32,128]{4,3,2,1,0:T(8,128)(2,1)S(1)} %collective-permute-done.3.refs_1_), channel_id=1, source_target_pairs={{0,1},{1,0},{2,3},{3,2},{4,5},{5,4},{6,7},{7,6},{8,9},{9,8},{10,11... | collective-permute-start | bytes 786440 | tf_op jit(solution)/shard_map/ppermute | solution.py:222
  41.7 0.0 collective-permute-done.6.refs_2_
  41.7 1.2 %collective-permute-done.7.refs_3_ = bf16[4,4,2,32,128]{4,3,2,1,0:T(8,128)(2,1)S(1)} collective-permute-done((bf16[4,4,2,32,128]{4,3,2,1,0:T(8,128)(2,1)S(1)}, bf16[4,4,2,32,128]{4,3,2,1,0:T(8,128)(2,1)S(1)}, u32[]{:S(2)}, u32[]{:S(2)}) %collective-permute-start.7) | collective-permute-done | bytes 262176 | tf_op jit(solution)/shard_map/ppermute | solution.py:222
  42.8 9.7 %cross.1 = bf16[2,128,32,512]{3,2,1,0:T(8,128)(2,1)} custom-call(s32[133]{0:T(256)S(1)} %pad_add_fusion.params_ref, bf16[4,4,2,32,128]{4,3,2,1,0:T(8,128)(2,1)S(1)} %constant_dynamic-update-slice_fusion.refs_0_, bf16[4,4,2,32,128]{4,3,2,1,0:T(8,128)(2,1)S(1)} %collective-permute-done.3.refs_1_, ...), custom_call_target="tpu_custom_call" | custom-call | tf_op jit(solution)/shard_map/cross/pallas_call | solution.py:313
  (4 shorter events, 0.1 us)
Async XLA Ops:
  0.0 0.9 %copy-start = (bf16[2,4,32,512]{3,2,1,0:T(8,128)(2,1)S(1)}, bf16[2,4,32,512]{3,2,1,0:T(8,128)(2,1)}, u32[]{:S(2)}) copy-start(bf16[2,4,32,512]{3,2,1,0:T(8,128)(2,1)} %cur_ref) | copy-start | bytes 786436
  1.0 0.7 %copy-start.2 = (s32[4,32]{1,0:T(4,128)S(1)}, s32[4,32]{1,0:T(4,128)}, u32[]{:S(2)}) copy-start(s32[4,32]{1,0:T(4,128)} %flags_ref.3) | copy-start | bytes 1540
  2.4 18.5 %all-to-all-start = ((bf16[16,80,128]{2,1,0:T(8,128)(2,1)}), bf16[16,80,128]{2,1,0:T(8,128)(2,1)S(1)}, u32[]{:S(2)}, u32[]{:S(2)}) async-start(bf16[16,80,128]{2,1,0:T(8,128)(2,1)} %split.1), calls=%async_computation | async-start | bytes 655360 | tf_op jit(solution)/shard_map/all_to_all | solution.py:246
  10.6 0.7 %copy-start.3 = (s32[4,32]{1,0:T(4,128)S(1)}, s32[4,32]{1,0:T(4,128)}, u32[]{:S(2)}) copy-start(s32[4,32]{1,0:T(4,128)} %flags_ref.3) | copy-start | bytes 1540
  11.3 0.7 %copy-start.4 = (f32[2,8,65]{2,1,0:T(8,128)S(1)}, f32[2,8,65]{2,1,0:T(8,128)}, u32[]{:S(2)}) copy-start(f32[2,8,65]{2,1,0:T(8,128)} %bank_ref.1) | copy-start | bytes 12484
  12.0 0.7 %copy-start.5 = (s32[512]{0:T(512)S(1)}, s32[512]{0:T(512)}, u32[]{:S(2)}) copy-start(s32[512]{0:T(512)} %param.8) | copy-start | bytes 6148
  21.9 8.9 %collective-permute-start.2 = (bf16[1,4,2,32,128]{4,3,2,1,0:T(8,128)(2,1)S(1)}, bf16[1,4,2,32,128]{4,3,2,1,0:T(8,128)(2,1)S(1)}, u32[]{:S(2)}, u32[]{:S(2)}) collective-permute-start(bf16[1,4,2,32,128]{4,3,2,1,0:T(8,128)(2,1)S(1)} %source_filter.1), channel_id=1, source_target_pairs={{0,12},{1,13},{2,14},{3,15},{4,8},{5,9},{6,10},{7,11},{8,4},{9,5},... | collective-permute-start | bytes 196616 | tf_op jit(solution)/shard_map/ppermute | solution.py:222
  23.1 7.7 %collective-permute-start.1 = (bf16[1,4,2,32,128]{4,3,2,1,0:T(8,128)(2,1)S(1)}, bf16[1,4,2,32,128]{4,3,2,1,0:T(8,128)(2,1)S(1)}, u32[]{:S(2)}, u32[]{:S(2)}) collective-permute-start(bf16[1,4,2,32,128]{4,3,2,1,0:T(8,128)(2,1)S(1)} %source_filter.1), channel_id=1, source_target_pairs={{0,8},{1,9},{2,10},{3,11},{4,12},{5,13},{6,14},{7,15},{8,0},{9,1},... | collective-permute-start | bytes 196616 | tf_op jit(solution)/shard_map/ppermute | solution.py:222
  23.7 7.0 %collective-permute-start = (bf16[1,4,2,32,128]{4,3,2,1,0:T(8,128)(2,1)S(1)}, bf16[1,4,2,32,128]{4,3,2,1,0:T(8,128)(2,1)S(1)}, u32[]{:S(2)}, u32[]{:S(2)}) collective-permute-start(bf16[1,4,2,32,128]{4,3,2,1,0:T(8,128)(2,1)S(1)} %source_filter.1), channel_id=1, source_target_pairs={{0,4},{1,5},{2,6},{3,7},{4,0},{5,1},{6,2},{7,3},{8,12},{9,13},{10,... | collective-permute-start | bytes 196616 | tf_op jit(solution)/shard_map/ppermute | solution.py:222
  26.4 6.3 %collective-permute-start.5 = (bf16[2,4,32,512]{3,2,1,0:T(8,128)(2,1)}, bf16[2,4,32,512]{3,2,1,0:T(8,128)(2,1)S(1)}, u32[]{:S(2)}, u32[]{:S(2)}) collective-permute-start(bf16[2,4,32,512]{3,2,1,0:T(8,128)(2,1)} %cur_ref), channel_id=1, source_target_pairs={{1,0},{2,1},{3,2},{4,3},{5,4},{6,5},{7,6},{8,7},{9,8},{10,9},{11,1... | collective-permute-start | bytes 786440 | tf_op jit(solution)/shard_map/ppermute | solution.py:288
  27.7 5.0 %collective-permute-start.4 = (bf16[2,4,32,512]{3,2,1,0:T(8,128)(2,1)}, bf16[2,4,32,512]{3,2,1,0:T(8,128)(2,1)S(1)}, u32[]{:S(2)}, u32[]{:S(2)}) collective-permute-start(bf16[2,4,32,512]{3,2,1,0:T(8,128)(2,1)} %cur_ref), channel_id=1, source_target_pairs={{0,1},{1,2},{2,3},{3,4},{4,5},{5,6},{6,7},{7,8},{8,9},{9,10},{10,1... | collective-permute-start | bytes 786440 | tf_op jit(solution)/shard_map/ppermute | solution.py:287
  30.8 8.8 %collective-permute-start.3 = (bf16[4,4,2,32,128]{4,3,2,1,0:T(8,128)(2,1)S(1)}, bf16[4,4,2,32,128]{4,3,2,1,0:T(8,128)(2,1)S(1)}, u32[]{:S(2)}, u32[]{:S(2)}) collective-permute-start(bf16[4,4,2,32,128]{4,3,2,1,0:T(8,128)(2,1)S(1)} %constant_dynamic-update-slice_fusion.refs_0_), channel_id=1, source_target_pairs={{0,2},{1,3},{2,0},{3,1},{4,6},{5,7},{6,4},{7,5},{8,10},{9,11},{10,... | collective-permute-start | bytes 786440 | tf_op jit(solution)/shard_map/ppermute | solution.py:222
  31.5 10.1 %collective-permute-start.6 = (bf16[4,4,2,32,128]{4,3,2,1,0:T(8,128)(2,1)S(1)}, bf16[4,4,2,32,128]{4,3,2,1,0:T(8,128)(2,1)S(1)}, u32[]{:S(2)}, u32[]{:S(2)}) collective-permute-start(bf16[4,4,2,32,128]{4,3,2,1,0:T(8,128)(2,1)S(1)} %constant_dynamic-update-slice_fusion.refs_0_), channel_id=1, source_target_pairs={{0,1},{1,0},{2,3},{3,2},{4,5},{5,4},{6,7},{7,6},{8,9},{9,8},{10,11... | collective-permute-start | bytes 786440 | tf_op jit(solution)/shard_map/ppermute | solution.py:222
  32.7 1.0 %copy-start.1 = (bf16[2,4,32,512]{3,2,1,0:T(8,128)(2,1)S(1)}, bf16[2,4,32,512]{3,2,1,0:T(8,128)(2,1)}, u32[]{:S(2)}) copy-start(bf16[2,4,32,512]{3,2,1,0:T(8,128)(2,1)} %cur_ref) | copy-start | bytes 786436
  39.6 3.2 %collective-permute-start.7 = (bf16[4,4,2,32,128]{4,3,2,1,0:T(8,128)(2,1)S(1)}, bf16[4,4,2,32,128]{4,3,2,1,0:T(8,128)(2,1)S(1)}, u32[]{:S(2)}, u32[]{:S(2)}) collective-permute-start(bf16[4,4,2,32,128]{4,3,2,1,0:T(8,128)(2,1)S(1)} %collective-permute-done.3.refs_1_), channel_id=1, source_target_pairs={{0,1},{1,0},{2,3},{3,2},{4,5},{5,4},{6,7},{7,6},{8,9},{9,8},{10,11... | collective-permute-start | bytes 786440 | tf_op jit(solution)/shard_map/ppermute | solution.py:222

commit v4 on v3

--- a/solution.py
+++ b/solution.py
@@ -25,10 +25,10 @@
         flags = jnp.broadcast_to(flags_ref[w : w + 1, :], (extra, ch)).astype(jnp.float32)
         for t in range(tiles):
             at = slice(t * LANES, (t + 1) * LANES)
-            piece_ref[w * tiles + t, :ch] = spectra_ref[0, w, :, at]
-            piece_ref[w * tiles + t, ch : 2 * ch] = spectra_ref[1, w, :, at]
-            piece_ref[w * tiles + t, 2 * ch :] = jnp.zeros((extra, LANES), jnp.bfloat16)
-            piece_ref[w * tiles + t, 2 * ch :, :ch] = flags.astype(jnp.bfloat16)
+            piece_ref[t * win + w, :ch] = spectra_ref[0, w, :, at]
+            piece_ref[t * win + w, ch : 2 * ch] = spectra_ref[1, w, :, at]
+            piece_ref[t * win + w, 2 * ch :] = jnp.zeros((extra, LANES), jnp.bfloat16)
+            piece_ref[t * win + w, 2 * ch :, :ch] = flags.astype(jnp.bfloat16)
 
 
 def prep_kernel(bank_ref, bins_ref, flags_ref, weight_ref, band_ref, index_ref, valid_ref, padded_ref):
@@ -90,16 +90,15 @@
     return lax.rsqrt((total[:count] + total[count:]) * (1.0 / SMOOTH) + WATER)
 
 
-def source_kernel(params_ref, x_ref, weight_ref, index_ref, out_ref):
+def source_kernel(params_ref, x_ref, weight_ref, index_ref, out_ref, *, win):
     n_chan = x_ref.shape[0]
     _, rounds, _, ch, _ = out_ref.shape
-    tiles = index_ref.shape[0]
-    tile = lax.rem(params_ref[0] + pl.program_id(0), tiles)
+    tile = lax.div(params_ref[0] + pl.program_id(0), win)
     zero = jnp.zeros((), jnp.bfloat16)
     gap = jnp.zeros((LANES - 3 * ch, LANES), jnp.bfloat16)
     columns = []
     for r in range(rounds):
-        block = params_ref[1 + r]
+        block = params_ref[2 + r]
         before = jnp.maximum(block - 1, 0)
         after = jnp.minimum(block + 1, n_chan - 1)
         parts = []
@@ -114,7 +113,7 @@
     index = jnp.concatenate([index_ref[tile]] * rounds, axis=1)
     pick = filtered_block(x, weight_ref, index, ch)
     for r in range(rounds):
-        flags = x_ref[params_ref[1 + r], 0, 2 * ch :].astype(jnp.float32)[:1, :ch]
+        flags = x_ref[params_ref[2 + r], 0, 2 * ch :].astype(jnp.float32)[:1, :ch]
         valid = flag_column(flags)
         for p in range(2):
             part = pick[p * ch : (p + 1) * ch, r * LANES : (r + 1) * LANES] * valid
@@ -144,11 +143,36 @@
     for p in range(2):
         white = (filt_ref[p] * scale).astype(jnp.bfloat16)
         for t in range(tiles):
-            out_ref[p, t] = white[:, t * LANES : (t + 1) * LANES]
-
-
-def spread_row(ref, r, p, ft, row, ch):
-    eight = ref[r, p, ft, pl.ds(row, 8, stride=0), :]
+            for w in range(win):
+                out_ref[p, t, w] = white[w * ch : (w + 1) * ch, t * LANES : (t + 1) * LANES]
+
+
+def column_kernel(params_ref, *refs):
+    band_ref, out_ref, piece_ref = refs[-3:]
+    parts = refs[:-3]
+    tiles, rounds, _, ch, _ = piece_ref.shape
+    if len(parts) == tiles:
+        place = params_ref[1]
+        for k, ref in enumerate(parts):
+            piece_ref[place ^ k] = ref[0]
+    else:
+        piece_ref[...] = parts[0][:, 0]
+    both = []
+    for p in range(2):
+        rows = [
+            jnp.concatenate([piece_ref[t, r, p] for t in range(tiles)], axis=1) for r in range(rounds)
+        ]
+        both.append(jnp.concatenate(rows, axis=0).astype(jnp.float32))
+    scale = running_scale(both[0], both[1], band_ref)
+    for p in range(2):
+        white = (both[p] * scale).astype(jnp.bfloat16)
+        for t in range(tiles):
+            for r in range(rounds):
+                out_ref[0, t, r, p] = white[r * ch : (r + 1) * ch, t * LANES : (t + 1) * LANES]
+
+
+def spread_row(ref, at, row, ch):
+    eight = ref[(*at, pl.ds(row, 8, stride=0), slice(None))]
     pair = jnp.concatenate([eight, eight], axis=0).astype(jnp.bfloat16)
     return jnp.concatenate([pair] * (ch // 16), axis=0)
 
@@ -160,59 +184,43 @@
     return terms[0]
 
 
-def cross_kernel(params_ref, *refs, masks):
-    filt_refs = refs[: len(masks)]
-    local_ref, band_ref, out_ref, piece_ref, source_ref = refs[len(masks) :]
+def cross_kernel(params_ref, *refs, masks, added):
+    column_refs = refs[: len(masks)]
+    local_ref, out_ref, source_ref = refs[len(masks)], refs[-2], refs[-1]
     ch = out_ref.shape[2]
-    pieces, rounds = piece_ref.shape[:2]
-    tiles = local_ref.shape[1]
-    win = pieces // tiles
+    tiles, win = local_ref.shape[1:3]
+    rounds = source_ref.shape[2]
     per_round = ch // SRC_STEP
     step = pl.program_id(0)
     r = step // per_round
-    first = 1 + rounds + step * SRC_STEP
+    first = 2 + rounds + step * SRC_STEP
+    here = lax.rem(params_ref[0], win)
 
     @pl.when(step == 0)
     def _():
-        stride = pieces // filt_refs[0].shape[0]
-        for mask, ref in zip(masks, filt_refs):
-            for k in range(ref.shape[0]):
-                piece_ref[params_ref[0] ^ (mask ^ (k * stride))] = ref[k]
-
-        def one_round(rr, _):
-            parts = []
-            for p in range(2):
-                rows = [
-                    jnp.concatenate([piece_ref[w * tiles + t, rr, p] for t in range(tiles)], axis=1)
-                    for w in range(win)
-                ]
-                parts.append(jnp.concatenate(rows, axis=0).astype(jnp.float32))
-            scale = running_scale(parts[0], parts[1], band_ref)
-            for p in range(2):
-                white = (parts[p] * scale).astype(jnp.bfloat16).astype(jnp.float32) * (1.0 / win)
-                for t in range(tiles):
-                    source_ref[rr, p, t] = white[:, t * LANES : (t + 1) * LANES]
-            return 0
-
-        lax.fori_loop(0, rounds, one_round, 0)
+        for i, ref in enumerate(column_refs):
+            for t in range(tiles):
+                source_ref[i, t] = ref[0, t].astype(jnp.float32) * (1.0 / win)
 
     def one_tile(ft, _):
         at = pl.ds(pl.multiple_of(ft * LANES, LANES), LANES)
-        mine = [
-            (local_ref[0, ft, w * ch : (w + 1) * ch, :], local_ref[1, ft, w * ch : (w + 1) * ch, :])
-            for w in range(win)
-        ]
+        mine = [(local_ref[0, ft, here ^ mask], local_ref[1, ft, here ^ mask]) for mask in masks]
         for j in range(SRC_STEP):
             row = params_ref[first + j]
             re = []
             im = []
-            for w in range(win):
-                sr, si = (spread_row(source_ref, r, p, ft, w * ch + row, ch) for p in range(2))
-                lr, li = mine[w]
+            for i in range(len(masks)):
+                sr, si = (spread_row(source_ref, (i, ft, r, p), row, ch) for p in range(2))
+                lr, li = mine[i]
                 re.append(sr * lr + si * li)
                 im.append(sr * li - si * lr)
-            out_ref[0, j, :, at] = pairwise(re)
-            out_ref[1, j, :, at] = pairwise(im)
+            re = pairwise(re)
+            im = pairwise(im)
+            if added:
+                re = re + refs[-3][0, j, :, at]
+                im = im + refs[-3][1, j, :, at]
+            out_ref[0, j, :, at] = re
+            out_ref[1, j, :, at] = im
         return 0
 
     lax.fori_loop(0, tiles, one_tile, 0)
@@ -232,14 +240,14 @@
     tiles = freq // LANES
     pieces = win * tiles
     sources = rounds * ch
-    in_parts = n_chan == pieces and n_chan >= 4 and n_chan & (n_chan - 1) == 0
+    in_parts = n_chan == pieces and win == 4 and tiles & (tiles - 1) == 0
     smem = pl.BlockSpec(memory_space=pltpu.SMEM)
     vmem = pl.BlockSpec(memory_space=pltpu.VMEM)
 
     split = pl.pallas_call(
         split_kernel,
         out_shape=jax.ShapeDtypeStruct((pieces, 2 * ch + 16, LANES), jnp.bfloat16),
-        compiler_params=room(6),
+        compiler_params=room(56),
         name="split",
     )(spectra, window_mask)
     if in_parts:
@@ -248,7 +256,12 @@
     else:
         held = lax.all_gather(split, "chan")
         first = jnp.int32(0)
-    params = jnp.concatenate([first[None], owner_order, source_offset.reshape(-1)])
+    params = jnp.concatenate([first[None], lax.div(first, jnp.int32(win))[None], owner_order, source_offset.reshape(-1)])
+
+    ends = n_chan - 1
+    before = lax.ppermute(spectra, "chan", [(i, i + 1) for i in range(ends)])
+    after = lax.ppermute(spectra, "chan", [(i + 1, i) for i in range(ends)])
+    held, before, after = lax.optimization_barrier((held, before, after))
 
     weight, band, index, valid = pl.pallas_call(
         prep_kernel,
@@ -265,7 +278,7 @@
 
     count_here = held.shape[1]
     filtered = pl.pallas_call(
-        source_kernel,
+        functools.partial(source_kernel, win=win),
         grid=(count_here,),
         in_specs=[
             smem,
@@ -279,17 +292,12 @@
         name="source_filter",
     )(params, held, weight, index)
 
-    spectra, filtered = lax.optimization_barrier((spectra, filtered))
     if in_parts:
-        masks = (0, 2, 1, 3)
-        column = [filtered] + [swap(filtered, m, n_chan) for m in range(4, n_chan, 4)]
-    ends = n_chan - 1
-    before = lax.ppermute(spectra, "chan", [(i, i + 1) for i in range(ends)])
-    after = lax.ppermute(spectra, "chan", [(i + 1, i) for i in range(ends)])
+        zparts = [filtered] + [swap(filtered, win * k, n_chan) for k in range(1, tiles)]
 
     local = pl.pallas_call(
         own_kernel,
-        out_shape=jax.ShapeDtypeStruct((2, tiles, count, LANES), jnp.bfloat16),
+        out_shape=jax.ShapeDtypeStruct((2, tiles, win, ch, LANES), jnp.bfloat16),
         in_specs=[vmem] * 7,
         out_specs=vmem,
         scratch_shapes=[pltpu.VMEM((2, count, freq), jnp.float32)],
@@ -300,29 +308,49 @@
         name="own_whiten",
     )(before, spectra, after, weight, band, index, valid)
 
+    shape = (tiles, rounds, 2, ch, LANES)
     if in_parts:
-        column = jnp.concatenate(column, axis=0)
-        far = swap(column, 2, n_chan)
-        beside = swap(column, 1, n_chan)
-        far, local = lax.optimization_barrier((far, local))
-        parts = (column, far, beside, swap(far, 1, n_chan))
+        zparts[-1], local = lax.optimization_barrier((zparts[-1], local))
+        windows = 1
+        specs = [vmem] * tiles
     else:
-        masks = (0,)
-        parts = (filtered,)
-
-    return pl.pallas_call(
-        functools.partial(cross_kernel, masks=masks),
-        grid=(sources // SRC_STEP,),
-        in_specs=[smem] + [vmem] * (len(parts) + 2),
-        out_specs=pl.BlockSpec((2, SRC_STEP, ch, freq), lambda s: (0, s, 0, 0)),
-        out_shape=jax.ShapeDtypeStruct((2, sources, ch, freq), jnp.bfloat16),
-        scratch_shapes=[
-            pltpu.VMEM((pieces, rounds, 2, ch, LANES), jnp.bfloat16),
-            pltpu.VMEM((rounds, 2, tiles, count, LANES), jnp.float32),
-        ],
-        compiler_params=room(24),
-        name="cross",
-    )(params, *parts, local, band)
+        windows = win
+        zparts = [filtered.reshape((tiles, win) + shape[1:])]
+        specs = [pl.BlockSpec((tiles, 1) + shape[1:], lambda s: (0, s, 0, 0, 0, 0))]
+    column = pl.pallas_call(
+        column_kernel,
+        grid=(windows,),
+        in_specs=[smem] + specs + [vmem],
+        out_specs=pl.BlockSpec((1,) + shape, lambda s: (s, 0, 0, 0, 0, 0)),
+        out_shape=jax.ShapeDtypeStruct((windows,) + shape, jnp.bfloat16),
+        scratch_shapes=[pltpu.VMEM(shape, jnp.bfloat16)],
+        compiler_params=room(16),
+        name="column_whiten",
+    )(params, *zparts, band)
+
+    def cross(masks, columns, earlier):
+        block = pl.BlockSpec((2, SRC_STEP, ch, freq), lambda s: (0, s, 0, 0))
+        return pl.pallas_call(
+            functools.partial(cross_kernel, masks=masks, added=len(earlier) > 0),
+            grid=(sources // SRC_STEP,),
+            in_specs=[smem] + [vmem] * (len(columns) + 1) + [block] * len(earlier),
+            out_specs=block,
+            out_shape=jax.ShapeDtypeStruct((2, sources, ch, freq), jnp.bfloat16),
+            scratch_shapes=[pltpu.VMEM((len(masks),) + shape, jnp.float32)],
+            compiler_params=room(24),
+            cost_estimate=pl.CostEstimate(
+                flops=16 * len(masks) * sources * ch * freq, bytes_accessed=16 << 20, transcendentals=0
+            ),
+            name="cross",
+        )(params, *columns, local, *earlier)
+
+    if not in_parts:
+        return cross(tuple(range(win)), [column[w : w + 1] for w in range(win)], [])
+    far = swap(column, 2, n_chan)
+    beside = swap(column, 1, n_chan)
+    partial = cross((0, 1), [column, beside], [])
+    far, partial = lax.optimization_barrier((far, partial))
+    return cross((2, 3), [far, swap(far, 1, n_chan)], [partial])
 
 
 def solution(mesh):

time: 52.9 us -> 50.6 us (0.957)
  Pallas kernels: 13.8 us -> 17.9 us
  waiting for transfers between devices: 12.3 us -> 9.11 us
  local copies, waits for them, and re-layouts: 5.46 us -> 3.77 us
  starting transfers between devices: 20.1 us -> 18.6 us
    all_to_all x1, waiting for transfers between devices: 7.28 us -> 3.66 us  [body(): held = lax.all_to_all(split, 'chan', 0, 0)[:, None]]
    pallas_call x3 -> x5, Pallas kernels: 12.7 us -> 15.9 us  [the longest x2 11.9 us: cross(): pl.pallas_call(functools.partial(cross_kernel, masks=masks, added=len(ear...]
    unnamed x15 -> x8, local copies, waits for them, and re-layouts: 4.68 us -> 3.01 us
    pallas_call x1, Pallas kernels: 0.78 us -> 1.73 us  [body(): pl.pallas_call(split_kernel, out_shape=jax.ShapeDtypeStruct((pieces, 2 *...]
    ppermute x6, starting transfers between devices: 8.38 us -> 7.63 us  [swap(): return lax.ppermute(x, 'chan', [(i, i ^ mask) for i in range(n_chan)])]
    ppermute x1, starting transfers between devices: 3.05 us -> 2.32 us  [body(): before = lax.ppermute(spectra, 'chan', [(i, i + 1) for i in range(ends)])]
  transfers between devices with their start and end apart: 9 -> 9, of which waited for: 3 -> 5; matrix products, arithmetic and copies ran while one was open for 3% -> 3% of each run, Pallas kernels for 4% -> 14%
where the time goes in v4:
time: 50.6 us; the launch traced here: 50.2 us
  starting transfers between devices  18.6 us (37%)
  Pallas kernels  17.9 us (35%)
  waiting for transfers between devices  9.11 us (18%)
  local copies, waits for them, and re-layouts  3.77 us (7%)
  other arithmetic  0.74 us (1%)
    pallas_call x2, Pallas kernels, cross(): pl.pallas_call(functools.partial(cross_kernel, masks=masks, added=len(ear...  11.9 us
    ppermute x6, starting transfers between devices, swap(): return lax.ppermute(x, 'chan', [(i, i ^ mask) for i in range(n_chan)])  7.63 us
    all_to_all x1, starting transfers between devices, body(): held = lax.all_to_all(split, 'chan', 0, 0)[:, None]  7.39 us
    ppermute x6, waiting for transfers between devices, swap(): return lax.ppermute(x, 'chan', [(i, i ^ mask) for i in range(n_chan)])  5.44 us
    all_to_all x1, waiting for transfers between devices, body(): held = lax.all_to_all(split, 'chan', 0, 0)[:, None]  3.66 us
    unnamed x8, local copies, waits for them, and re-layouts  3.01 us
    ppermute x1, starting transfers between devices, body(): before = lax.ppermute(spectra, 'chan', [(i, i + 1) for i in range(ends)])  2.32 us
    pallas_call x1, Pallas kernels, body(): pl.pallas_call(own_kernel, out_shape=jax.ShapeDtypeStruct((2, tiles, win,...  2.06 us
  transfers between devices with their start and end apart: 9, of which 5 were waited for; matrix products, arithmetic and copies ran while one was open for 3% of the time, Pallas kernels for 14%

profile of v4, /device:TPU:0, one launch (start us, length us, event | category | flops | bytes accessed | tf_op | source)
XLA Modules:
  0.0 50.2 jit_solution(7936293414516813840)
XLA Ops:
  0.0 1.7 %split.1 = bf16[16,80,128]{2,1,0:T(8,128)(2,1)} custom-call(bf16[2,4,32,512]{3,2,1,0:T(8,128)(2,1)} %cur_ref.1, s32[4,32]{1,0:T(4,128)} %flags_ref.3), custom_call_target="tpu_custom_call" | custom-call | tf_op jit(solution)/shard_map/split/pallas_call | solution.py:247
  1.7 7.4 %all-to-all-start = ((bf16[16,80,128]{2,1,0:T(8,128)(2,1)}), bf16[16,80,128]{2,1,0:T(8,128)(2,1)S(1)}, u32[]{:S(2)}, u32[]{:S(2)}) async-start(bf16[16,80,128]{2,1,0:T(8,128)(2,1)} %split.1), calls=%async_computation | async-start | bytes 655360 | tf_op jit(solution)/shard_map/all_to_all | solution.py:254
  9.1 2.3 %collective-permute-start = (bf16[2,4,32,512]{3,2,1,0:T(8,128)(2,1)}, bf16[2,4,32,512]{3,2,1,0:T(8,128)(2,1)S(1)}, u32[]{:S(2)}, u32[]{:S(2)}) collective-permute-start(bf16[2,4,32,512]{3,2,1,0:T(8,128)(2,1)} %cur_ref.1), channel_id=1, source_target_pairs={{0,1},{1,2},{2,3},{3,4},{4,5},{5,6},{6,7},{7,8},{8,9},{9,10},{10,1... | collective-permute-start | bytes 786440 | tf_op jit(solution)/shard_map/ppermute | solution.py:262
  11.5 1.3 %collective-permute-start.1 = (bf16[2,4,32,512]{3,2,1,0:T(8,128)(2,1)}, bf16[2,4,32,512]{3,2,1,0:T(8,128)(2,1)S(1)}, u32[]{:S(2)}, u32[]{:S(2)}) collective-permute-start(bf16[2,4,32,512]{3,2,1,0:T(8,128)(2,1)} %cur_ref.1), channel_id=1, source_target_pairs={{1,0},{2,1},{3,2},{4,3},{5,4},{6,5},{7,6},{8,7},{9,8},{10,9},{11,1... | collective-permute-start | bytes 786440 | tf_op jit(solution)/shard_map/ppermute | solution.py:263
  12.8 0.8 %reshape.6 = s32[128]{0:T(128)S(1)} reshape(s32[4,32]{1,0:T(4,128)} %param.11) | data formatting | bytes 1024 | tf_op jit(solution)/shard_map/reshape | solution.py:259
  13.5 0.0 copy-start.1
  13.5 0.7 %copy-done.1 = s32[4,32]{1,0:T(4,128)S(1)} copy-done((s32[4,32]{1,0:T(4,128)S(1)}, s32[4,32]{1,0:T(4,128)}, u32[]{:S(2)}) %copy-start.1) | copy-done | bytes 536
  14.2 0.0 copy-start.2
  14.2 0.7 %copy-done.2 = f32[2,8,65]{2,1,0:T(8,128)S(1)} copy-done((f32[2,8,65]{2,1,0:T(8,128)S(1)}, f32[2,8,65]{2,1,0:T(8,128)}, u32[]{:S(2)}) %copy-start.2) | copy-done | bytes 4184
  14.9 0.0 copy-start.3
  14.9 0.7 %copy-done.3 = s32[512]{0:T(512)S(1)} copy-done((s32[512]{0:T(512)S(1)}, s32[512]{0:T(512)}, u32[]{:S(2)}) %copy-start.3) | copy-done | bytes 2072
  15.6 0.2 prep.1
  15.8 0.7 %pad_add_fusion.params_ref = s32[134]{0:T(256)S(1)} fusion(s32[128]{0:T(128)S(1)} %reshape.6, s32[4]{0:T(128)} %param.10, s32[1]{0:T(128)} %bitcast.1, s32[1]{0:T(128)} %bitcast), kind=kLoop, calls=%fused_computation | loop fusion | flops 402 | bytes 1072 | tf_op jit(solution)/shard_map/concatenate | solution.py:259
  16.6 0.0 collective-permute-done.prev_ref
  16.6 0.0 collective-permute-done.1.next_ref
  16.6 3.7 %all-to-all-done = bf16[16,80,128]{2,1,0:T(8,128)(2,1)S(1)} async-done(((bf16[16,80,128]{2,1,0:T(8,128)(2,1)}), bf16[16,80,128]{2,1,0:T(8,128)(2,1)S(1)}, u32[]{:S(2)}, u32[]{:S(2)}) %all-to-all-start) | async-done | bytes 327712 | tf_op jit(solution)/shard_map/all_to_all | solution.py:254
  20.3 1.0 %source_filter.1.refs_0_ = bf16[1,4,2,32,128]{4,3,2,1,0:T(8,128)(2,1)S(1)} custom-call(s32[134]{0:T(256)S(1)} %pad_add_fusion.params_ref, bf16[16,1,80,128]{3,2,1,0:T(8,128)(2,1)S(1)} %bitcast.4, bf16[1024,256]{1,0:T(8,128)(2,1)S(1)} %get-tuple-element.17.weight_ref, s32[4,1,128]{2,1,0:T(1,128)S(1)} %get-tuple-element.18.index_ref), custom_call_target="tpu_custom_call" | custom-call | tf_op jit(solution)/shard_map/source_filter/pallas_call | solution.py:280
  21.3 3.5 %collective-permute-start.4 = (bf16[1,4,2,32,128]{4,3,2,1,0:T(8,128)(2,1)S(1)}, bf16[1,4,2,32,128]{4,3,2,1,0:T(8,128)(2,1)S(1)}, u32[]{:S(2)}, u32[]{:S(2)}) collective-permute-start(bf16[1,4,2,32,128]{4,3,2,1,0:T(8,128)(2,1)S(1)} %source_filter.1.refs_0_), channel_id=1, source_target_pairs={{0,12},{1,13},{2,14},{3,15},{4,8},{5,9},{6,10},{7,11},{8,4},{9,5},... | collective-permute-start | bytes 196616 | tf_op jit(solution)/shard_map/ppermute | solution.py:230
  24.8 1.0 %collective-permute-start.3 = (bf16[1,4,2,32,128]{4,3,2,1,0:T(8,128)(2,1)S(1)}, bf16[1,4,2,32,128]{4,3,2,1,0:T(8,128)(2,1)S(1)}, u32[]{:S(2)}, u32[]{:S(2)}) collective-permute-start(bf16[1,4,2,32,128]{4,3,2,1,0:T(8,128)(2,1)S(1)} %source_filter.1.refs_0_), channel_id=1, source_target_pairs={{0,8},{1,9},{2,10},{3,11},{4,12},{5,13},{6,14},{7,15},{8,0},{9,1},... | collective-permute-start | bytes 196616 | tf_op jit(solution)/shard_map/ppermute | solution.py:230
  25.7 0.5 collective-permute-start.2
  26.2 0.0 copy-start
  26.2 0.9 %copy-done = bf16[2,4,32,512]{3,2,1,0:T(8,128)(2,1)S(1)} copy-done((bf16[2,4,32,512]{3,2,1,0:T(8,128)(2,1)S(1)}, bf16[2,4,32,512]{3,2,1,0:T(8,128)(2,1)}, u32[]{:S(2)}) %copy-start) | copy-done | bytes 262168
  27.2 2.1 %own_whiten.1.refs_2_ = bf16[2,4,4,32,128]{4,3,2,1,0:T(8,128)(2,1)S(1)} custom-call(bf16[2,4,32,512]{3,2,1,0:T(8,128)(2,1)S(1)} %collective-permute-done.prev_ref, bf16[2,4,32,512]{3,2,1,0:T(8,128)(2,1)S(1)} %copy-done, bf16[2,4,32,512]{3,2,1,0:T(8,128)(2,1)S(1)} %collective-permute-done.1.next_ref, bf16[1024,256]{1,0:T(8,128)(2,1)S(1)} %get-tuple-element.17.weight_ref, ...), custom_call_target="tpu_custom_call" | custom-call | flops 1073741824 | bytes 3145728 | tf_op jit(solution)/shard_map/own_whiten/pallas_call | solution.py:298
  29.2 0.0 collective-permute-done.4.refs_3_
  29.2 1.1 %collective-permute-done.3.refs_2_ = bf16[1,4,2,32,128]{4,3,2,1,0:T(8,128)(2,1)S(1)} collective-permute-done((bf16[1,4,2,32,128]{4,3,2,1,0:T(8,128)(2,1)S(1)}, bf16[1,4,2,32,128]{4,3,2,1,0:T(8,128)(2,1)S(1)}, u32[]{:S(2)}, u32[]{:S(2)}) %collective-permute-start.3) | collective-permute-done | bytes 65568 | tf_op jit(solution)/shard_map/ppermute | solution.py:230
  30.3 0.7 %collective-permute-done.2.refs_1_ = bf16[1,4,2,32,128]{4,3,2,1,0:T(8,128)(2,1)S(1)} collective-permute-done((bf16[1,4,2,32,128]{4,3,2,1,0:T(8,128)(2,1)S(1)}, bf16[1,4,2,32,128]{4,3,2,1,0:T(8,128)(2,1)S(1)}, u32[]{:S(2)}, u32[]{:S(2)}) %collective-permute-start.2) | collective-permute-done | bytes 65568 | tf_op jit(solution)/shard_map/ppermute | solution.py:230
  31.0 0.9 %column_whiten.1.refs_0_ = bf16[1,4,4,2,32,128]{5,4,3,2,1,0:T(8,128)(2,1)S(1)} custom-call(s32[134]{0:T(256)S(1)} %pad_add_fusion.params_ref, bf16[1,4,2,32,128]{4,3,2,1,0:T(8,128)(2,1)S(1)} %source_filter.1.refs_0_, bf16[1,4,2,32,128]{4,3,2,1,0:T(8,128)(2,1)S(1)} %collective-permute-done.2.refs_1_, ...), custom_call_target="tpu_custom_call" | custom-call | tf_op jit(solution)/shard_map/column_whiten/pallas_call | solution.py:320
  31.9 1.2 %collective-permute-start.6 = (bf16[1,4,4,2,32,128]{5,4,3,2,1,0:T(8,128)(2,1)S(1)}, bf16[1,4,4,2,32,128]{5,4,3,2,1,0:T(8,128)(2,1)S(1)}, u32[]{:S(2)}, u32[]{:S(2)}) collective-permute-start(bf16[1,4,4,2,32,128]{5,4,3,2,1,0:T(8,128)(2,1)S(1)} %column_whiten.1.refs_0_), channel_id=1, source_target_pairs={{0,1},{1,0},{2,3},{3,2},{4,5},{5,4},{6,7},{7,6},{8,9},{9,8},{10,11... | collective-permute-start | bytes 786440 | tf_op jit(solution)/shard_map/ppermute | solution.py:230
  33.1 1.5 %collective-permute-start.5 = (bf16[1,4,4,2,32,128]{5,4,3,2,1,0:T(8,128)(2,1)S(1)}, bf16[1,4,4,2,32,128]{5,4,3,2,1,0:T(8,128)(2,1)S(1)}, u32[]{:S(2)}, u32[]{:S(2)}) collective-permute-start(bf16[1,4,4,2,32,128]{5,4,3,2,1,0:T(8,128)(2,1)S(1)} %column_whiten.1.refs_0_), channel_id=1, source_target_pairs={{0,2},{1,3},{2,0},{3,1},{4,6},{5,7},{6,4},{7,5},{8,10},{9,11},{10,... | collective-permute-start | bytes 786440 | tf_op jit(solution)/shard_map/ppermute | solution.py:230
  34.6 0.0 collective-permute-done.6.refs_1_
  34.6 4.8 %cross.2.refs_3_ = bf16[2,128,32,512]{3,2,1,0:T(8,128)(2,1)S(1)} custom-call(s32[134]{0:T(256)S(1)} %pad_add_fusion.params_ref, bf16[1,4,4,2,32,128]{5,4,3,2,1,0:T(8,128)(2,1)S(1)} %column_whiten.1.refs_0_, bf16[1,4,4,2,32,128]{5,4,3,2,1,0:T(8,128)(2,1)S(1)} %collective-permute-done.6.refs_1_, bf16[2,4,4,32,128]{4,3,2,1,0:T(8,128)(2,1)S(1)} %own_whiten.1.refs_2_), custom_call_target="tpu_custom_call" | custom-call | flops 67108864 | bytes 16777216 | tf_op jit(solution)/shard_map/cross/pallas_call | solution.py:333
  39.4 2.1 %collective-permute-done.5.refs_0_ = bf16[1,4,4,2,32,128]{5,4,3,2,1,0:T(8,128)(2,1)S(1)} collective-permute-done((bf16[1,4,4,2,32,128]{5,4,3,2,1,0:T(8,128)(2,1)S(1)}, bf16[1,4,4,2,32,128]{5,4,3,2,1,0:T(8,128)(2,1)S(1)}, u32[]{:S(2)}, u32[]{:S(2)}) %collective-permute-start.5) | collective-permute-done | bytes 262176 | tf_op jit(solution)/shard_map/ppermute | solution.py:230
  41.5 0.0 collective-permute-start.7
  41.5 1.5 %collective-permute-done.7.refs_1_ = bf16[1,4,4,2,32,128]{5,4,3,2,1,0:T(8,128)(2,1)S(1)} collective-permute-done((bf16[1,4,4,2,32,128]{5,4,3,2,1,0:T(8,128)(2,1)S(1)}, bf16[1,4,4,2,32,128]{5,4,3,2,1,0:T(8,128)(2,1)S(1)}, u32[]{:S(2)}, u32[]{:S(2)}) %collective-permute-start.7) | collective-permute-done | bytes 262176 | tf_op jit(solution)/shard_map/ppermute | solution.py:230
  43.0 7.2 %cross.3 = bf16[2,128,32,512]{3,2,1,0:T(8,128)(2,1)} custom-call(s32[134]{0:T(256)S(1)} %pad_add_fusion.params_ref, bf16[1,4,4,2,32,128]{5,4,3,2,1,0:T(8,128)(2,1)S(1)} %collective-permute-done.5.refs_0_, bf16[1,4,4,2,32,128]{5,4,3,2,1,0:T(8,128)(2,1)S(1)} %collective-permute-done.7.refs_1_, bf16[2,4,4,32,128]{4,3,2,1,0:T(8,128)(2,1)S(1)} %own_whiten.1.refs_2_, ...), custom_call_target="tpu_custom_call" | custom-call | flops 67108864 | bytes 16777216 | tf_op jit(solution)/shard_map/cross/pallas_call | solution.py:333
Async XLA Ops:
  1.7 18.5 %all-to-all-start = ((bf16[16,80,128]{2,1,0:T(8,128)(2,1)}), bf16[16,80,128]{2,1,0:T(8,128)(2,1)S(1)}, u32[]{:S(2)}, u32[]{:S(2)}) async-start(bf16[16,80,128]{2,1,0:T(8,128)(2,1)} %split.1), calls=%async_computation | async-start | bytes 655360 | tf_op jit(solution)/shard_map/all_to_all | solution.py:254
  9.1 7.5 %collective-permute-start = (bf16[2,4,32,512]{3,2,1,0:T(8,128)(2,1)}, bf16[2,4,32,512]{3,2,1,0:T(8,128)(2,1)S(1)}, u32[]{:S(2)}, u32[]{:S(2)}) collective-permute-start(bf16[2,4,32,512]{3,2,1,0:T(8,128)(2,1)} %cur_ref.1), channel_id=1, source_target_pairs={{0,1},{1,2},{2,3},{3,4},{4,5},{5,6},{6,7},{7,8},{8,9},{9,10},{10,1... | collective-permute-start | bytes 786440 | tf_op jit(solution)/shard_map/ppermute | solution.py:262
  11.5 5.1 %collective-permute-start.1 = (bf16[2,4,32,512]{3,2,1,0:T(8,128)(2,1)}, bf16[2,4,32,512]{3,2,1,0:T(8,128)(2,1)S(1)}, u32[]{:S(2)}, u32[]{:S(2)}) collective-permute-start(bf16[2,4,32,512]{3,2,1,0:T(8,128)(2,1)} %cur_ref.1), channel_id=1, source_target_pairs={{1,0},{2,1},{3,2},{4,3},{5,4},{6,5},{7,6},{8,7},{9,8},{10,9},{11,1... | collective-permute-start | bytes 786440 | tf_op jit(solution)/shard_map/ppermute | solution.py:263
  13.5 0.7 %copy-start.1 = (s32[4,32]{1,0:T(4,128)S(1)}, s32[4,32]{1,0:T(4,128)}, u32[]{:S(2)}) copy-start(s32[4,32]{1,0:T(4,128)} %flags_ref.3) | copy-start | bytes 1540
  14.2 0.7 %copy-start.2 = (f32[2,8,65]{2,1,0:T(8,128)S(1)}, f32[2,8,65]{2,1,0:T(8,128)}, u32[]{:S(2)}) copy-start(f32[2,8,65]{2,1,0:T(8,128)} %bank_ref.1) | copy-start | bytes 12484
  14.9 0.7 %copy-start.3 = (s32[512]{0:T(512)S(1)}, s32[512]{0:T(512)}, u32[]{:S(2)}) copy-start(s32[512]{0:T(512)} %param.8) | copy-start | bytes 6148
  21.3 8.0 %collective-permute-start.4 = (bf16[1,4,2,32,128]{4,3,2,1,0:T(8,128)(2,1)S(1)}, bf16[1,4,2,32,128]{4,3,2,1,0:T(8,128)(2,1)S(1)}, u32[]{:S(2)}, u32[]{:S(2)}) collective-permute-start(bf16[1,4,2,32,128]{4,3,2,1,0:T(8,128)(2,1)S(1)} %source_filter.1.refs_0_), channel_id=1, source_target_pairs={{0,12},{1,13},{2,14},{3,15},{4,8},{5,9},{6,10},{7,11},{8,4},{9,5},... | collective-permute-start | bytes 196616 | tf_op jit(solution)/shard_map/ppermute | solution.py:230
  24.8 5.5 %collective-permute-start.3 = (bf16[1,4,2,32,128]{4,3,2,1,0:T(8,128)(2,1)S(1)}, bf16[1,4,2,32,128]{4,3,2,1,0:T(8,128)(2,1)S(1)}, u32[]{:S(2)}, u32[]{:S(2)}) collective-permute-start(bf16[1,4,2,32,128]{4,3,2,1,0:T(8,128)(2,1)S(1)} %source_filter.1.refs_0_), channel_id=1, source_target_pairs={{0,8},{1,9},{2,10},{3,11},{4,12},{5,13},{6,14},{7,15},{8,0},{9,1},... | collective-permute-start | bytes 196616 | tf_op jit(solution)/shard_map/ppermute | solution.py:230
  25.7 5.3 %collective-permute-start.2 = (bf16[1,4,2,32,128]{4,3,2,1,0:T(8,128)(2,1)S(1)}, bf16[1,4,2,32,128]{4,3,2,1,0:T(8,128)(2,1)S(1)}, u32[]{:S(2)}, u32[]{:S(2)}) collective-permute-start(bf16[1,4,2,32,128]{4,3,2,1,0:T(8,128)(2,1)S(1)} %source_filter.1.refs_0_), channel_id=1, source_target_pairs={{0,4},{1,5},{2,6},{3,7},{4,0},{5,1},{6,2},{7,3},{8,12},{9,13},{10,... | collective-permute-start | bytes 196616 | tf_op jit(solution)/shard_map/ppermute | solution.py:230
  26.2 0.9 %copy-start = (bf16[2,4,32,512]{3,2,1,0:T(8,128)(2,1)S(1)}, bf16[2,4,32,512]{3,2,1,0:T(8,128)(2,1)}, u32[]{:S(2)}) copy-start(bf16[2,4,32,512]{3,2,1,0:T(8,128)(2,1)} %cur_ref.1) | copy-start | bytes 786436
  31.9 2.7 %collective-permute-start.6 = (bf16[1,4,4,2,32,128]{5,4,3,2,1,0:T(8,128)(2,1)S(1)}, bf16[1,4,4,2,32,128]{5,4,3,2,1,0:T(8,128)(2,1)S(1)}, u32[]{:S(2)}, u32[]{:S(2)}) collective-permute-start(bf16[1,4,4,2,32,128]{5,4,3,2,1,0:T(8,128)(2,1)S(1)} %column_whiten.1.refs_0_), channel_id=1, source_target_pairs={{0,1},{1,0},{2,3},{3,2},{4,5},{5,4},{6,7},{7,6},{8,9},{9,8},{10,11... | collective-permute-start | bytes 786440 | tf_op jit(solution)/shard_map/ppermute | solution.py:230
  33.1 8.4 %collective-permute-start.5 = (bf16[1,4,4,2,32,128]{5,4,3,2,1,0:T(8,128)(2,1)S(1)}, bf16[1,4,4,2,32,128]{5,4,3,2,1,0:T(8,128)(2,1)S(1)}, u32[]{:S(2)}, u32[]{:S(2)}) collective-permute-start(bf16[1,4,4,2,32,128]{5,4,3,2,1,0:T(8,128)(2,1)S(1)} %column_whiten.1.refs_0_), channel_id=1, source_target_pairs={{0,2},{1,3},{2,0},{3,1},{4,6},{5,7},{6,4},{7,5},{8,10},{9,11},{10,... | collective-permute-start | bytes 786440 | tf_op jit(solution)/shard_map/ppermute | solution.py:230
  41.5 1.5 %collective-permute-start.7 = (bf16[1,4,4,2,32,128]{5,4,3,2,1,0:T(8,128)(2,1)S(1)}, bf16[1,4,4,2,32,128]{5,4,3,2,1,0:T(8,128)(2,1)S(1)}, u32[]{:S(2)}, u32[]{:S(2)}) collective-permute-start(bf16[1,4,4,2,32,128]{5,4,3,2,1,0:T(8,128)(2,1)S(1)} %collective-permute-done.5.refs_0_), channel_id=1, source_target_pairs={{0,1},{1,0},{2,3},{3,2},{4,5},{5,4},{6,7},{7,6},{8,9},{9,8},{10,11... | collective-permute-start | bytes 786440 | tf_op jit(solution)/shard_map/ppermute | solution.py:230

commit v5 on v4

--- a/solution.py
+++ b/solution.py
@@ -187,8 +187,7 @@
 def cross_kernel(params_ref, *refs, masks, added):
     column_refs = refs[: len(masks)]
     local_ref, out_ref, source_ref = refs[len(masks)], refs[-2], refs[-1]
-    ch = out_ref.shape[2]
-    tiles, win = local_ref.shape[1:3]
+    tiles, win, ch = local_ref.shape[1:4]
     rounds = source_ref.shape[2]
     per_round = ch // SRC_STEP
     step = pl.program_id(0)
@@ -201,6 +200,8 @@
         for i, ref in enumerate(column_refs):
             for t in range(tiles):
                 source_ref[i, t] = ref[0, t].astype(jnp.float32) * (1.0 / win)
+
+    whole = out_ref.shape[1] > SRC_STEP
 
     def one_tile(ft, _):
         at = pl.ds(pl.multiple_of(ft * LANES, LANES), LANES)
@@ -217,10 +218,14 @@
             re = pairwise(re)
             im = pairwise(im)
             if added:
-                re = re + refs[-3][0, j, :, at]
-                im = im + refs[-3][1, j, :, at]
-            out_ref[0, j, :, at] = re
-            out_ref[1, j, :, at] = im
+                re = re + refs[-3][0, step * SRC_STEP + j, ft]
+                im = im + refs[-3][1, step * SRC_STEP + j, ft]
+            if whole:
+                out_ref[0, step * SRC_STEP + j, ft] = re
+                out_ref[1, step * SRC_STEP + j, ft] = im
+            else:
+                out_ref[0, j, :, at] = re
+                out_ref[1, j, :, at] = im
         return 0
 
     lax.fori_loop(0, tiles, one_tile, 0)
@@ -328,16 +333,21 @@
         name="column_whiten",
     )(params, *zparts, band)
 
-    def cross(masks, columns, earlier):
-        block = pl.BlockSpec((2, SRC_STEP, ch, freq), lambda s: (0, s, 0, 0))
+    def cross(masks, columns, earlier, final):
+        if final:
+            spec = pl.BlockSpec((2, SRC_STEP, ch, freq), lambda s: (0, s, 0, 0))
+            result = jax.ShapeDtypeStruct((2, sources, ch, freq), jnp.bfloat16)
+        else:
+            spec = vmem
+            result = jax.ShapeDtypeStruct((2, sources, tiles, ch, LANES), jnp.bfloat16)
         return pl.pallas_call(
             functools.partial(cross_kernel, masks=masks, added=len(earlier) > 0),
             grid=(sources // SRC_STEP,),
-            in_specs=[smem] + [vmem] * (len(columns) + 1) + [block] * len(earlier),
-            out_specs=block,
-            out_shape=jax.ShapeDtypeStruct((2, sources, ch, freq), jnp.bfloat16),
+            in_specs=[smem] + [vmem] * (len(columns) + 1 + len(earlier)),
+            out_specs=spec,
+            out_shape=result,
             scratch_shapes=[pltpu.VMEM((len(masks),) + shape, jnp.float32)],
-            compiler_params=room(24),
+            compiler_params=room(32),
             cost_estimate=pl.CostEstimate(
                 flops=16 * len(masks) * sources * ch * freq, bytes_accessed=16 << 20, transcendentals=0
             ),
@@ -345,12 +355,12 @@
         )(params, *columns, local, *earlier)
 
     if not in_parts:
-        return cross(tuple(range(win)), [column[w : w + 1] for w in range(win)], [])
+        return cross(tuple(range(win)), [column[w : w + 1] for w in range(win)], [], True)
     far = swap(column, 2, n_chan)
     beside = swap(column, 1, n_chan)
-    partial = cross((0, 1), [column, beside], [])
+    partial = cross((0, 1), [column, beside], [], False)
     far, partial = lax.optimization_barrier((far, partial))
-    return cross((2, 3), [far, swap(far, 1, n_chan)], [partial])
+    return cross((2, 3), [far, swap(far, 1, n_chan)], [partial], True)
 
 
 def solution(mesh):

time: 50.6 us -> 50.3 us (level)
  Pallas kernels: 17.9 us -> 17 us
  waiting for transfers between devices: 9.11 us -> 9.74 us
    pallas_call x2, Pallas kernels: 11.9 us -> 11 us  [cross(): pl.pallas_call(functools.partial(cross_kernel, masks=masks, added=len(ear...]
    ppermute x6, waiting for transfers between devices: 5.44 us -> 6.08 us  [swap(): return lax.ppermute(x, 'chan', [(i, i ^ mask) for i in range(n_chan)])]
  transfers between devices with their start and end apart: 9 -> 9, of which waited for: 5 -> 5; matrix products, arithmetic and copies ran while one was open for 3% -> 3% of each run, Pallas kernels for 14% -> 13%
where the time goes in v5:
time: 50.3 us; the launch traced here: 49.9 us
  starting transfers between devices  18.6 us (37%)
  Pallas kernels  17 us (34%)
  waiting for transfers between devices  9.74 us (19%)
  local copies, waits for them, and re-layouts  3.77 us (7%)
  other arithmetic  0.74 us (1%)
    pallas_call x2, Pallas kernels, cross(): pl.pallas_call(functools.partial(cross_kernel, masks=masks, added=len(ear...  11 us
    ppermute x6, starting transfers between devices, swap(): return lax.ppermute(x, 'chan', [(i, i ^ mask) for i in range(n_chan)])  7.6 us
    all_to_all x1, starting transfers between devices, body(): held = lax.all_to_all(split, 'chan', 0, 0)[:, None]  7.39 us
    ppermute x6, waiting for transfers between devices, swap(): return lax.ppermute(x, 'chan', [(i, i ^ mask) for i in range(n_chan)])  6.08 us
    all_to_all x1, waiting for transfers between devices, body(): held = lax.all_to_all(split, 'chan', 0, 0)[:, None]  3.66 us
    unnamed x8, local copies, waits for them, and re-layouts  3.01 us
    ppermute x1, starting transfers between devices, body(): before = lax.ppermute(spectra, 'chan', [(i, i + 1) for i in range(ends)])  2.32 us
    pallas_call x1, Pallas kernels, body(): pl.pallas_call(own_kernel, out_shape=jax.ShapeDtypeStruct((2, tiles, win,...  2.06 us
  transfers between devices with their start and end apart: 9, of which 5 were waited for; matrix products, arithmetic and copies ran while one was open for 3% of the time, Pallas kernels for 13%

profile of v5, /device:TPU:0, one launch (start us, length us, event | category | flops | bytes accessed | tf_op | source)
XLA Modules:
  0.0 49.9 jit_solution(10751367741022719033)
XLA Ops:
  0.0 1.7 %split.1 = bf16[16,80,128]{2,1,0:T(8,128)(2,1)} custom-call(bf16[2,4,32,512]{3,2,1,0:T(8,128)(2,1)} %cur_ref.1, s32[4,32]{1,0:T(4,128)} %flags_ref.3), custom_call_target="tpu_custom_call" | custom-call | tf_op jit(solution)/shard_map/split/pallas_call | solution.py:252
  1.7 7.4 %all-to-all-start = ((bf16[16,80,128]{2,1,0:T(8,128)(2,1)}), bf16[16,80,128]{2,1,0:T(8,128)(2,1)S(1)}, u32[]{:S(2)}, u32[]{:S(2)}) async-start(bf16[16,80,128]{2,1,0:T(8,128)(2,1)} %split.1), calls=%async_computation | async-start | bytes 655360 | tf_op jit(solution)/shard_map/all_to_all | solution.py:259
  9.1 2.3 %collective-permute-start = (bf16[2,4,32,512]{3,2,1,0:T(8,128)(2,1)}, bf16[2,4,32,512]{3,2,1,0:T(8,128)(2,1)S(1)}, u32[]{:S(2)}, u32[]{:S(2)}) collective-permute-start(bf16[2,4,32,512]{3,2,1,0:T(8,128)(2,1)} %cur_ref.1), channel_id=1, source_target_pairs={{0,1},{1,2},{2,3},{3,4},{4,5},{5,6},{6,7},{7,8},{8,9},{9,10},{10,1... | collective-permute-start | bytes 786440 | tf_op jit(solution)/shard_map/ppermute | solution.py:267
  11.5 1.3 %collective-permute-start.1 = (bf16[2,4,32,512]{3,2,1,0:T(8,128)(2,1)}, bf16[2,4,32,512]{3,2,1,0:T(8,128)(2,1)S(1)}, u32[]{:S(2)}, u32[]{:S(2)}) collective-permute-start(bf16[2,4,32,512]{3,2,1,0:T(8,128)(2,1)} %cur_ref.1), channel_id=1, source_target_pairs={{1,0},{2,1},{3,2},{4,3},{5,4},{6,5},{7,6},{8,7},{9,8},{10,9},{11,1... | collective-permute-start | bytes 786440 | tf_op jit(solution)/shard_map/ppermute | solution.py:268
  12.8 0.8 %reshape.6 = s32[128]{0:T(128)S(1)} reshape(s32[4,32]{1,0:T(4,128)} %param.11) | data formatting | bytes 1024 | tf_op jit(solution)/shard_map/reshape | solution.py:264
  13.5 0.0 copy-start.1
  13.5 0.7 %copy-done.1 = s32[4,32]{1,0:T(4,128)S(1)} copy-done((s32[4,32]{1,0:T(4,128)S(1)}, s32[4,32]{1,0:T(4,128)}, u32[]{:S(2)}) %copy-start.1) | copy-done | bytes 536
  14.2 0.0 copy-start.2
  14.2 0.7 %copy-done.2 = f32[2,8,65]{2,1,0:T(8,128)S(1)} copy-done((f32[2,8,65]{2,1,0:T(8,128)S(1)}, f32[2,8,65]{2,1,0:T(8,128)}, u32[]{:S(2)}) %copy-start.2) | copy-done | bytes 4184
  14.9 0.0 copy-start.3
  14.9 0.7 %copy-done.3 = s32[512]{0:T(512)S(1)} copy-done((s32[512]{0:T(512)S(1)}, s32[512]{0:T(512)}, u32[]{:S(2)}) %copy-start.3) | copy-done | bytes 2072
  15.6 0.2 prep.1
  15.8 0.7 %pad_add_fusion.params_ref = s32[134]{0:T(256)S(1)} fusion(s32[128]{0:T(128)S(1)} %reshape.6, s32[4]{0:T(128)} %param.10, s32[1]{0:T(128)} %bitcast.1, s32[1]{0:T(128)} %bitcast), kind=kLoop, calls=%fused_computation | loop fusion | flops 402 | bytes 1072 | tf_op jit(solution)/shard_map/concatenate | solution.py:264
  16.6 0.0 collective-permute-done.prev_ref
  16.6 0.0 collective-permute-done.1.next_ref
  16.6 3.7 %all-to-all-done = bf16[16,80,128]{2,1,0:T(8,128)(2,1)S(1)} async-done(((bf16[16,80,128]{2,1,0:T(8,128)(2,1)}), bf16[16,80,128]{2,1,0:T(8,128)(2,1)S(1)}, u32[]{:S(2)}, u32[]{:S(2)}) %all-to-all-start) | async-done | bytes 327712 | tf_op jit(solution)/shard_map/all_to_all | solution.py:259
  20.3 1.0 %source_filter.1.refs_0_ = bf16[1,4,2,32,128]{4,3,2,1,0:T(8,128)(2,1)S(1)} custom-call(s32[134]{0:T(256)S(1)} %pad_add_fusion.params_ref, bf16[16,1,80,128]{3,2,1,0:T(8,128)(2,1)S(1)} %bitcast.4, bf16[1024,256]{1,0:T(8,128)(2,1)S(1)} %get-tuple-element.17.weight_ref, s32[4,1,128]{2,1,0:T(1,128)S(1)} %get-tuple-element.18.index_ref), custom_call_target="tpu_custom_call" | custom-call | tf_op jit(solution)/shard_map/source_filter/pallas_call | solution.py:285
  21.3 3.5 %collective-permute-start.4 = (bf16[1,4,2,32,128]{4,3,2,1,0:T(8,128)(2,1)S(1)}, bf16[1,4,2,32,128]{4,3,2,1,0:T(8,128)(2,1)S(1)}, u32[]{:S(2)}, u32[]{:S(2)}) collective-permute-start(bf16[1,4,2,32,128]{4,3,2,1,0:T(8,128)(2,1)S(1)} %source_filter.1.refs_0_), channel_id=1, source_target_pairs={{0,12},{1,13},{2,14},{3,15},{4,8},{5,9},{6,10},{7,11},{8,4},{9,5},... | collective-permute-start | bytes 196616 | tf_op jit(solution)/shard_map/ppermute | solution.py:235
  24.8 1.0 %collective-permute-start.3 = (bf16[1,4,2,32,128]{4,3,2,1,0:T(8,128)(2,1)S(1)}, bf16[1,4,2,32,128]{4,3,2,1,0:T(8,128)(2,1)S(1)}, u32[]{:S(2)}, u32[]{:S(2)}) collective-permute-start(bf16[1,4,2,32,128]{4,3,2,1,0:T(8,128)(2,1)S(1)} %source_filter.1.refs_0_), channel_id=1, source_target_pairs={{0,8},{1,9},{2,10},{3,11},{4,12},{5,13},{6,14},{7,15},{8,0},{9,1},... | collective-permute-start | bytes 196616 | tf_op jit(solution)/shard_map/ppermute | solution.py:235
  25.7 0.5 collective-permute-start.2
  26.2 0.0 copy-start
  26.2 0.9 %copy-done = bf16[2,4,32,512]{3,2,1,0:T(8,128)(2,1)S(1)} copy-done((bf16[2,4,32,512]{3,2,1,0:T(8,128)(2,1)S(1)}, bf16[2,4,32,512]{3,2,1,0:T(8,128)(2,1)}, u32[]{:S(2)}) %copy-start) | copy-done | bytes 262168
  27.2 2.1 %own_whiten.1.refs_2_ = bf16[2,4,4,32,128]{4,3,2,1,0:T(8,128)(2,1)S(1)} custom-call(bf16[2,4,32,512]{3,2,1,0:T(8,128)(2,1)S(1)} %collective-permute-done.prev_ref, bf16[2,4,32,512]{3,2,1,0:T(8,128)(2,1)S(1)} %copy-done, bf16[2,4,32,512]{3,2,1,0:T(8,128)(2,1)S(1)} %collective-permute-done.1.next_ref, bf16[1024,256]{1,0:T(8,128)(2,1)S(1)} %get-tuple-element.17.weight_ref, ...), custom_call_target="tpu_custom_call" | custom-call | flops 1073741824 | bytes 3145728 | tf_op jit(solution)/shard_map/own_whiten/pallas_call | solution.py:303
  29.2 0.0 collective-permute-done.4.refs_3_
  29.2 1.1 %collective-permute-done.3.refs_2_ = bf16[1,4,2,32,128]{4,3,2,1,0:T(8,128)(2,1)S(1)} collective-permute-done((bf16[1,4,2,32,128]{4,3,2,1,0:T(8,128)(2,1)S(1)}, bf16[1,4,2,32,128]{4,3,2,1,0:T(8,128)(2,1)S(1)}, u32[]{:S(2)}, u32[]{:S(2)}) %collective-permute-start.3) | collective-permute-done | bytes 65568 | tf_op jit(solution)/shard_map/ppermute | solution.py:235
  30.3 0.8 %collective-permute-done.2.refs_1_ = bf16[1,4,2,32,128]{4,3,2,1,0:T(8,128)(2,1)S(1)} collective-permute-done((bf16[1,4,2,32,128]{4,3,2,1,0:T(8,128)(2,1)S(1)}, bf16[1,4,2,32,128]{4,3,2,1,0:T(8,128)(2,1)S(1)}, u32[]{:S(2)}, u32[]{:S(2)}) %collective-permute-start.2) | collective-permute-done | bytes 65568 | tf_op jit(solution)/shard_map/ppermute | solution.py:235
  31.1 0.9 %column_whiten.1.refs_0_ = bf16[1,4,4,2,32,128]{5,4,3,2,1,0:T(8,128)(2,1)S(1)} custom-call(s32[134]{0:T(256)S(1)} %pad_add_fusion.params_ref, bf16[1,4,2,32,128]{4,3,2,1,0:T(8,128)(2,1)S(1)} %source_filter.1.refs_0_, bf16[1,4,2,32,128]{4,3,2,1,0:T(8,128)(2,1)S(1)} %collective-permute-done.2.refs_1_, ...), custom_call_target="tpu_custom_call" | custom-call | tf_op jit(solution)/shard_map/column_whiten/pallas_call | solution.py:325
  32.0 1.1 %collective-permute-start.6 = (bf16[1,4,4,2,32,128]{5,4,3,2,1,0:T(8,128)(2,1)S(1)}, bf16[1,4,4,2,32,128]{5,4,3,2,1,0:T(8,128)(2,1)S(1)}, u32[]{:S(2)}, u32[]{:S(2)}) collective-permute-start(bf16[1,4,4,2,32,128]{5,4,3,2,1,0:T(8,128)(2,1)S(1)} %column_whiten.1.refs_0_), channel_id=1, source_target_pairs={{0,1},{1,0},{2,3},{3,2},{4,5},{5,4},{6,7},{7,6},{8,9},{9,8},{10,11... | collective-permute-start | bytes 786440 | tf_op jit(solution)/shard_map/ppermute | solution.py:235
  33.1 1.5 %collective-permute-start.5 = (bf16[1,4,4,2,32,128]{5,4,3,2,1,0:T(8,128)(2,1)S(1)}, bf16[1,4,4,2,32,128]{5,4,3,2,1,0:T(8,128)(2,1)S(1)}, u32[]{:S(2)}, u32[]{:S(2)}) collective-permute-start(bf16[1,4,4,2,32,128]{5,4,3,2,1,0:T(8,128)(2,1)S(1)} %column_whiten.1.refs_0_), channel_id=1, source_target_pairs={{0,2},{1,3},{2,0},{3,1},{4,6},{5,7},{6,4},{7,5},{8,10},{9,11},{10,... | collective-permute-start | bytes 786440 | tf_op jit(solution)/shard_map/ppermute | solution.py:235
  34.6 0.0 collective-permute-done.6.refs_1_
  34.6 4.2 %cross.2.refs_3_ = bf16[2,128,4,32,128]{4,3,2,1,0:T(8,128)(2,1)S(1)} custom-call(s32[134]{0:T(256)S(1)} %pad_add_fusion.params_ref, bf16[1,4,4,2,32,128]{5,4,3,2,1,0:T(8,128)(2,1)S(1)} %column_whiten.1.refs_0_, bf16[1,4,4,2,32,128]{5,4,3,2,1,0:T(8,128)(2,1)S(1)} %collective-permute-done.6.refs_1_, bf16[2,4,4,32,128]{4,3,2,1,0:T(8,128)(2,1)S(1)} %own_whiten.1.refs_2_), custom_call_target="tpu_custom_call" | custom-call | flops 67108864 | bytes 16777216 | tf_op jit(solution)/shard_map/cross/pallas_call | solution.py:343
  38.8 2.7 %collective-permute-done.5.refs_0_ = bf16[1,4,4,2,32,128]{5,4,3,2,1,0:T(8,128)(2,1)S(1)} collective-permute-done((bf16[1,4,4,2,32,128]{5,4,3,2,1,0:T(8,128)(2,1)S(1)}, bf16[1,4,4,2,32,128]{5,4,3,2,1,0:T(8,128)(2,1)S(1)}, u32[]{:S(2)}, u32[]{:S(2)}) %collective-permute-start.5) | collective-permute-done | bytes 262176 | tf_op jit(solution)/shard_map/ppermute | solution.py:235
  41.5 0.0 collective-permute-start.7
  41.5 1.5 %collective-permute-done.7.refs_1_ = bf16[1,4,4,2,32,128]{5,4,3,2,1,0:T(8,128)(2,1)S(1)} collective-permute-done((bf16[1,4,4,2,32,128]{5,4,3,2,1,0:T(8,128)(2,1)S(1)}, bf16[1,4,4,2,32,128]{5,4,3,2,1,0:T(8,128)(2,1)S(1)}, u32[]{:S(2)}, u32[]{:S(2)}) %collective-permute-start.7) | collective-permute-done | bytes 262176 | tf_op jit(solution)/shard_map/ppermute | solution.py:235
  43.0 6.9 %cross.3 = bf16[2,128,32,512]{3,2,1,0:T(8,128)(2,1)} custom-call(s32[134]{0:T(256)S(1)} %pad_add_fusion.params_ref, bf16[1,4,4,2,32,128]{5,4,3,2,1,0:T(8,128)(2,1)S(1)} %collective-permute-done.5.refs_0_, bf16[1,4,4,2,32,128]{5,4,3,2,1,0:T(8,128)(2,1)S(1)} %collective-permute-done.7.refs_1_, bf16[2,4,4,32,128]{4,3,2,1,0:T(8,128)(2,1)S(1)} %own_whiten.1.refs_2_, ...), custom_call_target="tpu_custom_call" | custom-call | flops 67108864 | bytes 16777216 | tf_op jit(solution)/shard_map/cross/pallas_call | solution.py:343
Async XLA Ops:
  1.7 18.5 %all-to-all-start = ((bf16[16,80,128]{2,1,0:T(8,128)(2,1)}), bf16[16,80,128]{2,1,0:T(8,128)(2,1)S(1)}, u32[]{:S(2)}, u32[]{:S(2)}) async-start(bf16[16,80,128]{2,1,0:T(8,128)(2,1)} %split.1), calls=%async_computation | async-start | bytes 655360 | tf_op jit(solution)/shard_map/all_to_all | solution.py:259
  9.1 7.5 %collective-permute-start = (bf16[2,4,32,512]{3,2,1,0:T(8,128)(2,1)}, bf16[2,4,32,512]{3,2,1,0:T(8,128)(2,1)S(1)}, u32[]{:S(2)}, u32[]{:S(2)}) collective-permute-start(bf16[2,4,32,512]{3,2,1,0:T(8,128)(2,1)} %cur_ref.1), channel_id=1, source_target_pairs={{0,1},{1,2},{2,3},{3,4},{4,5},{5,6},{6,7},{7,8},{8,9},{9,10},{10,1... | collective-permute-start | bytes 786440 | tf_op jit(solution)/shard_map/ppermute | solution.py:267
  11.5 5.1 %collective-permute-start.1 = (bf16[2,4,32,512]{3,2,1,0:T(8,128)(2,1)}, bf16[2,4,32,512]{3,2,1,0:T(8,128)(2,1)S(1)}, u32[]{:S(2)}, u32[]{:S(2)}) collective-permute-start(bf16[2,4,32,512]{3,2,1,0:T(8,128)(2,1)} %cur_ref.1), channel_id=1, source_target_pairs={{1,0},{2,1},{3,2},{4,3},{5,4},{6,5},{7,6},{8,7},{9,8},{10,9},{11,1... | collective-permute-start | bytes 786440 | tf_op jit(solution)/shard_map/ppermute | solution.py:268
  13.5 0.7 %copy-start.1 = (s32[4,32]{1,0:T(4,128)S(1)}, s32[4,32]{1,0:T(4,128)}, u32[]{:S(2)}) copy-start(s32[4,32]{1,0:T(4,128)} %flags_ref.3) | copy-start | bytes 1540
  14.2 0.7 %copy-start.2 = (f32[2,8,65]{2,1,0:T(8,128)S(1)}, f32[2,8,65]{2,1,0:T(8,128)}, u32[]{:S(2)}) copy-start(f32[2,8,65]{2,1,0:T(8,128)} %bank_ref.1) | copy-start | bytes 12484
  14.9 0.7 %copy-start.3 = (s32[512]{0:T(512)S(1)}, s32[512]{0:T(512)}, u32[]{:S(2)}) copy-start(s32[512]{0:T(512)} %param.8) | copy-start | bytes 6148
  21.3 8.0 %collective-permute-start.4 = (bf16[1,4,2,32,128]{4,3,2,1,0:T(8,128)(2,1)S(1)}, bf16[1,4,2,32,128]{4,3,2,1,0:T(8,128)(2,1)S(1)}, u32[]{:S(2)}, u32[]{:S(2)}) collective-permute-start(bf16[1,4,2,32,128]{4,3,2,1,0:T(8,128)(2,1)S(1)} %source_filter.1.refs_0_), channel_id=1, source_target_pairs={{0,12},{1,13},{2,14},{3,15},{4,8},{5,9},{6,10},{7,11},{8,4},{9,5},... | collective-permute-start | bytes 196616 | tf_op jit(solution)/shard_map/ppermute | solution.py:235
  24.8 5.5 %collective-permute-start.3 = (bf16[1,4,2,32,128]{4,3,2,1,0:T(8,128)(2,1)S(1)}, bf16[1,4,2,32,128]{4,3,2,1,0:T(8,128)(2,1)S(1)}, u32[]{:S(2)}, u32[]{:S(2)}) collective-permute-start(bf16[1,4,2,32,128]{4,3,2,1,0:T(8,128)(2,1)S(1)} %source_filter.1.refs_0_), channel_id=1, source_target_pairs={{0,8},{1,9},{2,10},{3,11},{4,12},{5,13},{6,14},{7,15},{8,0},{9,1},... | collective-permute-start | bytes 196616 | tf_op jit(solution)/shard_map/ppermute | solution.py:235
  25.7 5.3 %collective-permute-start.2 = (bf16[1,4,2,32,128]{4,3,2,1,0:T(8,128)(2,1)S(1)}, bf16[1,4,2,32,128]{4,3,2,1,0:T(8,128)(2,1)S(1)}, u32[]{:S(2)}, u32[]{:S(2)}) collective-permute-start(bf16[1,4,2,32,128]{4,3,2,1,0:T(8,128)(2,1)S(1)} %source_filter.1.refs_0_), channel_id=1, source_target_pairs={{0,4},{1,5},{2,6},{3,7},{4,0},{5,1},{6,2},{7,3},{8,12},{9,13},{10,... | collective-permute-start | bytes 196616 | tf_op jit(solution)/shard_map/ppermute | solution.py:235
  26.2 0.9 %copy-start = (bf16[2,4,32,512]{3,2,1,0:T(8,128)(2,1)S(1)}, bf16[2,4,32,512]{3,2,1,0:T(8,128)(2,1)}, u32[]{:S(2)}) copy-start(bf16[2,4,32,512]{3,2,1,0:T(8,128)(2,1)} %cur_ref.1) | copy-start | bytes 786436
  32.0 2.7 %collective-permute-start.6 = (bf16[1,4,4,2,32,128]{5,4,3,2,1,0:T(8,128)(2,1)S(1)}, bf16[1,4,4,2,32,128]{5,4,3,2,1,0:T(8,128)(2,1)S(1)}, u32[]{:S(2)}, u32[]{:S(2)}) collective-permute-start(bf16[1,4,4,2,32,128]{5,4,3,2,1,0:T(8,128)(2,1)S(1)} %column_whiten.1.refs_0_), channel_id=1, source_target_pairs={{0,1},{1,0},{2,3},{3,2},{4,5},{5,4},{6,7},{7,6},{8,9},{9,8},{10,11... | collective-permute-start | bytes 786440 | tf_op jit(solution)/shard_map/ppermute | solution.py:235
  33.1 8.4 %collective-permute-start.5 = (bf16[1,4,4,2,32,128]{5,4,3,2,1,0:T(8,128)(2,1)S(1)}, bf16[1,4,4,2,32,128]{5,4,3,2,1,0:T(8,128)(2,1)S(1)}, u32[]{:S(2)}, u32[]{:S(2)}) collective-permute-start(bf16[1,4,4,2,32,128]{5,4,3,2,1,0:T(8,128)(2,1)S(1)} %column_whiten.1.refs_0_), channel_id=1, source_target_pairs={{0,2},{1,3},{2,0},{3,1},{4,6},{5,7},{6,4},{7,5},{8,10},{9,11},{10,... | collective-permute-start | bytes 786440 | tf_op jit(solution)/shard_map/ppermute | solution.py:235
  41.5 1.5 %collective-permute-start.7 = (bf16[1,4,4,2,32,128]{5,4,3,2,1,0:T(8,128)(2,1)S(1)}, bf16[1,4,4,2,32,128]{5,4,3,2,1,0:T(8,128)(2,1)S(1)}, u32[]{:S(2)}, u32[]{:S(2)}) collective-permute-start(bf16[1,4,4,2,32,128]{5,4,3,2,1,0:T(8,128)(2,1)S(1)} %collective-permute-done.5.refs_0_), channel_id=1, source_target_pairs={{0,1},{1,0},{2,3},{3,2},{4,5},{5,4},{6,7},{7,6},{8,9},{9,8},{10,11... | collective-permute-start | bytes 786440 | tf_op jit(solution)/shard_map/ppermute | solution.py:235

commit v6 on v5

--- a/solution.py
+++ b/solution.py
@@ -11,6 +11,8 @@
 LANES = 128
 WATER = 0.05
 SRC_STEP = 16
+OUT_STEP = 8
+SLOTS = 4
 
 
 def room(mib):
@@ -184,16 +186,35 @@
     return terms[0]
 
 
-def cross_kernel(params_ref, *refs, masks, added):
+def cross_kernel(params_ref, *refs, masks, added, final):
     column_refs = refs[: len(masks)]
-    local_ref, out_ref, source_ref = refs[len(masks)], refs[-2], refs[-1]
+    local_ref = refs[len(masks)]
+    partial_ref = refs[len(masks) + 1]
+    if final:
+        out_ref, source_ref, stage_ref, sems = refs[-4:]
+        group = stage_ref.shape[2]
+    else:
+        out_ref, source_ref = refs[-2:]
+        group = SRC_STEP
     tiles, win, ch = local_ref.shape[1:4]
     rounds = source_ref.shape[2]
-    per_round = ch // SRC_STEP
+    per_round = ch // group
     step = pl.program_id(0)
+    steps = rounds * per_round
     r = step // per_round
-    first = 2 + rounds + step * SRC_STEP
+    begin = step * group
+    first = 2 + rounds + begin
     here = lax.rem(params_ref[0], win)
+    slot = lax.rem(step, SLOTS)
+
+    def copies(at_step):
+        at_slot = lax.rem(at_step, SLOTS)
+        return [
+            pltpu.make_async_copy(
+                stage_ref.at[at_slot, p], out_ref.at[p, pl.ds(at_step * group, group)], sems.at[at_slot, p]
+            )
+            for p in range(2)
+        ]
 
     @pl.when(step == 0)
     def _():
@@ -201,12 +222,17 @@
             for t in range(tiles):
                 source_ref[i, t] = ref[0, t].astype(jnp.float32) * (1.0 / win)
 
-    whole = out_ref.shape[1] > SRC_STEP
+    if final:
+
+        @pl.when(step >= SLOTS)
+        def _():
+            for copy in copies(step - SLOTS):
+                copy.wait()
 
     def one_tile(ft, _):
         at = pl.ds(pl.multiple_of(ft * LANES, LANES), LANES)
         mine = [(local_ref[0, ft, here ^ mask], local_ref[1, ft, here ^ mask]) for mask in masks]
-        for j in range(SRC_STEP):
+        for j in range(group):
             row = params_ref[first + j]
             re = []
             im = []
@@ -218,17 +244,27 @@
             re = pairwise(re)
             im = pairwise(im)
             if added:
-                re = re + refs[-3][0, step * SRC_STEP + j, ft]
-                im = im + refs[-3][1, step * SRC_STEP + j, ft]
-            if whole:
-                out_ref[0, step * SRC_STEP + j, ft] = re
-                out_ref[1, step * SRC_STEP + j, ft] = im
+                re = re + partial_ref[0, begin + j, ft]
+                im = im + partial_ref[1, begin + j, ft]
+            if final:
+                stage_ref[slot, 0, j, :, at] = re
+                stage_ref[slot, 1, j, :, at] = im
             else:
-                out_ref[0, j, :, at] = re
-                out_ref[1, j, :, at] = im
+                out_ref[0, begin + j, ft] = re
+                out_ref[1, begin + j, ft] = im
         return 0
 
     lax.fori_loop(0, tiles, one_tile, 0)
+
+    if final:
+        for copy in copies(step):
+            copy.start()
+
+        @pl.when(step == steps - 1)
+        def _():
+            for back in range(SLOTS):
+                for copy in copies(step - back):
+                    copy.wait()
 
 
 def swap(x, mask, n_chan):
@@ -334,19 +370,23 @@
     )(params, *zparts, band)
 
     def cross(masks, columns, earlier, final):
+        scratch = [pltpu.VMEM((len(masks),) + shape, jnp.float32)]
+        group = SRC_STEP
+        spec = vmem
+        result = jax.ShapeDtypeStruct((2, sources, tiles, ch, LANES), jnp.bfloat16)
         if final:
-            spec = pl.BlockSpec((2, SRC_STEP, ch, freq), lambda s: (0, s, 0, 0))
+            group = OUT_STEP
+            spec = pl.BlockSpec(memory_space=pl.ANY)
             result = jax.ShapeDtypeStruct((2, sources, ch, freq), jnp.bfloat16)
-        else:
-            spec = vmem
-            result = jax.ShapeDtypeStruct((2, sources, tiles, ch, LANES), jnp.bfloat16)
+            scratch.append(pltpu.VMEM((SLOTS, 2, group, ch, freq), jnp.bfloat16))
+            scratch.append(pltpu.SemaphoreType.DMA((SLOTS, 2)))
         return pl.pallas_call(
-            functools.partial(cross_kernel, masks=masks, added=len(earlier) > 0),
-            grid=(sources // SRC_STEP,),
+            functools.partial(cross_kernel, masks=masks, added=len(earlier) > 0, final=final),
+            grid=(sources // group,),
             in_specs=[smem] + [vmem] * (len(columns) + 1 + len(earlier)),
             out_specs=spec,
             out_shape=result,
-            scratch_shapes=[pltpu.VMEM((len(masks),) + shape, jnp.float32)],
+            scratch_shapes=scratch,
             compiler_params=room(32),
             cost_estimate=pl.CostEstimate(
                 flops=16 * len(masks) * sources * ch * freq, bytes_accessed=16 << 20, transcendentals=0

time: 50.3 us -> 49.8 us (0.990)
  Pallas kernels: 17 us -> 16.4 us
    pallas_call x2, Pallas kernels: 11 us -> 10.5 us  [cross(): pl.pallas_call(functools.partial(cross_kernel, masks=masks, added=len(ear...]
where the time goes in v6:
time: 49.8 us; the launch traced here: 49.4 us
  starting transfers between devices  18.6 us (37%)
  Pallas kernels  16.4 us (33%)
  waiting for transfers between devices  9.72 us (20%)
  local copies, waits for them, and re-layouts  3.77 us (8%)
  other arithmetic  0.74 us (1%)
    pallas_call x2, Pallas kernels, cross(): pl.pallas_call(functools.partial(cross_kernel, masks=masks, added=len(ear...  10.5 us
    ppermute x6, starting transfers between devices, swap(): return lax.ppermute(x, 'chan', [(i, i ^ mask) for i in range(n_chan)])  7.62 us
    all_to_all x1, starting transfers between devices, body(): held = lax.all_to_all(split, 'chan', 0, 0)[:, None]  7.39 us
    ppermute x6, waiting for transfers between devices, swap(): return lax.ppermute(x, 'chan', [(i, i ^ mask) for i in range(n_chan)])  6.05 us
    all_to_all x1, waiting for transfers between devices, body(): held = lax.all_to_all(split, 'chan', 0, 0)[:, None]  3.66 us
    unnamed x8, local copies, waits for them, and re-layouts  3.01 us
    ppermute x1, starting transfers between devices, body(): before = lax.ppermute(spectra, 'chan', [(i, i + 1) for i in range(ends)])  2.32 us
    pallas_call x1, Pallas kernels, body(): pl.pallas_call(own_kernel, out_shape=jax.ShapeDtypeStruct((2, tiles, win,...  2.06 us
  transfers between devices with their start and end apart: 9, of which 5 were waited for; matrix products, arithmetic and copies ran while one was open for 3% of the time, Pallas kernels for 13%

profile of v6, /device:TPU:0, one launch (start us, length us, event | category | flops | bytes accessed | tf_op | source)
XLA Modules:
  0.0 49.4 jit_solution(8950870389330548203)
XLA Ops:
  0.0 1.7 %split.1 = bf16[16,80,128]{2,1,0:T(8,128)(2,1)} custom-call(bf16[2,4,32,512]{3,2,1,0:T(8,128)(2,1)} %cur_ref.1, s32[4,32]{1,0:T(4,128)} %flags_ref.3), custom_call_target="tpu_custom_call" | custom-call | tf_op jit(solution)/shard_map/split/pallas_call | solution.py:288
  1.7 7.4 %all-to-all-start = ((bf16[16,80,128]{2,1,0:T(8,128)(2,1)}), bf16[16,80,128]{2,1,0:T(8,128)(2,1)S(1)}, u32[]{:S(2)}, u32[]{:S(2)}) async-start(bf16[16,80,128]{2,1,0:T(8,128)(2,1)} %split.1), calls=%async_computation | async-start | bytes 655360 | tf_op jit(solution)/shard_map/all_to_all | solution.py:295
  9.1 2.3 %collective-permute-start = (bf16[2,4,32,512]{3,2,1,0:T(8,128)(2,1)}, bf16[2,4,32,512]{3,2,1,0:T(8,128)(2,1)S(1)}, u32[]{:S(2)}, u32[]{:S(2)}) collective-permute-start(bf16[2,4,32,512]{3,2,1,0:T(8,128)(2,1)} %cur_ref.1), channel_id=1, source_target_pairs={{0,1},{1,2},{2,3},{3,4},{4,5},{5,6},{6,7},{7,8},{8,9},{9,10},{10,1... | collective-permute-start | bytes 786440 | tf_op jit(solution)/shard_map/ppermute | solution.py:303
  11.5 1.3 %collective-permute-start.1 = (bf16[2,4,32,512]{3,2,1,0:T(8,128)(2,1)}, bf16[2,4,32,512]{3,2,1,0:T(8,128)(2,1)S(1)}, u32[]{:S(2)}, u32[]{:S(2)}) collective-permute-start(bf16[2,4,32,512]{3,2,1,0:T(8,128)(2,1)} %cur_ref.1), channel_id=1, source_target_pairs={{1,0},{2,1},{3,2},{4,3},{5,4},{6,5},{7,6},{8,7},{9,8},{10,9},{11,1... | collective-permute-start | bytes 786440 | tf_op jit(solution)/shard_map/ppermute | solution.py:304
  12.8 0.8 %reshape.6 = s32[128]{0:T(128)S(1)} reshape(s32[4,32]{1,0:T(4,128)} %param.11) | data formatting | bytes 1024 | tf_op jit(solution)/shard_map/reshape | solution.py:300
  13.5 0.0 copy-start.1
  13.5 0.7 %copy-done.1 = s32[4,32]{1,0:T(4,128)S(1)} copy-done((s32[4,32]{1,0:T(4,128)S(1)}, s32[4,32]{1,0:T(4,128)}, u32[]{:S(2)}) %copy-start.1) | copy-done | bytes 536
  14.2 0.0 copy-start.2
  14.2 0.7 %copy-done.2 = f32[2,8,65]{2,1,0:T(8,128)S(1)} copy-done((f32[2,8,65]{2,1,0:T(8,128)S(1)}, f32[2,8,65]{2,1,0:T(8,128)}, u32[]{:S(2)}) %copy-start.2) | copy-done | bytes 4184
  14.9 0.0 copy-start.3
  14.9 0.7 %copy-done.3 = s32[512]{0:T(512)S(1)} copy-done((s32[512]{0:T(512)S(1)}, s32[512]{0:T(512)}, u32[]{:S(2)}) %copy-start.3) | copy-done | bytes 2072
  15.6 0.2 prep.1
  15.8 0.7 %pad_add_fusion.params_ref = s32[134]{0:T(256)S(1)} fusion(s32[128]{0:T(128)S(1)} %reshape.6, s32[4]{0:T(128)} %param.10, s32[1]{0:T(128)} %bitcast.1, s32[1]{0:T(128)} %bitcast), kind=kLoop, calls=%fused_computation | loop fusion | flops 402 | bytes 1072 | tf_op jit(solution)/shard_map/concatenate | solution.py:300
  16.6 0.0 collective-permute-done.prev_ref
  16.6 0.0 collective-permute-done.1.next_ref
  16.6 3.7 %all-to-all-done = bf16[16,80,128]{2,1,0:T(8,128)(2,1)S(1)} async-done(((bf16[16,80,128]{2,1,0:T(8,128)(2,1)}), bf16[16,80,128]{2,1,0:T(8,128)(2,1)S(1)}, u32[]{:S(2)}, u32[]{:S(2)}) %all-to-all-start) | async-done | bytes 327712 | tf_op jit(solution)/shard_map/all_to_all | solution.py:295
  20.3 1.0 %source_filter.1.refs_0_ = bf16[1,4,2,32,128]{4,3,2,1,0:T(8,128)(2,1)S(1)} custom-call(s32[134]{0:T(256)S(1)} %pad_add_fusion.params_ref, bf16[16,1,80,128]{3,2,1,0:T(8,128)(2,1)S(1)} %bitcast.4, bf16[1024,256]{1,0:T(8,128)(2,1)S(1)} %get-tuple-element.17.weight_ref, s32[4,1,128]{2,1,0:T(1,128)S(1)} %get-tuple-element.18.index_ref), custom_call_target="tpu_custom_call" | custom-call | tf_op jit(solution)/shard_map/source_filter/pallas_call | solution.py:321
  21.3 3.5 %collective-permute-start.4 = (bf16[1,4,2,32,128]{4,3,2,1,0:T(8,128)(2,1)S(1)}, bf16[1,4,2,32,128]{4,3,2,1,0:T(8,128)(2,1)S(1)}, u32[]{:S(2)}, u32[]{:S(2)}) collective-permute-start(bf16[1,4,2,32,128]{4,3,2,1,0:T(8,128)(2,1)S(1)} %source_filter.1.refs_0_), channel_id=1, source_target_pairs={{0,12},{1,13},{2,14},{3,15},{4,8},{5,9},{6,10},{7,11},{8,4},{9,5},... | collective-permute-start | bytes 196616 | tf_op jit(solution)/shard_map/ppermute | solution.py:271
  24.8 1.0 %collective-permute-start.3 = (bf16[1,4,2,32,128]{4,3,2,1,0:T(8,128)(2,1)S(1)}, bf16[1,4,2,32,128]{4,3,2,1,0:T(8,128)(2,1)S(1)}, u32[]{:S(2)}, u32[]{:S(2)}) collective-permute-start(bf16[1,4,2,32,128]{4,3,2,1,0:T(8,128)(2,1)S(1)} %source_filter.1.refs_0_), channel_id=1, source_target_pairs={{0,8},{1,9},{2,10},{3,11},{4,12},{5,13},{6,14},{7,15},{8,0},{9,1},... | collective-permute-start | bytes 196616 | tf_op jit(solution)/shard_map/ppermute | solution.py:271
  25.7 0.5 collective-permute-start.2
  26.2 0.0 copy-start
  26.2 0.9 %copy-done = bf16[2,4,32,512]{3,2,1,0:T(8,128)(2,1)S(1)} copy-done((bf16[2,4,32,512]{3,2,1,0:T(8,128)(2,1)S(1)}, bf16[2,4,32,512]{3,2,1,0:T(8,128)(2,1)}, u32[]{:S(2)}) %copy-start) | copy-done | bytes 262168
  27.2 2.1 %own_whiten.1.refs_2_ = bf16[2,4,4,32,128]{4,3,2,1,0:T(8,128)(2,1)S(1)} custom-call(bf16[2,4,32,512]{3,2,1,0:T(8,128)(2,1)S(1)} %collective-permute-done.prev_ref, bf16[2,4,32,512]{3,2,1,0:T(8,128)(2,1)S(1)} %copy-done, bf16[2,4,32,512]{3,2,1,0:T(8,128)(2,1)S(1)} %collective-permute-done.1.next_ref, bf16[1024,256]{1,0:T(8,128)(2,1)S(1)} %get-tuple-element.17.weight_ref, ...), custom_call_target="tpu_custom_call" | custom-call | flops 1073741824 | bytes 3145728 | tf_op jit(solution)/shard_map/own_whiten/pallas_call | solution.py:339
  29.2 0.0 collective-permute-done.4.refs_3_
  29.2 1.1 %collective-permute-done.3.refs_2_ = bf16[1,4,2,32,128]{4,3,2,1,0:T(8,128)(2,1)S(1)} collective-permute-done((bf16[1,4,2,32,128]{4,3,2,1,0:T(8,128)(2,1)S(1)}, bf16[1,4,2,32,128]{4,3,2,1,0:T(8,128)(2,1)S(1)}, u32[]{:S(2)}, u32[]{:S(2)}) %collective-permute-start.3) | collective-permute-done | bytes 65568 | tf_op jit(solution)/shard_map/ppermute | solution.py:271
  30.3 0.7 %collective-permute-done.2.refs_1_ = bf16[1,4,2,32,128]{4,3,2,1,0:T(8,128)(2,1)S(1)} collective-permute-done((bf16[1,4,2,32,128]{4,3,2,1,0:T(8,128)(2,1)S(1)}, bf16[1,4,2,32,128]{4,3,2,1,0:T(8,128)(2,1)S(1)}, u32[]{:S(2)}, u32[]{:S(2)}) %collective-permute-start.2) | collective-permute-done | bytes 65568 | tf_op jit(solution)/shard_map/ppermute | solution.py:271
  31.0 0.9 %column_whiten.1.refs_0_ = bf16[1,4,4,2,32,128]{5,4,3,2,1,0:T(8,128)(2,1)S(1)} custom-call(s32[134]{0:T(256)S(1)} %pad_add_fusion.params_ref, bf16[1,4,2,32,128]{4,3,2,1,0:T(8,128)(2,1)S(1)} %source_filter.1.refs_0_, bf16[1,4,2,32,128]{4,3,2,1,0:T(8,128)(2,1)S(1)} %collective-permute-done.2.refs_1_, ...), custom_call_target="tpu_custom_call" | custom-call | tf_op jit(solution)/shard_map/column_whiten/pallas_call | solution.py:361
  31.9 1.2 %collective-permute-start.6 = (bf16[1,4,4,2,32,128]{5,4,3,2,1,0:T(8,128)(2,1)S(1)}, bf16[1,4,4,2,32,128]{5,4,3,2,1,0:T(8,128)(2,1)S(1)}, u32[]{:S(2)}, u32[]{:S(2)}) collective-permute-start(bf16[1,4,4,2,32,128]{5,4,3,2,1,0:T(8,128)(2,1)S(1)} %column_whiten.1.refs_0_), channel_id=1, source_target_pairs={{0,1},{1,0},{2,3},{3,2},{4,5},{5,4},{6,7},{7,6},{8,9},{9,8},{10,11... | collective-permute-start | bytes 786440 | tf_op jit(solution)/shard_map/ppermute | solution.py:271
  33.1 1.5 %collective-permute-start.5 = (bf16[1,4,4,2,32,128]{5,4,3,2,1,0:T(8,128)(2,1)S(1)}, bf16[1,4,4,2,32,128]{5,4,3,2,1,0:T(8,128)(2,1)S(1)}, u32[]{:S(2)}, u32[]{:S(2)}) collective-permute-start(bf16[1,4,4,2,32,128]{5,4,3,2,1,0:T(8,128)(2,1)S(1)} %column_whiten.1.refs_0_), channel_id=1, source_target_pairs={{0,2},{1,3},{2,0},{3,1},{4,6},{5,7},{6,4},{7,5},{8,10},{9,11},{10,... | collective-permute-start | bytes 786440 | tf_op jit(solution)/shard_map/ppermute | solution.py:271
  34.6 0.0 collective-permute-done.6.refs_1_
  34.6 4.2 %cross.2.refs_3_ = bf16[2,128,4,32,128]{4,3,2,1,0:T(8,128)(2,1)S(1)} custom-call(s32[134]{0:T(256)S(1)} %pad_add_fusion.params_ref, bf16[1,4,4,2,32,128]{5,4,3,2,1,0:T(8,128)(2,1)S(1)} %column_whiten.1.refs_0_, bf16[1,4,4,2,32,128]{5,4,3,2,1,0:T(8,128)(2,1)S(1)} %collective-permute-done.6.refs_1_, bf16[2,4,4,32,128]{4,3,2,1,0:T(8,128)(2,1)S(1)} %own_whiten.1.refs_2_), custom_call_target="tpu_custom_call" | custom-call | flops 67108864 | bytes 16777216 | tf_op jit(solution)/shard_map/cross/pallas_call | solution.py:383
  38.8 2.7 %collective-permute-done.5.refs_0_ = bf16[1,4,4,2,32,128]{5,4,3,2,1,0:T(8,128)(2,1)S(1)} collective-permute-done((bf16[1,4,4,2,32,128]{5,4,3,2,1,0:T(8,128)(2,1)S(1)}, bf16[1,4,4,2,32,128]{5,4,3,2,1,0:T(8,128)(2,1)S(1)}, u32[]{:S(2)}, u32[]{:S(2)}) %collective-permute-start.5) | collective-permute-done | bytes 262176 | tf_op jit(solution)/shard_map/ppermute | solution.py:271
  41.5 0.0 collective-permute-start.7
  41.5 1.5 %collective-permute-done.7.refs_1_ = bf16[1,4,4,2,32,128]{5,4,3,2,1,0:T(8,128)(2,1)S(1)} collective-permute-done((bf16[1,4,4,2,32,128]{5,4,3,2,1,0:T(8,128)(2,1)S(1)}, bf16[1,4,4,2,32,128]{5,4,3,2,1,0:T(8,128)(2,1)S(1)}, u32[]{:S(2)}, u32[]{:S(2)}) %collective-permute-start.7) | collective-permute-done | bytes 262176 | tf_op jit(solution)/shard_map/ppermute | solution.py:271
  43.0 6.3 %cross.3 = bf16[2,128,32,512]{3,2,1,0:T(8,128)(2,1)} custom-call(s32[134]{0:T(256)S(1)} %pad_add_fusion.params_ref, bf16[1,4,4,2,32,128]{5,4,3,2,1,0:T(8,128)(2,1)S(1)} %collective-permute-done.5.refs_0_, bf16[1,4,4,2,32,128]{5,4,3,2,1,0:T(8,128)(2,1)S(1)} %collective-permute-done.7.refs_1_, bf16[2,4,4,32,128]{4,3,2,1,0:T(8,128)(2,1)S(1)} %own_whiten.1.refs_2_, ...), custom_call_target="tpu_custom_call" | custom-call | flops 67108864 | bytes 16777216 | tf_op jit(solution)/shard_map/cross/pallas_call | solution.py:383
Async XLA Ops:
  1.7 18.5 %all-to-all-start = ((bf16[16,80,128]{2,1,0:T(8,128)(2,1)}), bf16[16,80,128]{2,1,0:T(8,128)(2,1)S(1)}, u32[]{:S(2)}, u32[]{:S(2)}) async-start(bf16[16,80,128]{2,1,0:T(8,128)(2,1)} %split.1), calls=%async_computation | async-start | bytes 655360 | tf_op jit(solution)/shard_map/all_to_all | solution.py:295
  9.1 7.5 %collective-permute-start = (bf16[2,4,32,512]{3,2,1,0:T(8,128)(2,1)}, bf16[2,4,32,512]{3,2,1,0:T(8,128)(2,1)S(1)}, u32[]{:S(2)}, u32[]{:S(2)}) collective-permute-start(bf16[2,4,32,512]{3,2,1,0:T(8,128)(2,1)} %cur_ref.1), channel_id=1, source_target_pairs={{0,1},{1,2},{2,3},{3,4},{4,5},{5,6},{6,7},{7,8},{8,9},{9,10},{10,1... | collective-permute-start | bytes 786440 | tf_op jit(solution)/shard_map/ppermute | solution.py:303
  11.5 5.1 %collective-permute-start.1 = (bf16[2,4,32,512]{3,2,1,0:T(8,128)(2,1)}, bf16[2,4,32,512]{3,2,1,0:T(8,128)(2,1)S(1)}, u32[]{:S(2)}, u32[]{:S(2)}) collective-permute-start(bf16[2,4,32,512]{3,2,1,0:T(8,128)(2,1)} %cur_ref.1), channel_id=1, source_target_pairs={{1,0},{2,1},{3,2},{4,3},{5,4},{6,5},{7,6},{8,7},{9,8},{10,9},{11,1... | collective-permute-start | bytes 786440 | tf_op jit(solution)/shard_map/ppermute | solution.py:304
  13.5 0.7 %copy-start.1 = (s32[4,32]{1,0:T(4,128)S(1)}, s32[4,32]{1,0:T(4,128)}, u32[]{:S(2)}) copy-start(s32[4,32]{1,0:T(4,128)} %flags_ref.3) | copy-start | bytes 1540
  14.2 0.7 %copy-start.2 = (f32[2,8,65]{2,1,0:T(8,128)S(1)}, f32[2,8,65]{2,1,0:T(8,128)}, u32[]{:S(2)}) copy-start(f32[2,8,65]{2,1,0:T(8,128)} %bank_ref.1) | copy-start | bytes 12484
  14.9 0.7 %copy-start.3 = (s32[512]{0:T(512)S(1)}, s32[512]{0:T(512)}, u32[]{:S(2)}) copy-start(s32[512]{0:T(512)} %param.8) | copy-start | bytes 6148
  21.3 8.0 %collective-permute-start.4 = (bf16[1,4,2,32,128]{4,3,2,1,0:T(8,128)(2,1)S(1)}, bf16[1,4,2,32,128]{4,3,2,1,0:T(8,128)(2,1)S(1)}, u32[]{:S(2)}, u32[]{:S(2)}) collective-permute-start(bf16[1,4,2,32,128]{4,3,2,1,0:T(8,128)(2,1)S(1)} %source_filter.1.refs_0_), channel_id=1, source_target_pairs={{0,12},{1,13},{2,14},{3,15},{4,8},{5,9},{6,10},{7,11},{8,4},{9,5},... | collective-permute-start | bytes 196616 | tf_op jit(solution)/shard_map/ppermute | solution.py:271
  24.8 5.6 %collective-permute-start.3 = (bf16[1,4,2,32,128]{4,3,2,1,0:T(8,128)(2,1)S(1)}, bf16[1,4,2,32,128]{4,3,2,1,0:T(8,128)(2,1)S(1)}, u32[]{:S(2)}, u32[]{:S(2)}) collective-permute-start(bf16[1,4,2,32,128]{4,3,2,1,0:T(8,128)(2,1)S(1)} %source_filter.1.refs_0_), channel_id=1, source_target_pairs={{0,8},{1,9},{2,10},{3,11},{4,12},{5,13},{6,14},{7,15},{8,0},{9,1},... | collective-permute-start | bytes 196616 | tf_op jit(solution)/shard_map/ppermute | solution.py:271
  25.7 5.3 %collective-permute-start.2 = (bf16[1,4,2,32,128]{4,3,2,1,0:T(8,128)(2,1)S(1)}, bf16[1,4,2,32,128]{4,3,2,1,0:T(8,128)(2,1)S(1)}, u32[]{:S(2)}, u32[]{:S(2)}) collective-permute-start(bf16[1,4,2,32,128]{4,3,2,1,0:T(8,128)(2,1)S(1)} %source_filter.1.refs_0_), channel_id=1, source_target_pairs={{0,4},{1,5},{2,6},{3,7},{4,0},{5,1},{6,2},{7,3},{8,12},{9,13},{10,... | collective-permute-start | bytes 196616 | tf_op jit(solution)/shard_map/ppermute | solution.py:271
  26.2 0.9 %copy-start = (bf16[2,4,32,512]{3,2,1,0:T(8,128)(2,1)S(1)}, bf16[2,4,32,512]{3,2,1,0:T(8,128)(2,1)}, u32[]{:S(2)}) copy-start(bf16[2,4,32,512]{3,2,1,0:T(8,128)(2,1)} %cur_ref.1) | copy-start | bytes 786436
  31.9 2.7 %collective-permute-start.6 = (bf16[1,4,4,2,32,128]{5,4,3,2,1,0:T(8,128)(2,1)S(1)}, bf16[1,4,4,2,32,128]{5,4,3,2,1,0:T(8,128)(2,1)S(1)}, u32[]{:S(2)}, u32[]{:S(2)}) collective-permute-start(bf16[1,4,4,2,32,128]{5,4,3,2,1,0:T(8,128)(2,1)S(1)} %column_whiten.1.refs_0_), channel_id=1, source_target_pairs={{0,1},{1,0},{2,3},{3,2},{4,5},{5,4},{6,7},{7,6},{8,9},{9,8},{10,11... | collective-permute-start | bytes 786440 | tf_op jit(solution)/shard_map/ppermute | solution.py:271
  33.1 8.4 %collective-permute-start.5 = (bf16[1,4,4,2,32,128]{5,4,3,2,1,0:T(8,128)(2,1)S(1)}, bf16[1,4,4,2,32,128]{5,4,3,2,1,0:T(8,128)(2,1)S(1)}, u32[]{:S(2)}, u32[]{:S(2)}) collective-permute-start(bf16[1,4,4,2,32,128]{5,4,3,2,1,0:T(8,128)(2,1)S(1)} %column_whiten.1.refs_0_), channel_id=1, source_target_pairs={{0,2},{1,3},{2,0},{3,1},{4,6},{5,7},{6,4},{7,5},{8,10},{9,11},{10,... | collective-permute-start | bytes 786440 | tf_op jit(solution)/shard_map/ppermute | solution.py:271
  41.5 1.5 %collective-permute-start.7 = (bf16[1,4,4,2,32,128]{5,4,3,2,1,0:T(8,128)(2,1)S(1)}, bf16[1,4,4,2,32,128]{5,4,3,2,1,0:T(8,128)(2,1)S(1)}, u32[]{:S(2)}, u32[]{:S(2)}) collective-permute-start(bf16[1,4,4,2,32,128]{5,4,3,2,1,0:T(8,128)(2,1)S(1)} %collective-permute-done.5.refs_0_), channel_id=1, source_target_pairs={{0,1},{1,0},{2,3},{3,2},{4,5},{5,4},{6,7},{7,6},{8,9},{9,8},{10,11... | collective-permute-start | bytes 786440 | tf_op jit(solution)/shard_map/ppermute | solution.py:271

commit v7 on v6

--- a/solution.py
+++ b/solution.py
@@ -33,11 +33,17 @@
             piece_ref[t * win + w, 2 * ch :, :ch] = flags.astype(jnp.bfloat16)
 
 
-def prep_kernel(bank_ref, bins_ref, flags_ref, weight_ref, band_ref, index_ref, valid_ref, padded_ref):
+def prep_kernel(
+    bank_ref, bins_ref, flags_ref, offset_ref, weight_ref, band_ref, index_ref, valid_ref, pick_ref, padded_ref
+):
     _, banks, taps = bank_ref.shape
     half = weight_ref.shape[0] // 2
     ch = half // (2 * banks)
     index_ref[...] = bins_ref[...]
+    channel = lax.broadcasted_iota(jnp.int32, (ch, ch), 0)
+    for r in range(offset_ref.shape[0]):
+        picked = channel == offset_ref[r : r + 1, :]
+        pick_ref[r] = jnp.where(picked, 1.0, 0.0).astype(jnp.bfloat16)
     for w in range(flags_ref.shape[0]):
         column = flag_column(flags_ref[w : w + 1, :])
         valid_ref[w * ch : (w + 1) * ch, :] = jnp.broadcast_to(column, (ch, LANES))
@@ -150,8 +156,8 @@
 
 
 def column_kernel(params_ref, *refs):
-    band_ref, out_ref, piece_ref = refs[-3:]
-    parts = refs[:-3]
+    band_ref, pick_ref, out_ref, piece_ref = refs[-4:]
+    parts = refs[:-4]
     tiles, rounds, _, ch, _ = piece_ref.shape
     if len(parts) == tiles:
         place = params_ref[1]
@@ -161,10 +167,15 @@
         piece_ref[...] = parts[0][:, 0]
     both = []
     for p in range(2):
-        rows = [
-            jnp.concatenate([piece_ref[t, r, p] for t in range(tiles)], axis=1) for r in range(rounds)
-        ]
-        both.append(jnp.concatenate(rows, axis=0).astype(jnp.float32))
+        rows = []
+        for r in range(rounds):
+            row = jnp.concatenate([piece_ref[t, r, p] for t in range(tiles)], axis=1)
+            rows.append(
+                lax.dot_general(
+                    pick_ref[r], row, (((0,), (0,)), ((), ())), preferred_element_type=jnp.float32
+                )
+            )
+        both.append(jnp.concatenate(rows, axis=0))
     scale = running_scale(both[0], both[1], band_ref)
     for p in range(2):
         white = (both[p] * scale).astype(jnp.bfloat16)
@@ -174,7 +185,7 @@
 
 
 def spread_row(ref, at, row, ch):
-    eight = ref[(*at, pl.ds(row, 8, stride=0), slice(None))]
+    eight = ref[(*at, row // 8, pl.ds(row % 8, 8, stride=0), slice(None))]
     pair = jnp.concatenate([eight, eight], axis=0).astype(jnp.bfloat16)
     return jnp.concatenate([pair] * (ch // 16), axis=0)
 
@@ -197,13 +208,10 @@
         out_ref, source_ref = refs[-2:]
         group = SRC_STEP
     tiles, win, ch = local_ref.shape[1:4]
-    rounds = source_ref.shape[2]
-    per_round = ch // group
+    steps = source_ref.shape[2]
+    rounds = steps * group // ch
     step = pl.program_id(0)
-    steps = rounds * per_round
-    r = step // per_round
     begin = step * group
-    first = 2 + rounds + begin
     here = lax.rem(params_ref[0], win)
     slot = lax.rem(step, SLOTS)
 
@@ -220,7 +228,12 @@
     def _():
         for i, ref in enumerate(column_refs):
             for t in range(tiles):
-                source_ref[i, t] = ref[0, t].astype(jnp.float32) * (1.0 / win)
+                for rr in range(rounds):
+                    for p in range(2):
+                        rows = ref[0, t, rr, p].astype(jnp.float32) * (1.0 / win)
+                        source_ref[i, t, rr * (ch // group) : (rr + 1) * (ch // group), p] = rows.reshape(
+                            ch // group, group // 8, 8, LANES
+                        )
 
     if final:
 
@@ -233,11 +246,10 @@
         at = pl.ds(pl.multiple_of(ft * LANES, LANES), LANES)
         mine = [(local_ref[0, ft, here ^ mask], local_ref[1, ft, here ^ mask]) for mask in masks]
         for j in range(group):
-            row = params_ref[first + j]
             re = []
             im = []
             for i in range(len(masks)):
-                sr, si = (spread_row(source_ref, (i, ft, r, p), row, ch) for p in range(2))
+                sr, si = (spread_row(source_ref, (i, ft, step, p), j, ch) for p in range(2))
                 lr, li = mine[i]
                 re.append(sr * lr + si * li)
                 im.append(sr * li - si * lr)
@@ -297,25 +309,26 @@
     else:
         held = lax.all_gather(split, "chan")
         first = jnp.int32(0)
-    params = jnp.concatenate([first[None], lax.div(first, jnp.int32(win))[None], owner_order, source_offset.reshape(-1)])
+    params = jnp.concatenate([first[None], lax.div(first, jnp.int32(win))[None], owner_order])
 
     ends = n_chan - 1
     before = lax.ppermute(spectra, "chan", [(i, i + 1) for i in range(ends)])
     after = lax.ppermute(spectra, "chan", [(i + 1, i) for i in range(ends)])
     held, before, after = lax.optimization_barrier((held, before, after))
 
-    weight, band, index, valid = pl.pallas_call(
+    weight, band, index, valid, pick = pl.pallas_call(
         prep_kernel,
         out_shape=(
             jax.ShapeDtypeStruct((2 * banks * 2 * ch, 2 * LANES), jnp.bfloat16),
             jax.ShapeDtypeStruct((freq, freq), jnp.bfloat16),
             jax.ShapeDtypeStruct((tiles, 1, LANES), jnp.int32),
             jax.ShapeDtypeStruct((count, LANES), jnp.float32),
+            jax.ShapeDtypeStruct((rounds, ch, ch), jnp.bfloat16),
         ),
         scratch_shapes=[pltpu.VMEM((2, banks, LANES), jnp.float32)],
         compiler_params=room(8),
         name="prep",
-    )(filter_bank, band_index.reshape(tiles, 1, LANES), window_mask)
+    )(filter_bank, band_index.reshape(tiles, 1, LANES), window_mask, source_offset)
 
     count_here = held.shape[1]
     filtered = pl.pallas_call(
@@ -361,21 +374,21 @@
     column = pl.pallas_call(
         column_kernel,
         grid=(windows,),
-        in_specs=[smem] + specs + [vmem],
+        in_specs=[smem] + specs + [vmem, vmem],
         out_specs=pl.BlockSpec((1,) + shape, lambda s: (s, 0, 0, 0, 0, 0)),
         out_shape=jax.ShapeDtypeStruct((windows,) + shape, jnp.bfloat16),
         scratch_shapes=[pltpu.VMEM(shape, jnp.bfloat16)],
         compiler_params=room(16),
         name="column_whiten",
-    )(params, *zparts, band)
+    )(params, *zparts, band, pick)
 
     def cross(masks, columns, earlier, final):
-        scratch = [pltpu.VMEM((len(masks),) + shape, jnp.float32)]
-        group = SRC_STEP
+        group = OUT_STEP if final else SRC_STEP
+        rows = (len(masks), tiles, sources // group, 2, group // 8, 8, LANES)
+        scratch = [pltpu.VMEM(rows, jnp.float32)]
         spec = vmem
         result = jax.ShapeDtypeStruct((2, sources, tiles, ch, LANES), jnp.bfloat16)
         if final:
-            group = OUT_STEP
             spec = pl.BlockSpec(memory_space=pl.ANY)
             result = jax.ShapeDtypeStruct((2, sources, ch, freq), jnp.bfloat16)
             scratch.append(pltpu.VMEM((SLOTS, 2, group, ch, freq), jnp.bfloat16))

time: 49.8 us -> 49.7 us (level)
    reshape x1 -> x0, local copies, waits for them, and re-layouts: 0.77 us -> none  [body(): source_offset.reshape(-1)]
    unnamed x8 -> x10, local copies, waits for them, and re-layouts: 3.01 us -> 3.68 us
  transfers between devices with their start and end apart: 9 -> 9, of which waited for: 5 -> 5; matrix products, arithmetic and copies ran while one was open for 3% -> 1% of each run, Pallas kernels for 13% -> 13%
where the time goes in v7:
time: 49.7 us; the launch traced here: 49.2 us
  starting transfers between devices  18.6 us (37%)
  Pallas kernels  16.1 us (32%)
  waiting for transfers between devices  10 us (20%)
  local copies, waits for them, and re-layouts  3.68 us (7%)
  other arithmetic  0.74 us (1%)
    pallas_call x2, Pallas kernels, cross(): pl.pallas_call(functools.partial(cross_kernel, masks=masks, added=len(ear...  10 us
    ppermute x6, starting transfers between devices, swap(): return lax.ppermute(x, 'chan', [(i, i ^ mask) for i in range(n_chan)])  7.61 us
    all_to_all x1, starting transfers between devices, body(): held = lax.all_to_all(split, 'chan', 0, 0)[:, None]  7.39 us
    ppermute x6, waiting for transfers between devices, swap(): return lax.ppermute(x, 'chan', [(i, i ^ mask) for i in range(n_chan)])  6.25 us
    all_to_all x1, waiting for transfers between devices, body(): held = lax.all_to_all(split, 'chan', 0, 0)[:, None]  3.75 us
    unnamed x10, local copies, waits for them, and re-layouts  3.68 us
    ppermute x1, starting transfers between devices, body(): before = lax.ppermute(spectra, 'chan', [(i, i + 1) for i in range(ends)])  2.32 us
    pallas_call x1, Pallas kernels, body(): pl.pallas_call(own_kernel, out_shape=jax.ShapeDtypeStruct((2, tiles, win,...  2.06 us
  transfers between devices with their start and end apart: 9, of which 5 were waited for; matrix products, arithmetic and copies ran while one was open for 1% of the time, Pallas kernels for 13%

profile of v7, /device:TPU:0, one launch (start us, length us, event | category | flops | bytes accessed | tf_op | source)
XLA Modules:
  0.0 49.2 jit_solution(10931692061797529787)
XLA Ops:
  0.0 1.7 %split.1 = bf16[16,80,128]{2,1,0:T(8,128)(2,1)} custom-call(bf16[2,4,32,512]{3,2,1,0:T(8,128)(2,1)} %cur_ref.1, s32[4,32]{1,0:T(4,128)} %flags_ref.3), custom_call_target="tpu_custom_call" | custom-call | tf_op jit(solution)/shard_map/split/pallas_call | solution.py:300
  1.7 7.4 %all-to-all-start = ((bf16[16,80,128]{2,1,0:T(8,128)(2,1)}), bf16[16,80,128]{2,1,0:T(8,128)(2,1)S(1)}, u32[]{:S(2)}, u32[]{:S(2)}) async-start(bf16[16,80,128]{2,1,0:T(8,128)(2,1)} %split.1), calls=%async_computation | async-start | bytes 655360 | tf_op jit(solution)/shard_map/all_to_all | solution.py:307
  9.1 2.3 %collective-permute-start = (bf16[2,4,32,512]{3,2,1,0:T(8,128)(2,1)}, bf16[2,4,32,512]{3,2,1,0:T(8,128)(2,1)S(1)}, u32[]{:S(2)}, u32[]{:S(2)}) collective-permute-start(bf16[2,4,32,512]{3,2,1,0:T(8,128)(2,1)} %cur_ref.1), channel_id=1, source_target_pairs={{0,1},{1,2},{2,3},{3,4},{4,5},{5,6},{6,7},{7,8},{8,9},{9,10},{10,1... | collective-permute-start | bytes 786440 | tf_op jit(solution)/shard_map/ppermute | solution.py:315
  11.5 1.3 %collective-permute-start.1 = (bf16[2,4,32,512]{3,2,1,0:T(8,128)(2,1)}, bf16[2,4,32,512]{3,2,1,0:T(8,128)(2,1)S(1)}, u32[]{:S(2)}, u32[]{:S(2)}) collective-permute-start(bf16[2,4,32,512]{3,2,1,0:T(8,128)(2,1)} %cur_ref.1), channel_id=1, source_target_pairs={{1,0},{2,1},{3,2},{4,3},{5,4},{6,5},{7,6},{8,7},{9,8},{10,9},{11,1... | collective-permute-start | bytes 786440 | tf_op jit(solution)/shard_map/ppermute | solution.py:316
  12.8 0.0 copy-start.1
  12.8 0.7 %copy-done.1 = s32[4,32]{1,0:T(4,128)S(1)} copy-done((s32[4,32]{1,0:T(4,128)S(1)}, s32[4,32]{1,0:T(4,128)}, u32[]{:S(2)}) %copy-start.1) | copy-done | bytes 536
  13.4 0.0 copy-start.2
  13.4 0.7 %copy-done.2 = f32[2,8,65]{2,1,0:T(8,128)S(1)} copy-done((f32[2,8,65]{2,1,0:T(8,128)S(1)}, f32[2,8,65]{2,1,0:T(8,128)}, u32[]{:S(2)}) %copy-start.2) | copy-done | bytes 4184
  14.1 0.0 copy-start.3
  14.1 0.7 %copy-done.3 = s32[512]{0:T(512)S(1)} copy-done((s32[512]{0:T(512)S(1)}, s32[512]{0:T(512)}, u32[]{:S(2)}) %copy-start.3) | copy-done | bytes 2072
  14.8 0.0 copy-start.4
  14.8 0.7 %copy-done.4 = s32[4,32]{1,0:T(4,128)S(1)} copy-done((s32[4,32]{1,0:T(4,128)S(1)}, s32[4,32]{1,0:T(4,128)}, u32[]{:S(2)}) %copy-start.4) | copy-done | bytes 536
  15.5 0.2 prep.1
  15.8 0.7 %pad_add_fusion.params_ref = s32[6]{0:T(128)S(1)} fusion(s32[4]{0:T(128)} %param.10, s32[1]{0:T(128)} %bitcast.1, s32[1]{0:T(128)} %bitcast), kind=kLoop, calls=%fused_computation | loop fusion | flops 12 | bytes 48 | tf_op jit(solution)/shard_map/concatenate | solution.py:312
  16.5 0.0 collective-permute-done.prev_ref
  16.5 0.0 collective-permute-done.1.next_ref
  16.5 3.7 %all-to-all-done = bf16[16,80,128]{2,1,0:T(8,128)(2,1)S(1)} async-done(((bf16[16,80,128]{2,1,0:T(8,128)(2,1)}), bf16[16,80,128]{2,1,0:T(8,128)(2,1)S(1)}, u32[]{:S(2)}, u32[]{:S(2)}) %all-to-all-start) | async-done | bytes 327712 | tf_op jit(solution)/shard_map/all_to_all | solution.py:307
  20.3 1.0 %source_filter.1.refs_0_ = bf16[1,4,2,32,128]{4,3,2,1,0:T(8,128)(2,1)S(1)} custom-call(s32[6]{0:T(128)S(1)} %pad_add_fusion.params_ref, bf16[16,1,80,128]{3,2,1,0:T(8,128)(2,1)S(1)} %bitcast.4, bf16[1024,256]{1,0:T(8,128)(2,1)S(1)} %get-tuple-element.18.weight_ref, s32[4,1,128]{2,1,0:T(1,128)S(1)} %get-tuple-element.19.index_ref), custom_call_target="tpu_custom_call" | custom-call | tf_op jit(solution)/shard_map/source_filter/pallas_call | solution.py:334
  21.2 3.5 %collective-permute-start.4 = (bf16[1,4,2,32,128]{4,3,2,1,0:T(8,128)(2,1)S(1)}, bf16[1,4,2,32,128]{4,3,2,1,0:T(8,128)(2,1)S(1)}, u32[]{:S(2)}, u32[]{:S(2)}) collective-permute-start(bf16[1,4,2,32,128]{4,3,2,1,0:T(8,128)(2,1)S(1)} %source_filter.1.refs_0_), channel_id=1, source_target_pairs={{0,12},{1,13},{2,14},{3,15},{4,8},{5,9},{6,10},{7,11},{8,4},{9,5},... | collective-permute-start | bytes 196616 | tf_op jit(solution)/shard_map/ppermute | solution.py:283
  24.7 1.0 %collective-permute-start.3 = (bf16[1,4,2,32,128]{4,3,2,1,0:T(8,128)(2,1)S(1)}, bf16[1,4,2,32,128]{4,3,2,1,0:T(8,128)(2,1)S(1)}, u32[]{:S(2)}, u32[]{:S(2)}) collective-permute-start(bf16[1,4,2,32,128]{4,3,2,1,0:T(8,128)(2,1)S(1)} %source_filter.1.refs_0_), channel_id=1, source_target_pairs={{0,8},{1,9},{2,10},{3,11},{4,12},{5,13},{6,14},{7,15},{8,0},{9,1},... | collective-permute-start | bytes 196616 | tf_op jit(solution)/shard_map/ppermute | solution.py:283
  25.7 0.5 collective-permute-start.2
  26.2 0.0 copy-start
  26.2 0.9 %copy-done = bf16[2,4,32,512]{3,2,1,0:T(8,128)(2,1)S(1)} copy-done((bf16[2,4,32,512]{3,2,1,0:T(8,128)(2,1)S(1)}, bf16[2,4,32,512]{3,2,1,0:T(8,128)(2,1)}, u32[]{:S(2)}) %copy-start) | copy-done | bytes 262168
  27.1 2.1 %own_whiten.1.refs_2_ = bf16[2,4,4,32,128]{4,3,2,1,0:T(8,128)(2,1)S(1)} custom-call(bf16[2,4,32,512]{3,2,1,0:T(8,128)(2,1)S(1)} %collective-permute-done.prev_ref, bf16[2,4,32,512]{3,2,1,0:T(8,128)(2,1)S(1)} %copy-done, bf16[2,4,32,512]{3,2,1,0:T(8,128)(2,1)S(1)} %collective-permute-done.1.next_ref, bf16[1024,256]{1,0:T(8,128)(2,1)S(1)} %get-tuple-element.18.weight_ref, ...), custom_call_target="tpu_custom_call" | custom-call | flops 1073741824 | bytes 3145728 | tf_op jit(solution)/shard_map/own_whiten/pallas_call | solution.py:352
  29.2 0.0 collective-permute-done.4.refs_3_
  29.2 1.1 %collective-permute-done.3.refs_2_ = bf16[1,4,2,32,128]{4,3,2,1,0:T(8,128)(2,1)S(1)} collective-permute-done((bf16[1,4,2,32,128]{4,3,2,1,0:T(8,128)(2,1)S(1)}, bf16[1,4,2,32,128]{4,3,2,1,0:T(8,128)(2,1)S(1)}, u32[]{:S(2)}, u32[]{:S(2)}) %collective-permute-start.3) | collective-permute-done | bytes 65568 | tf_op jit(solution)/shard_map/ppermute | solution.py:283
  30.3 0.7 %collective-permute-done.2.refs_1_ = bf16[1,4,2,32,128]{4,3,2,1,0:T(8,128)(2,1)S(1)} collective-permute-done((bf16[1,4,2,32,128]{4,3,2,1,0:T(8,128)(2,1)S(1)}, bf16[1,4,2,32,128]{4,3,2,1,0:T(8,128)(2,1)S(1)}, u32[]{:S(2)}, u32[]{:S(2)}) %collective-permute-start.2) | collective-permute-done | bytes 65568 | tf_op jit(solution)/shard_map/ppermute | solution.py:283
  31.0 1.1 %column_whiten.1.refs_0_ = bf16[1,4,4,2,32,128]{5,4,3,2,1,0:T(8,128)(2,1)S(1)} custom-call(s32[6]{0:T(128)S(1)} %pad_add_fusion.params_ref, bf16[1,4,2,32,128]{4,3,2,1,0:T(8,128)(2,1)S(1)} %source_filter.1.refs_0_, bf16[1,4,2,32,128]{4,3,2,1,0:T(8,128)(2,1)S(1)} %collective-permute-done.2.refs_1_, ...), custom_call_target="tpu_custom_call" | custom-call | tf_op jit(solution)/shard_map/column_whiten/pallas_call | solution.py:374
  32.1 1.1 %collective-permute-start.6 = (bf16[1,4,4,2,32,128]{5,4,3,2,1,0:T(8,128)(2,1)S(1)}, bf16[1,4,4,2,32,128]{5,4,3,2,1,0:T(8,128)(2,1)S(1)}, u32[]{:S(2)}, u32[]{:S(2)}) collective-permute-start(bf16[1,4,4,2,32,128]{5,4,3,2,1,0:T(8,128)(2,1)S(1)} %column_whiten.1.refs_0_), channel_id=1, source_target_pairs={{0,1},{1,0},{2,3},{3,2},{4,5},{5,4},{6,7},{7,6},{8,9},{9,8},{10,11... | collective-permute-start | bytes 786440 | tf_op jit(solution)/shard_map/ppermute | solution.py:283
  33.3 1.5 %collective-permute-start.5 = (bf16[1,4,4,2,32,128]{5,4,3,2,1,0:T(8,128)(2,1)S(1)}, bf16[1,4,4,2,32,128]{5,4,3,2,1,0:T(8,128)(2,1)S(1)}, u32[]{:S(2)}, u32[]{:S(2)}) collective-permute-start(bf16[1,4,4,2,32,128]{5,4,3,2,1,0:T(8,128)(2,1)S(1)} %column_whiten.1.refs_0_), channel_id=1, source_target_pairs={{0,2},{1,3},{2,0},{3,1},{4,6},{5,7},{6,4},{7,5},{8,10},{9,11},{10,... | collective-permute-start | bytes 786440 | tf_op jit(solution)/shard_map/ppermute | solution.py:283
  34.8 0.0 collective-permute-done.6.refs_1_
  34.8 4.0 %cross.2.refs_3_ = bf16[2,128,4,32,128]{4,3,2,1,0:T(8,128)(2,1)S(1)} custom-call(s32[6]{0:T(128)S(1)} %pad_add_fusion.params_ref, bf16[1,4,4,2,32,128]{5,4,3,2,1,0:T(8,128)(2,1)S(1)} %column_whiten.1.refs_0_, bf16[1,4,4,2,32,128]{5,4,3,2,1,0:T(8,128)(2,1)S(1)} %collective-permute-done.6.refs_1_, bf16[2,4,4,32,128]{4,3,2,1,0:T(8,128)(2,1)S(1)} %own_whiten.1.refs_2_), custom_call_target="tpu_custom_call" | custom-call | flops 67108864 | bytes 16777216 | tf_op jit(solution)/shard_map/cross/pallas_call | solution.py:396
  38.8 2.9 %collective-permute-done.5.refs_0_ = bf16[1,4,4,2,32,128]{5,4,3,2,1,0:T(8,128)(2,1)S(1)} collective-permute-done((bf16[1,4,4,2,32,128]{5,4,3,2,1,0:T(8,128)(2,1)S(1)}, bf16[1,4,4,2,32,128]{5,4,3,2,1,0:T(8,128)(2,1)S(1)}, u32[]{:S(2)}, u32[]{:S(2)}) %collective-permute-start.5) | collective-permute-done | bytes 262176 | tf_op jit(solution)/shard_map/ppermute | solution.py:283
  41.7 0.0 collective-permute-start.7
  41.7 1.5 %collective-permute-done.7.refs_1_ = bf16[1,4,4,2,32,128]{5,4,3,2,1,0:T(8,128)(2,1)S(1)} collective-permute-done((bf16[1,4,4,2,32,128]{5,4,3,2,1,0:T(8,128)(2,1)S(1)}, bf16[1,4,4,2,32,128]{5,4,3,2,1,0:T(8,128)(2,1)S(1)}, u32[]{:S(2)}, u32[]{:S(2)}) %collective-permute-start.7) | collective-permute-done | bytes 262176 | tf_op jit(solution)/shard_map/ppermute | solution.py:283
  43.2 6.0 %cross.3 = bf16[2,128,32,512]{3,2,1,0:T(8,128)(2,1)} custom-call(s32[6]{0:T(128)S(1)} %pad_add_fusion.params_ref, bf16[1,4,4,2,32,128]{5,4,3,2,1,0:T(8,128)(2,1)S(1)} %collective-permute-done.5.refs_0_, bf16[1,4,4,2,32,128]{5,4,3,2,1,0:T(8,128)(2,1)S(1)} %collective-permute-done.7.refs_1_, bf16[2,4,4,32,128]{4,3,2,1,0:T(8,128)(2,1)S(1)} %own_whiten.1.refs_2_, ...), custom_call_target="tpu_custom_call" | custom-call | flops 67108864 | bytes 16777216 | tf_op jit(solution)/shard_map/cross/pallas_call | solution.py:396
Async XLA Ops:
  1.7 18.5 %all-to-all-start = ((bf16[16,80,128]{2,1,0:T(8,128)(2,1)}), bf16[16,80,128]{2,1,0:T(8,128)(2,1)S(1)}, u32[]{:S(2)}, u32[]{:S(2)}) async-start(bf16[16,80,128]{2,1,0:T(8,128)(2,1)} %split.1), calls=%async_computation | async-start | bytes 655360 | tf_op jit(solution)/shard_map/all_to_all | solution.py:307
  9.1 7.4 %collective-permute-start = (bf16[2,4,32,512]{3,2,1,0:T(8,128)(2,1)}, bf16[2,4,32,512]{3,2,1,0:T(8,128)(2,1)S(1)}, u32[]{:S(2)}, u32[]{:S(2)}) collective-permute-start(bf16[2,4,32,512]{3,2,1,0:T(8,128)(2,1)} %cur_ref.1), channel_id=1, source_target_pairs={{0,1},{1,2},{2,3},{3,4},{4,5},{5,6},{6,7},{7,8},{8,9},{9,10},{10,1... | collective-permute-start | bytes 786440 | tf_op jit(solution)/shard_map/ppermute | solution.py:315
  11.5 5.0 %collective-permute-start.1 = (bf16[2,4,32,512]{3,2,1,0:T(8,128)(2,1)}, bf16[2,4,32,512]{3,2,1,0:T(8,128)(2,1)S(1)}, u32[]{:S(2)}, u32[]{:S(2)}) collective-permute-start(bf16[2,4,32,512]{3,2,1,0:T(8,128)(2,1)} %cur_ref.1), channel_id=1, source_target_pairs={{1,0},{2,1},{3,2},{4,3},{5,4},{6,5},{7,6},{8,7},{9,8},{10,9},{11,1... | collective-permute-start | bytes 786440 | tf_op jit(solution)/shard_map/ppermute | solution.py:316
  12.8 0.7 %copy-start.1 = (s32[4,32]{1,0:T(4,128)S(1)}, s32[4,32]{1,0:T(4,128)}, u32[]{:S(2)}) copy-start(s32[4,32]{1,0:T(4,128)} %flags_ref.3) | copy-start | bytes 1540
  13.4 0.7 %copy-start.2 = (f32[2,8,65]{2,1,0:T(8,128)S(1)}, f32[2,8,65]{2,1,0:T(8,128)}, u32[]{:S(2)}) copy-start(f32[2,8,65]{2,1,0:T(8,128)} %bank_ref.1) | copy-start | bytes 12484
  14.1 0.7 %copy-start.3 = (s32[512]{0:T(512)S(1)}, s32[512]{0:T(512)}, u32[]{:S(2)}) copy-start(s32[512]{0:T(512)} %param.8) | copy-start | bytes 6148
  14.8 0.7 %copy-start.4 = (s32[4,32]{1,0:T(4,128)S(1)}, s32[4,32]{1,0:T(4,128)}, u32[]{:S(2)}) copy-start(s32[4,32]{1,0:T(4,128)} %offset_ref.1) | copy-start | bytes 1540
  21.2 8.0 %collective-permute-start.4 = (bf16[1,4,2,32,128]{4,3,2,1,0:T(8,128)(2,1)S(1)}, bf16[1,4,2,32,128]{4,3,2,1,0:T(8,128)(2,1)S(1)}, u32[]{:S(2)}, u32[]{:S(2)}) collective-permute-start(bf16[1,4,2,32,128]{4,3,2,1,0:T(8,128)(2,1)S(1)} %source_filter.1.refs_0_), channel_id=1, source_target_pairs={{0,12},{1,13},{2,14},{3,15},{4,8},{5,9},{6,10},{7,11},{8,4},{9,5},... | collective-permute-start | bytes 196616 | tf_op jit(solution)/shard_map/ppermute | solution.py:283
  24.7 5.5 %collective-permute-start.3 = (bf16[1,4,2,32,128]{4,3,2,1,0:T(8,128)(2,1)S(1)}, bf16[1,4,2,32,128]{4,3,2,1,0:T(8,128)(2,1)S(1)}, u32[]{:S(2)}, u32[]{:S(2)}) collective-permute-start(bf16[1,4,2,32,128]{4,3,2,1,0:T(8,128)(2,1)S(1)} %source_filter.1.refs_0_), channel_id=1, source_target_pairs={{0,8},{1,9},{2,10},{3,11},{4,12},{5,13},{6,14},{7,15},{8,0},{9,1},... | collective-permute-start | bytes 196616 | tf_op jit(solution)/shard_map/ppermute | solution.py:283
  25.7 5.3 %collective-permute-start.2 = (bf16[1,4,2,32,128]{4,3,2,1,0:T(8,128)(2,1)S(1)}, bf16[1,4,2,32,128]{4,3,2,1,0:T(8,128)(2,1)S(1)}, u32[]{:S(2)}, u32[]{:S(2)}) collective-permute-start(bf16[1,4,2,32,128]{4,3,2,1,0:T(8,128)(2,1)S(1)} %source_filter.1.refs_0_), channel_id=1, source_target_pairs={{0,4},{1,5},{2,6},{3,7},{4,0},{5,1},{6,2},{7,3},{8,12},{9,13},{10,... | collective-permute-start | bytes 196616 | tf_op jit(solution)/shard_map/ppermute | solution.py:283
  26.2 0.9 %copy-start = (bf16[2,4,32,512]{3,2,1,0:T(8,128)(2,1)S(1)}, bf16[2,4,32,512]{3,2,1,0:T(8,128)(2,1)}, u32[]{:S(2)}) copy-start(bf16[2,4,32,512]{3,2,1,0:T(8,128)(2,1)} %cur_ref.1) | copy-start | bytes 786436
  32.1 2.7 %collective-permute-start.6 = (bf16[1,4,4,2,32,128]{5,4,3,2,1,0:T(8,128)(2,1)S(1)}, bf16[1,4,4,2,32,128]{5,4,3,2,1,0:T(8,128)(2,1)S(1)}, u32[]{:S(2)}, u32[]{:S(2)}) collective-permute-start(bf16[1,4,4,2,32,128]{5,4,3,2,1,0:T(8,128)(2,1)S(1)} %column_whiten.1.refs_0_), channel_id=1, source_target_pairs={{0,1},{1,0},{2,3},{3,2},{4,5},{5,4},{6,7},{7,6},{8,9},{9,8},{10,11... | collective-permute-start | bytes 786440 | tf_op jit(solution)/shard_map/ppermute | solution.py:283
  33.3 8.4 %collective-permute-start.5 = (bf16[1,4,4,2,32,128]{5,4,3,2,1,0:T(8,128)(2,1)S(1)}, bf16[1,4,4,2,32,128]{5,4,3,2,1,0:T(8,128)(2,1)S(1)}, u32[]{:S(2)}, u32[]{:S(2)}) collective-permute-start(bf16[1,4,4,2,32,128]{5,4,3,2,1,0:T(8,128)(2,1)S(1)} %column_whiten.1.refs_0_), channel_id=1, source_target_pairs={{0,2},{1,3},{2,0},{3,1},{4,6},{5,7},{6,4},{7,5},{8,10},{9,11},{10,... | collective-permute-start | bytes 786440 | tf_op jit(solution)/shard_map/ppermute | solution.py:283
  41.7 1.5 %collective-permute-start.7 = (bf16[1,4,4,2,32,128]{5,4,3,2,1,0:T(8,128)(2,1)S(1)}, bf16[1,4,4,2,32,128]{5,4,3,2,1,0:T(8,128)(2,1)S(1)}, u32[]{:S(2)}, u32[]{:S(2)}) collective-permute-start(bf16[1,4,4,2,32,128]{5,4,3,2,1,0:T(8,128)(2,1)S(1)} %collective-permute-done.5.refs_0_), channel_id=1, source_target_pairs={{0,1},{1,0},{2,3},{3,2},{4,5},{5,4},{6,7},{7,6},{8,9},{9,8},{10,11... | collective-permute-start | bytes 786440 | tf_op jit(solution)/shard_map/ppermute | solution.py:283

commit v8 on v7

--- a/solution.py
+++ b/solution.py
@@ -10,7 +10,6 @@
 SMOOTH = 17
 LANES = 128
 WATER = 0.05
-SRC_STEP = 16
 OUT_STEP = 8
 SLOTS = 4
 
@@ -98,9 +97,10 @@
     return lax.rsqrt((total[:count] + total[count:]) * (1.0 / SMOOTH) + WATER)
 
 
-def source_kernel(params_ref, x_ref, weight_ref, index_ref, out_ref, *, win):
+def source_kernel(params_ref, x_ref, weight_ref, index_ref, *out_refs, win):
     n_chan = x_ref.shape[0]
-    _, rounds, _, ch, _ = out_ref.shape
+    _, some, _, ch, _ = out_refs[0].shape
+    rounds = some * len(out_refs)
     tile = lax.div(params_ref[0] + pl.program_id(0), win)
     zero = jnp.zeros((), jnp.bfloat16)
     gap = jnp.zeros((LANES - 3 * ch, LANES), jnp.bfloat16)
@@ -125,7 +125,7 @@
         valid = flag_column(flags)
         for p in range(2):
             part = pick[p * ch : (p + 1) * ch, r * LANES : (r + 1) * LANES] * valid
-            out_ref[0, r, p] = part.astype(jnp.bfloat16)
+            out_refs[r // some][0, r % some, p] = part.astype(jnp.bfloat16)
 
 
 def own_kernel(prev_ref, cur_ref, next_ref, weight_ref, band_ref, index_ref, valid_ref, out_ref, filt_ref):
@@ -155,7 +155,7 @@
                 out_ref[p, t, w] = white[w * ch : (w + 1) * ch, t * LANES : (t + 1) * LANES]
 
 
-def column_kernel(params_ref, *refs):
+def column_kernel(params_ref, *refs, start):
     band_ref, pick_ref, out_ref, piece_ref = refs[-4:]
     parts = refs[:-4]
     tiles, rounds, _, ch, _ = piece_ref.shape
@@ -172,7 +172,7 @@
             row = jnp.concatenate([piece_ref[t, r, p] for t in range(tiles)], axis=1)
             rows.append(
                 lax.dot_general(
-                    pick_ref[r], row, (((0,), (0,)), ((), ())), preferred_element_type=jnp.float32
+                    pick_ref[start + r], row, (((0,), (0,)), ((), ())), preferred_element_type=jnp.float32
                 )
             )
         both.append(jnp.concatenate(rows, axis=0))
@@ -197,30 +197,23 @@
     return terms[0]
 
 
-def cross_kernel(params_ref, *refs, masks, added, final):
+def cross_kernel(params_ref, *refs, masks, start):
     column_refs = refs[: len(masks)]
     local_ref = refs[len(masks)]
-    partial_ref = refs[len(masks) + 1]
-    if final:
-        out_ref, source_ref, stage_ref, sems = refs[-4:]
-        group = stage_ref.shape[2]
-    else:
-        out_ref, source_ref = refs[-2:]
-        group = SRC_STEP
+    out_ref, source_ref, stage_ref, sems = refs[-4:]
     tiles, win, ch = local_ref.shape[1:4]
     steps = source_ref.shape[2]
-    rounds = steps * group // ch
+    group = stage_ref.shape[2]
+    per_round = ch // group
     step = pl.program_id(0)
-    begin = step * group
     here = lax.rem(params_ref[0], win)
     slot = lax.rem(step, SLOTS)
 
     def copies(at_step):
         at_slot = lax.rem(at_step, SLOTS)
+        rows = pl.ds(start * ch + at_step * group, group)
         return [
-            pltpu.make_async_copy(
-                stage_ref.at[at_slot, p], out_ref.at[p, pl.ds(at_step * group, group)], sems.at[at_slot, p]
-            )
+            pltpu.make_async_copy(stage_ref.at[at_slot, p], out_ref.at[p, rows], sems.at[at_slot, p])
             for p in range(2)
         ]
 
@@ -228,19 +221,17 @@
     def _():
         for i, ref in enumerate(column_refs):
             for t in range(tiles):
-                for rr in range(rounds):
+                for r in range(steps // per_round):
                     for p in range(2):
-                        rows = ref[0, t, rr, p].astype(jnp.float32) * (1.0 / win)
-                        source_ref[i, t, rr * (ch // group) : (rr + 1) * (ch // group), p] = rows.reshape(
-                            ch // group, group // 8, 8, LANES
+                        rows = ref[0, t, r, p].astype(jnp.float32) * (1.0 / win)
+                        source_ref[i, t, r * per_round : (r + 1) * per_round, p] = rows.reshape(
+                            per_round, group // 8, 8, LANES
                         )
 
-    if final:
-
-        @pl.when(step >= SLOTS)
-        def _():
-            for copy in copies(step - SLOTS):
-                copy.wait()
+    @pl.when(step >= SLOTS)
+    def _():
+        for copy in copies(step - SLOTS):
+            copy.wait()
 
     def one_tile(ft, _):
         at = pl.ds(pl.multiple_of(ft * LANES, LANES), LANES)
@@ -253,30 +244,19 @@
                 lr, li = mine[i]
                 re.append(sr * lr + si * li)
                 im.append(sr * li - si * lr)
-            re = pairwise(re)
-            im = pairwise(im)
-            if added:
-                re = re + partial_ref[0, begin + j, ft]
-                im = im + partial_ref[1, begin + j, ft]
-            if final:
-                stage_ref[slot, 0, j, :, at] = re
-                stage_ref[slot, 1, j, :, at] = im
-            else:
-                out_ref[0, begin + j, ft] = re
-                out_ref[1, begin + j, ft] = im
+            stage_ref[slot, 0, j, :, at] = pairwise(re)
+            stage_ref[slot, 1, j, :, at] = pairwise(im)
         return 0
 
     lax.fori_loop(0, tiles, one_tile, 0)
-
-    if final:
-        for copy in copies(step):
-            copy.start()
-
-        @pl.when(step == steps - 1)
-        def _():
-            for back in range(SLOTS):
-                for copy in copies(step - back):
-                    copy.wait()
+    for copy in copies(step):
+        copy.start()
+
+    @pl.when(step == steps - 1)
+    def _():
+        for back in range(SLOTS):
+            for copy in copies(step - back):
+                copy.wait()
 
 
 def swap(x, mask, n_chan):
@@ -331,6 +311,8 @@
     )(filter_bank, band_index.reshape(tiles, 1, LANES), window_mask, source_offset)
 
     count_here = held.shape[1]
+    chunks = 2 if in_parts and rounds % 2 == 0 else 1
+    some = rounds // chunks
     filtered = pl.pallas_call(
         functools.partial(source_kernel, win=win),
         grid=(count_here,),
@@ -340,14 +322,11 @@
             vmem,
             vmem,
         ],
-        out_specs=pl.BlockSpec((1, rounds, 2, ch, LANES), lambda s: (s, 0, 0, 0, 0)),
-        out_shape=jax.ShapeDtypeStruct((count_here, rounds, 2, ch, LANES), jnp.bfloat16),
+        out_specs=[pl.BlockSpec((1, some, 2, ch, LANES), lambda s: (s, 0, 0, 0, 0))] * chunks,
+        out_shape=[jax.ShapeDtypeStruct((count_here, some, 2, ch, LANES), jnp.bfloat16)] * chunks,
         compiler_params=room(16),
         name="source_filter",
     )(params, held, weight, index)
-
-    if in_parts:
-        zparts = [filtered] + [swap(filtered, win * k, n_chan) for k in range(1, tiles)]
 
     local = pl.pallas_call(
         own_kernel,
@@ -362,58 +341,64 @@
         name="own_whiten",
     )(before, spectra, after, weight, band, index, valid)
 
-    shape = (tiles, rounds, 2, ch, LANES)
+    shape = (tiles, some, 2, ch, LANES)
     if in_parts:
-        zparts[-1], local = lax.optimization_barrier((zparts[-1], local))
         windows = 1
         specs = [vmem] * tiles
+        filtered = list(filtered)
+        filtered[-1], local = lax.optimization_barrier((filtered[-1], local))
+        zparts = [[f] + [swap(f, win * k, n_chan) for k in range(1, tiles)] for f in filtered]
     else:
         windows = win
-        zparts = [filtered.reshape((tiles, win) + shape[1:])]
+        zparts = [[f.reshape((tiles, win) + shape[1:])] for f in filtered]
         specs = [pl.BlockSpec((tiles, 1) + shape[1:], lambda s: (0, s, 0, 0, 0, 0))]
-    column = pl.pallas_call(
-        column_kernel,
-        grid=(windows,),
-        in_specs=[smem] + specs + [vmem, vmem],
-        out_specs=pl.BlockSpec((1,) + shape, lambda s: (s, 0, 0, 0, 0, 0)),
-        out_shape=jax.ShapeDtypeStruct((windows,) + shape, jnp.bfloat16),
-        scratch_shapes=[pltpu.VMEM(shape, jnp.bfloat16)],
-        compiler_params=room(16),
-        name="column_whiten",
-    )(params, *zparts, band, pick)
-
-    def cross(masks, columns, earlier, final):
-        group = OUT_STEP if final else SRC_STEP
-        rows = (len(masks), tiles, sources // group, 2, group // 8, 8, LANES)
-        scratch = [pltpu.VMEM(rows, jnp.float32)]
-        spec = vmem
-        result = jax.ShapeDtypeStruct((2, sources, tiles, ch, LANES), jnp.bfloat16)
-        if final:
-            spec = pl.BlockSpec(memory_space=pl.ANY)
-            result = jax.ShapeDtypeStruct((2, sources, ch, freq), jnp.bfloat16)
-            scratch.append(pltpu.VMEM((SLOTS, 2, group, ch, freq), jnp.bfloat16))
-            scratch.append(pltpu.SemaphoreType.DMA((SLOTS, 2)))
+
+    def whiten(c):
         return pl.pallas_call(
-            functools.partial(cross_kernel, masks=masks, added=len(earlier) > 0, final=final),
-            grid=(sources // group,),
-            in_specs=[smem] + [vmem] * (len(columns) + 1 + len(earlier)),
-            out_specs=spec,
-            out_shape=result,
-            scratch_shapes=scratch,
-            compiler_params=room(32),
+            functools.partial(column_kernel, start=c * some),
+            grid=(windows,),
+            in_specs=[smem] + specs + [vmem, vmem],
+            out_specs=pl.BlockSpec((1,) + shape, lambda s: (s, 0, 0, 0, 0, 0)),
+            out_shape=jax.ShapeDtypeStruct((windows,) + shape, jnp.bfloat16),
+            scratch_shapes=[pltpu.VMEM(shape, jnp.bfloat16)],
+            compiler_params=room(16),
+            name="column_whiten",
+        )(params, *zparts[c], band, pick)
+
+    def cross(c, masks, columns, earlier):
+        steps = some * ch // OUT_STEP
+        anywhere = pl.BlockSpec(memory_space=pl.ANY)
+        return pl.pallas_call(
+            functools.partial(cross_kernel, masks=masks, start=c * some),
+            grid=(steps,),
+            in_specs=[smem] + [vmem] * (len(columns) + 1) + [anywhere] * len(earlier),
+            out_specs=anywhere,
+            out_shape=jax.ShapeDtypeStruct((2, sources, ch, freq), jnp.bfloat16),
+            input_output_aliases={len(columns) + 2: 0} if earlier else {},
+            scratch_shapes=[
+                pltpu.VMEM((len(masks), tiles, steps, 2, OUT_STEP // 8, 8, LANES), jnp.float32),
+                pltpu.VMEM((SLOTS, 2, OUT_STEP, ch, freq), jnp.bfloat16),
+                pltpu.SemaphoreType.DMA((SLOTS, 2)),
+            ],
+            compiler_params=room(24),
             cost_estimate=pl.CostEstimate(
-                flops=16 * len(masks) * sources * ch * freq, bytes_accessed=16 << 20, transcendentals=0
+                flops=16 * win * sources * ch * freq // chunks, bytes_accessed=12 << 20, transcendentals=0
             ),
             name="cross",
         )(params, *columns, local, *earlier)
 
-    if not in_parts:
-        return cross(tuple(range(win)), [column[w : w + 1] for w in range(win)], [], True)
-    far = swap(column, 2, n_chan)
-    beside = swap(column, 1, n_chan)
-    partial = cross((0, 1), [column, beside], [], False)
-    far, partial = lax.optimization_barrier((far, partial))
-    return cross((2, 3), [far, swap(far, 1, n_chan)], [partial], True)
+    out = []
+    for c in range(chunks):
+        column = whiten(c)
+        if in_parts:
+            far = swap(column, 2, n_chan)
+            masks = (0, 1, 2, 3)
+            columns = [column, swap(column, 1, n_chan), far, swap(far, 1, n_chan)]
+        else:
+            masks = tuple(range(win))
+            columns = [column[w : w + 1] for w in range(win)]
+        out = [cross(c, masks, columns, out)]
+    return out[0]
 
 
 def solution(mesh):

time: 49.7 us -> 54.9 us (1.10)
  starting transfers between devices: 18.6 us -> 24.1 us
  waiting for transfers between devices: 10 us -> 8.99 us
  Pallas kernels: 16.1 us -> 16.8 us
    ppermute x6 -> x12, starting transfers between devices: 7.61 us -> 13.1 us  [swap(): return lax.ppermute(x, 'chan', [(i, i ^ mask) for i in range(n_chan)])]
    ppermute x6 -> x12, waiting for transfers between devices: 6.25 us -> 5.24 us  [swap(): return lax.ppermute(x, 'chan', [(i, i ^ mask) for i in range(n_chan)])]
    pallas_call x3 -> x4, Pallas kernels: 11.1 us -> 11.8 us  [the longest x2 9.87 us: cross(): pl.pallas_call(functools.partial(cross_kernel, masks=masks, start=c * som...]
  transfers between devices with their start and end apart: 9 -> 15, of which waited for: 5 -> 4; matrix products, arithmetic and copies ran while one was open for 1% -> 1% of each run, Pallas kernels for 13% -> 17%
where the time goes in v8:
time: 54.9 us; the launch traced here: 54.5 us
  starting transfers between devices  24.1 us (44%)
  Pallas kernels  16.8 us (31%)
  waiting for transfers between devices  8.99 us (16%)
  local copies, waits for them, and re-layouts  3.68 us (7%)
  other arithmetic  0.74 us (1%)
    ppermute x12, starting transfers between devices, swap(): return lax.ppermute(x, 'chan', [(i, i ^ mask) for i in range(n_chan)])  13.1 us
    pallas_call x2, Pallas kernels, cross(): pl.pallas_call(functools.partial(cross_kernel, masks=masks, start=c * som...  9.87 us
    all_to_all x1, starting transfers between devices, body(): held = lax.all_to_all(split, 'chan', 0, 0)[:, None]  7.39 us
    ppermute x12, waiting for transfers between devices, swap(): return lax.ppermute(x, 'chan', [(i, i ^ mask) for i in range(n_chan)])  5.24 us
    all_to_all x1, waiting for transfers between devices, body(): held = lax.all_to_all(split, 'chan', 0, 0)[:, None]  3.75 us
    unnamed x10, local copies, waits for them, and re-layouts  3.68 us
    ppermute x1, starting transfers between devices, body(): before = lax.ppermute(spectra, 'chan', [(i, i + 1) for i in range(ends)])  2.32 us
    pallas_call x1, Pallas kernels, body(): pl.pallas_call(own_kernel, out_shape=jax.ShapeDtypeStruct((2, tiles, win,...  2.06 us
  transfers between devices with their start and end apart: 15, of which 4 were waited for; matrix products, arithmetic and copies ran while one was open for 1% of the time, Pallas kernels for 17%

profile of v8, /device:TPU:0, one launch (start us, length us, event | category | flops | bytes accessed | tf_op | source)
XLA Modules:
  0.0 54.5 jit_solution(4275218075157702240)
XLA Ops:
  0.0 1.7 %split.1 = bf16[16,80,128]{2,1,0:T(8,128)(2,1)} custom-call(bf16[2,4,32,512]{3,2,1,0:T(8,128)(2,1)} %cur_ref.1, s32[4,32]{1,0:T(4,128)} %flags_ref.3), custom_call_target="tpu_custom_call" | custom-call | tf_op jit(solution)/shard_map/split/pallas_call | solution.py:280
  1.7 7.4 %all-to-all-start = ((bf16[16,80,128]{2,1,0:T(8,128)(2,1)}), bf16[16,80,128]{2,1,0:T(8,128)(2,1)S(1)}, u32[]{:S(2)}, u32[]{:S(2)}) async-start(bf16[16,80,128]{2,1,0:T(8,128)(2,1)} %split.1), calls=%async_computation | async-start | bytes 655360 | tf_op jit(solution)/shard_map/all_to_all | solution.py:287
  9.1 2.3 %collective-permute-start = (bf16[2,4,32,512]{3,2,1,0:T(8,128)(2,1)}, bf16[2,4,32,512]{3,2,1,0:T(8,128)(2,1)S(1)}, u32[]{:S(2)}, u32[]{:S(2)}) collective-permute-start(bf16[2,4,32,512]{3,2,1,0:T(8,128)(2,1)} %cur_ref.1), channel_id=1, source_target_pairs={{0,1},{1,2},{2,3},{3,4},{4,5},{5,6},{6,7},{7,8},{8,9},{9,10},{10,1... | collective-permute-start | bytes 786440 | tf_op jit(solution)/shard_map/ppermute | solution.py:295
  11.5 1.3 %collective-permute-start.1 = (bf16[2,4,32,512]{3,2,1,0:T(8,128)(2,1)}, bf16[2,4,32,512]{3,2,1,0:T(8,128)(2,1)S(1)}, u32[]{:S(2)}, u32[]{:S(2)}) collective-permute-start(bf16[2,4,32,512]{3,2,1,0:T(8,128)(2,1)} %cur_ref.1), channel_id=1, source_target_pairs={{1,0},{2,1},{3,2},{4,3},{5,4},{6,5},{7,6},{8,7},{9,8},{10,9},{11,1... | collective-permute-start | bytes 786440 | tf_op jit(solution)/shard_map/ppermute | solution.py:296
  12.8 0.0 copy-start.1
  12.8 0.7 %copy-done.1 = s32[4,32]{1,0:T(4,128)S(1)} copy-done((s32[4,32]{1,0:T(4,128)S(1)}, s32[4,32]{1,0:T(4,128)}, u32[]{:S(2)}) %copy-start.1) | copy-done | bytes 536
  13.4 0.0 copy-start.2
  13.4 0.7 %copy-done.2 = f32[2,8,65]{2,1,0:T(8,128)S(1)} copy-done((f32[2,8,65]{2,1,0:T(8,128)S(1)}, f32[2,8,65]{2,1,0:T(8,128)}, u32[]{:S(2)}) %copy-start.2) | copy-done | bytes 4184
  14.1 0.0 copy-start.3
  14.1 0.7 %copy-done.3 = s32[512]{0:T(512)S(1)} copy-done((s32[512]{0:T(512)S(1)}, s32[512]{0:T(512)}, u32[]{:S(2)}) %copy-start.3) | copy-done | bytes 2072
  14.8 0.0 copy-start.4
  14.8 0.7 %copy-done.4 = s32[4,32]{1,0:T(4,128)S(1)} copy-done((s32[4,32]{1,0:T(4,128)S(1)}, s32[4,32]{1,0:T(4,128)}, u32[]{:S(2)}) %copy-start.4) | copy-done | bytes 536
  15.5 0.2 prep.1
  15.8 0.7 %pad_add_fusion.params_ref = s32[6]{0:T(128)S(1)} fusion(s32[4]{0:T(128)} %param.10, s32[1]{0:T(128)} %bitcast.1, s32[1]{0:T(128)} %bitcast), kind=kLoop, calls=%fused_computation | loop fusion | flops 12 | bytes 48 | tf_op jit(solution)/shard_map/concatenate | solution.py:292
  16.5 0.0 collective-permute-done.prev_ref
  16.5 0.0 collective-permute-done.1.next_ref
  16.5 3.7 %all-to-all-done = bf16[16,80,128]{2,1,0:T(8,128)(2,1)S(1)} async-done(((bf16[16,80,128]{2,1,0:T(8,128)(2,1)}), bf16[16,80,128]{2,1,0:T(8,128)(2,1)S(1)}, u32[]{:S(2)}, u32[]{:S(2)}) %all-to-all-start) | async-done | bytes 327712 | tf_op jit(solution)/shard_map/all_to_all | solution.py:287
  20.3 1.0 %source_filter.1 = (bf16[1,2,2,32,128]{4,3,2,1,0:T(8,128)(2,1)S(1)}, bf16[1,2,2,32,128]{4,3,2,1,0:T(8,128)(2,1)S(1)}) custom-call(s32[6]{0:T(128)S(1)} %pad_add_fusion.params_ref, bf16[16,1,80,128]{3,2,1,0:T(8,128)(2,1)S(1)} %bitcast.4, bf16[1024,256]{1,0:T(8,128)(2,1)S(1)} %get-tuple-element.18.weight_ref, s32[4,1,128]{2,1,0:T(1,128)S(1)} %get-tuple-element.19.index_ref), custom_call_target="tpu_custom_call" | custom-call | tf_op jit(solution)/shard_map/source_filter/pallas_call | solution.py:316
  21.3 3.5 %collective-permute-start.10 = (bf16[1,2,2,32,128]{4,3,2,1,0:T(8,128)(2,1)S(1)}, bf16[1,2,2,32,128]{4,3,2,1,0:T(8,128)(2,1)S(1)}, u32[]{:S(2)}, u32[]{:S(2)}) collective-permute-start(bf16[1,2,2,32,128]{4,3,2,1,0:T(8,128)(2,1)S(1)} %get-tuple-element.28.refs_0_), channel_id=1, source_target_pairs={{0,12},{1,13},{2,14},{3,15},{4,8},{5,9},{6,10},{7,11},{8,4},{9,5},... | collective-permute-start | bytes 98312 | tf_op jit(solution)/shard_map/ppermute | solution.py:263
  24.8 1.0 %collective-permute-start.9 = (bf16[1,2,2,32,128]{4,3,2,1,0:T(8,128)(2,1)S(1)}, bf16[1,2,2,32,128]{4,3,2,1,0:T(8,128)(2,1)S(1)}, u32[]{:S(2)}, u32[]{:S(2)}) collective-permute-start(bf16[1,2,2,32,128]{4,3,2,1,0:T(8,128)(2,1)S(1)} %get-tuple-element.28.refs_0_), channel_id=1, source_target_pairs={{0,8},{1,9},{2,10},{3,11},{4,12},{5,13},{6,14},{7,15},{8,0},{9,1},... | collective-permute-start | bytes 98312 | tf_op jit(solution)/shard_map/ppermute | solution.py:263
  25.7 0.5 collective-permute-start.8
  26.2 0.0 copy-start
  26.2 0.9 %copy-done = bf16[2,4,32,512]{3,2,1,0:T(8,128)(2,1)S(1)} copy-done((bf16[2,4,32,512]{3,2,1,0:T(8,128)(2,1)S(1)}, bf16[2,4,32,512]{3,2,1,0:T(8,128)(2,1)}, u32[]{:S(2)}) %copy-start) | copy-done | bytes 262168
  27.1 2.1 %own_whiten.1.refs_4_ = bf16[2,4,4,32,128]{4,3,2,1,0:T(8,128)(2,1)S(1)} custom-call(bf16[2,4,32,512]{3,2,1,0:T(8,128)(2,1)S(1)} %collective-permute-done.prev_ref, bf16[2,4,32,512]{3,2,1,0:T(8,128)(2,1)S(1)} %copy-done, bf16[2,4,32,512]{3,2,1,0:T(8,128)(2,1)S(1)} %collective-permute-done.1.next_ref, bf16[1024,256]{1,0:T(8,128)(2,1)S(1)} %get-tuple-element.18.weight_ref, ...), custom_call_target="tpu_custom_call" | custom-call | flops 1073741824 | bytes 3145728 | tf_op jit(solution)/shard_map/own_whiten/pallas_call | solution.py:331
  29.2 3.0 %collective-permute-start.4 = (bf16[1,2,2,32,128]{4,3,2,1,0:T(8,128)(2,1)S(1)}, bf16[1,2,2,32,128]{4,3,2,1,0:T(8,128)(2,1)S(1)}, u32[]{:S(2)}, u32[]{:S(2)}) collective-permute-start(bf16[1,2,2,32,128]{4,3,2,1,0:T(8,128)(2,1)S(1)} %get-tuple-element.25.refs_0_), channel_id=1, source_target_pairs={{0,12},{1,13},{2,14},{3,15},{4,8},{5,9},{6,10},{7,11},{8,4},{9,5},... | collective-permute-start | bytes 98312 | tf_op jit(solution)/shard_map/ppermute | solution.py:263
  32.2 0.1 collective-permute-start.3
  32.3 0.0 collective-permute-done.10.refs_3_
  32.3 1.4 %collective-permute-start.2 = (bf16[1,2,2,32,128]{4,3,2,1,0:T(8,128)(2,1)S(1)}, bf16[1,2,2,32,128]{4,3,2,1,0:T(8,128)(2,1)S(1)}, u32[]{:S(2)}, u32[]{:S(2)}) collective-permute-start(bf16[1,2,2,32,128]{4,3,2,1,0:T(8,128)(2,1)S(1)} %get-tuple-element.25.refs_0_), channel_id=1, source_target_pairs={{0,4},{1,5},{2,6},{3,7},{4,0},{5,1},{6,2},{7,3},{8,12},{9,13},{10,... | collective-permute-start | bytes 98312 | tf_op jit(solution)/shard_map/ppermute | solution.py:263
  33.7 0.0 collective-permute-done.9.refs_2_
  33.7 0.0 collective-permute-done.8.refs_1_
  33.7 1.0 %column_whiten.3.refs_0_ = bf16[1,4,2,2,32,128]{5,4,3,2,1,0:T(8,128)(2,1)S(1)} custom-call(s32[6]{0:T(128)S(1)} %pad_add_fusion.params_ref, bf16[1,2,2,32,128]{4,3,2,1,0:T(8,128)(2,1)S(1)} %get-tuple-element.28.refs_0_, bf16[1,2,2,32,128]{4,3,2,1,0:T(8,128)(2,1)S(1)} %collective-permute-done.8.refs_1_, ...), custom_call_target="tpu_custom_call" | custom-call | tf_op jit(solution)/shard_map/column_whiten/pallas_call | solution.py:357
  34.6 1.9 %collective-permute-start.12 = (bf16[1,4,2,2,32,128]{5,4,3,2,1,0:T(8,128)(2,1)S(1)}, bf16[1,4,2,2,32,128]{5,4,3,2,1,0:T(8,128)(2,1)S(1)}, u32[]{:S(2)}, u32[]{:S(2)}) collective-permute-start(bf16[1,4,2,2,32,128]{5,4,3,2,1,0:T(8,128)(2,1)S(1)} %column_whiten.3.refs_0_), channel_id=1, source_target_pairs={{0,2},{1,3},{2,0},{3,1},{4,6},{5,7},{6,4},{7,5},{8,10},{9,11},{10,... | collective-permute-start | bytes 393224 | tf_op jit(solution)/shard_map/ppermute | solution.py:263
  36.6 0.0 collective-permute-done.4.refs_3_
  36.6 1.4 %collective-permute-done.3.refs_2_ = bf16[1,2,2,32,128]{4,3,2,1,0:T(8,128)(2,1)S(1)} collective-permute-done((bf16[1,2,2,32,128]{4,3,2,1,0:T(8,128)(2,1)S(1)}, bf16[1,2,2,32,128]{4,3,2,1,0:T(8,128)(2,1)S(1)}, u32[]{:S(2)}, u32[]{:S(2)}) %collective-permute-start.3) | collective-permute-done | bytes 32800 | tf_op jit(solution)/shard_map/ppermute | solution.py:263
  38.0 0.0 collective-permute-done.2.refs_1_
  38.0 1.0 %column_whiten.2.refs_0_ = bf16[1,4,2,2,32,128]{5,4,3,2,1,0:T(8,128)(2,1)S(1)} custom-call(s32[6]{0:T(128)S(1)} %pad_add_fusion.params_ref, bf16[1,2,2,32,128]{4,3,2,1,0:T(8,128)(2,1)S(1)} %get-tuple-element.25.refs_0_, bf16[1,2,2,32,128]{4,3,2,1,0:T(8,128)(2,1)S(1)} %collective-permute-done.2.refs_1_, ...), custom_call_target="tpu_custom_call" | custom-call | tf_op jit(solution)/shard_map/column_whiten/pallas_call | solution.py:357
  39.0 1.3 %collective-permute-start.6 = (bf16[1,4,2,2,32,128]{5,4,3,2,1,0:T(8,128)(2,1)S(1)}, bf16[1,4,2,2,32,128]{5,4,3,2,1,0:T(8,128)(2,1)S(1)}, u32[]{:S(2)}, u32[]{:S(2)}) collective-permute-start(bf16[1,4,2,2,32,128]{5,4,3,2,1,0:T(8,128)(2,1)S(1)} %column_whiten.2.refs_0_), channel_id=1, source_target_pairs={{0,2},{1,3},{2,0},{3,1},{4,6},{5,7},{6,4},{7,5},{8,10},{9,11},{10,... | collective-permute-start | bytes 393224 | tf_op jit(solution)/shard_map/ppermute | solution.py:263
  40.3 0.0 collective-permute-start.11
  40.3 0.5 collective-permute-done.12.refs_2_
  40.8 0.0 collective-permute-start.13
  40.8 0.5 collective-permute-start.5
  41.3 3.3 %collective-permute-done.6.refs_2_ = bf16[1,4,2,2,32,128]{5,4,3,2,1,0:T(8,128)(2,1)S(1)} collective-permute-done((bf16[1,4,2,2,32,128]{5,4,3,2,1,0:T(8,128)(2,1)S(1)}, bf16[1,4,2,2,32,128]{5,4,3,2,1,0:T(8,128)(2,1)S(1)}, u32[]{:S(2)}, u32[]{:S(2)}) %collective-permute-start.6) | collective-permute-done | bytes 131104 | tf_op jit(solution)/shard_map/ppermute | solution.py:263
  44.6 0.0 collective-permute-start.7
  44.6 0.0 collective-permute-done.11.refs_1_
  44.6 0.0 collective-permute-done.13.refs_3_
  44.6 4.9 %cross.2.refs_5_ = bf16[2,128,32,512]{3,2,1,0:T(8,128)(2,1)} custom-call(s32[6]{0:T(128)S(1)} %pad_add_fusion.params_ref, bf16[1,4,2,2,32,128]{5,4,3,2,1,0:T(8,128)(2,1)S(1)} %column_whiten.3.refs_0_, bf16[1,4,2,2,32,128]{5,4,3,2,1,0:T(8,128)(2,1)S(1)} %collective-permute-done.11.refs_1_, ...), custom_call_target="tpu_custom_call" | custom-call | flops 67108864 | bytes 12582912 | tf_op jit(solution)/shard_map/cross/pallas_call | solution.py:371
  49.5 0.0 collective-permute-done.5.refs_1_
  49.5 0.0 collective-permute-done.7.refs_3_
  49.5 4.9 %cross.3 = bf16[2,128,32,512]{3,2,1,0:T(8,128)(2,1)} custom-call(s32[6]{0:T(128)S(1)} %pad_add_fusion.params_ref, bf16[1,4,2,2,32,128]{5,4,3,2,1,0:T(8,128)(2,1)S(1)} %column_whiten.2.refs_0_, bf16[1,4,2,2,32,128]{5,4,3,2,1,0:T(8,128)(2,1)S(1)} %collective-permute-done.5.refs_1_, ...), custom_call_target="tpu_custom_call", output_to_operand_aliasing={{}: (6, {})} | custom-call | flops 67108864 | bytes 12582912 | tf_op jit(solution)/shard_map/cross/pallas_call | solution.py:371
Async XLA Ops:
  1.7 18.5 %all-to-all-start = ((bf16[16,80,128]{2,1,0:T(8,128)(2,1)}), bf16[16,80,128]{2,1,0:T(8,128)(2,1)S(1)}, u32[]{:S(2)}, u32[]{:S(2)}) async-start(bf16[16,80,128]{2,1,0:T(8,128)(2,1)} %split.1), calls=%async_computation | async-start | bytes 655360 | tf_op jit(solution)/shard_map/all_to_all | solution.py:287
  9.1 7.4 %collective-permute-start = (bf16[2,4,32,512]{3,2,1,0:T(8,128)(2,1)}, bf16[2,4,32,512]{3,2,1,0:T(8,128)(2,1)S(1)}, u32[]{:S(2)}, u32[]{:S(2)}) collective-permute-start(bf16[2,4,32,512]{3,2,1,0:T(8,128)(2,1)} %cur_ref.1), channel_id=1, source_target_pairs={{0,1},{1,2},{2,3},{3,4},{4,5},{5,6},{6,7},{7,8},{8,9},{9,10},{10,1... | collective-permute-start | bytes 786440 | tf_op jit(solution)/shard_map/ppermute | solution.py:295
  11.5 5.0 %collective-permute-start.1 = (bf16[2,4,32,512]{3,2,1,0:T(8,128)(2,1)}, bf16[2,4,32,512]{3,2,1,0:T(8,128)(2,1)S(1)}, u32[]{:S(2)}, u32[]{:S(2)}) collective-permute-start(bf16[2,4,32,512]{3,2,1,0:T(8,128)(2,1)} %cur_ref.1), channel_id=1, source_target_pairs={{1,0},{2,1},{3,2},{4,3},{5,4},{6,5},{7,6},{8,7},{9,8},{10,9},{11,1... | collective-permute-start | bytes 786440 | tf_op jit(solution)/shard_map/ppermute | solution.py:296
  12.8 0.7 %copy-start.1 = (s32[4,32]{1,0:T(4,128)S(1)}, s32[4,32]{1,0:T(4,128)}, u32[]{:S(2)}) copy-start(s32[4,32]{1,0:T(4,128)} %flags_ref.3) | copy-start | bytes 1540
  13.4 0.7 %copy-start.2 = (f32[2,8,65]{2,1,0:T(8,128)S(1)}, f32[2,8,65]{2,1,0:T(8,128)}, u32[]{:S(2)}) copy-start(f32[2,8,65]{2,1,0:T(8,128)} %bank_ref.1) | copy-start | bytes 12484
  14.1 0.7 %copy-start.3 = (s32[512]{0:T(512)S(1)}, s32[512]{0:T(512)}, u32[]{:S(2)}) copy-start(s32[512]{0:T(512)} %param.8) | copy-start | bytes 6148
  14.8 0.7 %copy-start.4 = (s32[4,32]{1,0:T(4,128)S(1)}, s32[4,32]{1,0:T(4,128)}, u32[]{:S(2)}) copy-start(s32[4,32]{1,0:T(4,128)} %offset_ref.1) | copy-start | bytes 1540
  21.3 11.0 %collective-permute-start.10 = (bf16[1,2,2,32,128]{4,3,2,1,0:T(8,128)(2,1)S(1)}, bf16[1,2,2,32,128]{4,3,2,1,0:T(8,128)(2,1)S(1)}, u32[]{:S(2)}, u32[]{:S(2)}) collective-permute-start(bf16[1,2,2,32,128]{4,3,2,1,0:T(8,128)(2,1)S(1)} %get-tuple-element.28.refs_0_), channel_id=1, source_target_pairs={{0,12},{1,13},{2,14},{3,15},{4,8},{5,9},{6,10},{7,11},{8,4},{9,5},... | collective-permute-start | bytes 98312 | tf_op jit(solution)/shard_map/ppermute | solution.py:263
  24.8 8.9 %collective-permute-start.9 = (bf16[1,2,2,32,128]{4,3,2,1,0:T(8,128)(2,1)S(1)}, bf16[1,2,2,32,128]{4,3,2,1,0:T(8,128)(2,1)S(1)}, u32[]{:S(2)}, u32[]{:S(2)}) collective-permute-start(bf16[1,2,2,32,128]{4,3,2,1,0:T(8,128)(2,1)S(1)} %get-tuple-element.28.refs_0_), channel_id=1, source_target_pairs={{0,8},{1,9},{2,10},{3,11},{4,12},{5,13},{6,14},{7,15},{8,0},{9,1},... | collective-permute-start | bytes 98312 | tf_op jit(solution)/shard_map/ppermute | solution.py:263
  25.7 8.0 %collective-permute-start.8 = (bf16[1,2,2,32,128]{4,3,2,1,0:T(8,128)(2,1)S(1)}, bf16[1,2,2,32,128]{4,3,2,1,0:T(8,128)(2,1)S(1)}, u32[]{:S(2)}, u32[]{:S(2)}) collective-permute-start(bf16[1,2,2,32,128]{4,3,2,1,0:T(8,128)(2,1)S(1)} %get-tuple-element.28.refs_0_), channel_id=1, source_target_pairs={{0,4},{1,5},{2,6},{3,7},{4,0},{5,1},{6,2},{7,3},{8,12},{9,13},{10,... | collective-permute-start | bytes 98312 | tf_op jit(solution)/shard_map/ppermute | solution.py:263
  26.2 0.9 %copy-start = (bf16[2,4,32,512]{3,2,1,0:T(8,128)(2,1)S(1)}, bf16[2,4,32,512]{3,2,1,0:T(8,128)(2,1)}, u32[]{:S(2)}) copy-start(bf16[2,4,32,512]{3,2,1,0:T(8,128)(2,1)} %cur_ref.1) | copy-start | bytes 786436
  29.2 7.4 %collective-permute-start.4 = (bf16[1,2,2,32,128]{4,3,2,1,0:T(8,128)(2,1)S(1)}, bf16[1,2,2,32,128]{4,3,2,1,0:T(8,128)(2,1)S(1)}, u32[]{:S(2)}, u32[]{:S(2)}) collective-permute-start(bf16[1,2,2,32,128]{4,3,2,1,0:T(8,128)(2,1)S(1)} %get-tuple-element.25.refs_0_), channel_id=1, source_target_pairs={{0,12},{1,13},{2,14},{3,15},{4,8},{5,9},{6,10},{7,11},{8,4},{9,5},... | collective-permute-start | bytes 98312 | tf_op jit(solution)/shard_map/ppermute | solution.py:263
  32.2 5.8 %collective-permute-start.3 = (bf16[1,2,2,32,128]{4,3,2,1,0:T(8,128)(2,1)S(1)}, bf16[1,2,2,32,128]{4,3,2,1,0:T(8,128)(2,1)S(1)}, u32[]{:S(2)}, u32[]{:S(2)}) collective-permute-start(bf16[1,2,2,32,128]{4,3,2,1,0:T(8,128)(2,1)S(1)} %get-tuple-element.25.refs_0_), channel_id=1, source_target_pairs={{0,8},{1,9},{2,10},{3,11},{4,12},{5,13},{6,14},{7,15},{8,0},{9,1},... | collective-permute-start | bytes 98312 | tf_op jit(solution)/shard_map/ppermute | solution.py:263
  32.3 5.7 %collective-permute-start.2 = (bf16[1,2,2,32,128]{4,3,2,1,0:T(8,128)(2,1)S(1)}, bf16[1,2,2,32,128]{4,3,2,1,0:T(8,128)(2,1)S(1)}, u32[]{:S(2)}, u32[]{:S(2)}) collective-permute-start(bf16[1,2,2,32,128]{4,3,2,1,0:T(8,128)(2,1)S(1)} %get-tuple-element.25.refs_0_), channel_id=1, source_target_pairs={{0,4},{1,5},{2,6},{3,7},{4,0},{5,1},{6,2},{7,3},{8,12},{9,13},{10,... | collective-permute-start | bytes 98312 | tf_op jit(solution)/shard_map/ppermute | solution.py:263
  34.6 6.1 %collective-permute-start.12 = (bf16[1,4,2,2,32,128]{5,4,3,2,1,0:T(8,128)(2,1)S(1)}, bf16[1,4,2,2,32,128]{5,4,3,2,1,0:T(8,128)(2,1)S(1)}, u32[]{:S(2)}, u32[]{:S(2)}) collective-permute-start(bf16[1,4,2,2,32,128]{5,4,3,2,1,0:T(8,128)(2,1)S(1)} %column_whiten.3.refs_0_), channel_id=1, source_target_pairs={{0,2},{1,3},{2,0},{3,1},{4,6},{5,7},{6,4},{7,5},{8,10},{9,11},{10,... | collective-permute-start | bytes 393224 | tf_op jit(solution)/shard_map/ppermute | solution.py:263
  39.0 5.6 %collective-permute-start.6 = (bf16[1,4,2,2,32,128]{5,4,3,2,1,0:T(8,128)(2,1)S(1)}, bf16[1,4,2,2,32,128]{5,4,3,2,1,0:T(8,128)(2,1)S(1)}, u32[]{:S(2)}, u32[]{:S(2)}) collective-permute-start(bf16[1,4,2,2,32,128]{5,4,3,2,1,0:T(8,128)(2,1)S(1)} %column_whiten.2.refs_0_), channel_id=1, source_target_pairs={{0,2},{1,3},{2,0},{3,1},{4,6},{5,7},{6,4},{7,5},{8,10},{9,11},{10,... | collective-permute-start | bytes 393224 | tf_op jit(solution)/shard_map/ppermute | solution.py:263
  40.3 4.3 %collective-permute-start.11 = (bf16[1,4,2,2,32,128]{5,4,3,2,1,0:T(8,128)(2,1)S(1)}, bf16[1,4,2,2,32,128]{5,4,3,2,1,0:T(8,128)(2,1)S(1)}, u32[]{:S(2)}, u32[]{:S(2)}) collective-permute-start(bf16[1,4,2,2,32,128]{5,4,3,2,1,0:T(8,128)(2,1)S(1)} %column_whiten.3.refs_0_), channel_id=1, source_target_pairs={{0,1},{1,0},{2,3},{3,2},{4,5},{5,4},{6,7},{7,6},{8,9},{9,8},{10,11... | collective-permute-start | bytes 393224 | tf_op jit(solution)/shard_map/ppermute | solution.py:263
  40.8 3.8 %collective-permute-start.13 = (bf16[1,4,2,2,32,128]{5,4,3,2,1,0:T(8,128)(2,1)S(1)}, bf16[1,4,2,2,32,128]{5,4,3,2,1,0:T(8,128)(2,1)S(1)}, u32[]{:S(2)}, u32[]{:S(2)}) collective-permute-start(bf16[1,4,2,2,32,128]{5,4,3,2,1,0:T(8,128)(2,1)S(1)} %collective-permute-done.12.refs_2_), channel_id=1, source_target_pairs={{0,1},{1,0},{2,3},{3,2},{4,5},{5,4},{6,7},{7,6},{8,9},{9,8},{10,11... | collective-permute-start | bytes 393224 | tf_op jit(solution)/shard_map/ppermute | solution.py:263
  40.8 8.7 %collective-permute-start.5 = (bf16[1,4,2,2,32,128]{5,4,3,2,1,0:T(8,128)(2,1)S(1)}, bf16[1,4,2,2,32,128]{5,4,3,2,1,0:T(8,128)(2,1)S(1)}, u32[]{:S(2)}, u32[]{:S(2)}) collective-permute-start(bf16[1,4,2,2,32,128]{5,4,3,2,1,0:T(8,128)(2,1)S(1)} %column_whiten.2.refs_0_), channel_id=1, source_target_pairs={{0,1},{1,0},{2,3},{3,2},{4,5},{5,4},{6,7},{7,6},{8,9},{9,8},{10,11... | collective-permute-start | bytes 393224 | tf_op jit(solution)/shard_map/ppermute | solution.py:263
  44.6 5.0 %collective-permute-start.7 = (bf16[1,4,2,2,32,128]{5,4,3,2,1,0:T(8,128)(2,1)S(1)}, bf16[1,4,2,2,32,128]{5,4,3,2,1,0:T(8,128)(2,1)S(1)}, u32[]{:S(2)}, u32[]{:S(2)}) collective-permute-start(bf16[1,4,2,2,32,128]{5,4,3,2,1,0:T(8,128)(2,1)S(1)} %collective-permute-done.6.refs_2_), channel_id=1, source_target_pairs={{0,1},{1,0},{2,3},{3,2},{4,5},{5,4},{6,7},{7,6},{8,9},{9,8},{10,11... | collective-permute-start | bytes 393224 | tf_op jit(solution)/shard_map/ppermute | solution.py:263

commit v9 on v7

--- a/solution.py
+++ b/solution.py
@@ -11,8 +11,7 @@
 LANES = 128
 WATER = 0.05
 SRC_STEP = 16
-OUT_STEP = 8
-SLOTS = 4
+SLOTS = 3
 
 
 def room(mib):
@@ -155,7 +154,7 @@
                 out_ref[p, t, w] = white[w * ch : (w + 1) * ch, t * LANES : (t + 1) * LANES]
 
 
-def column_kernel(params_ref, *refs):
+def column_kernel(params_ref, *refs, win):
     band_ref, pick_ref, out_ref, piece_ref = refs[-4:]
     parts = refs[:-4]
     tiles, rounds, _, ch, _ = piece_ref.shape
@@ -178,16 +177,14 @@
         both.append(jnp.concatenate(rows, axis=0))
     scale = running_scale(both[0], both[1], band_ref)
     for p in range(2):
-        white = (both[p] * scale).astype(jnp.bfloat16)
+        white = (both[p] * scale).astype(jnp.bfloat16) * jnp.bfloat16(1.0 / win)
         for t in range(tiles):
             for r in range(rounds):
                 out_ref[0, t, r, p] = white[r * ch : (r + 1) * ch, t * LANES : (t + 1) * LANES]
 
 
-def spread_row(ref, at, row, ch):
-    eight = ref[(*at, row // 8, pl.ds(row % 8, 8, stride=0), slice(None))]
-    pair = jnp.concatenate([eight, eight], axis=0).astype(jnp.bfloat16)
-    return jnp.concatenate([pair] * (ch // 16), axis=0)
+def spread_row(block, j, ch):
+    return jnp.broadcast_to(block[j : j + 1, :], (ch, block.shape[1]))
 
 
 def pairwise(terms):
@@ -202,16 +199,18 @@
     local_ref = refs[len(masks)]
     partial_ref = refs[len(masks) + 1]
     if final:
-        out_ref, source_ref, stage_ref, sems = refs[-4:]
-        group = stage_ref.shape[2]
+        out_ref, stage_ref, sems = refs[-3:]
     else:
-        out_ref, source_ref = refs[-2:]
-        group = SRC_STEP
+        out_ref = refs[-1]
     tiles, win, ch = local_ref.shape[1:4]
-    steps = source_ref.shape[2]
-    rounds = steps * group // ch
+    rounds = column_refs[0].shape[2]
+    group = SRC_STEP
+    per_round = ch // group
+    steps = rounds * per_round
     step = pl.program_id(0)
+    r = step // per_round
     begin = step * group
+    rows = pl.ds(pl.multiple_of(lax.rem(step, per_round) * group, group), group)
     here = lax.rem(params_ref[0], win)
     slot = lax.rem(step, SLOTS)
 
@@ -224,17 +223,6 @@
             for p in range(2)
         ]
 
-    @pl.when(step == 0)
-    def _():
-        for i, ref in enumerate(column_refs):
-            for t in range(tiles):
-                for rr in range(rounds):
-                    for p in range(2):
-                        rows = ref[0, t, rr, p].astype(jnp.float32) * (1.0 / win)
-                        source_ref[i, t, rr * (ch // group) : (rr + 1) * (ch // group), p] = rows.reshape(
-                            ch // group, group // 8, 8, LANES
-                        )
-
     if final:
 
         @pl.when(step >= SLOTS)
@@ -245,12 +233,12 @@
     def one_tile(ft, _):
         at = pl.ds(pl.multiple_of(ft * LANES, LANES), LANES)
         mine = [(local_ref[0, ft, here ^ mask], local_ref[1, ft, here ^ mask]) for mask in masks]
+        theirs = [(ref[0, ft, r, 0, rows, :], ref[0, ft, r, 1, rows, :]) for ref in column_refs]
         for j in range(group):
             re = []
             im = []
-            for i in range(len(masks)):
-                sr, si = (spread_row(source_ref, (i, ft, step, p), j, ch) for p in range(2))
-                lr, li = mine[i]
+            for (lr, li), block in zip(mine, theirs):
+                sr, si = (spread_row(part, j, ch) for part in block)
                 re.append(sr * lr + si * li)
                 im.append(sr * li - si * lr)
             re = pairwise(re)
@@ -372,7 +360,7 @@
         zparts = [filtered.reshape((tiles, win) + shape[1:])]
         specs = [pl.BlockSpec((tiles, 1) + shape[1:], lambda s: (0, s, 0, 0, 0, 0))]
     column = pl.pallas_call(
-        column_kernel,
+        functools.partial(column_kernel, win=win),
         grid=(windows,),
         in_specs=[smem] + specs + [vmem, vmem],
         out_specs=pl.BlockSpec((1,) + shape, lambda s: (s, 0, 0, 0, 0, 0)),
@@ -383,9 +371,8 @@
     )(params, *zparts, band, pick)
 
     def cross(masks, columns, earlier, final):
-        group = OUT_STEP if final else SRC_STEP
-        rows = (len(masks), tiles, sources // group, 2, group // 8, 8, LANES)
-        scratch = [pltpu.VMEM(rows, jnp.float32)]
+        group = SRC_STEP
+        scratch = []
         spec = vmem
         result = jax.ShapeDtypeStruct((2, sources, tiles, ch, LANES), jnp.bfloat16)
         if final:

time: 49.7 us -> 49.1 us (0.988)
  Pallas kernels: 16.1 us -> 15.4 us
    pallas_call x2, Pallas kernels: 10 us -> 9.28 us  [cross(): pl.pallas_call(functools.partial(cross_kernel, masks=masks, added=len(ear...]
  transfers between devices with their start and end apart: 9 -> 9, of which waited for: 5 -> 5; matrix products, arithmetic and copies ran while one was open for 1% -> 2% of each run, Pallas kernels for 13% -> 13%
where the time goes in v9:
time: 49.1 us; the launch traced here: 48.7 us
  starting transfers between devices  18.6 us (38%)
  Pallas kernels  15.4 us (31%)
  waiting for transfers between devices  10.1 us (21%)
  local copies, waits for them, and re-layouts  3.68 us (7%)
  other arithmetic  0.74 us (2%)
    pallas_call x2, Pallas kernels, cross(): pl.pallas_call(functools.partial(cross_kernel, masks=masks, added=len(ear...  9.28 us
    ppermute x6, starting transfers between devices, swap(): return lax.ppermute(x, 'chan', [(i, i ^ mask) for i in range(n_chan)])  7.61 us
    all_to_all x1, starting transfers between devices, body(): held = lax.all_to_all(split, 'chan', 0, 0)[:, None]  7.39 us
    ppermute x6, waiting for transfers between devices, swap(): return lax.ppermute(x, 'chan', [(i, i ^ mask) for i in range(n_chan)])  6.37 us
    all_to_all x1, waiting for transfers between devices, body(): held = lax.all_to_all(split, 'chan', 0, 0)[:, None]  3.75 us
    unnamed x10, local copies, waits for them, and re-layouts  3.68 us
    ppermute x1, starting transfers between devices, body(): before = lax.ppermute(spectra, 'chan', [(i, i + 1) for i in range(ends)])  2.32 us
    pallas_call x1, Pallas kernels, body(): pl.pallas_call(own_kernel, out_shape=jax.ShapeDtypeStruct((2, tiles, win,...  2.07 us
  transfers between devices with their start and end apart: 9, of which 5 were waited for; matrix products, arithmetic and copies ran while one was open for 2% of the time, Pallas kernels for 13%

profile of v9, /device:TPU:0, one launch (start us, length us, event | category | flops | bytes accessed | tf_op | source)
XLA Modules:
  0.0 48.7 jit_solution(14251002912709536825)
XLA Ops:
  0.0 1.7 %split.1 = bf16[16,80,128]{2,1,0:T(8,128)(2,1)} custom-call(bf16[2,4,32,512]{3,2,1,0:T(8,128)(2,1)} %cur_ref.1, s32[4,32]{1,0:T(4,128)} %flags_ref.3), custom_call_target="tpu_custom_call" | custom-call | tf_op jit(solution)/shard_map/split/pallas_call | solution.py:288
  1.7 7.4 %all-to-all-start = ((bf16[16,80,128]{2,1,0:T(8,128)(2,1)}), bf16[16,80,128]{2,1,0:T(8,128)(2,1)S(1)}, u32[]{:S(2)}, u32[]{:S(2)}) async-start(bf16[16,80,128]{2,1,0:T(8,128)(2,1)} %split.1), calls=%async_computation | async-start | bytes 655360 | tf_op jit(solution)/shard_map/all_to_all | solution.py:295
  9.1 2.3 %collective-permute-start = (bf16[2,4,32,512]{3,2,1,0:T(8,128)(2,1)}, bf16[2,4,32,512]{3,2,1,0:T(8,128)(2,1)S(1)}, u32[]{:S(2)}, u32[]{:S(2)}) collective-permute-start(bf16[2,4,32,512]{3,2,1,0:T(8,128)(2,1)} %cur_ref.1), channel_id=1, source_target_pairs={{0,1},{1,2},{2,3},{3,4},{4,5},{5,6},{6,7},{7,8},{8,9},{9,10},{10,1... | collective-permute-start | bytes 786440 | tf_op jit(solution)/shard_map/ppermute | solution.py:303
  11.5 1.3 %collective-permute-start.1 = (bf16[2,4,32,512]{3,2,1,0:T(8,128)(2,1)}, bf16[2,4,32,512]{3,2,1,0:T(8,128)(2,1)S(1)}, u32[]{:S(2)}, u32[]{:S(2)}) collective-permute-start(bf16[2,4,32,512]{3,2,1,0:T(8,128)(2,1)} %cur_ref.1), channel_id=1, source_target_pairs={{1,0},{2,1},{3,2},{4,3},{5,4},{6,5},{7,6},{8,7},{9,8},{10,9},{11,1... | collective-permute-start | bytes 786440 | tf_op jit(solution)/shard_map/ppermute | solution.py:304
  12.8 0.0 copy-start.1
  12.8 0.7 %copy-done.1 = s32[4,32]{1,0:T(4,128)S(1)} copy-done((s32[4,32]{1,0:T(4,128)S(1)}, s32[4,32]{1,0:T(4,128)}, u32[]{:S(2)}) %copy-start.1) | copy-done | bytes 536
  13.4 0.0 copy-start.2
  13.4 0.7 %copy-done.2 = f32[2,8,65]{2,1,0:T(8,128)S(1)} copy-done((f32[2,8,65]{2,1,0:T(8,128)S(1)}, f32[2,8,65]{2,1,0:T(8,128)}, u32[]{:S(2)}) %copy-start.2) | copy-done | bytes 4184
  14.1 0.0 copy-start.3
  14.1 0.7 %copy-done.3 = s32[512]{0:T(512)S(1)} copy-done((s32[512]{0:T(512)S(1)}, s32[512]{0:T(512)}, u32[]{:S(2)}) %copy-start.3) | copy-done | bytes 2072
  14.8 0.0 copy-start.4
  14.8 0.7 %copy-done.4 = s32[4,32]{1,0:T(4,128)S(1)} copy-done((s32[4,32]{1,0:T(4,128)S(1)}, s32[4,32]{1,0:T(4,128)}, u32[]{:S(2)}) %copy-start.4) | copy-done | bytes 536
  15.5 0.2 prep.1
  15.8 0.7 %pad_add_fusion.params_ref = s32[6]{0:T(128)S(1)} fusion(s32[4]{0:T(128)} %param.10, s32[1]{0:T(128)} %bitcast.1, s32[1]{0:T(128)} %bitcast), kind=kLoop, calls=%fused_computation | loop fusion | flops 12 | bytes 48 | tf_op jit(solution)/shard_map/concatenate | solution.py:300
  16.5 0.0 collective-permute-done.prev_ref
  16.5 0.0 collective-permute-done.1.next_ref
  16.5 3.7 %all-to-all-done = bf16[16,80,128]{2,1,0:T(8,128)(2,1)S(1)} async-done(((bf16[16,80,128]{2,1,0:T(8,128)(2,1)}), bf16[16,80,128]{2,1,0:T(8,128)(2,1)S(1)}, u32[]{:S(2)}, u32[]{:S(2)}) %all-to-all-start) | async-done | bytes 327712 | tf_op jit(solution)/shard_map/all_to_all | solution.py:295
  20.3 1.0 %source_filter.1.refs_0_ = bf16[1,4,2,32,128]{4,3,2,1,0:T(8,128)(2,1)S(1)} custom-call(s32[6]{0:T(128)S(1)} %pad_add_fusion.params_ref, bf16[16,1,80,128]{3,2,1,0:T(8,128)(2,1)S(1)} %bitcast.4, bf16[1024,256]{1,0:T(8,128)(2,1)S(1)} %get-tuple-element.18.weight_ref, s32[4,1,128]{2,1,0:T(1,128)S(1)} %get-tuple-element.19.index_ref), custom_call_target="tpu_custom_call" | custom-call | tf_op jit(solution)/shard_map/source_filter/pallas_call | solution.py:322
  21.2 3.5 %collective-permute-start.4 = (bf16[1,4,2,32,128]{4,3,2,1,0:T(8,128)(2,1)S(1)}, bf16[1,4,2,32,128]{4,3,2,1,0:T(8,128)(2,1)S(1)}, u32[]{:S(2)}, u32[]{:S(2)}) collective-permute-start(bf16[1,4,2,32,128]{4,3,2,1,0:T(8,128)(2,1)S(1)} %source_filter.1.refs_0_), channel_id=1, source_target_pairs={{0,12},{1,13},{2,14},{3,15},{4,8},{5,9},{6,10},{7,11},{8,4},{9,5},... | collective-permute-start | bytes 196616 | tf_op jit(solution)/shard_map/ppermute | solution.py:271
  24.7 1.0 %collective-permute-start.3 = (bf16[1,4,2,32,128]{4,3,2,1,0:T(8,128)(2,1)S(1)}, bf16[1,4,2,32,128]{4,3,2,1,0:T(8,128)(2,1)S(1)}, u32[]{:S(2)}, u32[]{:S(2)}) collective-permute-start(bf16[1,4,2,32,128]{4,3,2,1,0:T(8,128)(2,1)S(1)} %source_filter.1.refs_0_), channel_id=1, source_target_pairs={{0,8},{1,9},{2,10},{3,11},{4,12},{5,13},{6,14},{7,15},{8,0},{9,1},... | collective-permute-start | bytes 196616 | tf_op jit(solution)/shard_map/ppermute | solution.py:271
  25.7 0.5 %collective-permute-start.2 = (bf16[1,4,2,32,128]{4,3,2,1,0:T(8,128)(2,1)S(1)}, bf16[1,4,2,32,128]{4,3,2,1,0:T(8,128)(2,1)S(1)}, u32[]{:S(2)}, u32[]{:S(2)}) collective-permute-start(bf16[1,4,2,32,128]{4,3,2,1,0:T(8,128)(2,1)S(1)} %source_filter.1.refs_0_), channel_id=1, source_target_pairs={{0,4},{1,5},{2,6},{3,7},{4,0},{5,1},{6,2},{7,3},{8,12},{9,13},{10,... | collective-permute-start | bytes 196616 | tf_op jit(solution)/shard_map/ppermute | solution.py:271
  26.2 0.0 copy-start
  26.2 0.9 %copy-done = bf16[2,4,32,512]{3,2,1,0:T(8,128)(2,1)S(1)} copy-done((bf16[2,4,32,512]{3,2,1,0:T(8,128)(2,1)S(1)}, bf16[2,4,32,512]{3,2,1,0:T(8,128)(2,1)}, u32[]{:S(2)}) %copy-start) | copy-done | bytes 262168
  27.1 2.1 %own_whiten.1.refs_2_ = bf16[2,4,4,32,128]{4,3,2,1,0:T(8,128)(2,1)S(1)} custom-call(bf16[2,4,32,512]{3,2,1,0:T(8,128)(2,1)S(1)} %collective-permute-done.prev_ref, bf16[2,4,32,512]{3,2,1,0:T(8,128)(2,1)S(1)} %copy-done, bf16[2,4,32,512]{3,2,1,0:T(8,128)(2,1)S(1)} %collective-permute-done.1.next_ref, bf16[1024,256]{1,0:T(8,128)(2,1)S(1)} %get-tuple-element.18.weight_ref, ...), custom_call_target="tpu_custom_call" | custom-call | flops 1073741824 | bytes 3145728 | tf_op jit(solution)/shard_map/own_whiten/pallas_call | solution.py:340
  29.2 0.0 collective-permute-done.4.refs_3_
  29.2 1.1 %collective-permute-done.3.refs_2_ = bf16[1,4,2,32,128]{4,3,2,1,0:T(8,128)(2,1)S(1)} collective-permute-done((bf16[1,4,2,32,128]{4,3,2,1,0:T(8,128)(2,1)S(1)}, bf16[1,4,2,32,128]{4,3,2,1,0:T(8,128)(2,1)S(1)}, u32[]{:S(2)}, u32[]{:S(2)}) %collective-permute-start.3) | collective-permute-done | bytes 65568 | tf_op jit(solution)/shard_map/ppermute | solution.py:271
  30.3 0.7 %collective-permute-done.2.refs_1_ = bf16[1,4,2,32,128]{4,3,2,1,0:T(8,128)(2,1)S(1)} collective-permute-done((bf16[1,4,2,32,128]{4,3,2,1,0:T(8,128)(2,1)S(1)}, bf16[1,4,2,32,128]{4,3,2,1,0:T(8,128)(2,1)S(1)}, u32[]{:S(2)}, u32[]{:S(2)}) %collective-permute-start.2) | collective-permute-done | bytes 65568 | tf_op jit(solution)/shard_map/ppermute | solution.py:271
  31.0 1.1 %column_whiten.1.refs_0_ = bf16[1,4,4,2,32,128]{5,4,3,2,1,0:T(8,128)(2,1)S(1)} custom-call(s32[6]{0:T(128)S(1)} %pad_add_fusion.params_ref, bf16[1,4,2,32,128]{4,3,2,1,0:T(8,128)(2,1)S(1)} %source_filter.1.refs_0_, bf16[1,4,2,32,128]{4,3,2,1,0:T(8,128)(2,1)S(1)} %collective-permute-done.2.refs_1_, ...), custom_call_target="tpu_custom_call" | custom-call | tf_op jit(solution)/shard_map/column_whiten/pallas_call | solution.py:362
  32.1 1.1 %collective-permute-start.6 = (bf16[1,4,4,2,32,128]{5,4,3,2,1,0:T(8,128)(2,1)S(1)}, bf16[1,4,4,2,32,128]{5,4,3,2,1,0:T(8,128)(2,1)S(1)}, u32[]{:S(2)}, u32[]{:S(2)}) collective-permute-start(bf16[1,4,4,2,32,128]{5,4,3,2,1,0:T(8,128)(2,1)S(1)} %column_whiten.1.refs_0_), channel_id=1, source_target_pairs={{0,1},{1,0},{2,3},{3,2},{4,5},{5,4},{6,7},{7,6},{8,9},{9,8},{10,11... | collective-permute-start | bytes 786440 | tf_op jit(solution)/shard_map/ppermute | solution.py:271
  33.3 1.5 %collective-permute-start.5 = (bf16[1,4,4,2,32,128]{5,4,3,2,1,0:T(8,128)(2,1)S(1)}, bf16[1,4,4,2,32,128]{5,4,3,2,1,0:T(8,128)(2,1)S(1)}, u32[]{:S(2)}, u32[]{:S(2)}) collective-permute-start(bf16[1,4,4,2,32,128]{5,4,3,2,1,0:T(8,128)(2,1)S(1)} %column_whiten.1.refs_0_), channel_id=1, source_target_pairs={{0,2},{1,3},{2,0},{3,1},{4,6},{5,7},{6,4},{7,5},{8,10},{9,11},{10,... | collective-permute-start | bytes 786440 | tf_op jit(solution)/shard_map/ppermute | solution.py:271
  34.8 0.0 collective-permute-done.6.refs_1_
  34.8 3.9 %cross.2.refs_3_ = bf16[2,128,4,32,128]{4,3,2,1,0:T(8,128)(2,1)S(1)} custom-call(s32[6]{0:T(128)S(1)} %pad_add_fusion.params_ref, bf16[1,4,4,2,32,128]{5,4,3,2,1,0:T(8,128)(2,1)S(1)} %column_whiten.1.refs_0_, bf16[1,4,4,2,32,128]{5,4,3,2,1,0:T(8,128)(2,1)S(1)} %collective-permute-done.6.refs_1_, bf16[2,4,4,32,128]{4,3,2,1,0:T(8,128)(2,1)S(1)} %own_whiten.1.refs_2_), custom_call_target="tpu_custom_call" | custom-call | flops 67108864 | bytes 16777216 | tf_op jit(solution)/shard_map/cross/pallas_call | solution.py:383
  38.7 3.0 %collective-permute-done.5.refs_0_ = bf16[1,4,4,2,32,128]{5,4,3,2,1,0:T(8,128)(2,1)S(1)} collective-permute-done((bf16[1,4,4,2,32,128]{5,4,3,2,1,0:T(8,128)(2,1)S(1)}, bf16[1,4,4,2,32,128]{5,4,3,2,1,0:T(8,128)(2,1)S(1)}, u32[]{:S(2)}, u32[]{:S(2)}) %collective-permute-start.5) | collective-permute-done | bytes 262176 | tf_op jit(solution)/shard_map/ppermute | solution.py:271
  41.7 0.0 collective-permute-start.7
  41.7 1.5 %collective-permute-done.7.refs_1_ = bf16[1,4,4,2,32,128]{5,4,3,2,1,0:T(8,128)(2,1)S(1)} collective-permute-done((bf16[1,4,4,2,32,128]{5,4,3,2,1,0:T(8,128)(2,1)S(1)}, bf16[1,4,4,2,32,128]{5,4,3,2,1,0:T(8,128)(2,1)S(1)}, u32[]{:S(2)}, u32[]{:S(2)}) %collective-permute-start.7) | collective-permute-done | bytes 262176 | tf_op jit(solution)/shard_map/ppermute | solution.py:271
  43.2 5.4 %cross.3 = bf16[2,128,32,512]{3,2,1,0:T(8,128)(2,1)} custom-call(s32[6]{0:T(128)S(1)} %pad_add_fusion.params_ref, bf16[1,4,4,2,32,128]{5,4,3,2,1,0:T(8,128)(2,1)S(1)} %collective-permute-done.5.refs_0_, bf16[1,4,4,2,32,128]{5,4,3,2,1,0:T(8,128)(2,1)S(1)} %collective-permute-done.7.refs_1_, bf16[2,4,4,32,128]{4,3,2,1,0:T(8,128)(2,1)S(1)} %own_whiten.1.refs_2_, ...), custom_call_target="tpu_custom_call" | custom-call | flops 67108864 | bytes 16777216 | tf_op jit(solution)/shard_map/cross/pallas_call | solution.py:383
Async XLA Ops:
  1.7 18.5 %all-to-all-start = ((bf16[16,80,128]{2,1,0:T(8,128)(2,1)}), bf16[16,80,128]{2,1,0:T(8,128)(2,1)S(1)}, u32[]{:S(2)}, u32[]{:S(2)}) async-start(bf16[16,80,128]{2,1,0:T(8,128)(2,1)} %split.1), calls=%async_computation | async-start | bytes 655360 | tf_op jit(solution)/shard_map/all_to_all | solution.py:295
  9.1 7.4 %collective-permute-start = (bf16[2,4,32,512]{3,2,1,0:T(8,128)(2,1)}, bf16[2,4,32,512]{3,2,1,0:T(8,128)(2,1)S(1)}, u32[]{:S(2)}, u32[]{:S(2)}) collective-permute-start(bf16[2,4,32,512]{3,2,1,0:T(8,128)(2,1)} %cur_ref.1), channel_id=1, source_target_pairs={{0,1},{1,2},{2,3},{3,4},{4,5},{5,6},{6,7},{7,8},{8,9},{9,10},{10,1... | collective-permute-start | bytes 786440 | tf_op jit(solution)/shard_map/ppermute | solution.py:303
  11.5 5.0 %collective-permute-start.1 = (bf16[2,4,32,512]{3,2,1,0:T(8,128)(2,1)}, bf16[2,4,32,512]{3,2,1,0:T(8,128)(2,1)S(1)}, u32[]{:S(2)}, u32[]{:S(2)}) collective-permute-start(bf16[2,4,32,512]{3,2,1,0:T(8,128)(2,1)} %cur_ref.1), channel_id=1, source_target_pairs={{1,0},{2,1},{3,2},{4,3},{5,4},{6,5},{7,6},{8,7},{9,8},{10,9},{11,1... | collective-permute-start | bytes 786440 | tf_op jit(solution)/shard_map/ppermute | solution.py:304
  12.8 0.7 %copy-start.1 = (s32[4,32]{1,0:T(4,128)S(1)}, s32[4,32]{1,0:T(4,128)}, u32[]{:S(2)}) copy-start(s32[4,32]{1,0:T(4,128)} %flags_ref.3) | copy-start | bytes 1540
  13.4 0.7 %copy-start.2 = (f32[2,8,65]{2,1,0:T(8,128)S(1)}, f32[2,8,65]{2,1,0:T(8,128)}, u32[]{:S(2)}) copy-start(f32[2,8,65]{2,1,0:T(8,128)} %bank_ref.1) | copy-start | bytes 12484
  14.1 0.7 %copy-start.3 = (s32[512]{0:T(512)S(1)}, s32[512]{0:T(512)}, u32[]{:S(2)}) copy-start(s32[512]{0:T(512)} %param.8) | copy-start | bytes 6148
  14.8 0.7 %copy-start.4 = (s32[4,32]{1,0:T(4,128)S(1)}, s32[4,32]{1,0:T(4,128)}, u32[]{:S(2)}) copy-start(s32[4,32]{1,0:T(4,128)} %offset_ref.1) | copy-start | bytes 1540
  21.2 8.0 %collective-permute-start.4 = (bf16[1,4,2,32,128]{4,3,2,1,0:T(8,128)(2,1)S(1)}, bf16[1,4,2,32,128]{4,3,2,1,0:T(8,128)(2,1)S(1)}, u32[]{:S(2)}, u32[]{:S(2)}) collective-permute-start(bf16[1,4,2,32,128]{4,3,2,1,0:T(8,128)(2,1)S(1)} %source_filter.1.refs_0_), channel_id=1, source_target_pairs={{0,12},{1,13},{2,14},{3,15},{4,8},{5,9},{6,10},{7,11},{8,4},{9,5},... | collective-permute-start | bytes 196616 | tf_op jit(solution)/shard_map/ppermute | solution.py:271
  24.7 5.6 %collective-permute-start.3 = (bf16[1,4,2,32,128]{4,3,2,1,0:T(8,128)(2,1)S(1)}, bf16[1,4,2,32,128]{4,3,2,1,0:T(8,128)(2,1)S(1)}, u32[]{:S(2)}, u32[]{:S(2)}) collective-permute-start(bf16[1,4,2,32,128]{4,3,2,1,0:T(8,128)(2,1)S(1)} %source_filter.1.refs_0_), channel_id=1, source_target_pairs={{0,8},{1,9},{2,10},{3,11},{4,12},{5,13},{6,14},{7,15},{8,0},{9,1},... | collective-permute-start | bytes 196616 | tf_op jit(solution)/shard_map/ppermute | solution.py:271
  25.7 5.3 %collective-permute-start.2 = (bf16[1,4,2,32,128]{4,3,2,1,0:T(8,128)(2,1)S(1)}, bf16[1,4,2,32,128]{4,3,2,1,0:T(8,128)(2,1)S(1)}, u32[]{:S(2)}, u32[]{:S(2)}) collective-permute-start(bf16[1,4,2,32,128]{4,3,2,1,0:T(8,128)(2,1)S(1)} %source_filter.1.refs_0_), channel_id=1, source_target_pairs={{0,4},{1,5},{2,6},{3,7},{4,0},{5,1},{6,2},{7,3},{8,12},{9,13},{10,... | collective-permute-start | bytes 196616 | tf_op jit(solution)/shard_map/ppermute | solution.py:271
  26.2 0.9 %copy-start = (bf16[2,4,32,512]{3,2,1,0:T(8,128)(2,1)S(1)}, bf16[2,4,32,512]{3,2,1,0:T(8,128)(2,1)}, u32[]{:S(2)}) copy-start(bf16[2,4,32,512]{3,2,1,0:T(8,128)(2,1)} %cur_ref.1) | copy-start | bytes 786436
  32.1 2.7 %collective-permute-start.6 = (bf16[1,4,4,2,32,128]{5,4,3,2,1,0:T(8,128)(2,1)S(1)}, bf16[1,4,4,2,32,128]{5,4,3,2,1,0:T(8,128)(2,1)S(1)}, u32[]{:S(2)}, u32[]{:S(2)}) collective-permute-start(bf16[1,4,4,2,32,128]{5,4,3,2,1,0:T(8,128)(2,1)S(1)} %column_whiten.1.refs_0_), channel_id=1, source_target_pairs={{0,1},{1,0},{2,3},{3,2},{4,5},{5,4},{6,7},{7,6},{8,9},{9,8},{10,11... | collective-permute-start | bytes 786440 | tf_op jit(solution)/shard_map/ppermute | solution.py:271
  33.3 8.4 %collective-permute-start.5 = (bf16[1,4,4,2,32,128]{5,4,3,2,1,0:T(8,128)(2,1)S(1)}, bf16[1,4,4,2,32,128]{5,4,3,2,1,0:T(8,128)(2,1)S(1)}, u32[]{:S(2)}, u32[]{:S(2)}) collective-permute-start(bf16[1,4,4,2,32,128]{5,4,3,2,1,0:T(8,128)(2,1)S(1)} %column_whiten.1.refs_0_), channel_id=1, source_target_pairs={{0,2},{1,3},{2,0},{3,1},{4,6},{5,7},{6,4},{7,5},{8,10},{9,11},{10,... | collective-permute-start | bytes 786440 | tf_op jit(solution)/shard_map/ppermute | solution.py:271
  41.7 1.5 %collective-permute-start.7 = (bf16[1,4,4,2,32,128]{5,4,3,2,1,0:T(8,128)(2,1)S(1)}, bf16[1,4,4,2,32,128]{5,4,3,2,1,0:T(8,128)(2,1)S(1)}, u32[]{:S(2)}, u32[]{:S(2)}) collective-permute-start(bf16[1,4,4,2,32,128]{5,4,3,2,1,0:T(8,128)(2,1)S(1)} %collective-permute-done.5.refs_0_), channel_id=1, source_target_pairs={{0,1},{1,0},{2,3},{3,2},{4,5},{5,4},{6,7},{7,6},{8,9},{9,8},{10,11... | collective-permute-start | bytes 786440 | tf_op jit(solution)/shard_map/ppermute | solution.py:271

commit v10 on v9

--- a/solution.py
+++ b/solution.py
@@ -302,7 +302,7 @@
     ends = n_chan - 1
     before = lax.ppermute(spectra, "chan", [(i, i + 1) for i in range(ends)])
     after = lax.ppermute(spectra, "chan", [(i + 1, i) for i in range(ends)])
-    held, before, after = lax.optimization_barrier((held, before, after))
+    held, before = lax.optimization_barrier((held, before))
 
     weight, band, index, valid, pick = pl.pallas_call(
         prep_kernel,

time: 49.1 us -> 47.9 us (0.976)
  starting transfers between devices: 18.6 us -> 16.7 us
  waiting for transfers between devices: 10.1 us -> 10.9 us
    ppermute x6, starting transfers between devices: 7.61 us -> 5.67 us  [swap(): return lax.ppermute(x, 'chan', [(i, i ^ mask) for i in range(n_chan)])]
    ppermute x6, waiting for transfers between devices: 6.37 us -> 7.16 us  [swap(): return lax.ppermute(x, 'chan', [(i, i ^ mask) for i in range(n_chan)])]
  transfers between devices with their start and end apart: 9 -> 9, of which waited for: 5 -> 6; matrix products, arithmetic and copies ran while one was open for 2% -> 2% of each run, Pallas kernels for 13% -> 15%
where the time goes in v10:
time: 47.9 us; the launch traced here: 47.5 us
  starting transfers between devices  16.7 us (35%)
  Pallas kernels  15.4 us (32%)
  waiting for transfers between devices  10.9 us (23%)
  local copies, waits for them, and re-layouts  3.69 us (8%)
  other arithmetic  0.74 us (2%)
    pallas_call x2, Pallas kernels, cross(): pl.pallas_call(functools.partial(cross_kernel, masks=masks, added=len(ear...  9.28 us
    all_to_all x1, starting transfers between devices, body(): held = lax.all_to_all(split, 'chan', 0, 0)[:, None]  7.39 us
    ppermute x6, waiting for transfers between devices, swap(): return lax.ppermute(x, 'chan', [(i, i ^ mask) for i in range(n_chan)])  7.16 us
    ppermute x6, starting transfers between devices, swap(): return lax.ppermute(x, 'chan', [(i, i ^ mask) for i in range(n_chan)])  5.67 us
    all_to_all x1, waiting for transfers between devices, body(): held = lax.all_to_all(split, 'chan', 0, 0)[:, None]  3.75 us
    unnamed x10, local copies, waits for them, and re-layouts  3.69 us
    ppermute x1, starting transfers between devices, body(): before = lax.ppermute(spectra, 'chan', [(i, i + 1) for i in range(ends)])  2.32 us
    pallas_call x1, Pallas kernels, body(): pl.pallas_call(own_kernel, out_shape=jax.ShapeDtypeStruct((2, tiles, win,...  2.07 us
  transfers between devices with their start and end apart: 9, of which 6 were waited for; matrix products, arithmetic and copies ran while one was open for 2% of the time, Pallas kernels for 15%

profile of v10, /device:TPU:0, one launch (start us, length us, event | category | flops | bytes accessed | tf_op | source)
XLA Modules:
  0.0 47.5 jit_solution(10712770015230279813)
XLA Ops:
  0.0 1.7 %split.1 = bf16[16,80,128]{2,1,0:T(8,128)(2,1)} custom-call(bf16[2,4,32,512]{3,2,1,0:T(8,128)(2,1)} %cur_ref.1, s32[4,32]{1,0:T(4,128)} %flags_ref.3), custom_call_target="tpu_custom_call" | custom-call | tf_op jit(solution)/shard_map/split/pallas_call | solution.py:288
  1.7 7.4 %all-to-all-start = ((bf16[16,80,128]{2,1,0:T(8,128)(2,1)}), bf16[16,80,128]{2,1,0:T(8,128)(2,1)S(1)}, u32[]{:S(2)}, u32[]{:S(2)}) async-start(bf16[16,80,128]{2,1,0:T(8,128)(2,1)} %split.1), calls=%async_computation | async-start | bytes 655360 | tf_op jit(solution)/shard_map/all_to_all | solution.py:295
  9.1 2.3 %collective-permute-start = (bf16[2,4,32,512]{3,2,1,0:T(8,128)(2,1)}, bf16[2,4,32,512]{3,2,1,0:T(8,128)(2,1)S(1)}, u32[]{:S(2)}, u32[]{:S(2)}) collective-permute-start(bf16[2,4,32,512]{3,2,1,0:T(8,128)(2,1)} %cur_ref.1), channel_id=1, source_target_pairs={{0,1},{1,2},{2,3},{3,4},{4,5},{5,6},{6,7},{7,8},{8,9},{9,10},{10,1... | collective-permute-start | bytes 786440 | tf_op jit(solution)/shard_map/ppermute | solution.py:303
  11.5 1.3 %collective-permute-start.4 = (bf16[2,4,32,512]{3,2,1,0:T(8,128)(2,1)}, bf16[2,4,32,512]{3,2,1,0:T(8,128)(2,1)S(1)}, u32[]{:S(2)}, u32[]{:S(2)}) collective-permute-start(bf16[2,4,32,512]{3,2,1,0:T(8,128)(2,1)} %cur_ref.1), channel_id=1, source_target_pairs={{1,0},{2,1},{3,2},{4,3},{5,4},{6,5},{7,6},{8,7},{9,8},{10,9},{11,1... | collective-permute-start | bytes 786440 | tf_op jit(solution)/shard_map/ppermute | solution.py:304
  12.8 0.0 copy-start.1
  12.8 0.7 %copy-done.1 = s32[4,32]{1,0:T(4,128)S(1)} copy-done((s32[4,32]{1,0:T(4,128)S(1)}, s32[4,32]{1,0:T(4,128)}, u32[]{:S(2)}) %copy-start.1) | copy-done | bytes 536
  13.4 0.0 copy-start.2
  13.4 0.7 %copy-done.2 = f32[2,8,65]{2,1,0:T(8,128)S(1)} copy-done((f32[2,8,65]{2,1,0:T(8,128)S(1)}, f32[2,8,65]{2,1,0:T(8,128)}, u32[]{:S(2)}) %copy-start.2) | copy-done | bytes 4184
  14.1 0.0 copy-start.3
  14.1 0.7 %copy-done.3 = s32[512]{0:T(512)S(1)} copy-done((s32[512]{0:T(512)S(1)}, s32[512]{0:T(512)}, u32[]{:S(2)}) %copy-start.3) | copy-done | bytes 2072
  14.8 0.0 copy-start.4
  14.8 0.7 %copy-done.4 = s32[4,32]{1,0:T(4,128)S(1)} copy-done((s32[4,32]{1,0:T(4,128)S(1)}, s32[4,32]{1,0:T(4,128)}, u32[]{:S(2)}) %copy-start.4) | copy-done | bytes 536
  15.5 0.2 prep.1
  15.8 0.7 %pad_add_fusion.params_ref = s32[6]{0:T(128)S(1)} fusion(s32[4]{0:T(128)} %param.10, s32[1]{0:T(128)} %bitcast.1, s32[1]{0:T(128)} %bitcast), kind=kLoop, calls=%fused_computation | loop fusion | flops 12 | bytes 48 | tf_op jit(solution)/shard_map/concatenate | solution.py:300
  16.5 0.0 collective-permute-done.prev_ref
  16.5 3.8 %all-to-all-done = bf16[16,80,128]{2,1,0:T(8,128)(2,1)S(1)} async-done(((bf16[16,80,128]{2,1,0:T(8,128)(2,1)}), bf16[16,80,128]{2,1,0:T(8,128)(2,1)S(1)}, u32[]{:S(2)}, u32[]{:S(2)}) %all-to-all-start) | async-done | bytes 327712 | tf_op jit(solution)/shard_map/all_to_all | solution.py:295
  20.3 1.0 %source_filter.1.refs_0_ = bf16[1,4,2,32,128]{4,3,2,1,0:T(8,128)(2,1)S(1)} custom-call(s32[6]{0:T(128)S(1)} %pad_add_fusion.params_ref, bf16[16,1,80,128]{3,2,1,0:T(8,128)(2,1)S(1)} %bitcast.4, bf16[1024,256]{1,0:T(8,128)(2,1)S(1)} %get-tuple-element.17.weight_ref, s32[4,1,128]{2,1,0:T(1,128)S(1)} %get-tuple-element.18.index_ref), custom_call_target="tpu_custom_call" | custom-call | tf_op jit(solution)/shard_map/source_filter/pallas_call | solution.py:322
  21.3 3.5 %collective-permute-start.3 = (bf16[1,4,2,32,128]{4,3,2,1,0:T(8,128)(2,1)S(1)}, bf16[1,4,2,32,128]{4,3,2,1,0:T(8,128)(2,1)S(1)}, u32[]{:S(2)}, u32[]{:S(2)}) collective-permute-start(bf16[1,4,2,32,128]{4,3,2,1,0:T(8,128)(2,1)S(1)} %source_filter.1.refs_0_), channel_id=1, source_target_pairs={{0,12},{1,13},{2,14},{3,15},{4,8},{5,9},{6,10},{7,11},{8,4},{9,5},... | collective-permute-start | bytes 196616 | tf_op jit(solution)/shard_map/ppermute | solution.py:271
  24.7 1.0 %collective-permute-start.2 = (bf16[1,4,2,32,128]{4,3,2,1,0:T(8,128)(2,1)S(1)}, bf16[1,4,2,32,128]{4,3,2,1,0:T(8,128)(2,1)S(1)}, u32[]{:S(2)}, u32[]{:S(2)}) collective-permute-start(bf16[1,4,2,32,128]{4,3,2,1,0:T(8,128)(2,1)S(1)} %source_filter.1.refs_0_), channel_id=1, source_target_pairs={{0,8},{1,9},{2,10},{3,11},{4,12},{5,13},{6,14},{7,15},{8,0},{9,1},... | collective-permute-start | bytes 196616 | tf_op jit(solution)/shard_map/ppermute | solution.py:271
  25.7 0.5 %collective-permute-start.1 = (bf16[1,4,2,32,128]{4,3,2,1,0:T(8,128)(2,1)S(1)}, bf16[1,4,2,32,128]{4,3,2,1,0:T(8,128)(2,1)S(1)}, u32[]{:S(2)}, u32[]{:S(2)}) collective-permute-start(bf16[1,4,2,32,128]{4,3,2,1,0:T(8,128)(2,1)S(1)} %source_filter.1.refs_0_), channel_id=1, source_target_pairs={{0,4},{1,5},{2,6},{3,7},{4,0},{5,1},{6,2},{7,3},{8,12},{9,13},{10,... | collective-permute-start | bytes 196616 | tf_op jit(solution)/shard_map/ppermute | solution.py:271
  26.2 0.0 collective-permute-done.4.next_ref
  26.2 0.0 copy-start
  26.2 0.9 %copy-done = bf16[2,4,32,512]{3,2,1,0:T(8,128)(2,1)S(1)} copy-done((bf16[2,4,32,512]{3,2,1,0:T(8,128)(2,1)S(1)}, bf16[2,4,32,512]{3,2,1,0:T(8,128)(2,1)}, u32[]{:S(2)}) %copy-start) | copy-done | bytes 262168
  27.1 2.1 %own_whiten.1.refs_2_ = bf16[2,4,4,32,128]{4,3,2,1,0:T(8,128)(2,1)S(1)} custom-call(bf16[2,4,32,512]{3,2,1,0:T(8,128)(2,1)S(1)} %collective-permute-done.prev_ref, bf16[2,4,32,512]{3,2,1,0:T(8,128)(2,1)S(1)} %copy-done, bf16[2,4,32,512]{3,2,1,0:T(8,128)(2,1)S(1)} %collective-permute-done.4.next_ref, bf16[1024,256]{1,0:T(8,128)(2,1)S(1)} %get-tuple-element.17.weight_ref, ...), custom_call_target="tpu_custom_call" | custom-call | flops 1073741824 | bytes 3145728 | tf_op jit(solution)/shard_map/own_whiten/pallas_call | solution.py:340
  29.2 0.0 collective-permute-done.3.refs_3_
  29.2 0.8 %collective-permute-done.2.refs_2_ = bf16[1,4,2,32,128]{4,3,2,1,0:T(8,128)(2,1)S(1)} collective-permute-done((bf16[1,4,2,32,128]{4,3,2,1,0:T(8,128)(2,1)S(1)}, bf16[1,4,2,32,128]{4,3,2,1,0:T(8,128)(2,1)S(1)}, u32[]{:S(2)}, u32[]{:S(2)}) %collective-permute-start.2) | collective-permute-done | bytes 65568 | tf_op jit(solution)/shard_map/ppermute | solution.py:271
  30.1 0.6 %collective-permute-done.1.refs_1_ = bf16[1,4,2,32,128]{4,3,2,1,0:T(8,128)(2,1)S(1)} collective-permute-done((bf16[1,4,2,32,128]{4,3,2,1,0:T(8,128)(2,1)S(1)}, bf16[1,4,2,32,128]{4,3,2,1,0:T(8,128)(2,1)S(1)}, u32[]{:S(2)}, u32[]{:S(2)}) %collective-permute-start.1) | collective-permute-done | bytes 65568 | tf_op jit(solution)/shard_map/ppermute | solution.py:271
  30.7 1.1 %column_whiten.1.refs_0_ = bf16[1,4,4,2,32,128]{5,4,3,2,1,0:T(8,128)(2,1)S(1)} custom-call(s32[6]{0:T(128)S(1)} %pad_add_fusion.params_ref, bf16[1,4,2,32,128]{4,3,2,1,0:T(8,128)(2,1)S(1)} %source_filter.1.refs_0_, bf16[1,4,2,32,128]{4,3,2,1,0:T(8,128)(2,1)S(1)} %collective-permute-done.1.refs_1_, ...), custom_call_target="tpu_custom_call" | custom-call | tf_op jit(solution)/shard_map/column_whiten/pallas_call | solution.py:362
  31.8 0.1 collective-permute-start.6
  31.9 0.7 %collective-permute-start.5 = (bf16[1,4,4,2,32,128]{5,4,3,2,1,0:T(8,128)(2,1)S(1)}, bf16[1,4,4,2,32,128]{5,4,3,2,1,0:T(8,128)(2,1)S(1)}, u32[]{:S(2)}, u32[]{:S(2)}) collective-permute-start(bf16[1,4,4,2,32,128]{5,4,3,2,1,0:T(8,128)(2,1)S(1)} %column_whiten.1.refs_0_), channel_id=1, source_target_pairs={{0,2},{1,3},{2,0},{3,1},{4,6},{5,7},{6,4},{7,5},{8,10},{9,11},{10,... | collective-permute-start | bytes 786440 | tf_op jit(solution)/shard_map/ppermute | solution.py:271
  32.5 0.9 %collective-permute-done.6.refs_1_ = bf16[1,4,4,2,32,128]{5,4,3,2,1,0:T(8,128)(2,1)S(1)} collective-permute-done((bf16[1,4,4,2,32,128]{5,4,3,2,1,0:T(8,128)(2,1)S(1)}, bf16[1,4,4,2,32,128]{5,4,3,2,1,0:T(8,128)(2,1)S(1)}, u32[]{:S(2)}, u32[]{:S(2)}) %collective-permute-start.6) | collective-permute-done | bytes 262176 | tf_op jit(solution)/shard_map/ppermute | solution.py:271
  33.4 3.9 %cross.2.refs_3_ = bf16[2,128,4,32,128]{4,3,2,1,0:T(8,128)(2,1)S(1)} custom-call(s32[6]{0:T(128)S(1)} %pad_add_fusion.params_ref, bf16[1,4,4,2,32,128]{5,4,3,2,1,0:T(8,128)(2,1)S(1)} %column_whiten.1.refs_0_, bf16[1,4,4,2,32,128]{5,4,3,2,1,0:T(8,128)(2,1)S(1)} %collective-permute-done.6.refs_1_, bf16[2,4,4,32,128]{4,3,2,1,0:T(8,128)(2,1)S(1)} %own_whiten.1.refs_2_), custom_call_target="tpu_custom_call" | custom-call | flops 67108864 | bytes 16777216 | tf_op jit(solution)/shard_map/cross/pallas_call | solution.py:383
  37.2 3.3 %collective-permute-done.5.refs_0_ = bf16[1,4,4,2,32,128]{5,4,3,2,1,0:T(8,128)(2,1)S(1)} collective-permute-done((bf16[1,4,4,2,32,128]{5,4,3,2,1,0:T(8,128)(2,1)S(1)}, bf16[1,4,4,2,32,128]{5,4,3,2,1,0:T(8,128)(2,1)S(1)}, u32[]{:S(2)}, u32[]{:S(2)}) %collective-permute-start.5) | collective-permute-done | bytes 262176 | tf_op jit(solution)/shard_map/ppermute | solution.py:271
  40.6 0.0 collective-permute-start.7
  40.6 1.5 %collective-permute-done.7.refs_1_ = bf16[1,4,4,2,32,128]{5,4,3,2,1,0:T(8,128)(2,1)S(1)} collective-permute-done((bf16[1,4,4,2,32,128]{5,4,3,2,1,0:T(8,128)(2,1)S(1)}, bf16[1,4,4,2,32,128]{5,4,3,2,1,0:T(8,128)(2,1)S(1)}, u32[]{:S(2)}, u32[]{:S(2)}) %collective-permute-start.7) | collective-permute-done | bytes 262176 | tf_op jit(solution)/shard_map/ppermute | solution.py:271
  42.1 5.4 %cross.3 = bf16[2,128,32,512]{3,2,1,0:T(8,128)(2,1)} custom-call(s32[6]{0:T(128)S(1)} %pad_add_fusion.params_ref, bf16[1,4,4,2,32,128]{5,4,3,2,1,0:T(8,128)(2,1)S(1)} %collective-permute-done.5.refs_0_, bf16[1,4,4,2,32,128]{5,4,3,2,1,0:T(8,128)(2,1)S(1)} %collective-permute-done.7.refs_1_, bf16[2,4,4,32,128]{4,3,2,1,0:T(8,128)(2,1)S(1)} %own_whiten.1.refs_2_, ...), custom_call_target="tpu_custom_call" | custom-call | flops 67108864 | bytes 16777216 | tf_op jit(solution)/shard_map/cross/pallas_call | solution.py:383
Async XLA Ops:
  1.7 18.5 %all-to-all-start = ((bf16[16,80,128]{2,1,0:T(8,128)(2,1)}), bf16[16,80,128]{2,1,0:T(8,128)(2,1)S(1)}, u32[]{:S(2)}, u32[]{:S(2)}) async-start(bf16[16,80,128]{2,1,0:T(8,128)(2,1)} %split.1), calls=%async_computation | async-start | bytes 655360 | tf_op jit(solution)/shard_map/all_to_all | solution.py:295
  9.1 7.4 %collective-permute-start = (bf16[2,4,32,512]{3,2,1,0:T(8,128)(2,1)}, bf16[2,4,32,512]{3,2,1,0:T(8,128)(2,1)S(1)}, u32[]{:S(2)}, u32[]{:S(2)}) collective-permute-start(bf16[2,4,32,512]{3,2,1,0:T(8,128)(2,1)} %cur_ref.1), channel_id=1, source_target_pairs={{0,1},{1,2},{2,3},{3,4},{4,5},{5,6},{6,7},{7,8},{8,9},{9,10},{10,1... | collective-permute-start | bytes 786440 | tf_op jit(solution)/shard_map/ppermute | solution.py:303
  11.5 14.7 %collective-permute-start.4 = (bf16[2,4,32,512]{3,2,1,0:T(8,128)(2,1)}, bf16[2,4,32,512]{3,2,1,0:T(8,128)(2,1)S(1)}, u32[]{:S(2)}, u32[]{:S(2)}) collective-permute-start(bf16[2,4,32,512]{3,2,1,0:T(8,128)(2,1)} %cur_ref.1), channel_id=1, source_target_pairs={{1,0},{2,1},{3,2},{4,3},{5,4},{6,5},{7,6},{8,7},{9,8},{10,9},{11,1... | collective-permute-start | bytes 786440 | tf_op jit(solution)/shard_map/ppermute | solution.py:304
  12.8 0.7 %copy-start.1 = (s32[4,32]{1,0:T(4,128)S(1)}, s32[4,32]{1,0:T(4,128)}, u32[]{:S(2)}) copy-start(s32[4,32]{1,0:T(4,128)} %flags_ref.3) | copy-start | bytes 1540
  13.4 0.7 %copy-start.2 = (f32[2,8,65]{2,1,0:T(8,128)S(1)}, f32[2,8,65]{2,1,0:T(8,128)}, u32[]{:S(2)}) copy-start(f32[2,8,65]{2,1,0:T(8,128)} %bank_ref.1) | copy-start | bytes 12484
  14.1 0.7 %copy-start.3 = (s32[512]{0:T(512)S(1)}, s32[512]{0:T(512)}, u32[]{:S(2)}) copy-start(s32[512]{0:T(512)} %param.8) | copy-start | bytes 6148
  14.8 0.7 %copy-start.4 = (s32[4,32]{1,0:T(4,128)S(1)}, s32[4,32]{1,0:T(4,128)}, u32[]{:S(2)}) copy-start(s32[4,32]{1,0:T(4,128)} %offset_ref.1) | copy-start | bytes 1540
  21.3 8.0 %collective-permute-start.3 = (bf16[1,4,2,32,128]{4,3,2,1,0:T(8,128)(2,1)S(1)}, bf16[1,4,2,32,128]{4,3,2,1,0:T(8,128)(2,1)S(1)}, u32[]{:S(2)}, u32[]{:S(2)}) collective-permute-start(bf16[1,4,2,32,128]{4,3,2,1,0:T(8,128)(2,1)S(1)} %source_filter.1.refs_0_), channel_id=1, source_target_pairs={{0,12},{1,13},{2,14},{3,15},{4,8},{5,9},{6,10},{7,11},{8,4},{9,5},... | collective-permute-start | bytes 196616 | tf_op jit(solution)/shard_map/ppermute | solution.py:271
  24.7 5.3 %collective-permute-start.2 = (bf16[1,4,2,32,128]{4,3,2,1,0:T(8,128)(2,1)S(1)}, bf16[1,4,2,32,128]{4,3,2,1,0:T(8,128)(2,1)S(1)}, u32[]{:S(2)}, u32[]{:S(2)}) collective-permute-start(bf16[1,4,2,32,128]{4,3,2,1,0:T(8,128)(2,1)S(1)} %source_filter.1.refs_0_), channel_id=1, source_target_pairs={{0,8},{1,9},{2,10},{3,11},{4,12},{5,13},{6,14},{7,15},{8,0},{9,1},... | collective-permute-start | bytes 196616 | tf_op jit(solution)/shard_map/ppermute | solution.py:271
  25.7 5.0 %collective-permute-start.1 = (bf16[1,4,2,32,128]{4,3,2,1,0:T(8,128)(2,1)S(1)}, bf16[1,4,2,32,128]{4,3,2,1,0:T(8,128)(2,1)S(1)}, u32[]{:S(2)}, u32[]{:S(2)}) collective-permute-start(bf16[1,4,2,32,128]{4,3,2,1,0:T(8,128)(2,1)S(1)} %source_filter.1.refs_0_), channel_id=1, source_target_pairs={{0,4},{1,5},{2,6},{3,7},{4,0},{5,1},{6,2},{7,3},{8,12},{9,13},{10,... | collective-permute-start | bytes 196616 | tf_op jit(solution)/shard_map/ppermute | solution.py:271
  26.2 1.0 %copy-start = (bf16[2,4,32,512]{3,2,1,0:T(8,128)(2,1)S(1)}, bf16[2,4,32,512]{3,2,1,0:T(8,128)(2,1)}, u32[]{:S(2)}) copy-start(bf16[2,4,32,512]{3,2,1,0:T(8,128)(2,1)} %cur_ref.1) | copy-start | bytes 786436
  31.8 1.6 %collective-permute-start.6 = (bf16[1,4,4,2,32,128]{5,4,3,2,1,0:T(8,128)(2,1)S(1)}, bf16[1,4,4,2,32,128]{5,4,3,2,1,0:T(8,128)(2,1)S(1)}, u32[]{:S(2)}, u32[]{:S(2)}) collective-permute-start(bf16[1,4,4,2,32,128]{5,4,3,2,1,0:T(8,128)(2,1)S(1)} %column_whiten.1.refs_0_), channel_id=1, source_target_pairs={{0,1},{1,0},{2,3},{3,2},{4,5},{5,4},{6,7},{7,6},{8,9},{9,8},{10,11... | collective-permute-start | bytes 786440 | tf_op jit(solution)/shard_map/ppermute | solution.py:271
  31.9 8.7 %collective-permute-start.5 = (bf16[1,4,4,2,32,128]{5,4,3,2,1,0:T(8,128)(2,1)S(1)}, bf16[1,4,4,2,32,128]{5,4,3,2,1,0:T(8,128)(2,1)S(1)}, u32[]{:S(2)}, u32[]{:S(2)}) collective-permute-start(bf16[1,4,4,2,32,128]{5,4,3,2,1,0:T(8,128)(2,1)S(1)} %column_whiten.1.refs_0_), channel_id=1, source_target_pairs={{0,2},{1,3},{2,0},{3,1},{4,6},{5,7},{6,4},{7,5},{8,10},{9,11},{10,... | collective-permute-start | bytes 786440 | tf_op jit(solution)/shard_map/ppermute | solution.py:271
  40.6 1.5 %collective-permute-start.7 = (bf16[1,4,4,2,32,128]{5,4,3,2,1,0:T(8,128)(2,1)S(1)}, bf16[1,4,4,2,32,128]{5,4,3,2,1,0:T(8,128)(2,1)S(1)}, u32[]{:S(2)}, u32[]{:S(2)}) collective-permute-start(bf16[1,4,4,2,32,128]{5,4,3,2,1,0:T(8,128)(2,1)S(1)} %collective-permute-done.5.refs_0_), channel_id=1, source_target_pairs={{0,1},{1,0},{2,3},{3,2},{4,5},{5,4},{6,7},{7,6},{8,9},{9,8},{10,11... | collective-permute-start | bytes 786440 | tf_op jit(solution)/shard_map/ppermute | solution.py:271

commit v11 on v10

--- a/solution.py
+++ b/solution.py
@@ -302,7 +302,6 @@
     ends = n_chan - 1
     before = lax.ppermute(spectra, "chan", [(i, i + 1) for i in range(ends)])
     after = lax.ppermute(spectra, "chan", [(i + 1, i) for i in range(ends)])
-    held, before = lax.optimization_barrier((held, before))
 
     weight, band, index, valid, pick = pl.pallas_call(
         prep_kernel,

time: 47.9 us -> 47.7 us (level)
  starting transfers between devices: 16.7 us -> 16 us
    ppermute x6, starting transfers between devices: 5.67 us -> 5 us  [swap(): return lax.ppermute(x, 'chan', [(i, i ^ mask) for i in range(n_chan)])]
  transfers between devices with their start and end apart: 9 -> 9, of which waited for: 6 -> 5; matrix products, arithmetic and copies ran while one was open for 2% -> 2% of each run, Pallas kernels for 15% -> 15%
where the time goes in v11:
time: 47.7 us; the launch traced here: 47.3 us
  starting transfers between devices  16 us (34%)
  Pallas kernels  15.4 us (32%)
  waiting for transfers between devices  11.3 us (24%)
  local copies, waits for them, and re-layouts  3.68 us (8%)
  other arithmetic  0.74 us (2%)
    pallas_call x2, Pallas kernels, cross(): pl.pallas_call(functools.partial(cross_kernel, masks=masks, added=len(ear...  9.28 us
    ppermute x6, waiting for transfers between devices, swap(): return lax.ppermute(x, 'chan', [(i, i ^ mask) for i in range(n_chan)])  7.58 us
    all_to_all x1, starting transfers between devices, body(): held = lax.all_to_all(split, 'chan', 0, 0)[:, None]  7.39 us
    ppermute x6, starting transfers between devices, swap(): return lax.ppermute(x, 'chan', [(i, i ^ mask) for i in range(n_chan)])  5 us
    all_to_all x1, waiting for transfers between devices, body(): held = lax.all_to_all(split, 'chan', 0, 0)[:, None]  3.75 us
    unnamed x10, local copies, waits for them, and re-layouts  3.68 us
    ppermute x1, starting transfers between devices, body(): before = lax.ppermute(spectra, 'chan', [(i, i + 1) for i in range(ends)])  2.32 us
    pallas_call x1, Pallas kernels, body(): pl.pallas_call(own_kernel, out_shape=jax.ShapeDtypeStruct((2, tiles, win,...  2.07 us
  transfers between devices with their start and end apart: 9, of which 5 were waited for; matrix products, arithmetic and copies ran while one was open for 2% of the time, Pallas kernels for 15%

profile of v11, /device:TPU:0, one launch (start us, length us, event | category | flops | bytes accessed | tf_op | source)
XLA Modules:
  0.0 47.3 jit_solution(8916457292740729766)
XLA Ops:
  0.0 1.7 %split.1 = bf16[16,80,128]{2,1,0:T(8,128)(2,1)} custom-call(bf16[2,4,32,512]{3,2,1,0:T(8,128)(2,1)} %cur_ref.1, s32[4,32]{1,0:T(4,128)} %flags_ref.3), custom_call_target="tpu_custom_call" | custom-call | tf_op jit(solution)/shard_map/split/pallas_call | solution.py:288
  1.7 7.4 %all-to-all-start = ((bf16[16,80,128]{2,1,0:T(8,128)(2,1)}), bf16[16,80,128]{2,1,0:T(8,128)(2,1)S(1)}, u32[]{:S(2)}, u32[]{:S(2)}) async-start(bf16[16,80,128]{2,1,0:T(8,128)(2,1)} %split.1), calls=%async_computation | async-start | bytes 655360 | tf_op jit(solution)/shard_map/all_to_all | solution.py:295
  9.1 2.3 %collective-permute-start.3 = (bf16[2,4,32,512]{3,2,1,0:T(8,128)(2,1)}, bf16[2,4,32,512]{3,2,1,0:T(8,128)(2,1)S(1)}, u32[]{:S(2)}, u32[]{:S(2)}) collective-permute-start(bf16[2,4,32,512]{3,2,1,0:T(8,128)(2,1)} %cur_ref.1), channel_id=1, source_target_pairs={{0,1},{1,2},{2,3},{3,4},{4,5},{5,6},{6,7},{7,8},{8,9},{9,10},{10,1... | collective-permute-start | bytes 786440 | tf_op jit(solution)/shard_map/ppermute | solution.py:303
  11.5 1.3 %collective-permute-start.4 = (bf16[2,4,32,512]{3,2,1,0:T(8,128)(2,1)}, bf16[2,4,32,512]{3,2,1,0:T(8,128)(2,1)S(1)}, u32[]{:S(2)}, u32[]{:S(2)}) collective-permute-start(bf16[2,4,32,512]{3,2,1,0:T(8,128)(2,1)} %cur_ref.1), channel_id=1, source_target_pairs={{1,0},{2,1},{3,2},{4,3},{5,4},{6,5},{7,6},{8,7},{9,8},{10,9},{11,1... | collective-permute-start | bytes 786440 | tf_op jit(solution)/shard_map/ppermute | solution.py:304
  12.8 0.0 copy-start.1
  12.8 0.7 %copy-done.1 = s32[4,32]{1,0:T(4,128)S(1)} copy-done((s32[4,32]{1,0:T(4,128)S(1)}, s32[4,32]{1,0:T(4,128)}, u32[]{:S(2)}) %copy-start.1) | copy-done | bytes 536
  13.4 0.0 copy-start.2
  13.4 0.7 %copy-done.2 = f32[2,8,65]{2,1,0:T(8,128)S(1)} copy-done((f32[2,8,65]{2,1,0:T(8,128)S(1)}, f32[2,8,65]{2,1,0:T(8,128)}, u32[]{:S(2)}) %copy-start.2) | copy-done | bytes 4184
  14.1 0.0 copy-start.3
  14.1 0.7 %copy-done.3 = s32[512]{0:T(512)S(1)} copy-done((s32[512]{0:T(512)S(1)}, s32[512]{0:T(512)}, u32[]{:S(2)}) %copy-start.3) | copy-done | bytes 2072
  14.8 0.0 copy-start.4
  14.8 0.7 %copy-done.4 = s32[4,32]{1,0:T(4,128)S(1)} copy-done((s32[4,32]{1,0:T(4,128)S(1)}, s32[4,32]{1,0:T(4,128)}, u32[]{:S(2)}) %copy-start.4) | copy-done | bytes 536
  15.5 0.2 prep.1
  15.8 0.7 %pad_add_fusion.params_ref = s32[6]{0:T(128)S(1)} fusion(s32[4]{0:T(128)} %param.10, s32[1]{0:T(128)} %bitcast.1, s32[1]{0:T(128)} %bitcast), kind=kLoop, calls=%fused_computation | loop fusion | flops 12 | bytes 48 | tf_op jit(solution)/shard_map/concatenate | solution.py:300
  16.5 3.8 %all-to-all-done = bf16[16,80,128]{2,1,0:T(8,128)(2,1)S(1)} async-done(((bf16[16,80,128]{2,1,0:T(8,128)(2,1)}), bf16[16,80,128]{2,1,0:T(8,128)(2,1)S(1)}, u32[]{:S(2)}, u32[]{:S(2)}) %all-to-all-start) | async-done | bytes 327712 | tf_op jit(solution)/shard_map/all_to_all | solution.py:295
  20.3 1.0 %source_filter.1.refs_0_ = bf16[1,4,2,32,128]{4,3,2,1,0:T(8,128)(2,1)S(1)} custom-call(s32[6]{0:T(128)S(1)} %pad_add_fusion.params_ref, bf16[16,1,80,128]{3,2,1,0:T(8,128)(2,1)S(1)} %bitcast.4, bf16[1024,256]{1,0:T(8,128)(2,1)S(1)} %get-tuple-element.14.weight_ref, s32[4,1,128]{2,1,0:T(1,128)S(1)} %get-tuple-element.15.index_ref), custom_call_target="tpu_custom_call" | custom-call | tf_op jit(solution)/shard_map/source_filter/pallas_call | solution.py:321
  21.2 2.9 %collective-permute-start.2 = (bf16[1,4,2,32,128]{4,3,2,1,0:T(8,128)(2,1)S(1)}, bf16[1,4,2,32,128]{4,3,2,1,0:T(8,128)(2,1)S(1)}, u32[]{:S(2)}, u32[]{:S(2)}) collective-permute-start(bf16[1,4,2,32,128]{4,3,2,1,0:T(8,128)(2,1)S(1)} %source_filter.1.refs_0_), channel_id=1, source_target_pairs={{0,12},{1,13},{2,14},{3,15},{4,8},{5,9},{6,10},{7,11},{8,4},{9,5},... | collective-permute-start | bytes 196616 | tf_op jit(solution)/shard_map/ppermute | solution.py:271
  24.1 0.0 collective-permute-start.1
  24.1 1.6 %collective-permute-start = (bf16[1,4,2,32,128]{4,3,2,1,0:T(8,128)(2,1)S(1)}, bf16[1,4,2,32,128]{4,3,2,1,0:T(8,128)(2,1)S(1)}, u32[]{:S(2)}, u32[]{:S(2)}) collective-permute-start(bf16[1,4,2,32,128]{4,3,2,1,0:T(8,128)(2,1)S(1)} %source_filter.1.refs_0_), channel_id=1, source_target_pairs={{0,4},{1,5},{2,6},{3,7},{4,0},{5,1},{6,2},{7,3},{8,12},{9,13},{10,... | collective-permute-start | bytes 196616 | tf_op jit(solution)/shard_map/ppermute | solution.py:271
  25.7 0.0 collective-permute-done.3.prev_ref
  25.7 0.0 collective-permute-done.4.next_ref
  25.7 0.0 copy-start
  25.7 0.9 %copy-done = bf16[2,4,32,512]{3,2,1,0:T(8,128)(2,1)S(1)} copy-done((bf16[2,4,32,512]{3,2,1,0:T(8,128)(2,1)S(1)}, bf16[2,4,32,512]{3,2,1,0:T(8,128)(2,1)}, u32[]{:S(2)}) %copy-start) | copy-done | bytes 262168
  26.7 2.1 %own_whiten.1.refs_2_ = bf16[2,4,4,32,128]{4,3,2,1,0:T(8,128)(2,1)S(1)} custom-call(bf16[2,4,32,512]{3,2,1,0:T(8,128)(2,1)S(1)} %collective-permute-done.3.prev_ref, bf16[2,4,32,512]{3,2,1,0:T(8,128)(2,1)S(1)} %copy-done, bf16[2,4,32,512]{3,2,1,0:T(8,128)(2,1)S(1)} %collective-permute-done.4.next_ref, bf16[1024,256]{1,0:T(8,128)(2,1)S(1)} %get-tuple-element.14.weight_ref, ...), custom_call_target="tpu_custom_call" | custom-call | flops 1073741824 | bytes 3145728 | tf_op jit(solution)/shard_map/own_whiten/pallas_call | solution.py:339
  28.7 0.0 collective-permute-done.2.refs_3_
  28.7 1.7 %collective-permute-done.1.refs_2_ = bf16[1,4,2,32,128]{4,3,2,1,0:T(8,128)(2,1)S(1)} collective-permute-done((bf16[1,4,2,32,128]{4,3,2,1,0:T(8,128)(2,1)S(1)}, bf16[1,4,2,32,128]{4,3,2,1,0:T(8,128)(2,1)S(1)}, u32[]{:S(2)}, u32[]{:S(2)}) %collective-permute-start.1) | collective-permute-done | bytes 65568 | tf_op jit(solution)/shard_map/ppermute | solution.py:271
  30.4 0.0 collective-permute-done.refs_1_
  30.4 1.1 %column_whiten.1.refs_0_ = bf16[1,4,4,2,32,128]{5,4,3,2,1,0:T(8,128)(2,1)S(1)} custom-call(s32[6]{0:T(128)S(1)} %pad_add_fusion.params_ref, bf16[1,4,2,32,128]{4,3,2,1,0:T(8,128)(2,1)S(1)} %source_filter.1.refs_0_, bf16[1,4,2,32,128]{4,3,2,1,0:T(8,128)(2,1)S(1)} %collective-permute-done.refs_1_, ...), custom_call_target="tpu_custom_call" | custom-call | tf_op jit(solution)/shard_map/column_whiten/pallas_call | solution.py:361
  31.5 0.1 collective-permute-start.6
  31.6 0.5 collective-permute-start.5
  32.1 1.1 %collective-permute-done.6.refs_1_ = bf16[1,4,4,2,32,128]{5,4,3,2,1,0:T(8,128)(2,1)S(1)} collective-permute-done((bf16[1,4,4,2,32,128]{5,4,3,2,1,0:T(8,128)(2,1)S(1)}, bf16[1,4,4,2,32,128]{5,4,3,2,1,0:T(8,128)(2,1)S(1)}, u32[]{:S(2)}, u32[]{:S(2)}) %collective-permute-start.6) | collective-permute-done | bytes 262176 | tf_op jit(solution)/shard_map/ppermute | solution.py:271
  33.1 3.9 %cross.2.refs_3_ = bf16[2,128,4,32,128]{4,3,2,1,0:T(8,128)(2,1)S(1)} custom-call(s32[6]{0:T(128)S(1)} %pad_add_fusion.params_ref, bf16[1,4,4,2,32,128]{5,4,3,2,1,0:T(8,128)(2,1)S(1)} %column_whiten.1.refs_0_, bf16[1,4,4,2,32,128]{5,4,3,2,1,0:T(8,128)(2,1)S(1)} %collective-permute-done.6.refs_1_, bf16[2,4,4,32,128]{4,3,2,1,0:T(8,128)(2,1)S(1)} %own_whiten.1.refs_2_), custom_call_target="tpu_custom_call" | custom-call | flops 67108864 | bytes 16777216 | tf_op jit(solution)/shard_map/cross/pallas_call | solution.py:382
  37.0 3.3 %collective-permute-done.5.refs_0_ = bf16[1,4,4,2,32,128]{5,4,3,2,1,0:T(8,128)(2,1)S(1)} collective-permute-done((bf16[1,4,4,2,32,128]{5,4,3,2,1,0:T(8,128)(2,1)S(1)}, bf16[1,4,4,2,32,128]{5,4,3,2,1,0:T(8,128)(2,1)S(1)}, u32[]{:S(2)}, u32[]{:S(2)}) %collective-permute-start.5) | collective-permute-done | bytes 262176 | tf_op jit(solution)/shard_map/ppermute | solution.py:271
  40.3 0.0 collective-permute-start.7
  40.3 1.5 %collective-permute-done.7.refs_1_ = bf16[1,4,4,2,32,128]{5,4,3,2,1,0:T(8,128)(2,1)S(1)} collective-permute-done((bf16[1,4,4,2,32,128]{5,4,3,2,1,0:T(8,128)(2,1)S(1)}, bf16[1,4,4,2,32,128]{5,4,3,2,1,0:T(8,128)(2,1)S(1)}, u32[]{:S(2)}, u32[]{:S(2)}) %collective-permute-start.7) | collective-permute-done | bytes 262176 | tf_op jit(solution)/shard_map/ppermute | solution.py:271
  41.9 5.4 %cross.3 = bf16[2,128,32,512]{3,2,1,0:T(8,128)(2,1)} custom-call(s32[6]{0:T(128)S(1)} %pad_add_fusion.params_ref, bf16[1,4,4,2,32,128]{5,4,3,2,1,0:T(8,128)(2,1)S(1)} %collective-permute-done.5.refs_0_, bf16[1,4,4,2,32,128]{5,4,3,2,1,0:T(8,128)(2,1)S(1)} %collective-permute-done.7.refs_1_, bf16[2,4,4,32,128]{4,3,2,1,0:T(8,128)(2,1)S(1)} %own_whiten.1.refs_2_, ...), custom_call_target="tpu_custom_call" | custom-call | flops 67108864 | bytes 16777216 | tf_op jit(solution)/shard_map/cross/pallas_call | solution.py:382
Async XLA Ops:
  1.7 18.5 %all-to-all-start = ((bf16[16,80,128]{2,1,0:T(8,128)(2,1)}), bf16[16,80,128]{2,1,0:T(8,128)(2,1)S(1)}, u32[]{:S(2)}, u32[]{:S(2)}) async-start(bf16[16,80,128]{2,1,0:T(8,128)(2,1)} %split.1), calls=%async_computation | async-start | bytes 655360 | tf_op jit(solution)/shard_map/all_to_all | solution.py:295
  9.1 16.6 %collective-permute-start.3 = (bf16[2,4,32,512]{3,2,1,0:T(8,128)(2,1)}, bf16[2,4,32,512]{3,2,1,0:T(8,128)(2,1)S(1)}, u32[]{:S(2)}, u32[]{:S(2)}) collective-permute-start(bf16[2,4,32,512]{3,2,1,0:T(8,128)(2,1)} %cur_ref.1), channel_id=1, source_target_pairs={{0,1},{1,2},{2,3},{3,4},{4,5},{5,6},{6,7},{7,8},{8,9},{9,10},{10,1... | collective-permute-start | bytes 786440 | tf_op jit(solution)/shard_map/ppermute | solution.py:303
  11.5 14.3 %collective-permute-start.4 = (bf16[2,4,32,512]{3,2,1,0:T(8,128)(2,1)}, bf16[2,4,32,512]{3,2,1,0:T(8,128)(2,1)S(1)}, u32[]{:S(2)}, u32[]{:S(2)}) collective-permute-start(bf16[2,4,32,512]{3,2,1,0:T(8,128)(2,1)} %cur_ref.1), channel_id=1, source_target_pairs={{1,0},{2,1},{3,2},{4,3},{5,4},{6,5},{7,6},{8,7},{9,8},{10,9},{11,1... | collective-permute-start | bytes 786440 | tf_op jit(solution)/shard_map/ppermute | solution.py:304
  12.8 0.7 %copy-start.1 = (s32[4,32]{1,0:T(4,128)S(1)}, s32[4,32]{1,0:T(4,128)}, u32[]{:S(2)}) copy-start(s32[4,32]{1,0:T(4,128)} %flags_ref.3) | copy-start | bytes 1540
  13.4 0.7 %copy-start.2 = (f32[2,8,65]{2,1,0:T(8,128)S(1)}, f32[2,8,65]{2,1,0:T(8,128)}, u32[]{:S(2)}) copy-start(f32[2,8,65]{2,1,0:T(8,128)} %bank_ref.1) | copy-start | bytes 12484
  14.1 0.7 %copy-start.3 = (s32[512]{0:T(512)S(1)}, s32[512]{0:T(512)}, u32[]{:S(2)}) copy-start(s32[512]{0:T(512)} %param.8) | copy-start | bytes 6148
  14.8 0.7 %copy-start.4 = (s32[4,32]{1,0:T(4,128)S(1)}, s32[4,32]{1,0:T(4,128)}, u32[]{:S(2)}) copy-start(s32[4,32]{1,0:T(4,128)} %offset_ref.1) | copy-start | bytes 1540
  21.2 7.5 %collective-permute-start.2 = (bf16[1,4,2,32,128]{4,3,2,1,0:T(8,128)(2,1)S(1)}, bf16[1,4,2,32,128]{4,3,2,1,0:T(8,128)(2,1)S(1)}, u32[]{:S(2)}, u32[]{:S(2)}) collective-permute-start(bf16[1,4,2,32,128]{4,3,2,1,0:T(8,128)(2,1)S(1)} %source_filter.1.refs_0_), channel_id=1, source_target_pairs={{0,12},{1,13},{2,14},{3,15},{4,8},{5,9},{6,10},{7,11},{8,4},{9,5},... | collective-permute-start | bytes 196616 | tf_op jit(solution)/shard_map/ppermute | solution.py:271
  24.1 6.3 %collective-permute-start.1 = (bf16[1,4,2,32,128]{4,3,2,1,0:T(8,128)(2,1)S(1)}, bf16[1,4,2,32,128]{4,3,2,1,0:T(8,128)(2,1)S(1)}, u32[]{:S(2)}, u32[]{:S(2)}) collective-permute-start(bf16[1,4,2,32,128]{4,3,2,1,0:T(8,128)(2,1)S(1)} %source_filter.1.refs_0_), channel_id=1, source_target_pairs={{0,8},{1,9},{2,10},{3,11},{4,12},{5,13},{6,14},{7,15},{8,0},{9,1},... | collective-permute-start | bytes 196616 | tf_op jit(solution)/shard_map/ppermute | solution.py:271
  24.1 6.3 %collective-permute-start = (bf16[1,4,2,32,128]{4,3,2,1,0:T(8,128)(2,1)S(1)}, bf16[1,4,2,32,128]{4,3,2,1,0:T(8,128)(2,1)S(1)}, u32[]{:S(2)}, u32[]{:S(2)}) collective-permute-start(bf16[1,4,2,32,128]{4,3,2,1,0:T(8,128)(2,1)S(1)} %source_filter.1.refs_0_), channel_id=1, source_target_pairs={{0,4},{1,5},{2,6},{3,7},{4,0},{5,1},{6,2},{7,3},{8,12},{9,13},{10,... | collective-permute-start | bytes 196616 | tf_op jit(solution)/shard_map/ppermute | solution.py:271
  25.7 1.0 %copy-start = (bf16[2,4,32,512]{3,2,1,0:T(8,128)(2,1)S(1)}, bf16[2,4,32,512]{3,2,1,0:T(8,128)(2,1)}, u32[]{:S(2)}) copy-start(bf16[2,4,32,512]{3,2,1,0:T(8,128)(2,1)} %cur_ref.1) | copy-start | bytes 786436
  31.5 1.6 %collective-permute-start.6 = (bf16[1,4,4,2,32,128]{5,4,3,2,1,0:T(8,128)(2,1)S(1)}, bf16[1,4,4,2,32,128]{5,4,3,2,1,0:T(8,128)(2,1)S(1)}, u32[]{:S(2)}, u32[]{:S(2)}) collective-permute-start(bf16[1,4,4,2,32,128]{5,4,3,2,1,0:T(8,128)(2,1)S(1)} %column_whiten.1.refs_0_), channel_id=1, source_target_pairs={{0,1},{1,0},{2,3},{3,2},{4,5},{5,4},{6,7},{7,6},{8,9},{9,8},{10,11... | collective-permute-start | bytes 786440 | tf_op jit(solution)/shard_map/ppermute | solution.py:271
  31.6 8.7 %collective-permute-start.5 = (bf16[1,4,4,2,32,128]{5,4,3,2,1,0:T(8,128)(2,1)S(1)}, bf16[1,4,4,2,32,128]{5,4,3,2,1,0:T(8,128)(2,1)S(1)}, u32[]{:S(2)}, u32[]{:S(2)}) collective-permute-start(bf16[1,4,4,2,32,128]{5,4,3,2,1,0:T(8,128)(2,1)S(1)} %column_whiten.1.refs_0_), channel_id=1, source_target_pairs={{0,2},{1,3},{2,0},{3,1},{4,6},{5,7},{6,4},{7,5},{8,10},{9,11},{10,... | collective-permute-start | bytes 786440 | tf_op jit(solution)/shard_map/ppermute | solution.py:271
  40.3 1.5 %collective-permute-start.7 = (bf16[1,4,4,2,32,128]{5,4,3,2,1,0:T(8,128)(2,1)S(1)}, bf16[1,4,4,2,32,128]{5,4,3,2,1,0:T(8,128)(2,1)S(1)}, u32[]{:S(2)}, u32[]{:S(2)}) collective-permute-start(bf16[1,4,4,2,32,128]{5,4,3,2,1,0:T(8,128)(2,1)S(1)} %collective-permute-done.5.refs_0_), channel_id=1, source_target_pairs={{0,1},{1,0},{2,3},{3,2},{4,5},{5,4},{6,7},{7,6},{8,9},{9,8},{10,11... | collective-permute-start | bytes 786440 | tf_op jit(solution)/shard_map/ppermute | solution.py:271

commit v12 on v11

--- a/solution.py
+++ b/solution.py
@@ -18,11 +18,23 @@
     return pltpu.CompilerParams(vmem_limit_bytes=mib * 1024 * 1024)
 
 
-def split_kernel(spectra_ref, flags_ref, piece_ref):
-    _, win, ch, freq = spectra_ref.shape
+def fetch(pairs, sems):
+    copies = [pltpu.make_async_copy(src, dst, sems.at[i]) for i, (src, dst) in enumerate(pairs)]
+    for copy in copies:
+        copy.start()
+    return copies
+
+
+def split_kernel(whole_ref, valid_ref, piece_ref, flags_ref, spectra_ref, sems):
+    _, win, ch, freq = whole_ref.shape
     tiles = freq // LANES
     extra = piece_ref.shape[1] - 2 * ch
+    copies = fetch(
+        [(valid_ref, flags_ref)] + [(whole_ref.at[:, w], spectra_ref.at[:, w]) for w in range(win)], sems
+    )
+    copies[0].wait()
     for w in range(win):
+        copies[1 + w].wait()
         flags = jnp.broadcast_to(flags_ref[w : w + 1, :], (extra, ch)).astype(jnp.float32)
         for t in range(tiles):
             at = slice(t * LANES, (t + 1) * LANES)
@@ -32,9 +44,11 @@
             piece_ref[t * win + w, 2 * ch :, :ch] = flags.astype(jnp.bfloat16)
 
 
-def prep_kernel(
-    bank_ref, bins_ref, flags_ref, offset_ref, weight_ref, band_ref, index_ref, valid_ref, pick_ref, padded_ref
-):
+def prep_kernel(*refs):
+    sources, (weight_ref, band_ref, index_ref, valid_ref, pick_ref) = refs[:4], refs[4:9]
+    (bank_ref, bins_ref, flags_ref, offset_ref), padded_ref, sems = refs[9:13], refs[13], refs[14]
+    for copy in fetch(list(zip(sources, (bank_ref, bins_ref, flags_ref, offset_ref))), sems):
+        copy.wait()
     _, banks, taps = bank_ref.shape
     half = weight_ref.shape[0] // 2
     ch = half // (2 * banks)
@@ -127,8 +141,8 @@
             out_ref[0, r, p] = part.astype(jnp.bfloat16)
 
 
-def own_kernel(prev_ref, cur_ref, next_ref, weight_ref, band_ref, index_ref, valid_ref, out_ref, filt_ref):
-    _, win, ch, freq = cur_ref.shape
+def own_kernel(prev_ref, piece_ref, next_ref, weight_ref, band_ref, index_ref, valid_ref, out_ref, filt_ref):
+    _, win, ch, freq = prev_ref.shape
     tiles = freq // LANES
     gap = jnp.zeros((LANES - 3 * ch, freq), jnp.bfloat16)
     index = jnp.concatenate([index_ref[t] for t in range(tiles)], axis=1)
@@ -136,7 +150,9 @@
     def one_window(w, _):
         parts = []
         for p in range(2):
-            parts += [prev_ref[p, w], cur_ref[p, w], next_ref[p, w], gap]
+            at = slice(p * ch, (p + 1) * ch)
+            here = jnp.concatenate([piece_ref[t * win + w, at] for t in range(tiles)], axis=1)
+            parts += [prev_ref[p, w], here, next_ref[p, w], gap]
         x = jnp.concatenate(parts, axis=0)
         pick = filtered_block(x, weight_ref, index, ch)
         at = pl.ds(pl.multiple_of(w * ch, ch), ch)
@@ -284,11 +300,19 @@
     in_parts = n_chan == pieces and win == 4 and tiles & (tiles - 1) == 0
     smem = pl.BlockSpec(memory_space=pltpu.SMEM)
     vmem = pl.BlockSpec(memory_space=pltpu.VMEM)
+    hbm = pl.BlockSpec(memory_space=pltpu.HBM)
 
     split = pl.pallas_call(
         split_kernel,
         out_shape=jax.ShapeDtypeStruct((pieces, 2 * ch + 16, LANES), jnp.bfloat16),
-        compiler_params=room(56),
+        in_specs=[hbm, hbm],
+        out_specs=vmem,
+        scratch_shapes=[
+            pltpu.VMEM(window_mask.shape, jnp.int32),
+            pltpu.VMEM(spectra.shape, jnp.bfloat16),
+            pltpu.SemaphoreType.DMA((1 + win,)),
+        ],
+        compiler_params=room(6),
         name="split",
     )(spectra, window_mask)
     if in_parts:
@@ -312,7 +336,16 @@
             jax.ShapeDtypeStruct((count, LANES), jnp.float32),
             jax.ShapeDtypeStruct((rounds, ch, ch), jnp.bfloat16),
         ),
-        scratch_shapes=[pltpu.VMEM((2, banks, LANES), jnp.float32)],
+        in_specs=[hbm] * 4,
+        out_specs=[vmem] * 5,
+        scratch_shapes=[
+            pltpu.VMEM(filter_bank.shape, jnp.float32),
+            pltpu.VMEM((tiles, 1, LANES), jnp.int32),
+            pltpu.VMEM(window_mask.shape, jnp.int32),
+            pltpu.VMEM(source_offset.shape, jnp.int32),
+            pltpu.VMEM((2, banks, LANES), jnp.float32),
+            pltpu.SemaphoreType.DMA((4,)),
+        ],
         compiler_params=room(8),
         name="prep",
     )(filter_bank, band_index.reshape(tiles, 1, LANES), window_mask, source_offset)
@@ -347,7 +380,7 @@
             flops=4 * banks * 2 * ch * 2 * LANES * win * freq, bytes_accessed=3 << 20, transcendentals=0
         ),
         name="own_whiten",
-    )(before, spectra, after, weight, band, index, valid)
+    )(before, split, after, weight, band, index, valid)
 
     shape = (tiles, rounds, 2, ch, LANES)
     if in_parts:

time: 47.7 us -> 48.5 us (1.017)
  waiting for transfers between devices: 11.3 us -> 9.82 us
  starting transfers between devices: 16 us -> 17.3 us
  local copies, waits for them, and re-layouts: 3.68 us -> 4.37 us
    pallas_call x1, Pallas kernels: 2.07 us -> 3.05 us  [body(): pl.pallas_call(own_kernel, out_shape=jax.ShapeDtypeStruct((2, tiles, win,...]
    all_to_all x1, waiting for transfers between devices: 3.75 us -> 2.95 us  [body(): held = lax.all_to_all(split, 'chan', 0, 0)[:, None]]
    pallas_call x1, Pallas kernels: 1.73 us -> 0.99 us  [body(): pl.pallas_call(split_kernel, out_shape=jax.ShapeDtypeStruct((pieces, 2 *...]
    ppermute x1, starting transfers between devices: 2.32 us -> 3.05 us  [body(): before = lax.ppermute(spectra, 'chan', [(i, i + 1) for i in range(ends)])]
    ppermute x6, waiting for transfers between devices: 7.58 us -> 6.87 us  [swap(): return lax.ppermute(x, 'chan', [(i, i ^ mask) for i in range(n_chan)])]
    unnamed x10 -> x12, local copies, waits for them, and re-layouts: 3.68 us -> 4.37 us
    ppermute x6, starting transfers between devices: 5 us -> 5.57 us  [swap(): return lax.ppermute(x, 'chan', [(i, i ^ mask) for i in range(n_chan)])]
  transfers between devices with their start and end apart: 9 -> 9, of which waited for: 5 -> 5; matrix products, arithmetic and copies ran while one was open for 2% -> 2% of each run, Pallas kernels for 15% -> 17%
where the time goes in v12:
time: 48.5 us; the launch traced here: 48 us
  starting transfers between devices  17.3 us (36%)
  Pallas kernels  15.7 us (32%)
  waiting for transfers between devices  9.82 us (20%)
  local copies, waits for them, and re-layouts  4.37 us (9%)
  other arithmetic  0.74 us (2%)
    pallas_call x2, Pallas kernels, cross(): pl.pallas_call(functools.partial(cross_kernel, masks=masks, added=len(ear...  9.28 us
    all_to_all x1, starting transfers between devices, body(): held = lax.all_to_all(split, 'chan', 0, 0)[:, None]  7.4 us
    ppermute x6, waiting for transfers between devices, swap(): return lax.ppermute(x, 'chan', [(i, i ^ mask) for i in range(n_chan)])  6.87 us
    ppermute x6, starting transfers between devices, swap(): return lax.ppermute(x, 'chan', [(i, i ^ mask) for i in range(n_chan)])  5.57 us
    unnamed x12, local copies, waits for them, and re-layouts  4.37 us
    ppermute x1, starting transfers between devices, body(): before = lax.ppermute(spectra, 'chan', [(i, i + 1) for i in range(ends)])  3.05 us
    pallas_call x1, Pallas kernels, body(): pl.pallas_call(own_kernel, out_shape=jax.ShapeDtypeStruct((2, tiles, win,...  3.05 us
    all_to_all x1, waiting for transfers between devices, body(): held = lax.all_to_all(split, 'chan', 0, 0)[:, None]  2.95 us
  transfers between devices with their start and end apart: 9, of which 5 were waited for; matrix products, arithmetic and copies ran while one was open for 2% of the time, Pallas kernels for 17%

profile of v12, /device:TPU:0, one launch (start us, length us, event | category | flops | bytes accessed | tf_op | source)
XLA Modules:
  0.0 48.0 jit_solution(16091727843771567468)
XLA Ops:
  0.0 0.0 copy-start
  0.0 0.9 %copy-done = bf16[2,4,32,512]{3,2,1,0:T(8,128)(2,1)S(1)} copy-done((bf16[2,4,32,512]{3,2,1,0:T(8,128)(2,1)S(1)}, bf16[2,4,32,512]{3,2,1,0:T(8,128)(2,1)}, u32[]{:S(2)}) %copy-start) | copy-done | bytes 262168
  1.0 0.0 copy-start.1
  1.0 0.7 %copy-done.1 = s32[4,32]{1,0:T(4,128)S(1)} copy-done((s32[4,32]{1,0:T(4,128)S(1)}, s32[4,32]{1,0:T(4,128)}, u32[]{:S(2)}) %copy-start.1) | copy-done | bytes 536
  1.6 1.0 %split.1.piece_ref = bf16[16,80,128]{2,1,0:T(8,128)(2,1)} custom-call(bf16[2,4,32,512]{3,2,1,0:T(8,128)(2,1)S(1)} %copy-done, s32[4,32]{1,0:T(4,128)S(1)} %copy-done.1), custom_call_target="tpu_custom_call" | custom-call | tf_op jit(solution)/shard_map/split/pallas_call | solution.py:305
  2.6 7.4 %all-to-all-start = ((bf16[16,80,128]{2,1,0:T(8,128)(2,1)}), bf16[16,80,128]{2,1,0:T(8,128)(2,1)S(1)}, u32[]{:S(2)}, u32[]{:S(2)}) async-start(bf16[16,80,128]{2,1,0:T(8,128)(2,1)} %split.1.piece_ref), calls=%async_computation | async-start | bytes 655360 | tf_op jit(solution)/shard_map/all_to_all | solution.py:319
  10.0 1.3 %collective-permute-start.4 = (bf16[2,4,32,512]{3,2,1,0:T(8,128)(2,1)}, bf16[2,4,32,512]{3,2,1,0:T(8,128)(2,1)S(1)}, u32[]{:S(2)}, u32[]{:S(2)}) collective-permute-start(bf16[2,4,32,512]{3,2,1,0:T(8,128)(2,1)} %whole_ref.1), channel_id=1, source_target_pairs={{1,0},{2,1},{3,2},{4,3},{5,4},{6,5},{7,6},{8,7},{9,8},{10,9},{11,1... | collective-permute-start | bytes 786440 | tf_op jit(solution)/shard_map/ppermute | solution.py:328
  11.3 3.1 %collective-permute-start.3 = (bf16[2,4,32,512]{3,2,1,0:T(8,128)(2,1)}, bf16[2,4,32,512]{3,2,1,0:T(8,128)(2,1)S(1)}, u32[]{:S(2)}, u32[]{:S(2)}) collective-permute-start(bf16[2,4,32,512]{3,2,1,0:T(8,128)(2,1)} %whole_ref.1), channel_id=1, source_target_pairs={{0,1},{1,2},{2,3},{3,4},{4,5},{5,6},{6,7},{7,8},{8,9},{9,10},{10,1... | collective-permute-start | bytes 786440 | tf_op jit(solution)/shard_map/ppermute | solution.py:327
  14.4 0.0 copy-start.2
  14.4 0.7 %copy-done.2 = s32[4,32]{1,0:T(4,128)S(1)} copy-done((s32[4,32]{1,0:T(4,128)S(1)}, s32[4,32]{1,0:T(4,128)}, u32[]{:S(2)}) %copy-start.2) | copy-done | bytes 536
  15.1 0.0 copy-start.3
  15.1 0.7 %copy-done.3 = f32[2,8,65]{2,1,0:T(8,128)S(1)} copy-done((f32[2,8,65]{2,1,0:T(8,128)S(1)}, f32[2,8,65]{2,1,0:T(8,128)}, u32[]{:S(2)}) %copy-start.3) | copy-done | bytes 4184
  15.8 0.0 copy-start.4
  15.8 0.7 %copy-done.4 = s32[512]{0:T(512)S(1)} copy-done((s32[512]{0:T(512)S(1)}, s32[512]{0:T(512)}, u32[]{:S(2)}) %copy-start.4) | copy-done | bytes 2072
  16.5 0.0 copy-start.5
  16.5 0.7 %copy-done.5 = s32[4,32]{1,0:T(4,128)S(1)} copy-done((s32[4,32]{1,0:T(4,128)S(1)}, s32[4,32]{1,0:T(4,128)}, u32[]{:S(2)}) %copy-start.5) | copy-done | bytes 536
  17.1 0.3 prep.1
  17.5 0.7 %pad_add_fusion.params_ref = s32[6]{0:T(128)S(1)} fusion(s32[4]{0:T(128)} %param.10, s32[1]{0:T(128)} %bitcast.1, s32[1]{0:T(128)} %bitcast), kind=kLoop, calls=%fused_computation | loop fusion | flops 12 | bytes 48 | tf_op jit(solution)/shard_map/concatenate | solution.py:324
  18.2 2.9 %all-to-all-done = bf16[16,80,128]{2,1,0:T(8,128)(2,1)S(1)} async-done(((bf16[16,80,128]{2,1,0:T(8,128)(2,1)}), bf16[16,80,128]{2,1,0:T(8,128)(2,1)S(1)}, u32[]{:S(2)}, u32[]{:S(2)}) %all-to-all-start) | async-done | bytes 327712 | tf_op jit(solution)/shard_map/all_to_all | solution.py:319
  21.1 1.0 %source_filter.1.refs_0_ = bf16[1,4,2,32,128]{4,3,2,1,0:T(8,128)(2,1)S(1)} custom-call(s32[6]{0:T(128)S(1)} %pad_add_fusion.params_ref, bf16[16,1,80,128]{3,2,1,0:T(8,128)(2,1)S(1)} %bitcast.4, bf16[1024,256]{1,0:T(8,128)(2,1)S(1)} %get-tuple-element.14.weight_ref, s32[4,1,128]{2,1,0:T(1,128)S(1)} %get-tuple-element.15.index_ref), custom_call_target="tpu_custom_call" | custom-call | tf_op jit(solution)/shard_map/source_filter/pallas_call | solution.py:354
  22.1 1.5 %collective-permute-start.2 = (bf16[1,4,2,32,128]{4,3,2,1,0:T(8,128)(2,1)S(1)}, bf16[1,4,2,32,128]{4,3,2,1,0:T(8,128)(2,1)S(1)}, u32[]{:S(2)}, u32[]{:S(2)}) collective-permute-start(bf16[1,4,2,32,128]{4,3,2,1,0:T(8,128)(2,1)S(1)} %source_filter.1.refs_0_), channel_id=1, source_target_pairs={{0,12},{1,13},{2,14},{3,15},{4,8},{5,9},{6,10},{7,11},{8,4},{9,5},... | collective-permute-start | bytes 196616 | tf_op jit(solution)/shard_map/ppermute | solution.py:287
  23.7 0.4 collective-permute-start.1
  24.1 2.5 %collective-permute-start = (bf16[1,4,2,32,128]{4,3,2,1,0:T(8,128)(2,1)S(1)}, bf16[1,4,2,32,128]{4,3,2,1,0:T(8,128)(2,1)S(1)}, u32[]{:S(2)}, u32[]{:S(2)}) collective-permute-start(bf16[1,4,2,32,128]{4,3,2,1,0:T(8,128)(2,1)S(1)} %source_filter.1.refs_0_), channel_id=1, source_target_pairs={{0,4},{1,5},{2,6},{3,7},{4,0},{5,1},{6,2},{7,3},{8,12},{9,13},{10,... | collective-permute-start | bytes 196616 | tf_op jit(solution)/shard_map/ppermute | solution.py:287
  26.6 0.0 collective-permute-done.4.next_ref
  26.6 0.0 collective-permute-done.3.prev_ref
  26.6 3.0 %own_whiten.1.refs_2_ = bf16[2,4,4,32,128]{4,3,2,1,0:T(8,128)(2,1)S(1)} custom-call(bf16[2,4,32,512]{3,2,1,0:T(8,128)(2,1)S(1)} %collective-permute-done.3.prev_ref, bf16[16,80,128]{2,1,0:T(8,128)(2,1)} %split.1.piece_ref, bf16[2,4,32,512]{3,2,1,0:T(8,128)(2,1)S(1)} %collective-permute-done.4.next_ref, bf16[1024,256]{1,0:T(8,128)(2,1)S(1)} %get-tuple-element.14.weight_ref, ...), custom_call_target="tpu_custom_call" | custom-call | flops 1073741824 | bytes 3145728 | tf_op jit(solution)/shard_map/own_whiten/pallas_call | solution.py:372
  29.6 0.0 collective-permute-done.2.refs_3_
  29.7 1.5 %collective-permute-done.1.refs_2_ = bf16[1,4,2,32,128]{4,3,2,1,0:T(8,128)(2,1)S(1)} collective-permute-done((bf16[1,4,2,32,128]{4,3,2,1,0:T(8,128)(2,1)S(1)}, bf16[1,4,2,32,128]{4,3,2,1,0:T(8,128)(2,1)S(1)}, u32[]{:S(2)}, u32[]{:S(2)}) %collective-permute-start.1) | collective-permute-done | bytes 65568 | tf_op jit(solution)/shard_map/ppermute | solution.py:287
  31.2 0.0 collective-permute-done.refs_1_
  31.2 1.1 %column_whiten.1.refs_0_ = bf16[1,4,4,2,32,128]{5,4,3,2,1,0:T(8,128)(2,1)S(1)} custom-call(s32[6]{0:T(128)S(1)} %pad_add_fusion.params_ref, bf16[1,4,2,32,128]{4,3,2,1,0:T(8,128)(2,1)S(1)} %source_filter.1.refs_0_, bf16[1,4,2,32,128]{4,3,2,1,0:T(8,128)(2,1)S(1)} %collective-permute-done.refs_1_, ...), custom_call_target="tpu_custom_call" | custom-call | tf_op jit(solution)/shard_map/column_whiten/pallas_call | solution.py:394
  32.3 0.1 collective-permute-start.6
  32.4 1.0 %collective-permute-start.5 = (bf16[1,4,4,2,32,128]{5,4,3,2,1,0:T(8,128)(2,1)S(1)}, bf16[1,4,4,2,32,128]{5,4,3,2,1,0:T(8,128)(2,1)S(1)}, u32[]{:S(2)}, u32[]{:S(2)}) collective-permute-start(bf16[1,4,4,2,32,128]{5,4,3,2,1,0:T(8,128)(2,1)S(1)} %column_whiten.1.refs_0_), channel_id=1, source_target_pairs={{0,2},{1,3},{2,0},{3,1},{4,6},{5,7},{6,4},{7,5},{8,10},{9,11},{10,... | collective-permute-start | bytes 786440 | tf_op jit(solution)/shard_map/ppermute | solution.py:287
  33.4 0.5 %collective-permute-done.6.refs_1_ = bf16[1,4,4,2,32,128]{5,4,3,2,1,0:T(8,128)(2,1)S(1)} collective-permute-done((bf16[1,4,4,2,32,128]{5,4,3,2,1,0:T(8,128)(2,1)S(1)}, bf16[1,4,4,2,32,128]{5,4,3,2,1,0:T(8,128)(2,1)S(1)}, u32[]{:S(2)}, u32[]{:S(2)}) %collective-permute-start.6) | collective-permute-done | bytes 262176 | tf_op jit(solution)/shard_map/ppermute | solution.py:287
  33.9 3.9 %cross.2.refs_3_ = bf16[2,128,4,32,128]{4,3,2,1,0:T(8,128)(2,1)S(1)} custom-call(s32[6]{0:T(128)S(1)} %pad_add_fusion.params_ref, bf16[1,4,4,2,32,128]{5,4,3,2,1,0:T(8,128)(2,1)S(1)} %column_whiten.1.refs_0_, bf16[1,4,4,2,32,128]{5,4,3,2,1,0:T(8,128)(2,1)S(1)} %collective-permute-done.6.refs_1_, bf16[2,4,4,32,128]{4,3,2,1,0:T(8,128)(2,1)S(1)} %own_whiten.1.refs_2_), custom_call_target="tpu_custom_call" | custom-call | flops 67108864 | bytes 16777216 | tf_op jit(solution)/shard_map/cross/pallas_call | solution.py:415
  37.7 3.3 %collective-permute-done.5.refs_0_ = bf16[1,4,4,2,32,128]{5,4,3,2,1,0:T(8,128)(2,1)S(1)} collective-permute-done((bf16[1,4,4,2,32,128]{5,4,3,2,1,0:T(8,128)(2,1)S(1)}, bf16[1,4,4,2,32,128]{5,4,3,2,1,0:T(8,128)(2,1)S(1)}, u32[]{:S(2)}, u32[]{:S(2)}) %collective-permute-start.5) | collective-permute-done | bytes 262176 | tf_op jit(solution)/shard_map/ppermute | solution.py:287
  41.1 0.0 collective-permute-start.7
  41.1 1.5 %collective-permute-done.7.refs_1_ = bf16[1,4,4,2,32,128]{5,4,3,2,1,0:T(8,128)(2,1)S(1)} collective-permute-done((bf16[1,4,4,2,32,128]{5,4,3,2,1,0:T(8,128)(2,1)S(1)}, bf16[1,4,4,2,32,128]{5,4,3,2,1,0:T(8,128)(2,1)S(1)}, u32[]{:S(2)}, u32[]{:S(2)}) %collective-permute-start.7) | collective-permute-done | bytes 262176 | tf_op jit(solution)/shard_map/ppermute | solution.py:287
  42.6 5.4 %cross.3 = bf16[2,128,32,512]{3,2,1,0:T(8,128)(2,1)} custom-call(s32[6]{0:T(128)S(1)} %pad_add_fusion.params_ref, bf16[1,4,4,2,32,128]{5,4,3,2,1,0:T(8,128)(2,1)S(1)} %collective-permute-done.5.refs_0_, bf16[1,4,4,2,32,128]{5,4,3,2,1,0:T(8,128)(2,1)S(1)} %collective-permute-done.7.refs_1_, bf16[2,4,4,32,128]{4,3,2,1,0:T(8,128)(2,1)S(1)} %own_whiten.1.refs_2_, ...), custom_call_target="tpu_custom_call" | custom-call | flops 67108864 | bytes 16777216 | tf_op jit(solution)/shard_map/cross/pallas_call | solution.py:415
Async XLA Ops:
  0.0 0.9 %copy-start = (bf16[2,4,32,512]{3,2,1,0:T(8,128)(2,1)S(1)}, bf16[2,4,32,512]{3,2,1,0:T(8,128)(2,1)}, u32[]{:S(2)}) copy-start(bf16[2,4,32,512]{3,2,1,0:T(8,128)(2,1)} %whole_ref.1) | copy-start | bytes 786436
  1.0 0.7 %copy-start.1 = (s32[4,32]{1,0:T(4,128)S(1)}, s32[4,32]{1,0:T(4,128)}, u32[]{:S(2)}) copy-start(s32[4,32]{1,0:T(4,128)} %refs_2_.1) | copy-start | bytes 1540
  2.6 18.5 %all-to-all-start = ((bf16[16,80,128]{2,1,0:T(8,128)(2,1)}), bf16[16,80,128]{2,1,0:T(8,128)(2,1)S(1)}, u32[]{:S(2)}, u32[]{:S(2)}) async-start(bf16[16,80,128]{2,1,0:T(8,128)(2,1)} %split.1.piece_ref), calls=%async_computation | async-start | bytes 655360 | tf_op jit(solution)/shard_map/all_to_all | solution.py:319
  10.0 16.6 %collective-permute-start.4 = (bf16[2,4,32,512]{3,2,1,0:T(8,128)(2,1)}, bf16[2,4,32,512]{3,2,1,0:T(8,128)(2,1)S(1)}, u32[]{:S(2)}, u32[]{:S(2)}) collective-permute-start(bf16[2,4,32,512]{3,2,1,0:T(8,128)(2,1)} %whole_ref.1), channel_id=1, source_target_pairs={{1,0},{2,1},{3,2},{4,3},{5,4},{6,5},{7,6},{8,7},{9,8},{10,9},{11,1... | collective-permute-start | bytes 786440 | tf_op jit(solution)/shard_map/ppermute | solution.py:328
  11.3 15.3 %collective-permute-start.3 = (bf16[2,4,32,512]{3,2,1,0:T(8,128)(2,1)}, bf16[2,4,32,512]{3,2,1,0:T(8,128)(2,1)S(1)}, u32[]{:S(2)}, u32[]{:S(2)}) collective-permute-start(bf16[2,4,32,512]{3,2,1,0:T(8,128)(2,1)} %whole_ref.1), channel_id=1, source_target_pairs={{0,1},{1,2},{2,3},{3,4},{4,5},{5,6},{6,7},{7,8},{8,9},{9,10},{10,1... | collective-permute-start | bytes 786440 | tf_op jit(solution)/shard_map/ppermute | solution.py:327
  14.4 0.7 %copy-start.2 = (s32[4,32]{1,0:T(4,128)S(1)}, s32[4,32]{1,0:T(4,128)}, u32[]{:S(2)}) copy-start(s32[4,32]{1,0:T(4,128)} %refs_2_.1) | copy-start | bytes 1540
  15.1 0.7 %copy-start.3 = (f32[2,8,65]{2,1,0:T(8,128)S(1)}, f32[2,8,65]{2,1,0:T(8,128)}, u32[]{:S(2)}) copy-start(f32[2,8,65]{2,1,0:T(8,128)} %refs_0_.1) | copy-start | bytes 12484
  15.8 0.7 %copy-start.4 = (s32[512]{0:T(512)S(1)}, s32[512]{0:T(512)}, u32[]{:S(2)}) copy-start(s32[512]{0:T(512)} %param.8) | copy-start | bytes 6148
  16.5 0.7 %copy-start.5 = (s32[4,32]{1,0:T(4,128)S(1)}, s32[4,32]{1,0:T(4,128)}, u32[]{:S(2)}) copy-start(s32[4,32]{1,0:T(4,128)} %refs_3_.1) | copy-start | bytes 1540
  22.1 7.5 %collective-permute-start.2 = (bf16[1,4,2,32,128]{4,3,2,1,0:T(8,128)(2,1)S(1)}, bf16[1,4,2,32,128]{4,3,2,1,0:T(8,128)(2,1)S(1)}, u32[]{:S(2)}, u32[]{:S(2)}) collective-permute-start(bf16[1,4,2,32,128]{4,3,2,1,0:T(8,128)(2,1)S(1)} %source_filter.1.refs_0_), channel_id=1, source_target_pairs={{0,12},{1,13},{2,14},{3,15},{4,8},{5,9},{6,10},{7,11},{8,4},{9,5},... | collective-permute-start | bytes 196616 | tf_op jit(solution)/shard_map/ppermute | solution.py:287
  23.7 7.5 %collective-permute-start.1 = (bf16[1,4,2,32,128]{4,3,2,1,0:T(8,128)(2,1)S(1)}, bf16[1,4,2,32,128]{4,3,2,1,0:T(8,128)(2,1)S(1)}, u32[]{:S(2)}, u32[]{:S(2)}) collective-permute-start(bf16[1,4,2,32,128]{4,3,2,1,0:T(8,128)(2,1)S(1)} %source_filter.1.refs_0_), channel_id=1, source_target_pairs={{0,8},{1,9},{2,10},{3,11},{4,12},{5,13},{6,14},{7,15},{8,0},{9,1},... | collective-permute-start | bytes 196616 | tf_op jit(solution)/shard_map/ppermute | solution.py:287
  24.1 7.1 %collective-permute-start = (bf16[1,4,2,32,128]{4,3,2,1,0:T(8,128)(2,1)S(1)}, bf16[1,4,2,32,128]{4,3,2,1,0:T(8,128)(2,1)S(1)}, u32[]{:S(2)}, u32[]{:S(2)}) collective-permute-start(bf16[1,4,2,32,128]{4,3,2,1,0:T(8,128)(2,1)S(1)} %source_filter.1.refs_0_), channel_id=1, source_target_pairs={{0,4},{1,5},{2,6},{3,7},{4,0},{5,1},{6,2},{7,3},{8,12},{9,13},{10,... | collective-permute-start | bytes 196616 | tf_op jit(solution)/shard_map/ppermute | solution.py:287
  32.3 1.6 %collective-permute-start.6 = (bf16[1,4,4,2,32,128]{5,4,3,2,1,0:T(8,128)(2,1)S(1)}, bf16[1,4,4,2,32,128]{5,4,3,2,1,0:T(8,128)(2,1)S(1)}, u32[]{:S(2)}, u32[]{:S(2)}) collective-permute-start(bf16[1,4,4,2,32,128]{5,4,3,2,1,0:T(8,128)(2,1)S(1)} %column_whiten.1.refs_0_), channel_id=1, source_target_pairs={{0,1},{1,0},{2,3},{3,2},{4,5},{5,4},{6,7},{7,6},{8,9},{9,8},{10,11... | collective-permute-start | bytes 786440 | tf_op jit(solution)/shard_map/ppermute | solution.py:287
  32.4 8.7 %collective-permute-start.5 = (bf16[1,4,4,2,32,128]{5,4,3,2,1,0:T(8,128)(2,1)S(1)}, bf16[1,4,4,2,32,128]{5,4,3,2,1,0:T(8,128)(2,1)S(1)}, u32[]{:S(2)}, u32[]{:S(2)}) collective-permute-start(bf16[1,4,4,2,32,128]{5,4,3,2,1,0:T(8,128)(2,1)S(1)} %column_whiten.1.refs_0_), channel_id=1, source_target_pairs={{0,2},{1,3},{2,0},{3,1},{4,6},{5,7},{6,4},{7,5},{8,10},{9,11},{10,... | collective-permute-start | bytes 786440 | tf_op jit(solution)/shard_map/ppermute | solution.py:287
  41.1 1.5 %collective-permute-start.7 = (bf16[1,4,4,2,32,128]{5,4,3,2,1,0:T(8,128)(2,1)S(1)}, bf16[1,4,4,2,32,128]{5,4,3,2,1,0:T(8,128)(2,1)S(1)}, u32[]{:S(2)}, u32[]{:S(2)}) collective-permute-start(bf16[1,4,4,2,32,128]{5,4,3,2,1,0:T(8,128)(2,1)S(1)} %collective-permute-done.5.refs_0_), channel_id=1, source_target_pairs={{0,1},{1,0},{2,3},{3,2},{4,5},{5,4},{6,7},{7,6},{8,9},{9,8},{10,11... | collective-permute-start | bytes 786440 | tf_op jit(solution)/shard_map/ppermute | solution.py:287

commit v13 on v11

--- a/solution.py
+++ b/solution.py
@@ -214,24 +214,26 @@
     here = lax.rem(params_ref[0], win)
     slot = lax.rem(step, SLOTS)
 
-    def copies(at_step):
+    def copies(at_step, ft):
         at_slot = lax.rem(at_step, SLOTS)
+        bins = pl.ds(pl.multiple_of(ft * LANES, LANES), LANES)
         return [
             pltpu.make_async_copy(
-                stage_ref.at[at_slot, p], out_ref.at[p, pl.ds(at_step * group, group)], sems.at[at_slot, p]
+                stage_ref.at[at_slot, p, ft],
+                out_ref.at[p, pl.ds(at_step * group, group), :, bins],
+                sems.at[at_slot, p, ft],
             )
             for p in range(2)
         ]
 
-    if final:
-
-        @pl.when(step >= SLOTS)
-        def _():
-            for copy in copies(step - SLOTS):
-                copy.wait()
-
     def one_tile(ft, _):
-        at = pl.ds(pl.multiple_of(ft * LANES, LANES), LANES)
+        if final:
+
+            @pl.when(step >= SLOTS)
+            def _():
+                for copy in copies(step - SLOTS, ft):
+                    copy.wait()
+
         mine = [(local_ref[0, ft, here ^ mask], local_ref[1, ft, here ^ mask]) for mask in masks]
         theirs = [(ref[0, ft, r, 0, rows, :], ref[0, ft, r, 1, rows, :]) for ref in column_refs]
         for j in range(group):
@@ -247,24 +249,26 @@
                 re = re + partial_ref[0, begin + j, ft]
                 im = im + partial_ref[1, begin + j, ft]
             if final:
-                stage_ref[slot, 0, j, :, at] = re
-                stage_ref[slot, 1, j, :, at] = im
+                stage_ref[slot, 0, ft, j] = re
+                stage_ref[slot, 1, ft, j] = im
             else:
                 out_ref[0, begin + j, ft] = re
                 out_ref[1, begin + j, ft] = im
+        if final:
+            for copy in copies(step, ft):
+                copy.start()
         return 0
 
     lax.fori_loop(0, tiles, one_tile, 0)
 
     if final:
-        for copy in copies(step):
-            copy.start()
 
         @pl.when(step == steps - 1)
         def _():
-            for back in range(SLOTS):
-                for copy in copies(step - back):
-                    copy.wait()
+            for back in reversed(range(SLOTS)):
+                for ft in range(tiles):
+                    for copy in copies(step - back, ft):
+                        copy.wait()
 
 
 def swap(x, mask, n_chan):
@@ -377,8 +381,8 @@
         if final:
             spec = pl.BlockSpec(memory_space=pl.ANY)
             result = jax.ShapeDtypeStruct((2, sources, ch, freq), jnp.bfloat16)
-            scratch.append(pltpu.VMEM((SLOTS, 2, group, ch, freq), jnp.bfloat16))
-            scratch.append(pltpu.SemaphoreType.DMA((SLOTS, 2)))
+            scratch.append(pltpu.VMEM((SLOTS, 2, tiles, group, ch, LANES), jnp.bfloat16))
+            scratch.append(pltpu.SemaphoreType.DMA((SLOTS, 2, tiles)))
         return pl.pallas_call(
             functools.partial(cross_kernel, masks=masks, added=len(earlier) > 0, final=final),
             grid=(sources // group,),

time: 47.7 us -> 48 us (level)
  no operation moved by 1% of the time
where the time goes in v13:
time: 48 us; the launch traced here: 47.6 us
  starting transfers between devices  16 us (33%)
  Pallas kernels  15.7 us (33%)
  waiting for transfers between devices  11.3 us (24%)
  local copies, waits for them, and re-layouts  3.68 us (8%)
  other arithmetic  0.74 us (2%)
    pallas_call x2, Pallas kernels, cross(): pl.pallas_call(functools.partial(cross_kernel, masks=masks, added=len(ear...  9.6 us
    ppermute x6, waiting for transfers between devices, swap(): return lax.ppermute(x, 'chan', [(i, i ^ mask) for i in range(n_chan)])  7.58 us
    all_to_all x1, starting transfers between devices, body(): held = lax.all_to_all(split, 'chan', 0, 0)[:, None]  7.39 us
    ppermute x6, starting transfers between devices, swap(): return lax.ppermute(x, 'chan', [(i, i ^ mask) for i in range(n_chan)])  5 us
    all_to_all x1, waiting for transfers between devices, body(): held = lax.all_to_all(split, 'chan', 0, 0)[:, None]  3.75 us
    unnamed x10, local copies, waits for them, and re-layouts  3.68 us
    ppermute x1, starting transfers between devices, body(): before = lax.ppermute(spectra, 'chan', [(i, i + 1) for i in range(ends)])  2.32 us
    pallas_call x1, Pallas kernels, body(): pl.pallas_call(own_kernel, out_shape=jax.ShapeDtypeStruct((2, tiles, win,...  2.07 us
  transfers between devices with their start and end apart: 9, of which 5 were waited for; matrix products, arithmetic and copies ran while one was open for 2% of the time, Pallas kernels for 15%

profile of v13, /device:TPU:0, one launch (start us, length us, event | category | flops | bytes accessed | tf_op | source)
XLA Modules:
  0.0 47.6 jit_solution(9121953586442390427)
XLA Ops:
  0.0 1.7 %split.1 = bf16[16,80,128]{2,1,0:T(8,128)(2,1)} custom-call(bf16[2,4,32,512]{3,2,1,0:T(8,128)(2,1)} %cur_ref.1, s32[4,32]{1,0:T(4,128)} %flags_ref.3), custom_call_target="tpu_custom_call" | custom-call | tf_op jit(solution)/shard_map/split/pallas_call | solution.py:292
  1.7 7.4 %all-to-all-start = ((bf16[16,80,128]{2,1,0:T(8,128)(2,1)}), bf16[16,80,128]{2,1,0:T(8,128)(2,1)S(1)}, u32[]{:S(2)}, u32[]{:S(2)}) async-start(bf16[16,80,128]{2,1,0:T(8,128)(2,1)} %split.1), calls=%async_computation | async-start | bytes 655360 | tf_op jit(solution)/shard_map/all_to_all | solution.py:299
  9.1 2.3 %collective-permute-start.3 = (bf16[2,4,32,512]{3,2,1,0:T(8,128)(2,1)}, bf16[2,4,32,512]{3,2,1,0:T(8,128)(2,1)S(1)}, u32[]{:S(2)}, u32[]{:S(2)}) collective-permute-start(bf16[2,4,32,512]{3,2,1,0:T(8,128)(2,1)} %cur_ref.1), channel_id=1, source_target_pairs={{0,1},{1,2},{2,3},{3,4},{4,5},{5,6},{6,7},{7,8},{8,9},{9,10},{10,1... | collective-permute-start | bytes 786440 | tf_op jit(solution)/shard_map/ppermute | solution.py:307
  11.5 1.3 %collective-permute-start.4 = (bf16[2,4,32,512]{3,2,1,0:T(8,128)(2,1)}, bf16[2,4,32,512]{3,2,1,0:T(8,128)(2,1)S(1)}, u32[]{:S(2)}, u32[]{:S(2)}) collective-permute-start(bf16[2,4,32,512]{3,2,1,0:T(8,128)(2,1)} %cur_ref.1), channel_id=1, source_target_pairs={{1,0},{2,1},{3,2},{4,3},{5,4},{6,5},{7,6},{8,7},{9,8},{10,9},{11,1... | collective-permute-start | bytes 786440 | tf_op jit(solution)/shard_map/ppermute | solution.py:308
  12.8 0.0 copy-start.1
  12.8 0.7 %copy-done.1 = s32[4,32]{1,0:T(4,128)S(1)} copy-done((s32[4,32]{1,0:T(4,128)S(1)}, s32[4,32]{1,0:T(4,128)}, u32[]{:S(2)}) %copy-start.1) | copy-done | bytes 536
  13.4 0.0 copy-start.2
  13.4 0.7 %copy-done.2 = f32[2,8,65]{2,1,0:T(8,128)S(1)} copy-done((f32[2,8,65]{2,1,0:T(8,128)S(1)}, f32[2,8,65]{2,1,0:T(8,128)}, u32[]{:S(2)}) %copy-start.2) | copy-done | bytes 4184
  14.1 0.0 copy-start.3
  14.1 0.7 %copy-done.3 = s32[512]{0:T(512)S(1)} copy-done((s32[512]{0:T(512)S(1)}, s32[512]{0:T(512)}, u32[]{:S(2)}) %copy-start.3) | copy-done | bytes 2072
  14.8 0.0 copy-start.4
  14.8 0.7 %copy-done.4 = s32[4,32]{1,0:T(4,128)S(1)} copy-done((s32[4,32]{1,0:T(4,128)S(1)}, s32[4,32]{1,0:T(4,128)}, u32[]{:S(2)}) %copy-start.4) | copy-done | bytes 536
  15.5 0.2 prep.1
  15.8 0.7 %pad_add_fusion.params_ref = s32[6]{0:T(128)S(1)} fusion(s32[4]{0:T(128)} %param.10, s32[1]{0:T(128)} %bitcast.1, s32[1]{0:T(128)} %bitcast), kind=kLoop, calls=%fused_computation | loop fusion | flops 12 | bytes 48 | tf_op jit(solution)/shard_map/concatenate | solution.py:304
  16.5 3.8 %all-to-all-done = bf16[16,80,128]{2,1,0:T(8,128)(2,1)S(1)} async-done(((bf16[16,80,128]{2,1,0:T(8,128)(2,1)}), bf16[16,80,128]{2,1,0:T(8,128)(2,1)S(1)}, u32[]{:S(2)}, u32[]{:S(2)}) %all-to-all-start) | async-done | bytes 327712 | tf_op jit(solution)/shard_map/all_to_all | solution.py:299
  20.3 1.0 %source_filter.1.refs_0_ = bf16[1,4,2,32,128]{4,3,2,1,0:T(8,128)(2,1)S(1)} custom-call(s32[6]{0:T(128)S(1)} %pad_add_fusion.params_ref, bf16[16,1,80,128]{3,2,1,0:T(8,128)(2,1)S(1)} %bitcast.4, bf16[1024,256]{1,0:T(8,128)(2,1)S(1)} %get-tuple-element.14.weight_ref, s32[4,1,128]{2,1,0:T(1,128)S(1)} %get-tuple-element.15.index_ref), custom_call_target="tpu_custom_call" | custom-call | tf_op jit(solution)/shard_map/source_filter/pallas_call | solution.py:325
  21.2 2.9 %collective-permute-start.2 = (bf16[1,4,2,32,128]{4,3,2,1,0:T(8,128)(2,1)S(1)}, bf16[1,4,2,32,128]{4,3,2,1,0:T(8,128)(2,1)S(1)}, u32[]{:S(2)}, u32[]{:S(2)}) collective-permute-start(bf16[1,4,2,32,128]{4,3,2,1,0:T(8,128)(2,1)S(1)} %source_filter.1.refs_0_), channel_id=1, source_target_pairs={{0,12},{1,13},{2,14},{3,15},{4,8},{5,9},{6,10},{7,11},{8,4},{9,5},... | collective-permute-start | bytes 196616 | tf_op jit(solution)/shard_map/ppermute | solution.py:275
  24.1 0.0 collective-permute-start.1
  24.1 1.6 %collective-permute-start = (bf16[1,4,2,32,128]{4,3,2,1,0:T(8,128)(2,1)S(1)}, bf16[1,4,2,32,128]{4,3,2,1,0:T(8,128)(2,1)S(1)}, u32[]{:S(2)}, u32[]{:S(2)}) collective-permute-start(bf16[1,4,2,32,128]{4,3,2,1,0:T(8,128)(2,1)S(1)} %source_filter.1.refs_0_), channel_id=1, source_target_pairs={{0,4},{1,5},{2,6},{3,7},{4,0},{5,1},{6,2},{7,3},{8,12},{9,13},{10,... | collective-permute-start | bytes 196616 | tf_op jit(solution)/shard_map/ppermute | solution.py:275
  25.7 0.0 collective-permute-done.3.prev_ref
  25.7 0.0 collective-permute-done.4.next_ref
  25.7 0.0 copy-start
  25.7 0.9 %copy-done = bf16[2,4,32,512]{3,2,1,0:T(8,128)(2,1)S(1)} copy-done((bf16[2,4,32,512]{3,2,1,0:T(8,128)(2,1)S(1)}, bf16[2,4,32,512]{3,2,1,0:T(8,128)(2,1)}, u32[]{:S(2)}) %copy-start) | copy-done | bytes 262168
  26.7 2.1 %own_whiten.1.refs_2_ = bf16[2,4,4,32,128]{4,3,2,1,0:T(8,128)(2,1)S(1)} custom-call(bf16[2,4,32,512]{3,2,1,0:T(8,128)(2,1)S(1)} %collective-permute-done.3.prev_ref, bf16[2,4,32,512]{3,2,1,0:T(8,128)(2,1)S(1)} %copy-done, bf16[2,4,32,512]{3,2,1,0:T(8,128)(2,1)S(1)} %collective-permute-done.4.next_ref, bf16[1024,256]{1,0:T(8,128)(2,1)S(1)} %get-tuple-element.14.weight_ref, ...), custom_call_target="tpu_custom_call" | custom-call | flops 1073741824 | bytes 3145728 | tf_op jit(solution)/shard_map/own_whiten/pallas_call | solution.py:343
  28.7 0.0 collective-permute-done.2.refs_3_
  28.7 1.7 %collective-permute-done.1.refs_2_ = bf16[1,4,2,32,128]{4,3,2,1,0:T(8,128)(2,1)S(1)} collective-permute-done((bf16[1,4,2,32,128]{4,3,2,1,0:T(8,128)(2,1)S(1)}, bf16[1,4,2,32,128]{4,3,2,1,0:T(8,128)(2,1)S(1)}, u32[]{:S(2)}, u32[]{:S(2)}) %collective-permute-start.1) | collective-permute-done | bytes 65568 | tf_op jit(solution)/shard_map/ppermute | solution.py:275
  30.4 0.0 collective-permute-done.refs_1_
  30.4 1.1 %column_whiten.1.refs_0_ = bf16[1,4,4,2,32,128]{5,4,3,2,1,0:T(8,128)(2,1)S(1)} custom-call(s32[6]{0:T(128)S(1)} %pad_add_fusion.params_ref, bf16[1,4,2,32,128]{4,3,2,1,0:T(8,128)(2,1)S(1)} %source_filter.1.refs_0_, bf16[1,4,2,32,128]{4,3,2,1,0:T(8,128)(2,1)S(1)} %collective-permute-done.refs_1_, ...), custom_call_target="tpu_custom_call" | custom-call | tf_op jit(solution)/shard_map/column_whiten/pallas_call | solution.py:365
  31.5 0.1 collective-permute-start.6
  31.6 0.5 collective-permute-start.5
  32.1 1.1 %collective-permute-done.6.refs_1_ = bf16[1,4,4,2,32,128]{5,4,3,2,1,0:T(8,128)(2,1)S(1)} collective-permute-done((bf16[1,4,4,2,32,128]{5,4,3,2,1,0:T(8,128)(2,1)S(1)}, bf16[1,4,4,2,32,128]{5,4,3,2,1,0:T(8,128)(2,1)S(1)}, u32[]{:S(2)}, u32[]{:S(2)}) %collective-permute-start.6) | collective-permute-done | bytes 262176 | tf_op jit(solution)/shard_map/ppermute | solution.py:275
  33.1 3.9 %cross.2.refs_3_ = bf16[2,128,4,32,128]{4,3,2,1,0:T(8,128)(2,1)S(1)} custom-call(s32[6]{0:T(128)S(1)} %pad_add_fusion.params_ref, bf16[1,4,4,2,32,128]{5,4,3,2,1,0:T(8,128)(2,1)S(1)} %column_whiten.1.refs_0_, bf16[1,4,4,2,32,128]{5,4,3,2,1,0:T(8,128)(2,1)S(1)} %collective-permute-done.6.refs_1_, bf16[2,4,4,32,128]{4,3,2,1,0:T(8,128)(2,1)S(1)} %own_whiten.1.refs_2_), custom_call_target="tpu_custom_call" | custom-call | flops 67108864 | bytes 16777216 | tf_op jit(solution)/shard_map/cross/pallas_call | solution.py:386
  37.0 3.3 %collective-permute-done.5.refs_0_ = bf16[1,4,4,2,32,128]{5,4,3,2,1,0:T(8,128)(2,1)S(1)} collective-permute-done((bf16[1,4,4,2,32,128]{5,4,3,2,1,0:T(8,128)(2,1)S(1)}, bf16[1,4,4,2,32,128]{5,4,3,2,1,0:T(8,128)(2,1)S(1)}, u32[]{:S(2)}, u32[]{:S(2)}) %collective-permute-start.5) | collective-permute-done | bytes 262176 | tf_op jit(solution)/shard_map/ppermute | solution.py:275
  40.3 0.0 collective-permute-start.7
  40.3 1.5 %collective-permute-done.7.refs_1_ = bf16[1,4,4,2,32,128]{5,4,3,2,1,0:T(8,128)(2,1)S(1)} collective-permute-done((bf16[1,4,4,2,32,128]{5,4,3,2,1,0:T(8,128)(2,1)S(1)}, bf16[1,4,4,2,32,128]{5,4,3,2,1,0:T(8,128)(2,1)S(1)}, u32[]{:S(2)}, u32[]{:S(2)}) %collective-permute-start.7) | collective-permute-done | bytes 262176 | tf_op jit(solution)/shard_map/ppermute | solution.py:275
  41.9 5.7 %cross.3 = bf16[2,128,32,512]{3,2,1,0:T(8,128)(2,1)} custom-call(s32[6]{0:T(128)S(1)} %pad_add_fusion.params_ref, bf16[1,4,4,2,32,128]{5,4,3,2,1,0:T(8,128)(2,1)S(1)} %collective-permute-done.5.refs_0_, bf16[1,4,4,2,32,128]{5,4,3,2,1,0:T(8,128)(2,1)S(1)} %collective-permute-done.7.refs_1_, bf16[2,4,4,32,128]{4,3,2,1,0:T(8,128)(2,1)S(1)} %own_whiten.1.refs_2_, ...), custom_call_target="tpu_custom_call" | custom-call | flops 67108864 | bytes 16777216 | tf_op jit(solution)/shard_map/cross/pallas_call | solution.py:386
Async XLA Ops:
  1.7 18.5 %all-to-all-start = ((bf16[16,80,128]{2,1,0:T(8,128)(2,1)}), bf16[16,80,128]{2,1,0:T(8,128)(2,1)S(1)}, u32[]{:S(2)}, u32[]{:S(2)}) async-start(bf16[16,80,128]{2,1,0:T(8,128)(2,1)} %split.1), calls=%async_computation | async-start | bytes 655360 | tf_op jit(solution)/shard_map/all_to_all | solution.py:299
  9.1 16.6 %collective-permute-start.3 = (bf16[2,4,32,512]{3,2,1,0:T(8,128)(2,1)}, bf16[2,4,32,512]{3,2,1,0:T(8,128)(2,1)S(1)}, u32[]{:S(2)}, u32[]{:S(2)}) collective-permute-start(bf16[2,4,32,512]{3,2,1,0:T(8,128)(2,1)} %cur_ref.1), channel_id=1, source_target_pairs={{0,1},{1,2},{2,3},{3,4},{4,5},{5,6},{6,7},{7,8},{8,9},{9,10},{10,1... | collective-permute-start | bytes 786440 | tf_op jit(solution)/shard_map/ppermute | solution.py:307
  11.5 14.3 %collective-permute-start.4 = (bf16[2,4,32,512]{3,2,1,0:T(8,128)(2,1)}, bf16[2,4,32,512]{3,2,1,0:T(8,128)(2,1)S(1)}, u32[]{:S(2)}, u32[]{:S(2)}) collective-permute-start(bf16[2,4,32,512]{3,2,1,0:T(8,128)(2,1)} %cur_ref.1), channel_id=1, source_target_pairs={{1,0},{2,1},{3,2},{4,3},{5,4},{6,5},{7,6},{8,7},{9,8},{10,9},{11,1... | collective-permute-start | bytes 786440 | tf_op jit(solution)/shard_map/ppermute | solution.py:308
  12.8 0.7 %copy-start.1 = (s32[4,32]{1,0:T(4,128)S(1)}, s32[4,32]{1,0:T(4,128)}, u32[]{:S(2)}) copy-start(s32[4,32]{1,0:T(4,128)} %flags_ref.3) | copy-start | bytes 1540
  13.4 0.7 %copy-start.2 = (f32[2,8,65]{2,1,0:T(8,128)S(1)}, f32[2,8,65]{2,1,0:T(8,128)}, u32[]{:S(2)}) copy-start(f32[2,8,65]{2,1,0:T(8,128)} %bank_ref.1) | copy-start | bytes 12484
  14.1 0.7 %copy-start.3 = (s32[512]{0:T(512)S(1)}, s32[512]{0:T(512)}, u32[]{:S(2)}) copy-start(s32[512]{0:T(512)} %param.8) | copy-start | bytes 6148
  14.8 0.7 %copy-start.4 = (s32[4,32]{1,0:T(4,128)S(1)}, s32[4,32]{1,0:T(4,128)}, u32[]{:S(2)}) copy-start(s32[4,32]{1,0:T(4,128)} %offset_ref.1) | copy-start | bytes 1540
  21.2 7.5 %collective-permute-start.2 = (bf16[1,4,2,32,128]{4,3,2,1,0:T(8,128)(2,1)S(1)}, bf16[1,4,2,32,128]{4,3,2,1,0:T(8,128)(2,1)S(1)}, u32[]{:S(2)}, u32[]{:S(2)}) collective-permute-start(bf16[1,4,2,32,128]{4,3,2,1,0:T(8,128)(2,1)S(1)} %source_filter.1.refs_0_), channel_id=1, source_target_pairs={{0,12},{1,13},{2,14},{3,15},{4,8},{5,9},{6,10},{7,11},{8,4},{9,5},... | collective-permute-start | bytes 196616 | tf_op jit(solution)/shard_map/ppermute | solution.py:275
  24.1 6.3 %collective-permute-start.1 = (bf16[1,4,2,32,128]{4,3,2,1,0:T(8,128)(2,1)S(1)}, bf16[1,4,2,32,128]{4,3,2,1,0:T(8,128)(2,1)S(1)}, u32[]{:S(2)}, u32[]{:S(2)}) collective-permute-start(bf16[1,4,2,32,128]{4,3,2,1,0:T(8,128)(2,1)S(1)} %source_filter.1.refs_0_), channel_id=1, source_target_pairs={{0,8},{1,9},{2,10},{3,11},{4,12},{5,13},{6,14},{7,15},{8,0},{9,1},... | collective-permute-start | bytes 196616 | tf_op jit(solution)/shard_map/ppermute | solution.py:275
  24.1 6.3 %collective-permute-start = (bf16[1,4,2,32,128]{4,3,2,1,0:T(8,128)(2,1)S(1)}, bf16[1,4,2,32,128]{4,3,2,1,0:T(8,128)(2,1)S(1)}, u32[]{:S(2)}, u32[]{:S(2)}) collective-permute-start(bf16[1,4,2,32,128]{4,3,2,1,0:T(8,128)(2,1)S(1)} %source_filter.1.refs_0_), channel_id=1, source_target_pairs={{0,4},{1,5},{2,6},{3,7},{4,0},{5,1},{6,2},{7,3},{8,12},{9,13},{10,... | collective-permute-start | bytes 196616 | tf_op jit(solution)/shard_map/ppermute | solution.py:275
  25.7 1.0 %copy-start = (bf16[2,4,32,512]{3,2,1,0:T(8,128)(2,1)S(1)}, bf16[2,4,32,512]{3,2,1,0:T(8,128)(2,1)}, u32[]{:S(2)}) copy-start(bf16[2,4,32,512]{3,2,1,0:T(8,128)(2,1)} %cur_ref.1) | copy-start | bytes 786436
  31.5 1.6 %collective-permute-start.6 = (bf16[1,4,4,2,32,128]{5,4,3,2,1,0:T(8,128)(2,1)S(1)}, bf16[1,4,4,2,32,128]{5,4,3,2,1,0:T(8,128)(2,1)S(1)}, u32[]{:S(2)}, u32[]{:S(2)}) collective-permute-start(bf16[1,4,4,2,32,128]{5,4,3,2,1,0:T(8,128)(2,1)S(1)} %column_whiten.1.refs_0_), channel_id=1, source_target_pairs={{0,1},{1,0},{2,3},{3,2},{4,5},{5,4},{6,7},{7,6},{8,9},{9,8},{10,11... | collective-permute-start | bytes 786440 | tf_op jit(solution)/shard_map/ppermute | solution.py:275
  31.6 8.7 %collective-permute-start.5 = (bf16[1,4,4,2,32,128]{5,4,3,2,1,0:T(8,128)(2,1)S(1)}, bf16[1,4,4,2,32,128]{5,4,3,2,1,0:T(8,128)(2,1)S(1)}, u32[]{:S(2)}, u32[]{:S(2)}) collective-permute-start(bf16[1,4,4,2,32,128]{5,4,3,2,1,0:T(8,128)(2,1)S(1)} %column_whiten.1.refs_0_), channel_id=1, source_target_pairs={{0,2},{1,3},{2,0},{3,1},{4,6},{5,7},{6,4},{7,5},{8,10},{9,11},{10,... | collective-permute-start | bytes 786440 | tf_op jit(solution)/shard_map/ppermute | solution.py:275
  40.3 1.5 %collective-permute-start.7 = (bf16[1,4,4,2,32,128]{5,4,3,2,1,0:T(8,128)(2,1)S(1)}, bf16[1,4,4,2,32,128]{5,4,3,2,1,0:T(8,128)(2,1)S(1)}, u32[]{:S(2)}, u32[]{:S(2)}) collective-permute-start(bf16[1,4,4,2,32,128]{5,4,3,2,1,0:T(8,128)(2,1)S(1)} %collective-permute-done.5.refs_0_), channel_id=1, source_target_pairs={{0,1},{1,0},{2,3},{3,2},{4,5},{5,4},{6,7},{7,6},{8,9},{9,8},{10,11... | collective-permute-start | bytes 786440 | tf_op jit(solution)/shard_map/ppermute | solution.py:275

commit v14 on v11

--- a/solution.py
+++ b/solution.py
@@ -18,11 +18,17 @@
     return pltpu.CompilerParams(vmem_limit_bytes=mib * 1024 * 1024)
 
 
-def split_kernel(spectra_ref, flags_ref, piece_ref):
-    _, win, ch, freq = spectra_ref.shape
+def split_kernel(whole_ref, flags_ref, piece_ref, spectra_ref, sems):
+    _, win, ch, freq = whole_ref.shape
     tiles = freq // LANES
     extra = piece_ref.shape[1] - 2 * ch
+    copies = [
+        pltpu.make_async_copy(whole_ref.at[:, w], spectra_ref.at[:, w], sems.at[w]) for w in range(win)
+    ]
+    for copy in copies:
+        copy.start()
     for w in range(win):
+        copies[w].wait()
         flags = jnp.broadcast_to(flags_ref[w : w + 1, :], (extra, ch)).astype(jnp.float32)
         for t in range(tiles):
             at = slice(t * LANES, (t + 1) * LANES)
@@ -214,11 +220,15 @@
     here = lax.rem(params_ref[0], win)
     slot = lax.rem(step, SLOTS)
 
-    def copies(at_step):
+    half = group // 2
+
+    def copies(at_step, h):
         at_slot = lax.rem(at_step, SLOTS)
         return [
             pltpu.make_async_copy(
-                stage_ref.at[at_slot, p], out_ref.at[p, pl.ds(at_step * group, group)], sems.at[at_slot, p]
+                stage_ref.at[at_slot, p, pl.ds(h * half, half)],
+                out_ref.at[p, pl.ds(at_step * group + h * half, half)],
+                sems.at[at_slot, p, h],
             )
             for p in range(2)
         ]
@@ -227,14 +237,14 @@
 
         @pl.when(step >= SLOTS)
         def _():
-            for copy in copies(step - SLOTS):
+            for copy in copies(step - SLOTS, 0) + copies(step - SLOTS, 1):
                 copy.wait()
 
-    def one_tile(ft, _):
+    def one_tile(h, ft, _):
         at = pl.ds(pl.multiple_of(ft * LANES, LANES), LANES)
         mine = [(local_ref[0, ft, here ^ mask], local_ref[1, ft, here ^ mask]) for mask in masks]
         theirs = [(ref[0, ft, r, 0, rows, :], ref[0, ft, r, 1, rows, :]) for ref in column_refs]
-        for j in range(group):
+        for j in range(h * half, (h + 1) * half):
             re = []
             im = []
             for (lr, li), block in zip(mine, theirs):
@@ -254,16 +264,18 @@
                 out_ref[1, begin + j, ft] = im
         return 0
 
-    lax.fori_loop(0, tiles, one_tile, 0)
+    for h in range(2):
+        lax.fori_loop(0, tiles, functools.partial(one_tile, h), 0)
+        if final:
+            for copy in copies(step, h):
+                copy.start()
 
     if final:
-        for copy in copies(step):
-            copy.start()
 
         @pl.when(step == steps - 1)
         def _():
-            for back in range(SLOTS):
-                for copy in copies(step - back):
+            for back in reversed(range(SLOTS)):
+                for copy in copies(step - back, 0) + copies(step - back, 1):
                     copy.wait()
 
 
@@ -288,6 +300,9 @@
     split = pl.pallas_call(
         split_kernel,
         out_shape=jax.ShapeDtypeStruct((pieces, 2 * ch + 16, LANES), jnp.bfloat16),
+        in_specs=[pl.BlockSpec(memory_space=pl.ANY), vmem],
+        out_specs=vmem,
+        scratch_shapes=[pltpu.VMEM(spectra.shape, jnp.bfloat16), pltpu.SemaphoreType.DMA((win,))],
         compiler_params=room(56),
         name="split",
     )(spectra, window_mask)
@@ -378,7 +393,7 @@
             spec = pl.BlockSpec(memory_space=pl.ANY)
             result = jax.ShapeDtypeStruct((2, sources, ch, freq), jnp.bfloat16)
             scratch.append(pltpu.VMEM((SLOTS, 2, group, ch, freq), jnp.bfloat16))
-            scratch.append(pltpu.SemaphoreType.DMA((SLOTS, 2)))
+            scratch.append(pltpu.SemaphoreType.DMA((SLOTS, 2, 2)))
         return pl.pallas_call(
             functools.partial(cross_kernel, masks=masks, added=len(earlier) > 0, final=final),
             grid=(sources // group,),

time: 47.7 us -> 48.7 us (1.021)
  Pallas kernels: 15.4 us -> 16.6 us
    pallas_call x1, Pallas kernels: 1.73 us -> 2.39 us  [body(): pl.pallas_call(split_kernel, out_shape=jax.ShapeDtypeStruct((pieces, 2 *...]
    pallas_call x2, Pallas kernels: 9.28 us -> 9.81 us  [cross(): pl.pallas_call(functools.partial(cross_kernel, masks=masks, added=len(ear...]
where the time goes in v14:
time: 48.7 us; the launch traced here: 48.2 us
  Pallas kernels  16.6 us (34%)
  starting transfers between devices  16 us (33%)
  waiting for transfers between devices  11.1 us (23%)
  local copies, waits for them, and re-layouts  3.68 us (8%)
  other arithmetic  0.74 us (2%)
    pallas_call x2, Pallas kernels, cross(): pl.pallas_call(functools.partial(cross_kernel, masks=masks, added=len(ear...  9.81 us
    all_to_all x1, starting transfers between devices, body(): held = lax.all_to_all(split, 'chan', 0, 0)[:, None]  7.4 us
    ppermute x6, waiting for transfers between devices, swap(): return lax.ppermute(x, 'chan', [(i, i ^ mask) for i in range(n_chan)])  7.33 us
    ppermute x6, starting transfers between devices, swap(): return lax.ppermute(x, 'chan', [(i, i ^ mask) for i in range(n_chan)])  5 us
    all_to_all x1, waiting for transfers between devices, body(): held = lax.all_to_all(split, 'chan', 0, 0)[:, None]  3.75 us
    unnamed x10, local copies, waits for them, and re-layouts  3.68 us
    pallas_call x1, Pallas kernels, body(): pl.pallas_call(split_kernel, out_shape=jax.ShapeDtypeStruct((pieces, 2 *...  2.39 us
    ppermute x1, starting transfers between devices, body(): before = lax.ppermute(spectra, 'chan', [(i, i + 1) for i in range(ends)])  2.32 us
  transfers between devices with their start and end apart: 9, of which 5 were waited for; matrix products, arithmetic and copies ran while one was open for 2% of the time, Pallas kernels for 15%

profile of v14, /device:TPU:0, one launch (start us, length us, event | category | flops | bytes accessed | tf_op | source)
XLA Modules:
  0.0 48.2 jit_solution(15812159505700574360)
XLA Ops:
  0.0 2.4 %split.1 = bf16[16,80,128]{2,1,0:T(8,128)(2,1)} custom-call(bf16[2,4,32,512]{3,2,1,0:T(8,128)(2,1)} %cur_ref.1, s32[4,32]{1,0:T(4,128)} %flags_ref.3), custom_call_target="tpu_custom_call" | custom-call | tf_op jit(solution)/shard_map/split/pallas_call | solution.py:300
  2.4 7.4 %all-to-all-start = ((bf16[16,80,128]{2,1,0:T(8,128)(2,1)}), bf16[16,80,128]{2,1,0:T(8,128)(2,1)S(1)}, u32[]{:S(2)}, u32[]{:S(2)}) async-start(bf16[16,80,128]{2,1,0:T(8,128)(2,1)} %split.1), calls=%async_computation | async-start | bytes 655360 | tf_op jit(solution)/shard_map/all_to_all | solution.py:310
  9.8 2.3 %collective-permute-start.3 = (bf16[2,4,32,512]{3,2,1,0:T(8,128)(2,1)}, bf16[2,4,32,512]{3,2,1,0:T(8,128)(2,1)S(1)}, u32[]{:S(2)}, u32[]{:S(2)}) collective-permute-start(bf16[2,4,32,512]{3,2,1,0:T(8,128)(2,1)} %cur_ref.1), channel_id=1, source_target_pairs={{0,1},{1,2},{2,3},{3,4},{4,5},{5,6},{6,7},{7,8},{8,9},{9,10},{10,1... | collective-permute-start | bytes 786440 | tf_op jit(solution)/shard_map/ppermute | solution.py:318
  12.1 1.3 %collective-permute-start.4 = (bf16[2,4,32,512]{3,2,1,0:T(8,128)(2,1)}, bf16[2,4,32,512]{3,2,1,0:T(8,128)(2,1)S(1)}, u32[]{:S(2)}, u32[]{:S(2)}) collective-permute-start(bf16[2,4,32,512]{3,2,1,0:T(8,128)(2,1)} %cur_ref.1), channel_id=1, source_target_pairs={{1,0},{2,1},{3,2},{4,3},{5,4},{6,5},{7,6},{8,7},{9,8},{10,9},{11,1... | collective-permute-start | bytes 786440 | tf_op jit(solution)/shard_map/ppermute | solution.py:319
  13.4 0.0 copy-start.1
  13.4 0.7 %copy-done.1 = s32[4,32]{1,0:T(4,128)S(1)} copy-done((s32[4,32]{1,0:T(4,128)S(1)}, s32[4,32]{1,0:T(4,128)}, u32[]{:S(2)}) %copy-start.1) | copy-done | bytes 536
  14.1 0.0 copy-start.2
  14.1 0.7 %copy-done.2 = f32[2,8,65]{2,1,0:T(8,128)S(1)} copy-done((f32[2,8,65]{2,1,0:T(8,128)S(1)}, f32[2,8,65]{2,1,0:T(8,128)}, u32[]{:S(2)}) %copy-start.2) | copy-done | bytes 4184
  14.8 0.0 copy-start.3
  14.8 0.7 %copy-done.3 = s32[512]{0:T(512)S(1)} copy-done((s32[512]{0:T(512)S(1)}, s32[512]{0:T(512)}, u32[]{:S(2)}) %copy-start.3) | copy-done | bytes 2072
  15.5 0.0 copy-start.4
  15.5 0.7 %copy-done.4 = s32[4,32]{1,0:T(4,128)S(1)} copy-done((s32[4,32]{1,0:T(4,128)S(1)}, s32[4,32]{1,0:T(4,128)}, u32[]{:S(2)}) %copy-start.4) | copy-done | bytes 536
  16.2 0.2 prep.1
  16.4 0.7 %pad_add_fusion.params_ref = s32[6]{0:T(128)S(1)} fusion(s32[4]{0:T(128)} %param.10, s32[1]{0:T(128)} %bitcast.1, s32[1]{0:T(128)} %bitcast), kind=kLoop, calls=%fused_computation | loop fusion | flops 12 | bytes 48 | tf_op jit(solution)/shard_map/concatenate | solution.py:315
  17.2 3.8 %all-to-all-done = bf16[16,80,128]{2,1,0:T(8,128)(2,1)S(1)} async-done(((bf16[16,80,128]{2,1,0:T(8,128)(2,1)}), bf16[16,80,128]{2,1,0:T(8,128)(2,1)S(1)}, u32[]{:S(2)}, u32[]{:S(2)}) %all-to-all-start) | async-done | bytes 327712 | tf_op jit(solution)/shard_map/all_to_all | solution.py:310
  20.9 1.0 %source_filter.1.refs_0_ = bf16[1,4,2,32,128]{4,3,2,1,0:T(8,128)(2,1)S(1)} custom-call(s32[6]{0:T(128)S(1)} %pad_add_fusion.params_ref, bf16[16,1,80,128]{3,2,1,0:T(8,128)(2,1)S(1)} %bitcast.4, bf16[1024,256]{1,0:T(8,128)(2,1)S(1)} %get-tuple-element.14.weight_ref, s32[4,1,128]{2,1,0:T(1,128)S(1)} %get-tuple-element.15.index_ref), custom_call_target="tpu_custom_call" | custom-call | tf_op jit(solution)/shard_map/source_filter/pallas_call | solution.py:336
  21.9 2.9 %collective-permute-start.2 = (bf16[1,4,2,32,128]{4,3,2,1,0:T(8,128)(2,1)S(1)}, bf16[1,4,2,32,128]{4,3,2,1,0:T(8,128)(2,1)S(1)}, u32[]{:S(2)}, u32[]{:S(2)}) collective-permute-start(bf16[1,4,2,32,128]{4,3,2,1,0:T(8,128)(2,1)S(1)} %source_filter.1.refs_0_), channel_id=1, source_target_pairs={{0,12},{1,13},{2,14},{3,15},{4,8},{5,9},{6,10},{7,11},{8,4},{9,5},... | collective-permute-start | bytes 196616 | tf_op jit(solution)/shard_map/ppermute | solution.py:283
  24.8 0.0 collective-permute-start.1
  24.8 1.6 %collective-permute-start = (bf16[1,4,2,32,128]{4,3,2,1,0:T(8,128)(2,1)S(1)}, bf16[1,4,2,32,128]{4,3,2,1,0:T(8,128)(2,1)S(1)}, u32[]{:S(2)}, u32[]{:S(2)}) collective-permute-start(bf16[1,4,2,32,128]{4,3,2,1,0:T(8,128)(2,1)S(1)} %source_filter.1.refs_0_), channel_id=1, source_target_pairs={{0,4},{1,5},{2,6},{3,7},{4,0},{5,1},{6,2},{7,3},{8,12},{9,13},{10,... | collective-permute-start | bytes 196616 | tf_op jit(solution)/shard_map/ppermute | solution.py:283
  26.4 0.0 collective-permute-done.3.prev_ref
  26.4 0.0 collective-permute-done.4.next_ref
  26.4 0.0 copy-start
  26.4 0.9 %copy-done = bf16[2,4,32,512]{3,2,1,0:T(8,128)(2,1)S(1)} copy-done((bf16[2,4,32,512]{3,2,1,0:T(8,128)(2,1)S(1)}, bf16[2,4,32,512]{3,2,1,0:T(8,128)(2,1)}, u32[]{:S(2)}) %copy-start) | copy-done | bytes 262168
  27.3 2.1 %own_whiten.1.refs_2_ = bf16[2,4,4,32,128]{4,3,2,1,0:T(8,128)(2,1)S(1)} custom-call(bf16[2,4,32,512]{3,2,1,0:T(8,128)(2,1)S(1)} %collective-permute-done.3.prev_ref, bf16[2,4,32,512]{3,2,1,0:T(8,128)(2,1)S(1)} %copy-done, bf16[2,4,32,512]{3,2,1,0:T(8,128)(2,1)S(1)} %collective-permute-done.4.next_ref, bf16[1024,256]{1,0:T(8,128)(2,1)S(1)} %get-tuple-element.14.weight_ref, ...), custom_call_target="tpu_custom_call" | custom-call | flops 1073741824 | bytes 3145728 | tf_op jit(solution)/shard_map/own_whiten/pallas_call | solution.py:354
  29.4 0.0 collective-permute-done.2.refs_3_
  29.4 1.7 %collective-permute-done.1.refs_2_ = bf16[1,4,2,32,128]{4,3,2,1,0:T(8,128)(2,1)S(1)} collective-permute-done((bf16[1,4,2,32,128]{4,3,2,1,0:T(8,128)(2,1)S(1)}, bf16[1,4,2,32,128]{4,3,2,1,0:T(8,128)(2,1)S(1)}, u32[]{:S(2)}, u32[]{:S(2)}) %collective-permute-start.1) | collective-permute-done | bytes 65568 | tf_op jit(solution)/shard_map/ppermute | solution.py:283
  31.1 0.0 collective-permute-done.refs_1_
  31.1 1.1 %column_whiten.1.refs_0_ = bf16[1,4,4,2,32,128]{5,4,3,2,1,0:T(8,128)(2,1)S(1)} custom-call(s32[6]{0:T(128)S(1)} %pad_add_fusion.params_ref, bf16[1,4,2,32,128]{4,3,2,1,0:T(8,128)(2,1)S(1)} %source_filter.1.refs_0_, bf16[1,4,2,32,128]{4,3,2,1,0:T(8,128)(2,1)S(1)} %collective-permute-done.refs_1_, ...), custom_call_target="tpu_custom_call" | custom-call | tf_op jit(solution)/shard_map/column_whiten/pallas_call | solution.py:376
  32.2 0.1 collective-permute-start.6
  32.3 0.5 collective-permute-start.5
  32.7 1.0 %collective-permute-done.6.refs_1_ = bf16[1,4,4,2,32,128]{5,4,3,2,1,0:T(8,128)(2,1)S(1)} collective-permute-done((bf16[1,4,4,2,32,128]{5,4,3,2,1,0:T(8,128)(2,1)S(1)}, bf16[1,4,4,2,32,128]{5,4,3,2,1,0:T(8,128)(2,1)S(1)}, u32[]{:S(2)}, u32[]{:S(2)}) %collective-permute-start.6) | collective-permute-done | bytes 262176 | tf_op jit(solution)/shard_map/ppermute | solution.py:283
  33.8 4.1 %cross.2.refs_3_ = bf16[2,128,4,32,128]{4,3,2,1,0:T(8,128)(2,1)S(1)} custom-call(s32[6]{0:T(128)S(1)} %pad_add_fusion.params_ref, bf16[1,4,4,2,32,128]{5,4,3,2,1,0:T(8,128)(2,1)S(1)} %column_whiten.1.refs_0_, bf16[1,4,4,2,32,128]{5,4,3,2,1,0:T(8,128)(2,1)S(1)} %collective-permute-done.6.refs_1_, bf16[2,4,4,32,128]{4,3,2,1,0:T(8,128)(2,1)S(1)} %own_whiten.1.refs_2_), custom_call_target="tpu_custom_call" | custom-call | flops 67108864 | bytes 16777216 | tf_op jit(solution)/shard_map/cross/pallas_call | solution.py:397
  37.9 3.1 %collective-permute-done.5.refs_0_ = bf16[1,4,4,2,32,128]{5,4,3,2,1,0:T(8,128)(2,1)S(1)} collective-permute-done((bf16[1,4,4,2,32,128]{5,4,3,2,1,0:T(8,128)(2,1)S(1)}, bf16[1,4,4,2,32,128]{5,4,3,2,1,0:T(8,128)(2,1)S(1)}, u32[]{:S(2)}, u32[]{:S(2)}) %collective-permute-start.5) | collective-permute-done | bytes 262176 | tf_op jit(solution)/shard_map/ppermute | solution.py:283
  41.0 0.0 collective-permute-start.7
  41.0 1.5 %collective-permute-done.7.refs_1_ = bf16[1,4,4,2,32,128]{5,4,3,2,1,0:T(8,128)(2,1)S(1)} collective-permute-done((bf16[1,4,4,2,32,128]{5,4,3,2,1,0:T(8,128)(2,1)S(1)}, bf16[1,4,4,2,32,128]{5,4,3,2,1,0:T(8,128)(2,1)S(1)}, u32[]{:S(2)}, u32[]{:S(2)}) %collective-permute-start.7) | collective-permute-done | bytes 262176 | tf_op jit(solution)/shard_map/ppermute | solution.py:283
  42.5 5.7 %cross.3 = bf16[2,128,32,512]{3,2,1,0:T(8,128)(2,1)} custom-call(s32[6]{0:T(128)S(1)} %pad_add_fusion.params_ref, bf16[1,4,4,2,32,128]{5,4,3,2,1,0:T(8,128)(2,1)S(1)} %collective-permute-done.5.refs_0_, bf16[1,4,4,2,32,128]{5,4,3,2,1,0:T(8,128)(2,1)S(1)} %collective-permute-done.7.refs_1_, bf16[2,4,4,32,128]{4,3,2,1,0:T(8,128)(2,1)S(1)} %own_whiten.1.refs_2_, ...), custom_call_target="tpu_custom_call" | custom-call | flops 67108864 | bytes 16777216 | tf_op jit(solution)/shard_map/cross/pallas_call | solution.py:397
Async XLA Ops:
  2.4 18.5 %all-to-all-start = ((bf16[16,80,128]{2,1,0:T(8,128)(2,1)}), bf16[16,80,128]{2,1,0:T(8,128)(2,1)S(1)}, u32[]{:S(2)}, u32[]{:S(2)}) async-start(bf16[16,80,128]{2,1,0:T(8,128)(2,1)} %split.1), calls=%async_computation | async-start | bytes 655360 | tf_op jit(solution)/shard_map/all_to_all | solution.py:310
  9.8 16.6 %collective-permute-start.3 = (bf16[2,4,32,512]{3,2,1,0:T(8,128)(2,1)}, bf16[2,4,32,512]{3,2,1,0:T(8,128)(2,1)S(1)}, u32[]{:S(2)}, u32[]{:S(2)}) collective-permute-start(bf16[2,4,32,512]{3,2,1,0:T(8,128)(2,1)} %cur_ref.1), channel_id=1, source_target_pairs={{0,1},{1,2},{2,3},{3,4},{4,5},{5,6},{6,7},{7,8},{8,9},{9,10},{10,1... | collective-permute-start | bytes 786440 | tf_op jit(solution)/shard_map/ppermute | solution.py:318
  12.1 14.3 %collective-permute-start.4 = (bf16[2,4,32,512]{3,2,1,0:T(8,128)(2,1)}, bf16[2,4,32,512]{3,2,1,0:T(8,128)(2,1)S(1)}, u32[]{:S(2)}, u32[]{:S(2)}) collective-permute-start(bf16[2,4,32,512]{3,2,1,0:T(8,128)(2,1)} %cur_ref.1), channel_id=1, source_target_pairs={{1,0},{2,1},{3,2},{4,3},{5,4},{6,5},{7,6},{8,7},{9,8},{10,9},{11,1... | collective-permute-start | bytes 786440 | tf_op jit(solution)/shard_map/ppermute | solution.py:319
  13.4 0.7 %copy-start.1 = (s32[4,32]{1,0:T(4,128)S(1)}, s32[4,32]{1,0:T(4,128)}, u32[]{:S(2)}) copy-start(s32[4,32]{1,0:T(4,128)} %flags_ref.3) | copy-start | bytes 1540
  14.1 0.7 %copy-start.2 = (f32[2,8,65]{2,1,0:T(8,128)S(1)}, f32[2,8,65]{2,1,0:T(8,128)}, u32[]{:S(2)}) copy-start(f32[2,8,65]{2,1,0:T(8,128)} %bank_ref.1) | copy-start | bytes 12484
  14.8 0.7 %copy-start.3 = (s32[512]{0:T(512)S(1)}, s32[512]{0:T(512)}, u32[]{:S(2)}) copy-start(s32[512]{0:T(512)} %param.8) | copy-start | bytes 6148
  15.5 0.7 %copy-start.4 = (s32[4,32]{1,0:T(4,128)S(1)}, s32[4,32]{1,0:T(4,128)}, u32[]{:S(2)}) copy-start(s32[4,32]{1,0:T(4,128)} %offset_ref.1) | copy-start | bytes 1540
  21.9 7.5 %collective-permute-start.2 = (bf16[1,4,2,32,128]{4,3,2,1,0:T(8,128)(2,1)S(1)}, bf16[1,4,2,32,128]{4,3,2,1,0:T(8,128)(2,1)S(1)}, u32[]{:S(2)}, u32[]{:S(2)}) collective-permute-start(bf16[1,4,2,32,128]{4,3,2,1,0:T(8,128)(2,1)S(1)} %source_filter.1.refs_0_), channel_id=1, source_target_pairs={{0,12},{1,13},{2,14},{3,15},{4,8},{5,9},{6,10},{7,11},{8,4},{9,5},... | collective-permute-start | bytes 196616 | tf_op jit(solution)/shard_map/ppermute | solution.py:283
  24.8 6.3 %collective-permute-start.1 = (bf16[1,4,2,32,128]{4,3,2,1,0:T(8,128)(2,1)S(1)}, bf16[1,4,2,32,128]{4,3,2,1,0:T(8,128)(2,1)S(1)}, u32[]{:S(2)}, u32[]{:S(2)}) collective-permute-start(bf16[1,4,2,32,128]{4,3,2,1,0:T(8,128)(2,1)S(1)} %source_filter.1.refs_0_), channel_id=1, source_target_pairs={{0,8},{1,9},{2,10},{3,11},{4,12},{5,13},{6,14},{7,15},{8,0},{9,1},... | collective-permute-start | bytes 196616 | tf_op jit(solution)/shard_map/ppermute | solution.py:283
  24.8 6.3 %collective-permute-start = (bf16[1,4,2,32,128]{4,3,2,1,0:T(8,128)(2,1)S(1)}, bf16[1,4,2,32,128]{4,3,2,1,0:T(8,128)(2,1)S(1)}, u32[]{:S(2)}, u32[]{:S(2)}) collective-permute-start(bf16[1,4,2,32,128]{4,3,2,1,0:T(8,128)(2,1)S(1)} %source_filter.1.refs_0_), channel_id=1, source_target_pairs={{0,4},{1,5},{2,6},{3,7},{4,0},{5,1},{6,2},{7,3},{8,12},{9,13},{10,... | collective-permute-start | bytes 196616 | tf_op jit(solution)/shard_map/ppermute | solution.py:283
  26.4 1.0 %copy-start = (bf16[2,4,32,512]{3,2,1,0:T(8,128)(2,1)S(1)}, bf16[2,4,32,512]{3,2,1,0:T(8,128)(2,1)}, u32[]{:S(2)}) copy-start(bf16[2,4,32,512]{3,2,1,0:T(8,128)(2,1)} %cur_ref.1) | copy-start | bytes 786436
  32.2 1.6 %collective-permute-start.6 = (bf16[1,4,4,2,32,128]{5,4,3,2,1,0:T(8,128)(2,1)S(1)}, bf16[1,4,4,2,32,128]{5,4,3,2,1,0:T(8,128)(2,1)S(1)}, u32[]{:S(2)}, u32[]{:S(2)}) collective-permute-start(bf16[1,4,4,2,32,128]{5,4,3,2,1,0:T(8,128)(2,1)S(1)} %column_whiten.1.refs_0_), channel_id=1, source_target_pairs={{0,1},{1,0},{2,3},{3,2},{4,5},{5,4},{6,7},{7,6},{8,9},{9,8},{10,11... | collective-permute-start | bytes 786440 | tf_op jit(solution)/shard_map/ppermute | solution.py:283
  32.3 8.7 %collective-permute-start.5 = (bf16[1,4,4,2,32,128]{5,4,3,2,1,0:T(8,128)(2,1)S(1)}, bf16[1,4,4,2,32,128]{5,4,3,2,1,0:T(8,128)(2,1)S(1)}, u32[]{:S(2)}, u32[]{:S(2)}) collective-permute-start(bf16[1,4,4,2,32,128]{5,4,3,2,1,0:T(8,128)(2,1)S(1)} %column_whiten.1.refs_0_), channel_id=1, source_target_pairs={{0,2},{1,3},{2,0},{3,1},{4,6},{5,7},{6,4},{7,5},{8,10},{9,11},{10,... | collective-permute-start | bytes 786440 | tf_op jit(solution)/shard_map/ppermute | solution.py:283
  41.0 1.5 %collective-permute-start.7 = (bf16[1,4,4,2,32,128]{5,4,3,2,1,0:T(8,128)(2,1)S(1)}, bf16[1,4,4,2,32,128]{5,4,3,2,1,0:T(8,128)(2,1)S(1)}, u32[]{:S(2)}, u32[]{:S(2)}) collective-permute-start(bf16[1,4,4,2,32,128]{5,4,3,2,1,0:T(8,128)(2,1)S(1)} %collective-permute-done.5.refs_0_), channel_id=1, source_target_pairs={{0,1},{1,0},{2,3},{3,2},{4,5},{5,4},{6,7},{7,6},{8,9},{9,8},{10,11... | collective-permute-start | bytes 786440 | tf_op jit(solution)/shard_map/ppermute | solution.py:283

commit v15 on v11

--- a/solution.py
+++ b/solution.py
@@ -11,7 +11,7 @@
 LANES = 128
 WATER = 0.05
 SRC_STEP = 16
-SLOTS = 3
+SLOTS = 6
 
 
 def room(mib):

time: 47.7 us -> 48 us (level)
  no operation moved by 1% of the time
where the time goes in v15:
time: 48 us; the launch traced here: 47.6 us
  starting transfers between devices  16 us (33%)
  Pallas kernels  15.7 us (33%)
  waiting for transfers between devices  11.4 us (24%)
  local copies, waits for them, and re-layouts  3.68 us (8%)
  other arithmetic  0.74 us (2%)
    pallas_call x2, Pallas kernels, cross(): pl.pallas_call(functools.partial(cross_kernel, masks=masks, added=len(ear...  9.57 us
    ppermute x6, waiting for transfers between devices, swap(): return lax.ppermute(x, 'chan', [(i, i ^ mask) for i in range(n_chan)])  7.6 us
    all_to_all x1, starting transfers between devices, body(): held = lax.all_to_all(split, 'chan', 0, 0)[:, None]  7.39 us
    ppermute x6, starting transfers between devices, swap(): return lax.ppermute(x, 'chan', [(i, i ^ mask) for i in range(n_chan)])  4.99 us
    all_to_all x1, waiting for transfers between devices, body(): held = lax.all_to_all(split, 'chan', 0, 0)[:, None]  3.75 us
    unnamed x10, local copies, waits for them, and re-layouts  3.68 us
    ppermute x1, starting transfers between devices, body(): before = lax.ppermute(spectra, 'chan', [(i, i + 1) for i in range(ends)])  2.32 us
    pallas_call x1, Pallas kernels, body(): pl.pallas_call(own_kernel, out_shape=jax.ShapeDtypeStruct((2, tiles, win,...  2.06 us
  transfers between devices with their start and end apart: 9, of which 5 were waited for; matrix products, arithmetic and copies ran while one was open for 2% of the time, Pallas kernels for 15%

profile of v15, /device:TPU:0, one launch (start us, length us, event | category | flops | bytes accessed | tf_op | source)
XLA Modules:
  0.0 47.6 jit_solution(17644027407330205753)
XLA Ops:
  0.0 1.7 %split.1 = bf16[16,80,128]{2,1,0:T(8,128)(2,1)} custom-call(bf16[2,4,32,512]{3,2,1,0:T(8,128)(2,1)} %cur_ref.1, s32[4,32]{1,0:T(4,128)} %flags_ref.3), custom_call_target="tpu_custom_call" | custom-call | tf_op jit(solution)/shard_map/split/pallas_call | solution.py:288
  1.7 7.4 %all-to-all-start = ((bf16[16,80,128]{2,1,0:T(8,128)(2,1)}), bf16[16,80,128]{2,1,0:T(8,128)(2,1)S(1)}, u32[]{:S(2)}, u32[]{:S(2)}) async-start(bf16[16,80,128]{2,1,0:T(8,128)(2,1)} %split.1), calls=%async_computation | async-start | bytes 655360 | tf_op jit(solution)/shard_map/all_to_all | solution.py:295
  9.1 2.3 %collective-permute-start.3 = (bf16[2,4,32,512]{3,2,1,0:T(8,128)(2,1)}, bf16[2,4,32,512]{3,2,1,0:T(8,128)(2,1)S(1)}, u32[]{:S(2)}, u32[]{:S(2)}) collective-permute-start(bf16[2,4,32,512]{3,2,1,0:T(8,128)(2,1)} %cur_ref.1), channel_id=1, source_target_pairs={{0,1},{1,2},{2,3},{3,4},{4,5},{5,6},{6,7},{7,8},{8,9},{9,10},{10,1... | collective-permute-start | bytes 786440 | tf_op jit(solution)/shard_map/ppermute | solution.py:303
  11.5 1.3 %collective-permute-start.4 = (bf16[2,4,32,512]{3,2,1,0:T(8,128)(2,1)}, bf16[2,4,32,512]{3,2,1,0:T(8,128)(2,1)S(1)}, u32[]{:S(2)}, u32[]{:S(2)}) collective-permute-start(bf16[2,4,32,512]{3,2,1,0:T(8,128)(2,1)} %cur_ref.1), channel_id=1, source_target_pairs={{1,0},{2,1},{3,2},{4,3},{5,4},{6,5},{7,6},{8,7},{9,8},{10,9},{11,1... | collective-permute-start | bytes 786440 | tf_op jit(solution)/shard_map/ppermute | solution.py:304
  12.8 0.0 copy-start.1
  12.8 0.7 %copy-done.1 = s32[4,32]{1,0:T(4,128)S(1)} copy-done((s32[4,32]{1,0:T(4,128)S(1)}, s32[4,32]{1,0:T(4,128)}, u32[]{:S(2)}) %copy-start.1) | copy-done | bytes 536
  13.4 0.0 copy-start.2
  13.4 0.7 %copy-done.2 = f32[2,8,65]{2,1,0:T(8,128)S(1)} copy-done((f32[2,8,65]{2,1,0:T(8,128)S(1)}, f32[2,8,65]{2,1,0:T(8,128)}, u32[]{:S(2)}) %copy-start.2) | copy-done | bytes 4184
  14.1 0.0 copy-start.3
  14.1 0.7 %copy-done.3 = s32[512]{0:T(512)S(1)} copy-done((s32[512]{0:T(512)S(1)}, s32[512]{0:T(512)}, u32[]{:S(2)}) %copy-start.3) | copy-done | bytes 2072
  14.8 0.0 copy-start.4
  14.8 0.7 %copy-done.4 = s32[4,32]{1,0:T(4,128)S(1)} copy-done((s32[4,32]{1,0:T(4,128)S(1)}, s32[4,32]{1,0:T(4,128)}, u32[]{:S(2)}) %copy-start.4) | copy-done | bytes 536
  15.5 0.2 prep.1
  15.8 0.7 %pad_add_fusion.params_ref = s32[6]{0:T(128)S(1)} fusion(s32[4]{0:T(128)} %param.10, s32[1]{0:T(128)} %bitcast.1, s32[1]{0:T(128)} %bitcast), kind=kLoop, calls=%fused_computation | loop fusion | flops 12 | bytes 48 | tf_op jit(solution)/shard_map/concatenate | solution.py:300
  16.5 3.8 %all-to-all-done = bf16[16,80,128]{2,1,0:T(8,128)(2,1)S(1)} async-done(((bf16[16,80,128]{2,1,0:T(8,128)(2,1)}), bf16[16,80,128]{2,1,0:T(8,128)(2,1)S(1)}, u32[]{:S(2)}, u32[]{:S(2)}) %all-to-all-start) | async-done | bytes 327712 | tf_op jit(solution)/shard_map/all_to_all | solution.py:295
  20.3 1.0 %source_filter.1.refs_0_ = bf16[1,4,2,32,128]{4,3,2,1,0:T(8,128)(2,1)S(1)} custom-call(s32[6]{0:T(128)S(1)} %pad_add_fusion.params_ref, bf16[16,1,80,128]{3,2,1,0:T(8,128)(2,1)S(1)} %bitcast.4, bf16[1024,256]{1,0:T(8,128)(2,1)S(1)} %get-tuple-element.14.weight_ref, s32[4,1,128]{2,1,0:T(1,128)S(1)} %get-tuple-element.15.index_ref), custom_call_target="tpu_custom_call" | custom-call | tf_op jit(solution)/shard_map/source_filter/pallas_call | solution.py:321
  21.3 2.9 %collective-permute-start.2 = (bf16[1,4,2,32,128]{4,3,2,1,0:T(8,128)(2,1)S(1)}, bf16[1,4,2,32,128]{4,3,2,1,0:T(8,128)(2,1)S(1)}, u32[]{:S(2)}, u32[]{:S(2)}) collective-permute-start(bf16[1,4,2,32,128]{4,3,2,1,0:T(8,128)(2,1)S(1)} %source_filter.1.refs_0_), channel_id=1, source_target_pairs={{0,12},{1,13},{2,14},{3,15},{4,8},{5,9},{6,10},{7,11},{8,4},{9,5},... | collective-permute-start | bytes 196616 | tf_op jit(solution)/shard_map/ppermute | solution.py:271
  24.1 0.0 collective-permute-start.1
  24.1 1.6 %collective-permute-start = (bf16[1,4,2,32,128]{4,3,2,1,0:T(8,128)(2,1)S(1)}, bf16[1,4,2,32,128]{4,3,2,1,0:T(8,128)(2,1)S(1)}, u32[]{:S(2)}, u32[]{:S(2)}) collective-permute-start(bf16[1,4,2,32,128]{4,3,2,1,0:T(8,128)(2,1)S(1)} %source_filter.1.refs_0_), channel_id=1, source_target_pairs={{0,4},{1,5},{2,6},{3,7},{4,0},{5,1},{6,2},{7,3},{8,12},{9,13},{10,... | collective-permute-start | bytes 196616 | tf_op jit(solution)/shard_map/ppermute | solution.py:271
  25.7 0.0 collective-permute-done.3.prev_ref
  25.7 0.0 collective-permute-done.4.next_ref
  25.7 0.0 copy-start
  25.7 0.9 %copy-done = bf16[2,4,32,512]{3,2,1,0:T(8,128)(2,1)S(1)} copy-done((bf16[2,4,32,512]{3,2,1,0:T(8,128)(2,1)S(1)}, bf16[2,4,32,512]{3,2,1,0:T(8,128)(2,1)}, u32[]{:S(2)}) %copy-start) | copy-done | bytes 262168
  26.7 2.1 %own_whiten.1.refs_2_ = bf16[2,4,4,32,128]{4,3,2,1,0:T(8,128)(2,1)S(1)} custom-call(bf16[2,4,32,512]{3,2,1,0:T(8,128)(2,1)S(1)} %collective-permute-done.3.prev_ref, bf16[2,4,32,512]{3,2,1,0:T(8,128)(2,1)S(1)} %copy-done, bf16[2,4,32,512]{3,2,1,0:T(8,128)(2,1)S(1)} %collective-permute-done.4.next_ref, bf16[1024,256]{1,0:T(8,128)(2,1)S(1)} %get-tuple-element.14.weight_ref, ...), custom_call_target="tpu_custom_call" | custom-call | flops 1073741824 | bytes 3145728 | tf_op jit(solution)/shard_map/own_whiten/pallas_call | solution.py:339
  28.7 0.0 collective-permute-done.2.refs_3_
  28.7 1.7 %collective-permute-done.1.refs_2_ = bf16[1,4,2,32,128]{4,3,2,1,0:T(8,128)(2,1)S(1)} collective-permute-done((bf16[1,4,2,32,128]{4,3,2,1,0:T(8,128)(2,1)S(1)}, bf16[1,4,2,32,128]{4,3,2,1,0:T(8,128)(2,1)S(1)}, u32[]{:S(2)}, u32[]{:S(2)}) %collective-permute-start.1) | collective-permute-done | bytes 65568 | tf_op jit(solution)/shard_map/ppermute | solution.py:271
  30.4 0.0 collective-permute-done.refs_1_
  30.4 1.1 %column_whiten.1.refs_0_ = bf16[1,4,4,2,32,128]{5,4,3,2,1,0:T(8,128)(2,1)S(1)} custom-call(s32[6]{0:T(128)S(1)} %pad_add_fusion.params_ref, bf16[1,4,2,32,128]{4,3,2,1,0:T(8,128)(2,1)S(1)} %source_filter.1.refs_0_, bf16[1,4,2,32,128]{4,3,2,1,0:T(8,128)(2,1)S(1)} %collective-permute-done.refs_1_, ...), custom_call_target="tpu_custom_call" | custom-call | tf_op jit(solution)/shard_map/column_whiten/pallas_call | solution.py:361
  31.5 0.1 collective-permute-start.6
  31.6 0.5 collective-permute-start.5
  32.1 1.1 %collective-permute-done.6.refs_1_ = bf16[1,4,4,2,32,128]{5,4,3,2,1,0:T(8,128)(2,1)S(1)} collective-permute-done((bf16[1,4,4,2,32,128]{5,4,3,2,1,0:T(8,128)(2,1)S(1)}, bf16[1,4,4,2,32,128]{5,4,3,2,1,0:T(8,128)(2,1)S(1)}, u32[]{:S(2)}, u32[]{:S(2)}) %collective-permute-start.6) | collective-permute-done | bytes 262176 | tf_op jit(solution)/shard_map/ppermute | solution.py:271
  33.1 3.9 %cross.2.refs_3_ = bf16[2,128,4,32,128]{4,3,2,1,0:T(8,128)(2,1)S(1)} custom-call(s32[6]{0:T(128)S(1)} %pad_add_fusion.params_ref, bf16[1,4,4,2,32,128]{5,4,3,2,1,0:T(8,128)(2,1)S(1)} %column_whiten.1.refs_0_, bf16[1,4,4,2,32,128]{5,4,3,2,1,0:T(8,128)(2,1)S(1)} %collective-permute-done.6.refs_1_, bf16[2,4,4,32,128]{4,3,2,1,0:T(8,128)(2,1)S(1)} %own_whiten.1.refs_2_), custom_call_target="tpu_custom_call" | custom-call | flops 67108864 | bytes 16777216 | tf_op jit(solution)/shard_map/cross/pallas_call | solution.py:382
  37.0 3.3 %collective-permute-done.5.refs_0_ = bf16[1,4,4,2,32,128]{5,4,3,2,1,0:T(8,128)(2,1)S(1)} collective-permute-done((bf16[1,4,4,2,32,128]{5,4,3,2,1,0:T(8,128)(2,1)S(1)}, bf16[1,4,4,2,32,128]{5,4,3,2,1,0:T(8,128)(2,1)S(1)}, u32[]{:S(2)}, u32[]{:S(2)}) %collective-permute-start.5) | collective-permute-done | bytes 262176 | tf_op jit(solution)/shard_map/ppermute | solution.py:271
  40.3 0.0 collective-permute-start.7
  40.3 1.5 %collective-permute-done.7.refs_1_ = bf16[1,4,4,2,32,128]{5,4,3,2,1,0:T(8,128)(2,1)S(1)} collective-permute-done((bf16[1,4,4,2,32,128]{5,4,3,2,1,0:T(8,128)(2,1)S(1)}, bf16[1,4,4,2,32,128]{5,4,3,2,1,0:T(8,128)(2,1)S(1)}, u32[]{:S(2)}, u32[]{:S(2)}) %collective-permute-start.7) | collective-permute-done | bytes 262176 | tf_op jit(solution)/shard_map/ppermute | solution.py:271
  41.9 5.7 %cross.3 = bf16[2,128,32,512]{3,2,1,0:T(8,128)(2,1)} custom-call(s32[6]{0:T(128)S(1)} %pad_add_fusion.params_ref, bf16[1,4,4,2,32,128]{5,4,3,2,1,0:T(8,128)(2,1)S(1)} %collective-permute-done.5.refs_0_, bf16[1,4,4,2,32,128]{5,4,3,2,1,0:T(8,128)(2,1)S(1)} %collective-permute-done.7.refs_1_, bf16[2,4,4,32,128]{4,3,2,1,0:T(8,128)(2,1)S(1)} %own_whiten.1.refs_2_, ...), custom_call_target="tpu_custom_call" | custom-call | flops 67108864 | bytes 16777216 | tf_op jit(solution)/shard_map/cross/pallas_call | solution.py:382
Async XLA Ops:
  1.7 18.5 %all-to-all-start = ((bf16[16,80,128]{2,1,0:T(8,128)(2,1)}), bf16[16,80,128]{2,1,0:T(8,128)(2,1)S(1)}, u32[]{:S(2)}, u32[]{:S(2)}) async-start(bf16[16,80,128]{2,1,0:T(8,128)(2,1)} %split.1), calls=%async_computation | async-start | bytes 655360 | tf_op jit(solution)/shard_map/all_to_all | solution.py:295
  9.1 16.6 %collective-permute-start.3 = (bf16[2,4,32,512]{3,2,1,0:T(8,128)(2,1)}, bf16[2,4,32,512]{3,2,1,0:T(8,128)(2,1)S(1)}, u32[]{:S(2)}, u32[]{:S(2)}) collective-permute-start(bf16[2,4,32,512]{3,2,1,0:T(8,128)(2,1)} %cur_ref.1), channel_id=1, source_target_pairs={{0,1},{1,2},{2,3},{3,4},{4,5},{5,6},{6,7},{7,8},{8,9},{9,10},{10,1... | collective-permute-start | bytes 786440 | tf_op jit(solution)/shard_map/ppermute | solution.py:303
  11.5 14.3 %collective-permute-start.4 = (bf16[2,4,32,512]{3,2,1,0:T(8,128)(2,1)}, bf16[2,4,32,512]{3,2,1,0:T(8,128)(2,1)S(1)}, u32[]{:S(2)}, u32[]{:S(2)}) collective-permute-start(bf16[2,4,32,512]{3,2,1,0:T(8,128)(2,1)} %cur_ref.1), channel_id=1, source_target_pairs={{1,0},{2,1},{3,2},{4,3},{5,4},{6,5},{7,6},{8,7},{9,8},{10,9},{11,1... | collective-permute-start | bytes 786440 | tf_op jit(solution)/shard_map/ppermute | solution.py:304
  12.8 0.7 %copy-start.1 = (s32[4,32]{1,0:T(4,128)S(1)}, s32[4,32]{1,0:T(4,128)}, u32[]{:S(2)}) copy-start(s32[4,32]{1,0:T(4,128)} %flags_ref.3) | copy-start | bytes 1540
  13.4 0.7 %copy-start.2 = (f32[2,8,65]{2,1,0:T(8,128)S(1)}, f32[2,8,65]{2,1,0:T(8,128)}, u32[]{:S(2)}) copy-start(f32[2,8,65]{2,1,0:T(8,128)} %bank_ref.1) | copy-start | bytes 12484
  14.1 0.7 %copy-start.3 = (s32[512]{0:T(512)S(1)}, s32[512]{0:T(512)}, u32[]{:S(2)}) copy-start(s32[512]{0:T(512)} %param.8) | copy-start | bytes 6148
  14.8 0.7 %copy-start.4 = (s32[4,32]{1,0:T(4,128)S(1)}, s32[4,32]{1,0:T(4,128)}, u32[]{:S(2)}) copy-start(s32[4,32]{1,0:T(4,128)} %offset_ref.1) | copy-start | bytes 1540
  21.3 7.5 %collective-permute-start.2 = (bf16[1,4,2,32,128]{4,3,2,1,0:T(8,128)(2,1)S(1)}, bf16[1,4,2,32,128]{4,3,2,1,0:T(8,128)(2,1)S(1)}, u32[]{:S(2)}, u32[]{:S(2)}) collective-permute-start(bf16[1,4,2,32,128]{4,3,2,1,0:T(8,128)(2,1)S(1)} %source_filter.1.refs_0_), channel_id=1, source_target_pairs={{0,12},{1,13},{2,14},{3,15},{4,8},{5,9},{6,10},{7,11},{8,4},{9,5},... | collective-permute-start | bytes 196616 | tf_op jit(solution)/shard_map/ppermute | solution.py:271
  24.1 6.3 %collective-permute-start.1 = (bf16[1,4,2,32,128]{4,3,2,1,0:T(8,128)(2,1)S(1)}, bf16[1,4,2,32,128]{4,3,2,1,0:T(8,128)(2,1)S(1)}, u32[]{:S(2)}, u32[]{:S(2)}) collective-permute-start(bf16[1,4,2,32,128]{4,3,2,1,0:T(8,128)(2,1)S(1)} %source_filter.1.refs_0_), channel_id=1, source_target_pairs={{0,8},{1,9},{2,10},{3,11},{4,12},{5,13},{6,14},{7,15},{8,0},{9,1},... | collective-permute-start | bytes 196616 | tf_op jit(solution)/shard_map/ppermute | solution.py:271
  24.1 6.3 %collective-permute-start = (bf16[1,4,2,32,128]{4,3,2,1,0:T(8,128)(2,1)S(1)}, bf16[1,4,2,32,128]{4,3,2,1,0:T(8,128)(2,1)S(1)}, u32[]{:S(2)}, u32[]{:S(2)}) collective-permute-start(bf16[1,4,2,32,128]{4,3,2,1,0:T(8,128)(2,1)S(1)} %source_filter.1.refs_0_), channel_id=1, source_target_pairs={{0,4},{1,5},{2,6},{3,7},{4,0},{5,1},{6,2},{7,3},{8,12},{9,13},{10,... | collective-permute-start | bytes 196616 | tf_op jit(solution)/shard_map/ppermute | solution.py:271
  25.7 1.0 %copy-start = (bf16[2,4,32,512]{3,2,1,0:T(8,128)(2,1)S(1)}, bf16[2,4,32,512]{3,2,1,0:T(8,128)(2,1)}, u32[]{:S(2)}) copy-start(bf16[2,4,32,512]{3,2,1,0:T(8,128)(2,1)} %cur_ref.1) | copy-start | bytes 786436
  31.5 1.6 %collective-permute-start.6 = (bf16[1,4,4,2,32,128]{5,4,3,2,1,0:T(8,128)(2,1)S(1)}, bf16[1,4,4,2,32,128]{5,4,3,2,1,0:T(8,128)(2,1)S(1)}, u32[]{:S(2)}, u32[]{:S(2)}) collective-permute-start(bf16[1,4,4,2,32,128]{5,4,3,2,1,0:T(8,128)(2,1)S(1)} %column_whiten.1.refs_0_), channel_id=1, source_target_pairs={{0,1},{1,0},{2,3},{3,2},{4,5},{5,4},{6,7},{7,6},{8,9},{9,8},{10,11... | collective-permute-start | bytes 786440 | tf_op jit(solution)/shard_map/ppermute | solution.py:271
  31.6 8.7 %collective-permute-start.5 = (bf16[1,4,4,2,32,128]{5,4,3,2,1,0:T(8,128)(2,1)S(1)}, bf16[1,4,4,2,32,128]{5,4,3,2,1,0:T(8,128)(2,1)S(1)}, u32[]{:S(2)}, u32[]{:S(2)}) collective-permute-start(bf16[1,4,4,2,32,128]{5,4,3,2,1,0:T(8,128)(2,1)S(1)} %column_whiten.1.refs_0_), channel_id=1, source_target_pairs={{0,2},{1,3},{2,0},{3,1},{4,6},{5,7},{6,4},{7,5},{8,10},{9,11},{10,... | collective-permute-start | bytes 786440 | tf_op jit(solution)/shard_map/ppermute | solution.py:271
  40.3 1.5 %collective-permute-start.7 = (bf16[1,4,4,2,32,128]{5,4,3,2,1,0:T(8,128)(2,1)S(1)}, bf16[1,4,4,2,32,128]{5,4,3,2,1,0:T(8,128)(2,1)S(1)}, u32[]{:S(2)}, u32[]{:S(2)}) collective-permute-start(bf16[1,4,4,2,32,128]{5,4,3,2,1,0:T(8,128)(2,1)S(1)} %collective-permute-done.5.refs_0_), channel_id=1, source_target_pairs={{0,1},{1,0},{2,3},{3,2},{4,5},{5,4},{6,7},{7,6},{8,9},{9,8},{10,11... | collective-permute-start | bytes 786440 | tf_op jit(solution)/shard_map/ppermute | solution.py:271

commit v16 on v15

--- a/solution.py
+++ b/solution.py
@@ -11,7 +11,7 @@
 LANES = 128
 WATER = 0.05
 SRC_STEP = 16
-SLOTS = 6
+SLOTS = 2
 
 
 def room(mib):

time: 48 us -> 48.9 us (1.019)
  Pallas kernels: 15.7 us -> 16.6 us
    pallas_call x2, Pallas kernels: 9.57 us -> 10.4 us  [cross(): pl.pallas_call(functools.partial(cross_kernel, masks=masks, added=len(ear...]
where the time goes in v16:
time: 48.9 us; the launch traced here: 48.4 us
  Pallas kernels  16.6 us (34%)
  starting transfers between devices  16 us (33%)
  waiting for transfers between devices  11.3 us (23%)
  local copies, waits for them, and re-layouts  3.68 us (8%)
  other arithmetic  0.74 us (2%)
    pallas_call x2, Pallas kernels, cross(): pl.pallas_call(functools.partial(cross_kernel, masks=masks, added=len(ear...  10.4 us
    ppermute x6, waiting for transfers between devices, swap(): return lax.ppermute(x, 'chan', [(i, i ^ mask) for i in range(n_chan)])  7.57 us
    all_to_all x1, starting transfers between devices, body(): held = lax.all_to_all(split, 'chan', 0, 0)[:, None]  7.39 us
    ppermute x6, starting transfers between devices, swap(): return lax.ppermute(x, 'chan', [(i, i ^ mask) for i in range(n_chan)])  5 us
    all_to_all x1, waiting for transfers between devices, body(): held = lax.all_to_all(split, 'chan', 0, 0)[:, None]  3.75 us
    unnamed x10, local copies, waits for them, and re-layouts  3.68 us
    ppermute x1, starting transfers between devices, body(): before = lax.ppermute(spectra, 'chan', [(i, i + 1) for i in range(ends)])  2.32 us
    pallas_call x1, Pallas kernels, body(): pl.pallas_call(own_kernel, out_shape=jax.ShapeDtypeStruct((2, tiles, win,...  2.07 us
  transfers between devices with their start and end apart: 9, of which 5 were waited for; matrix products, arithmetic and copies ran while one was open for 2% of the time, Pallas kernels for 15%

profile of v16, /device:TPU:0, one launch (start us, length us, event | category | flops | bytes accessed | tf_op | source)
XLA Modules:
  0.0 48.4 jit_solution(4529933005408952814)
XLA Ops:
  0.0 1.7 %split.1 = bf16[16,80,128]{2,1,0:T(8,128)(2,1)} custom-call(bf16[2,4,32,512]{3,2,1,0:T(8,128)(2,1)} %cur_ref.1, s32[4,32]{1,0:T(4,128)} %flags_ref.3), custom_call_target="tpu_custom_call" | custom-call | tf_op jit(solution)/shard_map/split/pallas_call | solution.py:288
  1.7 7.4 %all-to-all-start = ((bf16[16,80,128]{2,1,0:T(8,128)(2,1)}), bf16[16,80,128]{2,1,0:T(8,128)(2,1)S(1)}, u32[]{:S(2)}, u32[]{:S(2)}) async-start(bf16[16,80,128]{2,1,0:T(8,128)(2,1)} %split.1), calls=%async_computation | async-start | bytes 655360 | tf_op jit(solution)/shard_map/all_to_all | solution.py:295
  9.1 2.3 %collective-permute-start.3 = (bf16[2,4,32,512]{3,2,1,0:T(8,128)(2,1)}, bf16[2,4,32,512]{3,2,1,0:T(8,128)(2,1)S(1)}, u32[]{:S(2)}, u32[]{:S(2)}) collective-permute-start(bf16[2,4,32,512]{3,2,1,0:T(8,128)(2,1)} %cur_ref.1), channel_id=1, source_target_pairs={{0,1},{1,2},{2,3},{3,4},{4,5},{5,6},{6,7},{7,8},{8,9},{9,10},{10,1... | collective-permute-start | bytes 786440 | tf_op jit(solution)/shard_map/ppermute | solution.py:303
  11.5 1.3 %collective-permute-start.4 = (bf16[2,4,32,512]{3,2,1,0:T(8,128)(2,1)}, bf16[2,4,32,512]{3,2,1,0:T(8,128)(2,1)S(1)}, u32[]{:S(2)}, u32[]{:S(2)}) collective-permute-start(bf16[2,4,32,512]{3,2,1,0:T(8,128)(2,1)} %cur_ref.1), channel_id=1, source_target_pairs={{1,0},{2,1},{3,2},{4,3},{5,4},{6,5},{7,6},{8,7},{9,8},{10,9},{11,1... | collective-permute-start | bytes 786440 | tf_op jit(solution)/shard_map/ppermute | solution.py:304
  12.8 0.0 copy-start.1
  12.8 0.7 %copy-done.1 = s32[4,32]{1,0:T(4,128)S(1)} copy-done((s32[4,32]{1,0:T(4,128)S(1)}, s32[4,32]{1,0:T(4,128)}, u32[]{:S(2)}) %copy-start.1) | copy-done | bytes 536
  13.4 0.0 copy-start.2
  13.4 0.7 %copy-done.2 = f32[2,8,65]{2,1,0:T(8,128)S(1)} copy-done((f32[2,8,65]{2,1,0:T(8,128)S(1)}, f32[2,8,65]{2,1,0:T(8,128)}, u32[]{:S(2)}) %copy-start.2) | copy-done | bytes 4184
  14.1 0.0 copy-start.3
  14.1 0.7 %copy-done.3 = s32[512]{0:T(512)S(1)} copy-done((s32[512]{0:T(512)S(1)}, s32[512]{0:T(512)}, u32[]{:S(2)}) %copy-start.3) | copy-done | bytes 2072
  14.8 0.0 copy-start.4
  14.8 0.7 %copy-done.4 = s32[4,32]{1,0:T(4,128)S(1)} copy-done((s32[4,32]{1,0:T(4,128)S(1)}, s32[4,32]{1,0:T(4,128)}, u32[]{:S(2)}) %copy-start.4) | copy-done | bytes 536
  15.5 0.2 prep.1
  15.8 0.7 %pad_add_fusion.params_ref = s32[6]{0:T(128)S(1)} fusion(s32[4]{0:T(128)} %param.10, s32[1]{0:T(128)} %bitcast.1, s32[1]{0:T(128)} %bitcast), kind=kLoop, calls=%fused_computation | loop fusion | flops 12 | bytes 48 | tf_op jit(solution)/shard_map/concatenate | solution.py:300
  16.5 3.8 %all-to-all-done = bf16[16,80,128]{2,1,0:T(8,128)(2,1)S(1)} async-done(((bf16[16,80,128]{2,1,0:T(8,128)(2,1)}), bf16[16,80,128]{2,1,0:T(8,128)(2,1)S(1)}, u32[]{:S(2)}, u32[]{:S(2)}) %all-to-all-start) | async-done | bytes 327712 | tf_op jit(solution)/shard_map/all_to_all | solution.py:295
  20.3 1.0 %source_filter.1.refs_0_ = bf16[1,4,2,32,128]{4,3,2,1,0:T(8,128)(2,1)S(1)} custom-call(s32[6]{0:T(128)S(1)} %pad_add_fusion.params_ref, bf16[16,1,80,128]{3,2,1,0:T(8,128)(2,1)S(1)} %bitcast.4, bf16[1024,256]{1,0:T(8,128)(2,1)S(1)} %get-tuple-element.14.weight_ref, s32[4,1,128]{2,1,0:T(1,128)S(1)} %get-tuple-element.15.index_ref), custom_call_target="tpu_custom_call" | custom-call | tf_op jit(solution)/shard_map/source_filter/pallas_call | solution.py:321
  21.3 2.9 %collective-permute-start.2 = (bf16[1,4,2,32,128]{4,3,2,1,0:T(8,128)(2,1)S(1)}, bf16[1,4,2,32,128]{4,3,2,1,0:T(8,128)(2,1)S(1)}, u32[]{:S(2)}, u32[]{:S(2)}) collective-permute-start(bf16[1,4,2,32,128]{4,3,2,1,0:T(8,128)(2,1)S(1)} %source_filter.1.refs_0_), channel_id=1, source_target_pairs={{0,12},{1,13},{2,14},{3,15},{4,8},{5,9},{6,10},{7,11},{8,4},{9,5},... | collective-permute-start | bytes 196616 | tf_op jit(solution)/shard_map/ppermute | solution.py:271
  24.1 0.0 collective-permute-start.1
  24.1 1.6 %collective-permute-start = (bf16[1,4,2,32,128]{4,3,2,1,0:T(8,128)(2,1)S(1)}, bf16[1,4,2,32,128]{4,3,2,1,0:T(8,128)(2,1)S(1)}, u32[]{:S(2)}, u32[]{:S(2)}) collective-permute-start(bf16[1,4,2,32,128]{4,3,2,1,0:T(8,128)(2,1)S(1)} %source_filter.1.refs_0_), channel_id=1, source_target_pairs={{0,4},{1,5},{2,6},{3,7},{4,0},{5,1},{6,2},{7,3},{8,12},{9,13},{10,... | collective-permute-start | bytes 196616 | tf_op jit(solution)/shard_map/ppermute | solution.py:271
  25.7 0.0 collective-permute-done.3.prev_ref
  25.7 0.0 collective-permute-done.4.next_ref
  25.7 0.0 copy-start
  25.7 0.9 %copy-done = bf16[2,4,32,512]{3,2,1,0:T(8,128)(2,1)S(1)} copy-done((bf16[2,4,32,512]{3,2,1,0:T(8,128)(2,1)S(1)}, bf16[2,4,32,512]{3,2,1,0:T(8,128)(2,1)}, u32[]{:S(2)}) %copy-start) | copy-done | bytes 262168
  26.7 2.1 %own_whiten.1.refs_2_ = bf16[2,4,4,32,128]{4,3,2,1,0:T(8,128)(2,1)S(1)} custom-call(bf16[2,4,32,512]{3,2,1,0:T(8,128)(2,1)S(1)} %collective-permute-done.3.prev_ref, bf16[2,4,32,512]{3,2,1,0:T(8,128)(2,1)S(1)} %copy-done, bf16[2,4,32,512]{3,2,1,0:T(8,128)(2,1)S(1)} %collective-permute-done.4.next_ref, bf16[1024,256]{1,0:T(8,128)(2,1)S(1)} %get-tuple-element.14.weight_ref, ...), custom_call_target="tpu_custom_call" | custom-call | flops 1073741824 | bytes 3145728 | tf_op jit(solution)/shard_map/own_whiten/pallas_call | solution.py:339
  28.7 0.0 collective-permute-done.2.refs_3_
  28.8 1.7 %collective-permute-done.1.refs_2_ = bf16[1,4,2,32,128]{4,3,2,1,0:T(8,128)(2,1)S(1)} collective-permute-done((bf16[1,4,2,32,128]{4,3,2,1,0:T(8,128)(2,1)S(1)}, bf16[1,4,2,32,128]{4,3,2,1,0:T(8,128)(2,1)S(1)}, u32[]{:S(2)}, u32[]{:S(2)}) %collective-permute-start.1) | collective-permute-done | bytes 65568 | tf_op jit(solution)/shard_map/ppermute | solution.py:271
  30.4 0.0 collective-permute-done.refs_1_
  30.4 1.1 %column_whiten.1.refs_0_ = bf16[1,4,4,2,32,128]{5,4,3,2,1,0:T(8,128)(2,1)S(1)} custom-call(s32[6]{0:T(128)S(1)} %pad_add_fusion.params_ref, bf16[1,4,2,32,128]{4,3,2,1,0:T(8,128)(2,1)S(1)} %source_filter.1.refs_0_, bf16[1,4,2,32,128]{4,3,2,1,0:T(8,128)(2,1)S(1)} %collective-permute-done.refs_1_, ...), custom_call_target="tpu_custom_call" | custom-call | tf_op jit(solution)/shard_map/column_whiten/pallas_call | solution.py:361
  31.5 0.1 collective-permute-start.6
  31.6 0.5 collective-permute-start.5
  32.1 1.0 %collective-permute-done.6.refs_1_ = bf16[1,4,4,2,32,128]{5,4,3,2,1,0:T(8,128)(2,1)S(1)} collective-permute-done((bf16[1,4,4,2,32,128]{5,4,3,2,1,0:T(8,128)(2,1)S(1)}, bf16[1,4,4,2,32,128]{5,4,3,2,1,0:T(8,128)(2,1)S(1)}, u32[]{:S(2)}, u32[]{:S(2)}) %collective-permute-start.6) | collective-permute-done | bytes 262176 | tf_op jit(solution)/shard_map/ppermute | solution.py:271
  33.1 3.9 %cross.2.refs_3_ = bf16[2,128,4,32,128]{4,3,2,1,0:T(8,128)(2,1)S(1)} custom-call(s32[6]{0:T(128)S(1)} %pad_add_fusion.params_ref, bf16[1,4,4,2,32,128]{5,4,3,2,1,0:T(8,128)(2,1)S(1)} %column_whiten.1.refs_0_, bf16[1,4,4,2,32,128]{5,4,3,2,1,0:T(8,128)(2,1)S(1)} %collective-permute-done.6.refs_1_, bf16[2,4,4,32,128]{4,3,2,1,0:T(8,128)(2,1)S(1)} %own_whiten.1.refs_2_), custom_call_target="tpu_custom_call" | custom-call | flops 67108864 | bytes 16777216 | tf_op jit(solution)/shard_map/cross/pallas_call | solution.py:382
  37.0 3.3 %collective-permute-done.5.refs_0_ = bf16[1,4,4,2,32,128]{5,4,3,2,1,0:T(8,128)(2,1)S(1)} collective-permute-done((bf16[1,4,4,2,32,128]{5,4,3,2,1,0:T(8,128)(2,1)S(1)}, bf16[1,4,4,2,32,128]{5,4,3,2,1,0:T(8,128)(2,1)S(1)}, u32[]{:S(2)}, u32[]{:S(2)}) %collective-permute-start.5) | collective-permute-done | bytes 262176 | tf_op jit(solution)/shard_map/ppermute | solution.py:271
  40.3 0.0 collective-permute-start.7
  40.3 1.5 %collective-permute-done.7.refs_1_ = bf16[1,4,4,2,32,128]{5,4,3,2,1,0:T(8,128)(2,1)S(1)} collective-permute-done((bf16[1,4,4,2,32,128]{5,4,3,2,1,0:T(8,128)(2,1)S(1)}, bf16[1,4,4,2,32,128]{5,4,3,2,1,0:T(8,128)(2,1)S(1)}, u32[]{:S(2)}, u32[]{:S(2)}) %collective-permute-start.7) | collective-permute-done | bytes 262176 | tf_op jit(solution)/shard_map/ppermute | solution.py:271
  41.9 6.6 %cross.3 = bf16[2,128,32,512]{3,2,1,0:T(8,128)(2,1)} custom-call(s32[6]{0:T(128)S(1)} %pad_add_fusion.params_ref, bf16[1,4,4,2,32,128]{5,4,3,2,1,0:T(8,128)(2,1)S(1)} %collective-permute-done.5.refs_0_, bf16[1,4,4,2,32,128]{5,4,3,2,1,0:T(8,128)(2,1)S(1)} %collective-permute-done.7.refs_1_, bf16[2,4,4,32,128]{4,3,2,1,0:T(8,128)(2,1)S(1)} %own_whiten.1.refs_2_, ...), custom_call_target="tpu_custom_call" | custom-call | flops 67108864 | bytes 16777216 | tf_op jit(solution)/shard_map/cross/pallas_call | solution.py:382
Async XLA Ops:
  1.7 18.5 %all-to-all-start = ((bf16[16,80,128]{2,1,0:T(8,128)(2,1)}), bf16[16,80,128]{2,1,0:T(8,128)(2,1)S(1)}, u32[]{:S(2)}, u32[]{:S(2)}) async-start(bf16[16,80,128]{2,1,0:T(8,128)(2,1)} %split.1), calls=%async_computation | async-start | bytes 655360 | tf_op jit(solution)/shard_map/all_to_all | solution.py:295
  9.1 16.6 %collective-permute-start.3 = (bf16[2,4,32,512]{3,2,1,0:T(8,128)(2,1)}, bf16[2,4,32,512]{3,2,1,0:T(8,128)(2,1)S(1)}, u32[]{:S(2)}, u32[]{:S(2)}) collective-permute-start(bf16[2,4,32,512]{3,2,1,0:T(8,128)(2,1)} %cur_ref.1), channel_id=1, source_target_pairs={{0,1},{1,2},{2,3},{3,4},{4,5},{5,6},{6,7},{7,8},{8,9},{9,10},{10,1... | collective-permute-start | bytes 786440 | tf_op jit(solution)/shard_map/ppermute | solution.py:303
  11.5 14.3 %collective-permute-start.4 = (bf16[2,4,32,512]{3,2,1,0:T(8,128)(2,1)}, bf16[2,4,32,512]{3,2,1,0:T(8,128)(2,1)S(1)}, u32[]{:S(2)}, u32[]{:S(2)}) collective-permute-start(bf16[2,4,32,512]{3,2,1,0:T(8,128)(2,1)} %cur_ref.1), channel_id=1, source_target_pairs={{1,0},{2,1},{3,2},{4,3},{5,4},{6,5},{7,6},{8,7},{9,8},{10,9},{11,1... | collective-permute-start | bytes 786440 | tf_op jit(solution)/shard_map/ppermute | solution.py:304
  12.8 0.7 %copy-start.1 = (s32[4,32]{1,0:T(4,128)S(1)}, s32[4,32]{1,0:T(4,128)}, u32[]{:S(2)}) copy-start(s32[4,32]{1,0:T(4,128)} %flags_ref.3) | copy-start | bytes 1540
  13.4 0.7 %copy-start.2 = (f32[2,8,65]{2,1,0:T(8,128)S(1)}, f32[2,8,65]{2,1,0:T(8,128)}, u32[]{:S(2)}) copy-start(f32[2,8,65]{2,1,0:T(8,128)} %bank_ref.1) | copy-start | bytes 12484
  14.1 0.7 %copy-start.3 = (s32[512]{0:T(512)S(1)}, s32[512]{0:T(512)}, u32[]{:S(2)}) copy-start(s32[512]{0:T(512)} %param.8) | copy-start | bytes 6148
  14.8 0.7 %copy-start.4 = (s32[4,32]{1,0:T(4,128)S(1)}, s32[4,32]{1,0:T(4,128)}, u32[]{:S(2)}) copy-start(s32[4,32]{1,0:T(4,128)} %offset_ref.1) | copy-start | bytes 1540
  21.3 7.5 %collective-permute-start.2 = (bf16[1,4,2,32,128]{4,3,2,1,0:T(8,128)(2,1)S(1)}, bf16[1,4,2,32,128]{4,3,2,1,0:T(8,128)(2,1)S(1)}, u32[]{:S(2)}, u32[]{:S(2)}) collective-permute-start(bf16[1,4,2,32,128]{4,3,2,1,0:T(8,128)(2,1)S(1)} %source_filter.1.refs_0_), channel_id=1, source_target_pairs={{0,12},{1,13},{2,14},{3,15},{4,8},{5,9},{6,10},{7,11},{8,4},{9,5},... | collective-permute-start | bytes 196616 | tf_op jit(solution)/shard_map/ppermute | solution.py:271
  24.1 6.3 %collective-permute-start.1 = (bf16[1,4,2,32,128]{4,3,2,1,0:T(8,128)(2,1)S(1)}, bf16[1,4,2,32,128]{4,3,2,1,0:T(8,128)(2,1)S(1)}, u32[]{:S(2)}, u32[]{:S(2)}) collective-permute-start(bf16[1,4,2,32,128]{4,3,2,1,0:T(8,128)(2,1)S(1)} %source_filter.1.refs_0_), channel_id=1, source_target_pairs={{0,8},{1,9},{2,10},{3,11},{4,12},{5,13},{6,14},{7,15},{8,0},{9,1},... | collective-permute-start | bytes 196616 | tf_op jit(solution)/shard_map/ppermute | solution.py:271
  24.1 6.3 %collective-permute-start = (bf16[1,4,2,32,128]{4,3,2,1,0:T(8,128)(2,1)S(1)}, bf16[1,4,2,32,128]{4,3,2,1,0:T(8,128)(2,1)S(1)}, u32[]{:S(2)}, u32[]{:S(2)}) collective-permute-start(bf16[1,4,2,32,128]{4,3,2,1,0:T(8,128)(2,1)S(1)} %source_filter.1.refs_0_), channel_id=1, source_target_pairs={{0,4},{1,5},{2,6},{3,7},{4,0},{5,1},{6,2},{7,3},{8,12},{9,13},{10,... | collective-permute-start | bytes 196616 | tf_op jit(solution)/shard_map/ppermute | solution.py:271
  25.7 1.0 %copy-start = (bf16[2,4,32,512]{3,2,1,0:T(8,128)(2,1)S(1)}, bf16[2,4,32,512]{3,2,1,0:T(8,128)(2,1)}, u32[]{:S(2)}) copy-start(bf16[2,4,32,512]{3,2,1,0:T(8,128)(2,1)} %cur_ref.1) | copy-start | bytes 786436
  31.5 1.6 %collective-permute-start.6 = (bf16[1,4,4,2,32,128]{5,4,3,2,1,0:T(8,128)(2,1)S(1)}, bf16[1,4,4,2,32,128]{5,4,3,2,1,0:T(8,128)(2,1)S(1)}, u32[]{:S(2)}, u32[]{:S(2)}) collective-permute-start(bf16[1,4,4,2,32,128]{5,4,3,2,1,0:T(8,128)(2,1)S(1)} %column_whiten.1.refs_0_), channel_id=1, source_target_pairs={{0,1},{1,0},{2,3},{3,2},{4,5},{5,4},{6,7},{7,6},{8,9},{9,8},{10,11... | collective-permute-start | bytes 786440 | tf_op jit(solution)/shard_map/ppermute | solution.py:271
  31.6 8.7 %collective-permute-start.5 = (bf16[1,4,4,2,32,128]{5,4,3,2,1,0:T(8,128)(2,1)S(1)}, bf16[1,4,4,2,32,128]{5,4,3,2,1,0:T(8,128)(2,1)S(1)}, u32[]{:S(2)}, u32[]{:S(2)}) collective-permute-start(bf16[1,4,4,2,32,128]{5,4,3,2,1,0:T(8,128)(2,1)S(1)} %column_whiten.1.refs_0_), channel_id=1, source_target_pairs={{0,2},{1,3},{2,0},{3,1},{4,6},{5,7},{6,4},{7,5},{8,10},{9,11},{10,... | collective-permute-start | bytes 786440 | tf_op jit(solution)/shard_map/ppermute | solution.py:271
  40.3 1.5 %collective-permute-start.7 = (bf16[1,4,4,2,32,128]{5,4,3,2,1,0:T(8,128)(2,1)S(1)}, bf16[1,4,4,2,32,128]{5,4,3,2,1,0:T(8,128)(2,1)S(1)}, u32[]{:S(2)}, u32[]{:S(2)}) collective-permute-start(bf16[1,4,4,2,32,128]{5,4,3,2,1,0:T(8,128)(2,1)S(1)} %collective-permute-done.5.refs_0_), channel_id=1, source_target_pairs={{0,1},{1,0},{2,3},{3,2},{4,5},{5,4},{6,7},{7,6},{8,9},{9,8},{10,11... | collective-permute-start | bytes 786440 | tf_op jit(solution)/shard_map/ppermute | solution.py:271

commit v17 on v16

--- a/solution.py
+++ b/solution.py
@@ -11,7 +11,7 @@
 LANES = 128
 WATER = 0.05
 SRC_STEP = 16
-SLOTS = 2
+SLOTS = 4
 
 
 def room(mib):

time: 48.9 us -> 47.7 us (0.975)
  Pallas kernels: 16.6 us -> 15.4 us
    pallas_call x2, Pallas kernels: 10.4 us -> 9.25 us  [cross(): pl.pallas_call(functools.partial(cross_kernel, masks=masks, added=len(ear...]
where the time goes in v17:
time: 47.7 us; the launch traced here: 47.2 us
  starting transfers between devices  16 us (34%)
  Pallas kernels  15.4 us (32%)
  waiting for transfers between devices  11.3 us (24%)
  local copies, waits for them, and re-layouts  3.68 us (8%)
  other arithmetic  0.74 us (2%)
    pallas_call x2, Pallas kernels, cross(): pl.pallas_call(functools.partial(cross_kernel, masks=masks, added=len(ear...  9.25 us
    ppermute x6, waiting for transfers between devices, swap(): return lax.ppermute(x, 'chan', [(i, i ^ mask) for i in range(n_chan)])  7.58 us
    all_to_all x1, starting transfers between devices, body(): held = lax.all_to_all(split, 'chan', 0, 0)[:, None]  7.39 us
    ppermute x6, starting transfers between devices, swap(): return lax.ppermute(x, 'chan', [(i, i ^ mask) for i in range(n_chan)])  5 us
    all_to_all x1, waiting for transfers between devices, body(): held = lax.all_to_all(split, 'chan', 0, 0)[:, None]  3.75 us
    unnamed x10, local copies, waits for them, and re-layouts  3.68 us
    ppermute x1, starting transfers between devices, body(): before = lax.ppermute(spectra, 'chan', [(i, i + 1) for i in range(ends)])  2.32 us
    pallas_call x1, Pallas kernels, body(): pl.pallas_call(own_kernel, out_shape=jax.ShapeDtypeStruct((2, tiles, win,...  2.07 us
  transfers between devices with their start and end apart: 9, of which 5 were waited for; matrix products, arithmetic and copies ran while one was open for 2% of the time, Pallas kernels for 15%

profile of v17, /device:TPU:0, one launch (start us, length us, event | category | flops | bytes accessed | tf_op | source)
XLA Modules:
  0.0 47.2 jit_solution(1855498422812804351)
XLA Ops:
  0.0 1.7 %split.1 = bf16[16,80,128]{2,1,0:T(8,128)(2,1)} custom-call(bf16[2,4,32,512]{3,2,1,0:T(8,128)(2,1)} %cur_ref.1, s32[4,32]{1,0:T(4,128)} %flags_ref.3), custom_call_target="tpu_custom_call" | custom-call | tf_op jit(solution)/shard_map/split/pallas_call | solution.py:288
  1.7 7.4 %all-to-all-start = ((bf16[16,80,128]{2,1,0:T(8,128)(2,1)}), bf16[16,80,128]{2,1,0:T(8,128)(2,1)S(1)}, u32[]{:S(2)}, u32[]{:S(2)}) async-start(bf16[16,80,128]{2,1,0:T(8,128)(2,1)} %split.1), calls=%async_computation | async-start | bytes 655360 | tf_op jit(solution)/shard_map/all_to_all | solution.py:295
  9.1 2.3 %collective-permute-start.3 = (bf16[2,4,32,512]{3,2,1,0:T(8,128)(2,1)}, bf16[2,4,32,512]{3,2,1,0:T(8,128)(2,1)S(1)}, u32[]{:S(2)}, u32[]{:S(2)}) collective-permute-start(bf16[2,4,32,512]{3,2,1,0:T(8,128)(2,1)} %cur_ref.1), channel_id=1, source_target_pairs={{0,1},{1,2},{2,3},{3,4},{4,5},{5,6},{6,7},{7,8},{8,9},{9,10},{10,1... | collective-permute-start | bytes 786440 | tf_op jit(solution)/shard_map/ppermute | solution.py:303
  11.5 1.3 %collective-permute-start.4 = (bf16[2,4,32,512]{3,2,1,0:T(8,128)(2,1)}, bf16[2,4,32,512]{3,2,1,0:T(8,128)(2,1)S(1)}, u32[]{:S(2)}, u32[]{:S(2)}) collective-permute-start(bf16[2,4,32,512]{3,2,1,0:T(8,128)(2,1)} %cur_ref.1), channel_id=1, source_target_pairs={{1,0},{2,1},{3,2},{4,3},{5,4},{6,5},{7,6},{8,7},{9,8},{10,9},{11,1... | collective-permute-start | bytes 786440 | tf_op jit(solution)/shard_map/ppermute | solution.py:304
  12.8 0.0 copy-start.1
  12.8 0.7 %copy-done.1 = s32[4,32]{1,0:T(4,128)S(1)} copy-done((s32[4,32]{1,0:T(4,128)S(1)}, s32[4,32]{1,0:T(4,128)}, u32[]{:S(2)}) %copy-start.1) | copy-done | bytes 536
  13.4 0.0 copy-start.2
  13.4 0.7 %copy-done.2 = f32[2,8,65]{2,1,0:T(8,128)S(1)} copy-done((f32[2,8,65]{2,1,0:T(8,128)S(1)}, f32[2,8,65]{2,1,0:T(8,128)}, u32[]{:S(2)}) %copy-start.2) | copy-done | bytes 4184
  14.1 0.0 copy-start.3
  14.1 0.7 %copy-done.3 = s32[512]{0:T(512)S(1)} copy-done((s32[512]{0:T(512)S(1)}, s32[512]{0:T(512)}, u32[]{:S(2)}) %copy-start.3) | copy-done | bytes 2072
  14.8 0.0 copy-start.4
  14.8 0.7 %copy-done.4 = s32[4,32]{1,0:T(4,128)S(1)} copy-done((s32[4,32]{1,0:T(4,128)S(1)}, s32[4,32]{1,0:T(4,128)}, u32[]{:S(2)}) %copy-start.4) | copy-done | bytes 536
  15.5 0.2 prep.1
  15.8 0.7 %pad_add_fusion.params_ref = s32[6]{0:T(128)S(1)} fusion(s32[4]{0:T(128)} %param.10, s32[1]{0:T(128)} %bitcast.1, s32[1]{0:T(128)} %bitcast), kind=kLoop, calls=%fused_computation | loop fusion | flops 12 | bytes 48 | tf_op jit(solution)/shard_map/concatenate | solution.py:300
  16.5 3.8 %all-to-all-done = bf16[16,80,128]{2,1,0:T(8,128)(2,1)S(1)} async-done(((bf16[16,80,128]{2,1,0:T(8,128)(2,1)}), bf16[16,80,128]{2,1,0:T(8,128)(2,1)S(1)}, u32[]{:S(2)}, u32[]{:S(2)}) %all-to-all-start) | async-done | bytes 327712 | tf_op jit(solution)/shard_map/all_to_all | solution.py:295
  20.3 1.0 %source_filter.1.refs_0_ = bf16[1,4,2,32,128]{4,3,2,1,0:T(8,128)(2,1)S(1)} custom-call(s32[6]{0:T(128)S(1)} %pad_add_fusion.params_ref, bf16[16,1,80,128]{3,2,1,0:T(8,128)(2,1)S(1)} %bitcast.4, bf16[1024,256]{1,0:T(8,128)(2,1)S(1)} %get-tuple-element.14.weight_ref, s32[4,1,128]{2,1,0:T(1,128)S(1)} %get-tuple-element.15.index_ref), custom_call_target="tpu_custom_call" | custom-call | tf_op jit(solution)/shard_map/source_filter/pallas_call | solution.py:321
  21.3 2.9 %collective-permute-start.2 = (bf16[1,4,2,32,128]{4,3,2,1,0:T(8,128)(2,1)S(1)}, bf16[1,4,2,32,128]{4,3,2,1,0:T(8,128)(2,1)S(1)}, u32[]{:S(2)}, u32[]{:S(2)}) collective-permute-start(bf16[1,4,2,32,128]{4,3,2,1,0:T(8,128)(2,1)S(1)} %source_filter.1.refs_0_), channel_id=1, source_target_pairs={{0,12},{1,13},{2,14},{3,15},{4,8},{5,9},{6,10},{7,11},{8,4},{9,5},... | collective-permute-start | bytes 196616 | tf_op jit(solution)/shard_map/ppermute | solution.py:271
  24.1 0.0 collective-permute-start.1
  24.1 1.6 %collective-permute-start = (bf16[1,4,2,32,128]{4,3,2,1,0:T(8,128)(2,1)S(1)}, bf16[1,4,2,32,128]{4,3,2,1,0:T(8,128)(2,1)S(1)}, u32[]{:S(2)}, u32[]{:S(2)}) collective-permute-start(bf16[1,4,2,32,128]{4,3,2,1,0:T(8,128)(2,1)S(1)} %source_filter.1.refs_0_), channel_id=1, source_target_pairs={{0,4},{1,5},{2,6},{3,7},{4,0},{5,1},{6,2},{7,3},{8,12},{9,13},{10,... | collective-permute-start | bytes 196616 | tf_op jit(solution)/shard_map/ppermute | solution.py:271
  25.7 0.0 collective-permute-done.3.prev_ref
  25.7 0.0 collective-permute-done.4.next_ref
  25.7 0.0 copy-start
  25.7 0.9 %copy-done = bf16[2,4,32,512]{3,2,1,0:T(8,128)(2,1)S(1)} copy-done((bf16[2,4,32,512]{3,2,1,0:T(8,128)(2,1)S(1)}, bf16[2,4,32,512]{3,2,1,0:T(8,128)(2,1)}, u32[]{:S(2)}) %copy-start) | copy-done | bytes 262168
  26.7 2.1 %own_whiten.1.refs_2_ = bf16[2,4,4,32,128]{4,3,2,1,0:T(8,128)(2,1)S(1)} custom-call(bf16[2,4,32,512]{3,2,1,0:T(8,128)(2,1)S(1)} %collective-permute-done.3.prev_ref, bf16[2,4,32,512]{3,2,1,0:T(8,128)(2,1)S(1)} %copy-done, bf16[2,4,32,512]{3,2,1,0:T(8,128)(2,1)S(1)} %collective-permute-done.4.next_ref, bf16[1024,256]{1,0:T(8,128)(2,1)S(1)} %get-tuple-element.14.weight_ref, ...), custom_call_target="tpu_custom_call" | custom-call | flops 1073741824 | bytes 3145728 | tf_op jit(solution)/shard_map/own_whiten/pallas_call | solution.py:339
  28.7 0.0 collective-permute-done.2.refs_3_
  28.8 1.7 %collective-permute-done.1.refs_2_ = bf16[1,4,2,32,128]{4,3,2,1,0:T(8,128)(2,1)S(1)} collective-permute-done((bf16[1,4,2,32,128]{4,3,2,1,0:T(8,128)(2,1)S(1)}, bf16[1,4,2,32,128]{4,3,2,1,0:T(8,128)(2,1)S(1)}, u32[]{:S(2)}, u32[]{:S(2)}) %collective-permute-start.1) | collective-permute-done | bytes 65568 | tf_op jit(solution)/shard_map/ppermute | solution.py:271
  30.4 0.0 collective-permute-done.refs_1_
  30.4 1.1 %column_whiten.1.refs_0_ = bf16[1,4,4,2,32,128]{5,4,3,2,1,0:T(8,128)(2,1)S(1)} custom-call(s32[6]{0:T(128)S(1)} %pad_add_fusion.params_ref, bf16[1,4,2,32,128]{4,3,2,1,0:T(8,128)(2,1)S(1)} %source_filter.1.refs_0_, bf16[1,4,2,32,128]{4,3,2,1,0:T(8,128)(2,1)S(1)} %collective-permute-done.refs_1_, ...), custom_call_target="tpu_custom_call" | custom-call | tf_op jit(solution)/shard_map/column_whiten/pallas_call | solution.py:361
  31.5 0.1 collective-permute-start.6
  31.6 0.5 collective-permute-start.5
  32.1 1.1 %collective-permute-done.6.refs_1_ = bf16[1,4,4,2,32,128]{5,4,3,2,1,0:T(8,128)(2,1)S(1)} collective-permute-done((bf16[1,4,4,2,32,128]{5,4,3,2,1,0:T(8,128)(2,1)S(1)}, bf16[1,4,4,2,32,128]{5,4,3,2,1,0:T(8,128)(2,1)S(1)}, u32[]{:S(2)}, u32[]{:S(2)}) %collective-permute-start.6) | collective-permute-done | bytes 262176 | tf_op jit(solution)/shard_map/ppermute | solution.py:271
  33.1 3.9 %cross.2.refs_3_ = bf16[2,128,4,32,128]{4,3,2,1,0:T(8,128)(2,1)S(1)} custom-call(s32[6]{0:T(128)S(1)} %pad_add_fusion.params_ref, bf16[1,4,4,2,32,128]{5,4,3,2,1,0:T(8,128)(2,1)S(1)} %column_whiten.1.refs_0_, bf16[1,4,4,2,32,128]{5,4,3,2,1,0:T(8,128)(2,1)S(1)} %collective-permute-done.6.refs_1_, bf16[2,4,4,32,128]{4,3,2,1,0:T(8,128)(2,1)S(1)} %own_whiten.1.refs_2_), custom_call_target="tpu_custom_call" | custom-call | flops 67108864 | bytes 16777216 | tf_op jit(solution)/shard_map/cross/pallas_call | solution.py:382
  37.0 3.3 %collective-permute-done.5.refs_0_ = bf16[1,4,4,2,32,128]{5,4,3,2,1,0:T(8,128)(2,1)S(1)} collective-permute-done((bf16[1,4,4,2,32,128]{5,4,3,2,1,0:T(8,128)(2,1)S(1)}, bf16[1,4,4,2,32,128]{5,4,3,2,1,0:T(8,128)(2,1)S(1)}, u32[]{:S(2)}, u32[]{:S(2)}) %collective-permute-start.5) | collective-permute-done | bytes 262176 | tf_op jit(solution)/shard_map/ppermute | solution.py:271
  40.3 0.0 collective-permute-start.7
  40.3 1.5 %collective-permute-done.7.refs_1_ = bf16[1,4,4,2,32,128]{5,4,3,2,1,0:T(8,128)(2,1)S(1)} collective-permute-done((bf16[1,4,4,2,32,128]{5,4,3,2,1,0:T(8,128)(2,1)S(1)}, bf16[1,4,4,2,32,128]{5,4,3,2,1,0:T(8,128)(2,1)S(1)}, u32[]{:S(2)}, u32[]{:S(2)}) %collective-permute-start.7) | collective-permute-done | bytes 262176 | tf_op jit(solution)/shard_map/ppermute | solution.py:271
  41.9 5.4 %cross.3 = bf16[2,128,32,512]{3,2,1,0:T(8,128)(2,1)} custom-call(s32[6]{0:T(128)S(1)} %pad_add_fusion.params_ref, bf16[1,4,4,2,32,128]{5,4,3,2,1,0:T(8,128)(2,1)S(1)} %collective-permute-done.5.refs_0_, bf16[1,4,4,2,32,128]{5,4,3,2,1,0:T(8,128)(2,1)S(1)} %collective-permute-done.7.refs_1_, bf16[2,4,4,32,128]{4,3,2,1,0:T(8,128)(2,1)S(1)} %own_whiten.1.refs_2_, ...), custom_call_target="tpu_custom_call" | custom-call | flops 67108864 | bytes 16777216 | tf_op jit(solution)/shard_map/cross/pallas_call | solution.py:382
Async XLA Ops:
  1.7 18.5 %all-to-all-start = ((bf16[16,80,128]{2,1,0:T(8,128)(2,1)}), bf16[16,80,128]{2,1,0:T(8,128)(2,1)S(1)}, u32[]{:S(2)}, u32[]{:S(2)}) async-start(bf16[16,80,128]{2,1,0:T(8,128)(2,1)} %split.1), calls=%async_computation | async-start | bytes 655360 | tf_op jit(solution)/shard_map/all_to_all | solution.py:295
  9.1 16.6 %collective-permute-start.3 = (bf16[2,4,32,512]{3,2,1,0:T(8,128)(2,1)}, bf16[2,4,32,512]{3,2,1,0:T(8,128)(2,1)S(1)}, u32[]{:S(2)}, u32[]{:S(2)}) collective-permute-start(bf16[2,4,32,512]{3,2,1,0:T(8,128)(2,1)} %cur_ref.1), channel_id=1, source_target_pairs={{0,1},{1,2},{2,3},{3,4},{4,5},{5,6},{6,7},{7,8},{8,9},{9,10},{10,1... | collective-permute-start | bytes 786440 | tf_op jit(solution)/shard_map/ppermute | solution.py:303
  11.5 14.3 %collective-permute-start.4 = (bf16[2,4,32,512]{3,2,1,0:T(8,128)(2,1)}, bf16[2,4,32,512]{3,2,1,0:T(8,128)(2,1)S(1)}, u32[]{:S(2)}, u32[]{:S(2)}) collective-permute-start(bf16[2,4,32,512]{3,2,1,0:T(8,128)(2,1)} %cur_ref.1), channel_id=1, source_target_pairs={{1,0},{2,1},{3,2},{4,3},{5,4},{6,5},{7,6},{8,7},{9,8},{10,9},{11,1... | collective-permute-start | bytes 786440 | tf_op jit(solution)/shard_map/ppermute | solution.py:304
  12.8 0.7 %copy-start.1 = (s32[4,32]{1,0:T(4,128)S(1)}, s32[4,32]{1,0:T(4,128)}, u32[]{:S(2)}) copy-start(s32[4,32]{1,0:T(4,128)} %flags_ref.3) | copy-start | bytes 1540
  13.4 0.7 %copy-start.2 = (f32[2,8,65]{2,1,0:T(8,128)S(1)}, f32[2,8,65]{2,1,0:T(8,128)}, u32[]{:S(2)}) copy-start(f32[2,8,65]{2,1,0:T(8,128)} %bank_ref.1) | copy-start | bytes 12484
  14.1 0.7 %copy-start.3 = (s32[512]{0:T(512)S(1)}, s32[512]{0:T(512)}, u32[]{:S(2)}) copy-start(s32[512]{0:T(512)} %param.8) | copy-start | bytes 6148
  14.8 0.7 %copy-start.4 = (s32[4,32]{1,0:T(4,128)S(1)}, s32[4,32]{1,0:T(4,128)}, u32[]{:S(2)}) copy-start(s32[4,32]{1,0:T(4,128)} %offset_ref.1) | copy-start | bytes 1540
  21.3 7.5 %collective-permute-start.2 = (bf16[1,4,2,32,128]{4,3,2,1,0:T(8,128)(2,1)S(1)}, bf16[1,4,2,32,128]{4,3,2,1,0:T(8,128)(2,1)S(1)}, u32[]{:S(2)}, u32[]{:S(2)}) collective-permute-start(bf16[1,4,2,32,128]{4,3,2,1,0:T(8,128)(2,1)S(1)} %source_filter.1.refs_0_), channel_id=1, source_target_pairs={{0,12},{1,13},{2,14},{3,15},{4,8},{5,9},{6,10},{7,11},{8,4},{9,5},... | collective-permute-start | bytes 196616 | tf_op jit(solution)/shard_map/ppermute | solution.py:271
  24.1 6.3 %collective-permute-start.1 = (bf16[1,4,2,32,128]{4,3,2,1,0:T(8,128)(2,1)S(1)}, bf16[1,4,2,32,128]{4,3,2,1,0:T(8,128)(2,1)S(1)}, u32[]{:S(2)}, u32[]{:S(2)}) collective-permute-start(bf16[1,4,2,32,128]{4,3,2,1,0:T(8,128)(2,1)S(1)} %source_filter.1.refs_0_), channel_id=1, source_target_pairs={{0,8},{1,9},{2,10},{3,11},{4,12},{5,13},{6,14},{7,15},{8,0},{9,1},... | collective-permute-start | bytes 196616 | tf_op jit(solution)/shard_map/ppermute | solution.py:271
  24.1 6.3 %collective-permute-start = (bf16[1,4,2,32,128]{4,3,2,1,0:T(8,128)(2,1)S(1)}, bf16[1,4,2,32,128]{4,3,2,1,0:T(8,128)(2,1)S(1)}, u32[]{:S(2)}, u32[]{:S(2)}) collective-permute-start(bf16[1,4,2,32,128]{4,3,2,1,0:T(8,128)(2,1)S(1)} %source_filter.1.refs_0_), channel_id=1, source_target_pairs={{0,4},{1,5},{2,6},{3,7},{4,0},{5,1},{6,2},{7,3},{8,12},{9,13},{10,... | collective-permute-start | bytes 196616 | tf_op jit(solution)/shard_map/ppermute | solution.py:271
  25.7 1.0 %copy-start = (bf16[2,4,32,512]{3,2,1,0:T(8,128)(2,1)S(1)}, bf16[2,4,32,512]{3,2,1,0:T(8,128)(2,1)}, u32[]{:S(2)}) copy-start(bf16[2,4,32,512]{3,2,1,0:T(8,128)(2,1)} %cur_ref.1) | copy-start | bytes 786436
  31.5 1.6 %collective-permute-start.6 = (bf16[1,4,4,2,32,128]{5,4,3,2,1,0:T(8,128)(2,1)S(1)}, bf16[1,4,4,2,32,128]{5,4,3,2,1,0:T(8,128)(2,1)S(1)}, u32[]{:S(2)}, u32[]{:S(2)}) collective-permute-start(bf16[1,4,4,2,32,128]{5,4,3,2,1,0:T(8,128)(2,1)S(1)} %column_whiten.1.refs_0_), channel_id=1, source_target_pairs={{0,1},{1,0},{2,3},{3,2},{4,5},{5,4},{6,7},{7,6},{8,9},{9,8},{10,11... | collective-permute-start | bytes 786440 | tf_op jit(solution)/shard_map/ppermute | solution.py:271
  31.6 8.7 %collective-permute-start.5 = (bf16[1,4,4,2,32,128]{5,4,3,2,1,0:T(8,128)(2,1)S(1)}, bf16[1,4,4,2,32,128]{5,4,3,2,1,0:T(8,128)(2,1)S(1)}, u32[]{:S(2)}, u32[]{:S(2)}) collective-permute-start(bf16[1,4,4,2,32,128]{5,4,3,2,1,0:T(8,128)(2,1)S(1)} %column_whiten.1.refs_0_), channel_id=1, source_target_pairs={{0,2},{1,3},{2,0},{3,1},{4,6},{5,7},{6,4},{7,5},{8,10},{9,11},{10,... | collective-permute-start | bytes 786440 | tf_op jit(solution)/shard_map/ppermute | solution.py:271
  40.3 1.5 %collective-permute-start.7 = (bf16[1,4,4,2,32,128]{5,4,3,2,1,0:T(8,128)(2,1)S(1)}, bf16[1,4,4,2,32,128]{5,4,3,2,1,0:T(8,128)(2,1)S(1)}, u32[]{:S(2)}, u32[]{:S(2)}) collective-permute-start(bf16[1,4,4,2,32,128]{5,4,3,2,1,0:T(8,128)(2,1)S(1)} %collective-permute-done.5.refs_0_), channel_id=1, source_target_pairs={{0,1},{1,0},{2,3},{3,2},{4,5},{5,4},{6,7},{7,6},{8,9},{9,8},{10,11... | collective-permute-start | bytes 786440 | tf_op jit(solution)/shard_map/ppermute | solution.py:271

commit v18 on v17

--- a/solution.py
+++ b/solution.py
@@ -11,7 +11,7 @@
 LANES = 128
 WATER = 0.05
 SRC_STEP = 16
-SLOTS = 4
+SLOTS = 5
 
 
 def room(mib):

time: 47.7 us -> 47.9 us (level)
  no operation moved by 1% of the time
where the time goes in v18:
time: 47.9 us; the launch traced here: 47.5 us
  starting transfers between devices  16 us (33%)
  Pallas kernels  15.6 us (33%)
  waiting for transfers between devices  11.4 us (24%)
  local copies, waits for them, and re-layouts  3.68 us (8%)
  other arithmetic  0.74 us (2%)
    pallas_call x2, Pallas kernels, cross(): pl.pallas_call(functools.partial(cross_kernel, masks=masks, added=len(ear...  9.47 us
    ppermute x6, waiting for transfers between devices, swap(): return lax.ppermute(x, 'chan', [(i, i ^ mask) for i in range(n_chan)])  7.6 us
    all_to_all x1, starting transfers between devices, body(): held = lax.all_to_all(split, 'chan', 0, 0)[:, None]  7.39 us
    ppermute x6, starting transfers between devices, swap(): return lax.ppermute(x, 'chan', [(i, i ^ mask) for i in range(n_chan)])  4.99 us
    all_to_all x1, waiting for transfers between devices, body(): held = lax.all_to_all(split, 'chan', 0, 0)[:, None]  3.75 us
    unnamed x10, local copies, waits for them, and re-layouts  3.68 us
    ppermute x1, starting transfers between devices, body(): before = lax.ppermute(spectra, 'chan', [(i, i + 1) for i in range(ends)])  2.32 us
    pallas_call x1, Pallas kernels, body(): pl.pallas_call(own_kernel, out_shape=jax.ShapeDtypeStruct((2, tiles, win,...  2.06 us
  transfers between devices with their start and end apart: 9, of which 5 were waited for; matrix products, arithmetic and copies ran while one was open for 2% of the time, Pallas kernels for 15%

profile of v18, /device:TPU:0, one launch (start us, length us, event | category | flops | bytes accessed | tf_op | source)
XLA Modules:
  0.0 47.5 jit_solution(14244756922545589143)
XLA Ops:
  0.0 1.7 %split.1 = bf16[16,80,128]{2,1,0:T(8,128)(2,1)} custom-call(bf16[2,4,32,512]{3,2,1,0:T(8,128)(2,1)} %cur_ref.1, s32[4,32]{1,0:T(4,128)} %flags_ref.3), custom_call_target="tpu_custom_call" | custom-call | tf_op jit(solution)/shard_map/split/pallas_call | solution.py:288
  1.7 7.4 %all-to-all-start = ((bf16[16,80,128]{2,1,0:T(8,128)(2,1)}), bf16[16,80,128]{2,1,0:T(8,128)(2,1)S(1)}, u32[]{:S(2)}, u32[]{:S(2)}) async-start(bf16[16,80,128]{2,1,0:T(8,128)(2,1)} %split.1), calls=%async_computation | async-start | bytes 655360 | tf_op jit(solution)/shard_map/all_to_all | solution.py:295
  9.1 2.3 %collective-permute-start.3 = (bf16[2,4,32,512]{3,2,1,0:T(8,128)(2,1)}, bf16[2,4,32,512]{3,2,1,0:T(8,128)(2,1)S(1)}, u32[]{:S(2)}, u32[]{:S(2)}) collective-permute-start(bf16[2,4,32,512]{3,2,1,0:T(8,128)(2,1)} %cur_ref.1), channel_id=1, source_target_pairs={{0,1},{1,2},{2,3},{3,4},{4,5},{5,6},{6,7},{7,8},{8,9},{9,10},{10,1... | collective-permute-start | bytes 786440 | tf_op jit(solution)/shard_map/ppermute | solution.py:303
  11.5 1.3 %collective-permute-start.4 = (bf16[2,4,32,512]{3,2,1,0:T(8,128)(2,1)}, bf16[2,4,32,512]{3,2,1,0:T(8,128)(2,1)S(1)}, u32[]{:S(2)}, u32[]{:S(2)}) collective-permute-start(bf16[2,4,32,512]{3,2,1,0:T(8,128)(2,1)} %cur_ref.1), channel_id=1, source_target_pairs={{1,0},{2,1},{3,2},{4,3},{5,4},{6,5},{7,6},{8,7},{9,8},{10,9},{11,1... | collective-permute-start | bytes 786440 | tf_op jit(solution)/shard_map/ppermute | solution.py:304
  12.8 0.0 copy-start.1
  12.8 0.7 %copy-done.1 = s32[4,32]{1,0:T(4,128)S(1)} copy-done((s32[4,32]{1,0:T(4,128)S(1)}, s32[4,32]{1,0:T(4,128)}, u32[]{:S(2)}) %copy-start.1) | copy-done | bytes 536
  13.4 0.0 copy-start.2
  13.4 0.7 %copy-done.2 = f32[2,8,65]{2,1,0:T(8,128)S(1)} copy-done((f32[2,8,65]{2,1,0:T(8,128)S(1)}, f32[2,8,65]{2,1,0:T(8,128)}, u32[]{:S(2)}) %copy-start.2) | copy-done | bytes 4184
  14.1 0.0 copy-start.3
  14.1 0.7 %copy-done.3 = s32[512]{0:T(512)S(1)} copy-done((s32[512]{0:T(512)S(1)}, s32[512]{0:T(512)}, u32[]{:S(2)}) %copy-start.3) | copy-done | bytes 2072
  14.8 0.0 copy-start.4
  14.8 0.7 %copy-done.4 = s32[4,32]{1,0:T(4,128)S(1)} copy-done((s32[4,32]{1,0:T(4,128)S(1)}, s32[4,32]{1,0:T(4,128)}, u32[]{:S(2)}) %copy-start.4) | copy-done | bytes 536
  15.5 0.2 prep.1
  15.8 0.7 %pad_add_fusion.params_ref = s32[6]{0:T(128)S(1)} fusion(s32[4]{0:T(128)} %param.10, s32[1]{0:T(128)} %bitcast.1, s32[1]{0:T(128)} %bitcast), kind=kLoop, calls=%fused_computation | loop fusion | flops 12 | bytes 48 | tf_op jit(solution)/shard_map/concatenate | solution.py:300
  16.5 3.8 %all-to-all-done = bf16[16,80,128]{2,1,0:T(8,128)(2,1)S(1)} async-done(((bf16[16,80,128]{2,1,0:T(8,128)(2,1)}), bf16[16,80,128]{2,1,0:T(8,128)(2,1)S(1)}, u32[]{:S(2)}, u32[]{:S(2)}) %all-to-all-start) | async-done | bytes 327712 | tf_op jit(solution)/shard_map/all_to_all | solution.py:295
  20.3 1.0 %source_filter.1.refs_0_ = bf16[1,4,2,32,128]{4,3,2,1,0:T(8,128)(2,1)S(1)} custom-call(s32[6]{0:T(128)S(1)} %pad_add_fusion.params_ref, bf16[16,1,80,128]{3,2,1,0:T(8,128)(2,1)S(1)} %bitcast.4, bf16[1024,256]{1,0:T(8,128)(2,1)S(1)} %get-tuple-element.14.weight_ref, s32[4,1,128]{2,1,0:T(1,128)S(1)} %get-tuple-element.15.index_ref), custom_call_target="tpu_custom_call" | custom-call | tf_op jit(solution)/shard_map/source_filter/pallas_call | solution.py:321
  21.3 2.9 %collective-permute-start.2 = (bf16[1,4,2,32,128]{4,3,2,1,0:T(8,128)(2,1)S(1)}, bf16[1,4,2,32,128]{4,3,2,1,0:T(8,128)(2,1)S(1)}, u32[]{:S(2)}, u32[]{:S(2)}) collective-permute-start(bf16[1,4,2,32,128]{4,3,2,1,0:T(8,128)(2,1)S(1)} %source_filter.1.refs_0_), channel_id=1, source_target_pairs={{0,12},{1,13},{2,14},{3,15},{4,8},{5,9},{6,10},{7,11},{8,4},{9,5},... | collective-permute-start | bytes 196616 | tf_op jit(solution)/shard_map/ppermute | solution.py:271
  24.1 0.0 collective-permute-start.1
  24.1 1.6 %collective-permute-start = (bf16[1,4,2,32,128]{4,3,2,1,0:T(8,128)(2,1)S(1)}, bf16[1,4,2,32,128]{4,3,2,1,0:T(8,128)(2,1)S(1)}, u32[]{:S(2)}, u32[]{:S(2)}) collective-permute-start(bf16[1,4,2,32,128]{4,3,2,1,0:T(8,128)(2,1)S(1)} %source_filter.1.refs_0_), channel_id=1, source_target_pairs={{0,4},{1,5},{2,6},{3,7},{4,0},{5,1},{6,2},{7,3},{8,12},{9,13},{10,... | collective-permute-start | bytes 196616 | tf_op jit(solution)/shard_map/ppermute | solution.py:271
  25.7 0.0 collective-permute-done.3.prev_ref
  25.7 0.0 collective-permute-done.4.next_ref
  25.7 0.0 copy-start
  25.7 0.9 %copy-done = bf16[2,4,32,512]{3,2,1,0:T(8,128)(2,1)S(1)} copy-done((bf16[2,4,32,512]{3,2,1,0:T(8,128)(2,1)S(1)}, bf16[2,4,32,512]{3,2,1,0:T(8,128)(2,1)}, u32[]{:S(2)}) %copy-start) | copy-done | bytes 262168
  26.7 2.1 %own_whiten.1.refs_2_ = bf16[2,4,4,32,128]{4,3,2,1,0:T(8,128)(2,1)S(1)} custom-call(bf16[2,4,32,512]{3,2,1,0:T(8,128)(2,1)S(1)} %collective-permute-done.3.prev_ref, bf16[2,4,32,512]{3,2,1,0:T(8,128)(2,1)S(1)} %copy-done, bf16[2,4,32,512]{3,2,1,0:T(8,128)(2,1)S(1)} %collective-permute-done.4.next_ref, bf16[1024,256]{1,0:T(8,128)(2,1)S(1)} %get-tuple-element.14.weight_ref, ...), custom_call_target="tpu_custom_call" | custom-call | flops 1073741824 | bytes 3145728 | tf_op jit(solution)/shard_map/own_whiten/pallas_call | solution.py:339
  28.7 0.0 collective-permute-done.2.refs_3_
  28.7 1.7 %collective-permute-done.1.refs_2_ = bf16[1,4,2,32,128]{4,3,2,1,0:T(8,128)(2,1)S(1)} collective-permute-done((bf16[1,4,2,32,128]{4,3,2,1,0:T(8,128)(2,1)S(1)}, bf16[1,4,2,32,128]{4,3,2,1,0:T(8,128)(2,1)S(1)}, u32[]{:S(2)}, u32[]{:S(2)}) %collective-permute-start.1) | collective-permute-done | bytes 65568 | tf_op jit(solution)/shard_map/ppermute | solution.py:271
  30.4 0.0 collective-permute-done.refs_1_
  30.4 1.1 %column_whiten.1.refs_0_ = bf16[1,4,4,2,32,128]{5,4,3,2,1,0:T(8,128)(2,1)S(1)} custom-call(s32[6]{0:T(128)S(1)} %pad_add_fusion.params_ref, bf16[1,4,2,32,128]{4,3,2,1,0:T(8,128)(2,1)S(1)} %source_filter.1.refs_0_, bf16[1,4,2,32,128]{4,3,2,1,0:T(8,128)(2,1)S(1)} %collective-permute-done.refs_1_, ...), custom_call_target="tpu_custom_call" | custom-call | tf_op jit(solution)/shard_map/column_whiten/pallas_call | solution.py:361
  31.5 0.1 collective-permute-start.6
  31.6 0.5 collective-permute-start.5
  32.1 1.1 %collective-permute-done.6.refs_1_ = bf16[1,4,4,2,32,128]{5,4,3,2,1,0:T(8,128)(2,1)S(1)} collective-permute-done((bf16[1,4,4,2,32,128]{5,4,3,2,1,0:T(8,128)(2,1)S(1)}, bf16[1,4,4,2,32,128]{5,4,3,2,1,0:T(8,128)(2,1)S(1)}, u32[]{:S(2)}, u32[]{:S(2)}) %collective-permute-start.6) | collective-permute-done | bytes 262176 | tf_op jit(solution)/shard_map/ppermute | solution.py:271
  33.1 3.9 %cross.2.refs_3_ = bf16[2,128,4,32,128]{4,3,2,1,0:T(8,128)(2,1)S(1)} custom-call(s32[6]{0:T(128)S(1)} %pad_add_fusion.params_ref, bf16[1,4,4,2,32,128]{5,4,3,2,1,0:T(8,128)(2,1)S(1)} %column_whiten.1.refs_0_, bf16[1,4,4,2,32,128]{5,4,3,2,1,0:T(8,128)(2,1)S(1)} %collective-permute-done.6.refs_1_, bf16[2,4,4,32,128]{4,3,2,1,0:T(8,128)(2,1)S(1)} %own_whiten.1.refs_2_), custom_call_target="tpu_custom_call" | custom-call | flops 67108864 | bytes 16777216 | tf_op jit(solution)/shard_map/cross/pallas_call | solution.py:382
  37.0 3.3 %collective-permute-done.5.refs_0_ = bf16[1,4,4,2,32,128]{5,4,3,2,1,0:T(8,128)(2,1)S(1)} collective-permute-done((bf16[1,4,4,2,32,128]{5,4,3,2,1,0:T(8,128)(2,1)S(1)}, bf16[1,4,4,2,32,128]{5,4,3,2,1,0:T(8,128)(2,1)S(1)}, u32[]{:S(2)}, u32[]{:S(2)}) %collective-permute-start.5) | collective-permute-done | bytes 262176 | tf_op jit(solution)/shard_map/ppermute | solution.py:271
  40.3 0.0 collective-permute-start.7
  40.3 1.5 %collective-permute-done.7.refs_1_ = bf16[1,4,4,2,32,128]{5,4,3,2,1,0:T(8,128)(2,1)S(1)} collective-permute-done((bf16[1,4,4,2,32,128]{5,4,3,2,1,0:T(8,128)(2,1)S(1)}, bf16[1,4,4,2,32,128]{5,4,3,2,1,0:T(8,128)(2,1)S(1)}, u32[]{:S(2)}, u32[]{:S(2)}) %collective-permute-start.7) | collective-permute-done | bytes 262176 | tf_op jit(solution)/shard_map/ppermute | solution.py:271
  41.9 5.6 %cross.3 = bf16[2,128,32,512]{3,2,1,0:T(8,128)(2,1)} custom-call(s32[6]{0:T(128)S(1)} %pad_add_fusion.params_ref, bf16[1,4,4,2,32,128]{5,4,3,2,1,0:T(8,128)(2,1)S(1)} %collective-permute-done.5.refs_0_, bf16[1,4,4,2,32,128]{5,4,3,2,1,0:T(8,128)(2,1)S(1)} %collective-permute-done.7.refs_1_, bf16[2,4,4,32,128]{4,3,2,1,0:T(8,128)(2,1)S(1)} %own_whiten.1.refs_2_, ...), custom_call_target="tpu_custom_call" | custom-call | flops 67108864 | bytes 16777216 | tf_op jit(solution)/shard_map/cross/pallas_call | solution.py:382
Async XLA Ops:
  1.7 18.5 %all-to-all-start = ((bf16[16,80,128]{2,1,0:T(8,128)(2,1)}), bf16[16,80,128]{2,1,0:T(8,128)(2,1)S(1)}, u32[]{:S(2)}, u32[]{:S(2)}) async-start(bf16[16,80,128]{2,1,0:T(8,128)(2,1)} %split.1), calls=%async_computation | async-start | bytes 655360 | tf_op jit(solution)/shard_map/all_to_all | solution.py:295
  9.1 16.6 %collective-permute-start.3 = (bf16[2,4,32,512]{3,2,1,0:T(8,128)(2,1)}, bf16[2,4,32,512]{3,2,1,0:T(8,128)(2,1)S(1)}, u32[]{:S(2)}, u32[]{:S(2)}) collective-permute-start(bf16[2,4,32,512]{3,2,1,0:T(8,128)(2,1)} %cur_ref.1), channel_id=1, source_target_pairs={{0,1},{1,2},{2,3},{3,4},{4,5},{5,6},{6,7},{7,8},{8,9},{9,10},{10,1... | collective-permute-start | bytes 786440 | tf_op jit(solution)/shard_map/ppermute | solution.py:303
  11.5 14.3 %collective-permute-start.4 = (bf16[2,4,32,512]{3,2,1,0:T(8,128)(2,1)}, bf16[2,4,32,512]{3,2,1,0:T(8,128)(2,1)S(1)}, u32[]{:S(2)}, u32[]{:S(2)}) collective-permute-start(bf16[2,4,32,512]{3,2,1,0:T(8,128)(2,1)} %cur_ref.1), channel_id=1, source_target_pairs={{1,0},{2,1},{3,2},{4,3},{5,4},{6,5},{7,6},{8,7},{9,8},{10,9},{11,1... | collective-permute-start | bytes 786440 | tf_op jit(solution)/shard_map/ppermute | solution.py:304
  12.8 0.7 %copy-start.1 = (s32[4,32]{1,0:T(4,128)S(1)}, s32[4,32]{1,0:T(4,128)}, u32[]{:S(2)}) copy-start(s32[4,32]{1,0:T(4,128)} %flags_ref.3) | copy-start | bytes 1540
  13.4 0.7 %copy-start.2 = (f32[2,8,65]{2,1,0:T(8,128)S(1)}, f32[2,8,65]{2,1,0:T(8,128)}, u32[]{:S(2)}) copy-start(f32[2,8,65]{2,1,0:T(8,128)} %bank_ref.1) | copy-start | bytes 12484
  14.1 0.7 %copy-start.3 = (s32[512]{0:T(512)S(1)}, s32[512]{0:T(512)}, u32[]{:S(2)}) copy-start(s32[512]{0:T(512)} %param.8) | copy-start | bytes 6148
  14.8 0.7 %copy-start.4 = (s32[4,32]{1,0:T(4,128)S(1)}, s32[4,32]{1,0:T(4,128)}, u32[]{:S(2)}) copy-start(s32[4,32]{1,0:T(4,128)} %offset_ref.1) | copy-start | bytes 1540
  21.3 7.5 %collective-permute-start.2 = (bf16[1,4,2,32,128]{4,3,2,1,0:T(8,128)(2,1)S(1)}, bf16[1,4,2,32,128]{4,3,2,1,0:T(8,128)(2,1)S(1)}, u32[]{:S(2)}, u32[]{:S(2)}) collective-permute-start(bf16[1,4,2,32,128]{4,3,2,1,0:T(8,128)(2,1)S(1)} %source_filter.1.refs_0_), channel_id=1, source_target_pairs={{0,12},{1,13},{2,14},{3,15},{4,8},{5,9},{6,10},{7,11},{8,4},{9,5},... | collective-permute-start | bytes 196616 | tf_op jit(solution)/shard_map/ppermute | solution.py:271
  24.1 6.3 %collective-permute-start.1 = (bf16[1,4,2,32,128]{4,3,2,1,0:T(8,128)(2,1)S(1)}, bf16[1,4,2,32,128]{4,3,2,1,0:T(8,128)(2,1)S(1)}, u32[]{:S(2)}, u32[]{:S(2)}) collective-permute-start(bf16[1,4,2,32,128]{4,3,2,1,0:T(8,128)(2,1)S(1)} %source_filter.1.refs_0_), channel_id=1, source_target_pairs={{0,8},{1,9},{2,10},{3,11},{4,12},{5,13},{6,14},{7,15},{8,0},{9,1},... | collective-permute-start | bytes 196616 | tf_op jit(solution)/shard_map/ppermute | solution.py:271
  24.1 6.3 %collective-permute-start = (bf16[1,4,2,32,128]{4,3,2,1,0:T(8,128)(2,1)S(1)}, bf16[1,4,2,32,128]{4,3,2,1,0:T(8,128)(2,1)S(1)}, u32[]{:S(2)}, u32[]{:S(2)}) collective-permute-start(bf16[1,4,2,32,128]{4,3,2,1,0:T(8,128)(2,1)S(1)} %source_filter.1.refs_0_), channel_id=1, source_target_pairs={{0,4},{1,5},{2,6},{3,7},{4,0},{5,1},{6,2},{7,3},{8,12},{9,13},{10,... | collective-permute-start | bytes 196616 | tf_op jit(solution)/shard_map/ppermute | solution.py:271
  25.7 1.0 %copy-start = (bf16[2,4,32,512]{3,2,1,0:T(8,128)(2,1)S(1)}, bf16[2,4,32,512]{3,2,1,0:T(8,128)(2,1)}, u32[]{:S(2)}) copy-start(bf16[2,4,32,512]{3,2,1,0:T(8,128)(2,1)} %cur_ref.1) | copy-start | bytes 786436
  31.5 1.6 %collective-permute-start.6 = (bf16[1,4,4,2,32,128]{5,4,3,2,1,0:T(8,128)(2,1)S(1)}, bf16[1,4,4,2,32,128]{5,4,3,2,1,0:T(8,128)(2,1)S(1)}, u32[]{:S(2)}, u32[]{:S(2)}) collective-permute-start(bf16[1,4,4,2,32,128]{5,4,3,2,1,0:T(8,128)(2,1)S(1)} %column_whiten.1.refs_0_), channel_id=1, source_target_pairs={{0,1},{1,0},{2,3},{3,2},{4,5},{5,4},{6,7},{7,6},{8,9},{9,8},{10,11... | collective-permute-start | bytes 786440 | tf_op jit(solution)/shard_map/ppermute | solution.py:271
  31.6 8.7 %collective-permute-start.5 = (bf16[1,4,4,2,32,128]{5,4,3,2,1,0:T(8,128)(2,1)S(1)}, bf16[1,4,4,2,32,128]{5,4,3,2,1,0:T(8,128)(2,1)S(1)}, u32[]{:S(2)}, u32[]{:S(2)}) collective-permute-start(bf16[1,4,4,2,32,128]{5,4,3,2,1,0:T(8,128)(2,1)S(1)} %column_whiten.1.refs_0_), channel_id=1, source_target_pairs={{0,2},{1,3},{2,0},{3,1},{4,6},{5,7},{6,4},{7,5},{8,10},{9,11},{10,... | collective-permute-start | bytes 786440 | tf_op jit(solution)/shard_map/ppermute | solution.py:271
  40.3 1.5 %collective-permute-start.7 = (bf16[1,4,4,2,32,128]{5,4,3,2,1,0:T(8,128)(2,1)S(1)}, bf16[1,4,4,2,32,128]{5,4,3,2,1,0:T(8,128)(2,1)S(1)}, u32[]{:S(2)}, u32[]{:S(2)}) collective-permute-start(bf16[1,4,4,2,32,128]{5,4,3,2,1,0:T(8,128)(2,1)S(1)} %collective-permute-done.5.refs_0_), channel_id=1, source_target_pairs={{0,1},{1,0},{2,3},{3,2},{4,5},{5,4},{6,7},{7,6},{8,9},{9,8},{10,11... | collective-permute-start | bytes 786440 | tf_op jit(solution)/shard_map/ppermute | solution.py:271
